TPU v7x, 128 devices: a whole 4x4x4 slice. The times are simulated.
128 devices in a mesh: tok: 4 (over x_hi, core), fin: 8 (over z, x_lo), fout: 4 (over y).
Axes of the slice: x: 4 (x_hi: 2, x_lo: 2; x = x_hi * 2 + x_lo), y: 4, z: 4, core: 2. Of those that a mesh axis runs over, the one named last changes fastest.
Arguments:
- inputs: bfloat16 [1024, 8192], P('tok', 'fin'), may hold values from -6 to 6
- upstream: bfloat16 [1024, 8192], P('tok', 'fin'), may hold values from -6 to 6
- loss_weight: int32 [1024], P('tok'), may hold values from 1 to 4
- pair_ids: int32 [1024], P('tok'), may hold values from 0 to 31
- margin: float32 [16], replicated, may hold values from -6 to 6
- w_gate: bfloat16 [8192, 16384], P('fin', ('tok', 'fout')), may hold values from -0.0625 to 0.0625
- w_up: bfloat16 [8192, 16384], P('fin', ('tok', 'fout')), may hold values from -0.0625 to 0.0625
- w_down: bfloat16 [16384, 8192], P(('tok', 'fout'), 'fin'), may hold values from -0.046875 to 0.046875
Outputs:
- grad_inputs: bfloat16 [1024, 8192], P(('tok', 'fout'), 'fin')
- grad_gate: bfloat16 [8192, 16384], P('fin', ('tok', 'fout'))
- grad_up: bfloat16 [8192, 16384], P('fin', ('tok', 'fout'))
- grad_down: bfloat16 [16384, 8192], P(('tok', 'fout'), 'fin')
Inputs may be any that keep to these rules, and one draw needn't show every extreme that they name: pair_ids[t] // 2 is the pair of token t; even ids mark the chosen side, odd ids the rejected side.
All inputs are finite; a program needn't handle non-finite values.
Results may differ from a plain program's by a relative error of at most 0.0059.
Values may be sent and summed in bfloat16 or wider, within the bound.
No kernel may reach another device: no remote copies, remote signals or barrier semaphores. Data moves between devices by JAX's collectives and lax.ppermute only.
A program may use at most 128 MiB of HBM per device.

v0:
```python
import jax
import jax.numpy as jnp
from jax import lax
from jax.sharding import PartitionSpec as P


def gate_backward(pre_gate, pre_up, grad_hidden):
    sigmoid_gate = jax.nn.sigmoid(pre_gate)
    activated = pre_gate * sigmoid_gate
    hidden = (activated * pre_up).astype(jnp.bfloat16)
    grad_pre_gate = (
        grad_hidden * pre_up * sigmoid_gate * (1.0 + pre_gate * (1.0 - sigmoid_gate))
    ).astype(jnp.bfloat16)
    grad_pre_up = (grad_hidden * activated).astype(jnp.bfloat16)
    return (hidden, grad_pre_gate, grad_pre_up)


def body(inputs, upstream, loss_weight, pair_ids, margin, w_gate, w_up, w_down):
    coefficient = jax.nn.sigmoid(-margin)
    side_table = jnp.stack([-coefficient, coefficient], axis=1).reshape(-1)
    columns = jnp.arange(side_table.shape[0], dtype=jnp.int32)
    picked = jnp.where(pair_ids[:, None] == columns[None, :], side_table[None, :], 0.0)
    row_scale = loss_weight.astype(jnp.float32) * jnp.sum(picked, axis=1)
    grad_out = (row_scale[:, None] * upstream.astype(jnp.float32)).astype(jnp.bfloat16)
    all_inputs, all_grad_out = (
        lax.all_gather(inputs, "tok", axis=0, tiled=True),
        lax.all_gather(grad_out, "tok", axis=0, tiled=True),
    )
    part_gate = jnp.dot(all_inputs, w_gate, preferred_element_type=jnp.float32)
    part_up = jnp.dot(all_inputs, w_up, preferred_element_type=jnp.float32)
    part_hidden = lax.dot_general(
        all_grad_out, w_down, (((1,), (1,)), ((), ())), preferred_element_type=jnp.float32
    )
    pre_gate, pre_up, grad_hidden = lax.psum((part_gate, part_up, part_hidden), "fin")
    hidden, grad_pre_gate, grad_pre_up = gate_backward(pre_gate, pre_up, grad_hidden)
    first = lax.dot_general(
        grad_pre_gate, w_gate, (((1,), (1,)), ((), ())), preferred_element_type=jnp.float32
    )
    second = lax.dot_general(
        grad_pre_up, w_up, (((1,), (1,)), ((), ())), preferred_element_type=jnp.float32
    )
    grad_inputs = lax.psum_scatter(
        first + second, ("tok", "fout"), scatter_dimension=0, tiled=True
    ).astype(jnp.bfloat16)
    grad_gate = lax.dot_general(
        all_inputs, grad_pre_gate, (((0,), (0,)), ((), ())), preferred_element_type=jnp.float32
    ).astype(jnp.bfloat16)
    grad_up = lax.dot_general(
        all_inputs, grad_pre_up, (((0,), (0,)), ((), ())), preferred_element_type=jnp.float32
    ).astype(jnp.bfloat16)
    grad_down = lax.dot_general(
        hidden, all_grad_out, (((0,), (0,)), ((), ())), preferred_element_type=jnp.float32
    ).astype(jnp.bfloat16)
    return (grad_inputs, grad_gate, grad_up, grad_down)


def solution(mesh):
    placed = (
        P("tok", "fin"),
        P("tok", "fin"),
        P("tok"),
        P("tok"),
        P(),
        P("fin", ("tok", "fout")),
        P("fin", ("tok", "fout")),
        P(("tok", "fout"), "fin"),
    )
    return jax.shard_map(
        body,
        mesh=mesh,
        in_specs=placed,
        out_specs=(
            P(("tok", "fout"), "fin"),
            P("fin", ("tok", "fout")),
            P("fin", ("tok", "fout")),
            P(("tok", "fout"), "fin"),
        ),
        check_vma=False,
    )
```

profile of v0, /device:TPU:0, one launch (start us, length us, event | category | flops | bytes accessed | tf_op | source)
XLA Modules:
  0.0 675.1 jit_solution(4658297857575994686)
XLA Ops:
  7.2 0.0 copy-start
  7.2 0.0 all-gather.5.cloned.1.call-start
  7.2 0.7 all-gather.5.cloned.1.call-update
  7.9 0.0 all-gather.3.cloned.1.call-start
  8.0 0.7 negate_bitcast_fusion
  8.6 0.1 copy.18
  8.7 0.1 broadcast_in_dim.17
  8.8 0.8 select_reduce_fusion
  9.6 0.7 convert_multiply_fusion
  10.3 2.0 multiply_convert_fusion.6
  12.3 0.0 all-gather.3.cloned.1.call-update
  12.3 0.0 all-reduce.3.cloned.1.call-start
  12.3 26.5 %all-gather.5.cloned.1.call-done = bf16[1024,1024]{1,0:T(8,128)(2,1)} async-done(((bf16[256,1024]{1,0:T(8,128)(2,1)}), bf16[1024,1024]{1,0:T(8,128)(2,1)}) %all-gather.5.cloned.1.call-update) | async-done | bytes 2097168 | tf_op jit(solution)/shard_map/all_gather | solution.py:26
  38.8 0.0 copy-done
  38.8 0.0 copy-start.3
  38.8 0.0 copy-start.5
  38.8 6.0 fusion.7
  44.8 0.0 copy-done.3
  44.8 0.0 copy-done.5
  44.8 4.3 fusion.6
  49.1 18.0 %all-gather.3.cloned.1.call-done = bf16[1024,1024]{1,0:T(8,128)(2,1)} async-done(((bf16[256,1024]{1,0:T(8,128)(2,1)}), bf16[1024,1024]{1,0:T(8,128)(2,1)}) %all-gather.3.cloned.1.call-update) | async-done | bytes 2097168 | tf_op jit(solution)/shard_map/all_gather | solution.py:27
  67.1 6.5 fusion.5
  73.7 0.0 all-reduce.3.cloned.1.call-update
  73.7 0.2 reduce-scatter.2.cloned.1.call-start
  73.9 497.9 %all-reduce.3.cloned.1.call-done = (f32[1024,1024]{1,0:T(8,128)}, f32[1024,1024]{1,0:T(8,128)}, f32[1024,1024]{1,0:T(8,128)}) async-done(((f32[1024,1024]{1,0:T(8,128)}, f32[1024,1024]{1,0:T(8,128)}, f32[1024,1024]{1,0:T(8,128)}), (f32[1024,1024]{1,0:T(8,128)}, f32[1024,1024]{1,0:T(8,128)}, f32[1024,1024]{1,0:T(8,128)})) %all-reduce.3.cloned.1.call-update) | async-done | bytes 12582928 | tf_op jit(solution)/shard_map/psum | solution.py:34
  571.8 5.9 multiply_convert_fusion.1
  577.7 0.0 copy-start.2
  577.7 0.0 copy-start.1
  577.8 0.0 copy-start.4
  577.8 2.4 fusion.8
  580.1 0.0 copy-done.2
  580.1 0.0 copy-done.1
  580.2 0.7 copy-done.4
  580.9 4.3 convolution_add_fusion
  585.2 0.0 reduce-scatter.2.cloned.1.call-update
  585.2 5.9 convert_bitcast_fusion.1
  591.2 3.9 copy.19
  595.1 6.2 convert_bitcast_fusion
  601.3 4.0 copy.20
  605.3 8.4 %fusion.2 = bf16[1024,1024]{1,0:T(8,128)(2,1)} fusion(bf16[1024,1024]{1,0:T(8,128)(2,1)} %all-gather.3.cloned.1.call-done, f32[1024,1024]{1,0:T(8,128)} %get-tuple-element.18, f32[1024,1024]{1,0:T(8,128)} %get-tuple-element.16), kind=kOutput, calls=%fused_computation.9 | convolution fusion | flops 2154823680 | bytes 12582912 | tf_op jit(solution)/shard_map/dot_general | solution.py:51
  613.7 53.3 %reduce-scatter.2.cloned.1.call-done = f32[64,1024]{1,0:T(8,128)} async-done(((f32[1024,1024]{1,0:T(8,128)}), f32[64,1024]{1,0:T(8,128)}) %reduce-scatter.2.cloned.1.call-update) | async-done | bytes 262160 | tf_op jit(solution)/shard_map/reduce_scatter | solution.py:42
  666.9 1.6 convert_element_type.41
  (1 shorter events, 0.0 us)
Async XLA Ops:
  7.2 31.6 %copy-start = (bf16[1024,1024]{1,0:T(8,128)(2,1)S(1)}, bf16[1024,1024]{1,0:T(8,128)(2,1)}, u32[]{:S(2)}) copy-start(bf16[1024,1024]{1,0:T(8,128)(2,1)} %param.13) | copy-start | bytes 6291460
  7.2 31.6 %all-gather.5.cloned.1.call-start = ((), (), s32[]{:S(2)}) async-start(), calls=%async_computation.2 | async-start | bytes 2621440 | tf_op jit(solution)/shard_map/all_gather | solution.py:26
  7.9 59.2 %all-gather.3.cloned.1.call-start = ((), (), s32[]{:S(2)}) async-start(), calls=%async_computation.1 | async-start | bytes 2621440 | tf_op jit(solution)/shard_map/all_gather | solution.py:27
  12.3 559.5 %all-reduce.3.cloned.1.call-start = ((), (), s32[]{:S(2)}) async-start(), calls=%async_computation.4 | async-start | bytes 25165824 | tf_op jit(solution)/shard_map/psum | solution.py:34
  38.8 6.0 copy-start.3
  38.8 6.0 copy-start.5
  73.7 593.2 %reduce-scatter.2.cloned.1.call-start = ((), (), s32[]{:S(2)}) async-start(), calls=%async_computation.3 | async-start | bytes 4456448 | tf_op jit(solution)/shard_map/reduce_scatter | solution.py:42
  577.7 2.4 copy-start.2
  577.7 2.4 copy-start.1
  577.8 3.1 copy-start.4
Sparse Core Ops, SparseCore 0:
  9.7 29.0 all-gather.4
  41.0 26.0 all-gather.2
  73.8 497.9 all-reduce.2
  585.3 81.5 reduce-scatter.1
where the time goes:
time: 675 us
  waiting for transfers between devices  596 us (88%)
  matrix products  44 us (7%)
  between operations  13.8 us (2%)
  other arithmetic  11.6 us (2%)
  local copies, waits for them, and re-layouts  8.86 us (1%)
    psum x1, waiting for transfers between devices, body(): lax.psum((part_gate, part_up, part_hidden), 'fin')  498 us
    reduce_scatter x1, waiting for transfers between devices, body(): lax.psum_scatter(first + second, ('tok', 'fout'), scatter_dimension=0, ti...  53.3 us
    all_gather x1, waiting for transfers between devices, body(): lax.all_gather(inputs, 'tok', axis=0, tiled=True)  26.5 us
    all_gather x1, waiting for transfers between devices, body(): lax.all_gather(grad_out, 'tok', axis=0, tiled=True)  18 us
  transfers between devices with their start and end apart: 4, of which 4 were waited for; matrix products, arithmetic and copies ran while one was open for 6% of the time, Pallas kernels for 0%

commit v1 on v0

v1 whole, which is shorter than its diff:
```python
import jax
import jax.numpy as jnp
from jax import lax
from jax.experimental import pallas as pl
from jax.experimental.pallas import tpu as pltpu
from jax.sharding import PartitionSpec as P

BF = jnp.bfloat16
F32 = jnp.float32
NT = (((1,), (1,)), ((), ()))
VMEM_LIMIT = 48 * 1024 * 1024


def params():
    return pltpu.CompilerParams(vmem_limit_bytes=VMEM_LIMIT)


def cost(flops, nbytes):
    return pl.CostEstimate(flops=flops, bytes_accessed=nbytes, transcendentals=0)


def fin_perm(x, dz, dx):
    pairs = [(z * 2 + l, ((z + dz) % 4) * 2 + (l ^ dx)) for z in range(4) for l in range(2)]
    return lax.ppermute(x, "fin", pairs)


def tok_perm(x, dh, dc):
    pairs = [(h * 2 + c, (h ^ dh) * 2 + (c ^ dc)) for h in range(2) for c in range(2)]
    return lax.ppermute(x, "tok", pairs)


def y_perm(x, dy):
    return lax.ppermute(x, "fout", [(y, (y + dy) % 4) for y in range(4)])


def row_start(z, lo, r, s):
    return pl.multiple_of((lax.rem(z + r, 4) * 2 + lax.bitwise_xor(lo, s)) * 32, 32)


def forward_kernel(idx, x, g, wg, wu, wd, plus, minus, keep, own, acc):
    z, lo = idx[0], idx[1]
    acc[0] = jnp.dot(x[...], wg[...], preferred_element_type=F32)
    acc[1] = jnp.dot(x[...], wu[...], preferred_element_type=F32)
    acc[2] = lax.dot_general(g[...], wd[...], NT, preferred_element_type=F32)

    def block(r, s):
        return acc[:, pl.ds(row_start(z, lo, r, s), 32), :]

    plus[0] = block(2, 0).astype(BF)
    plus[1] = block(1, 1).astype(BF)
    minus[0] = block(2, 1).astype(BF)
    minus[1] = block(3, 0).astype(BF)
    keep[0] = block(1, 0)
    keep[1] = block(3, 1)
    own[0] = block(0, 0)
    own[1] = block(0, 1)


def forward(idx, x, g, wg, wu, wd):
    tokens, depth = x.shape
    width = wg.shape[1]
    tile = 256
    full = pl.BlockSpec((tokens, depth), lambda i, s: (0, 0))
    part = pl.BlockSpec((2, 3, 32, tile), lambda i, s: (0, 0, 0, i))
    return pl.pallas_call(
        forward_kernel,
        grid_spec=pltpu.PrefetchScalarGridSpec(
            num_scalar_prefetch=1,
            grid=(width // tile,),
            in_specs=[
                full,
                full,
                pl.BlockSpec((depth, tile), lambda i, s: (0, i)),
                pl.BlockSpec((depth, tile), lambda i, s: (0, i)),
                pl.BlockSpec((tile, depth), lambda i, s: (i, 0)),
            ],
            out_specs=[part] * 4,
            scratch_shapes=[pltpu.VMEM((3, tokens, tile), F32)],
        ),
        out_shape=[
            jax.ShapeDtypeStruct((2, 3, 32, width), BF),
            jax.ShapeDtypeStruct((2, 3, 32, width), BF),
            jax.ShapeDtypeStruct((2, 3, 32, width), F32),
            jax.ShapeDtypeStruct((2, 3, 32, width), F32),
        ],
        compiler_params=params(),
        cost_estimate=cost(6 * tokens * depth * width, 6 * depth * width + 5 * 2**20),
        name="forward",
    )(idx, x, g, wg, wu, wd)


def pass_on_kernel(keep, from_minus, from_plus, plus, minus):
    plus[...] = (keep[0] + from_minus[0].astype(F32)).astype(BF)
    minus[...] = (keep[1] + from_plus[0].astype(F32)).astype(BF)


def pass_on(keep, from_minus, from_plus):
    shape = jax.ShapeDtypeStruct(keep.shape[1:], BF)
    return pl.pallas_call(
        pass_on_kernel,
        out_shape=[shape, shape],
        compiler_params=params(),
        cost_estimate=cost(keep.size, keep.size * 8),
        name="pass_on",
    )(keep, from_minus, from_plus)


def other_kernel(own, from_minus, last_plus, out):
    out[...] = (own[1] + from_minus[1].astype(F32) + last_plus[...].astype(F32)).astype(BF)


def other_half(own, from_minus, last_plus):
    return pl.pallas_call(
        other_kernel,
        out_shape=jax.ShapeDtypeStruct(own.shape[1:], BF),
        compiler_params=params(),
        cost_estimate=cost(own.size, own.size * 4),
        name="other_half",
    )(own, from_minus, last_plus)


def gate_kernel(own, from_plus, last_minus, across, out):
    total = own[0] + from_plus[1].astype(F32) + last_minus[...].astype(F32) + across[...].astype(F32)
    pre_gate, pre_up, grad_hidden = total[0], total[1], total[2]
    s = jax.nn.sigmoid(pre_gate)
    activated = pre_gate * s
    out[0] = (activated * pre_up).astype(BF)
    out[1] = (grad_hidden * pre_up * s * (1.0 + pre_gate * (1.0 - s))).astype(BF)
    out[2] = (grad_hidden * activated).astype(BF)


def gate(own, from_plus, last_minus, across):
    return pl.pallas_call(
        gate_kernel,
        out_shape=jax.ShapeDtypeStruct(own.shape[1:], BF),
        compiler_params=params(),
        cost_estimate=cost(own.size * 8, own.size * 5),
        name="gate",
    )(own, from_plus, last_minus, across)


def input_grad_kernel(idx, *refs):
    blocks, (wg, wu, plus, minus, keep, own, acts, acc) = refs[:8], refs[8:]
    z, lo, y = idx[0], idx[1], idx[2]

    @pl.when(pl.program_id(0) == 0)
    def _():
        for r in range(4):
            for s in range(2):
                acts[:, pl.ds(row_start(z, lo, r, s), 32), :] = blocks[2 * r + s][...]

    acc[...] = lax.dot_general(acts[1], wg[...], NT, preferred_element_type=F32) + lax.dot_general(
        acts[2], wu[...], NT, preferred_element_type=F32
    )

    def block(r, s):
        return acc[pl.ds(row_start(y, 0, r, s), 32), :]

    plus[0] = block(2, 0).astype(BF)
    plus[1] = block(1, 1).astype(BF)
    minus[0] = block(2, 1).astype(BF)
    minus[1] = block(3, 0).astype(BF)
    keep[0] = block(1, 0)
    keep[1] = block(3, 1)
    own[0] = block(0, 0)
    own[1] = block(0, 1)


def input_grad(idx, blocks, wg, wu):
    depth, width = wg.shape
    tile = 256
    part = pl.BlockSpec((2, 32, tile), lambda i, s: (0, 0, i))
    small = pl.BlockSpec((3, 32, width), lambda i, s: (0, 0, 0))
    weight = pl.BlockSpec((tile, width), lambda i, s: (i, 0))
    return pl.pallas_call(
        input_grad_kernel,
        grid_spec=pltpu.PrefetchScalarGridSpec(
            num_scalar_prefetch=1,
            grid=(depth // tile,),
            in_specs=[small] * 8 + [weight] * 2,
            out_specs=[part] * 4 + [pl.BlockSpec((3, 256, width), lambda i, s: (0, 0, 0))],
            scratch_shapes=[pltpu.VMEM((256, tile), F32)],
        ),
        out_shape=[
            jax.ShapeDtypeStruct((2, 32, depth), BF),
            jax.ShapeDtypeStruct((2, 32, depth), BF),
            jax.ShapeDtypeStruct((2, 32, depth), F32),
            jax.ShapeDtypeStruct((2, 32, depth), F32),
            jax.ShapeDtypeStruct((3, 256, width), BF),
        ],
        compiler_params=params(),
        cost_estimate=cost(4 * 256 * depth * width, 4 * depth * width + 4 * 2**20),
        name="input_grad",
    )(idx, *blocks, wg, wu)


def owned_kernel(own, from_minus, from_plus, last_minus, last_plus, out):
    out[0] = (own[0] + from_plus[1].astype(F32) + last_minus[...].astype(F32)).astype(out.dtype)
    out[1] = (own[1] + from_minus[1].astype(F32) + last_plus[...].astype(F32)).astype(out.dtype)


def owned(own, from_minus, from_plus, last_minus, last_plus, dtype):
    return pl.pallas_call(
        owned_kernel,
        out_shape=jax.ShapeDtypeStruct(own.shape, dtype),
        compiler_params=params(),
        cost_estimate=cost(own.size * 4, own.size * 10),
        name="owned",
    )(own, from_minus, from_plus, last_minus, last_plus)


def weight_grad_kernel(*refs):
    n = len(refs) // 3 - 1
    xs, gs, acts = refs[:n], refs[n : 2 * n], refs[2 * n : 3 * n]
    gate_out, up_out, down_out, xt = refs[3 * n :]

    @pl.when(pl.program_id(0) == 0)
    def _():
        for k in range(n):
            xt[:, k * 256 : (k + 1) * 256] = xs[k][...].T

    g = jnp.concatenate([r[...] for r in gs], axis=0)
    hidden = jnp.concatenate([r[0] for r in acts], axis=0)
    grad_gate = jnp.concatenate([r[1] for r in acts], axis=0)
    grad_up = jnp.concatenate([r[2] for r in acts], axis=0)
    gate_out[...] = jnp.dot(xt[...], grad_gate, preferred_element_type=F32).astype(BF)
    up_out[...] = jnp.dot(xt[...], grad_up, preferred_element_type=F32).astype(BF)
    down_out[...] = jnp.dot(hidden.T, g, preferred_element_type=F32).astype(BF)


def weight_grad(xs, gs, acts):
    tokens, depth = xs[0].shape
    width = acts[0].shape[2]
    n = len(xs)
    tile = 256
    full = pl.BlockSpec((tokens, depth), lambda i: (0, 0))
    return pl.pallas_call(
        weight_grad_kernel,
        grid=(width // tile,),
        in_specs=[full] * (2 * n) + [pl.BlockSpec((3, tokens, tile), lambda i: (0, 0, i))] * n,
        out_specs=[
            pl.BlockSpec((depth, tile), lambda i: (0, i)),
            pl.BlockSpec((depth, tile), lambda i: (0, i)),
            pl.BlockSpec((tile, depth), lambda i: (i, 0)),
        ],
        out_shape=[
            jax.ShapeDtypeStruct((depth, width), BF),
            jax.ShapeDtypeStruct((depth, width), BF),
            jax.ShapeDtypeStruct((width, depth), BF),
        ],
        scratch_shapes=[pltpu.VMEM((depth, n * tokens), BF)],
        compiler_params=params(),
        cost_estimate=cost(6 * n * tokens * depth * width, 16 * 2**20),
        name="weight_grad",
    )(*xs, *gs, *acts)


def body(inputs, upstream, loss_weight, pair_ids, margin, w_gate, w_up, w_down):
    fin = lax.axis_index("fin")
    idx = jnp.stack([fin // 2, fin % 2, lax.axis_index("fout")]).astype(jnp.int32)

    coefficient = jax.nn.sigmoid(-margin)
    side_table = jnp.stack([-coefficient, coefficient], axis=1).reshape(-1)
    columns = jnp.arange(side_table.shape[0], dtype=jnp.int32)
    picked = jnp.where(pair_ids[:, None] == columns[None, :], side_table[None, :], 0.0)
    row_scale = loss_weight.astype(F32) * jnp.sum(picked, axis=1)
    grad_out = (row_scale[:, None] * upstream.astype(F32)).astype(BF)

    x1, x2 = tok_perm(inputs, 0, 1), tok_perm(inputs, 1, 0)
    g1, g2 = tok_perm(grad_out, 0, 1), tok_perm(grad_out, 1, 0)
    x3, g3 = tok_perm(x2, 0, 1), tok_perm(g2, 0, 1)
    xs, gs = [inputs, x1, x2, x3], [grad_out, g1, g2, g3]

    acts, sums = [], []
    for k, offset in enumerate([(0, 0), (0, 1), (1, 0), (1, 1)]):
        plus, minus, keep, own = forward(idx, xs[k], gs[k], w_gate, w_up, w_down)
        from_minus, from_plus = fin_perm(plus, 1, 0), fin_perm(minus, 3, 0)
        plus, minus = pass_on(keep, from_minus, from_plus)
        last_minus, last_plus = fin_perm(plus, 1, 0), fin_perm(minus, 3, 0)
        across = fin_perm(other_half(own, from_minus, last_plus), 0, 1)
        mine = gate(own, from_plus, last_minus, across)

        theirs = fin_perm(mine, 0, 1)
        m_minus, m_plus = fin_perm(mine, 1, 0), fin_perm(mine, 3, 0)
        t_minus, t_plus = fin_perm(theirs, 1, 0), fin_perm(theirs, 3, 0)
        m_far, t_far = fin_perm(m_minus, 1, 0), fin_perm(t_plus, 3, 0)
        blocks = [mine, theirs, m_plus, t_plus, m_far, t_far, m_minus, t_minus]

        plus, minus, keep, own, act = input_grad(idx, blocks, w_gate, w_up)
        acts.append(act)
        from_minus, from_plus = y_perm(plus, 1), y_perm(minus, 3)
        plus, minus = pass_on(keep, from_minus, from_plus)
        last_minus, last_plus = y_perm(plus, 1), y_perm(minus, 3)
        part = owned(own, from_minus, from_plus, last_minus, last_plus, BF if k else F32)
        sums.append(tok_perm(part, *offset) if k else part)
    grad_gate, grad_up, grad_down = weight_grad(xs, gs, acts)
    total = sums[0] + sums[1].astype(F32) + sums[2].astype(F32) + sums[3].astype(F32)
    grad_inputs = total.astype(BF).reshape(-1, total.shape[-1])
    return (grad_inputs, grad_gate, grad_up, grad_down)


def solution(mesh):
    placed = (
        P("tok", "fin"),
        P("tok", "fin"),
        P("tok"),
        P("tok"),
        P(),
        P("fin", ("tok", "fout")),
        P("fin", ("tok", "fout")),
        P(("tok", "fout"), "fin"),
    )
    return jax.shard_map(
        body,
        mesh=mesh,
        in_specs=placed,
        out_specs=(
            P(("tok", "fout"), "fin"),
            P("fin", ("tok", "fout")),
            P("fin", ("tok", "fout")),
            P(("tok", "fout"), "fin"),
        ),
        check_vma=False,
    )
```

time: 675 us -> 217 us (0.32)
  waiting for transfers between devices: 596 us -> 66.5 us
  starting transfers between devices: 0.34 us -> 87.4 us
  Pallas kernels: 0 us -> 51.6 us
  matrix products: 44 us -> 0 us
  between operations: 13.8 us -> 1.16 us
  other arithmetic: 11.6 us -> 4.12 us
    psum x1 -> x0, waiting for transfers between devices: 498 us -> none  [body(): lax.psum((part_gate, part_up, part_hidden), 'fin')]
    ppermute x0 -> x73, starting transfers between devices: none -> 87.4 us  [the longest x48 54 us: fin_perm(): return lax.ppermute(x, 'fin', pairs)]
    ppermute x0 -> x73, waiting for transfers between devices: none -> 66.5 us  [the longest x48 54.9 us: fin_perm(): return lax.ppermute(x, 'fin', pairs)]
    reduce_scatter x1 -> x0, waiting for transfers between devices: 53.3 us -> none  [body(): lax.psum_scatter(first + second, ('tok', 'fout'), scatter_dimension=0, ti...]
    pallas_call x0 -> x29, Pallas kernels: none -> 51.6 us  [the longest x4 22 us: forward(): pl.pallas_call(forward_kernel, grid_spec=pltpu.PrefetchScalarGridSpec(num...]
    all_gather x2 -> x0, waiting for transfers between devices: 44.5 us -> none  [the longest x1 26.5 us: body(): lax.all_gather(inputs, 'tok', axis=0, tiled=True)]
    dot_general x8 -> x0, matrix products: 44 us -> none  [the longest x1 8.38 us: body(): lax.dot_general(hidden, all_grad_out, (((0,), (0,)), ((), ())), preferred...]
    convert_element_type x3 -> x2, other arithmetic: 9.51 us -> 1.92 us  [the longest x1 1.19 us: body(): grad_out = (row_scale[:, None] * upstream.astype(F32)).astype(BF)]
  transfers between devices with their start and end apart: 4 -> 73, of which waited for: 4 -> 18; matrix products, arithmetic and copies ran while one was open for 6% -> 0% of each run, Pallas kernels for 0% -> 21%
where the time goes in v1:
time: 217 us; the launch traced here: 215 us
  starting transfers between devices  87.4 us (40%)
  waiting for transfers between devices  66.5 us (31%)
  Pallas kernels  51.6 us (24%)
  other arithmetic  4.12 us (2%)
  local copies, waits for them, and re-layouts  4.06 us (2%)
    ppermute x48, waiting for transfers between devices, fin_perm(): return lax.ppermute(x, 'fin', pairs)  54.9 us
    ppermute x48, starting transfers between devices, fin_perm(): return lax.ppermute(x, 'fin', pairs)  54 us
    ppermute x16, starting transfers between devices, y_perm(): return lax.ppermute(x, 'fout', [(y, (y + dy) % 4) for y in range(4)])  26 us
    pallas_call x4, Pallas kernels, forward(): pl.pallas_call(forward_kernel, grid_spec=pltpu.PrefetchScalarGridSpec(num...  22 us
    pallas_call x4, Pallas kernels, input_grad(): pl.pallas_call(input_grad_kernel, grid_spec=pltpu.PrefetchScalarGridSpec(...  17.8 us
    ppermute x9, waiting for transfers between devices, tok_perm(): return lax.ppermute(x, 'tok', pairs)  11.4 us
    pallas_call x1, Pallas kernels, weight_grad(): pl.pallas_call(weight_grad_kernel, grid=(width // tile,), in_specs=[full]...  10.3 us
    ppermute x9, starting transfers between devices, tok_perm(): return lax.ppermute(x, 'tok', pairs)  7.48 us
  transfers between devices with their start and end apart: 73, of which 18 were waited for; matrix products, arithmetic and copies ran while one was open for 0% of the time, Pallas kernels for 21%

profile of v1, /device:TPU:0, one launch (start us, length us, event | category | flops | bytes accessed | tf_op | source)
XLA Modules:
  0.0 214.9 jit_solution(18133551243946811119)
XLA Ops:
  5.8 5.6 %forward.4 = (bf16[2,3,32,1024]{3,2,1,0:T(8,128)(2,1)S(1)}, bf16[2,3,32,1024]{3,2,1,0:T(8,128)(2,1)S(1)}, f32[2,3,32,1024]{3,2,1,0:T(8,128)S(1)}, f32[2,3,32,1024]{3,2,1,0:T(8,128)S(1)}) custom-call(s32[3]{0:T(128)S(1)} %pad_add_fusion.idx, bf16[256,1024]{1,0:T(8,128)(2,1)} %refs_0_.1, bf16[256,1024]{1,0:T(8,128)(2,1)S(1)} %multiply_convert_fusion.g.refs_4_, ...), custom_call_target="tpu_custom_call" | custom-call | flops 1610612736 | bytes 11534336 | tf_op jit(solution)/shard_map/forward/pallas_call | solution.py:65
  11.5 4.2 %collective-permute-start = (bf16[2,3,32,1024]{3,2,1,0:T(8,128)(2,1)S(1)}, bf16[2,3,32,1024]{3,2,1,0:T(8,128)(2,1)S(1)}, u32[]{:S(2)}, u32[]{:S(2)}) collective-permute-start(bf16[2,3,32,1024]{3,2,1,0:T(8,128)(2,1)S(1)} %get-tuple-element.60), channel_id=1, source_target_pairs={{0,24},{4,28},{8,0},{12,4},{16,8},{20,12},{24,16},{28,20},{1,25},{... | collective-permute-start | bytes 1179656 | tf_op jit(solution)/shard_map/ppermute | solution.py:24
  15.7 3.0 %collective-permute-start.35 = (bf16[256,1024]{1,0:T(8,128)(2,1)}, bf16[256,1024]{1,0:T(8,128)(2,1)S(1)}, u32[]{:S(2)}, u32[]{:S(2)}) collective-permute-start(bf16[256,1024]{1,0:T(8,128)(2,1)} %refs_0_.1), channel_id=1, source_target_pairs={{0,64},{32,96},{64,0},{96,32},{1,65},{33,97},{65,1},{97,33},{2,66}... | collective-permute-start | bytes 1572872 | tf_op jit(solution)/shard_map/ppermute | solution.py:29
  19.2 4.8 %collective-permute-done.from_plus = bf16[2,3,32,1024]{3,2,1,0:T(8,128)(2,1)S(1)} collective-permute-done((bf16[2,3,32,1024]{3,2,1,0:T(8,128)(2,1)S(1)}, bf16[2,3,32,1024]{3,2,1,0:T(8,128)(2,1)S(1)}, u32[]{:S(2)}, u32[]{:S(2)}) %collective-permute-start) | collective-permute-done | bytes 393248 | tf_op jit(solution)/shard_map/ppermute | solution.py:24
  24.0 6.4 %collective-permute-done.1.from_minus = bf16[2,3,32,1024]{3,2,1,0:T(8,128)(2,1)S(1)} collective-permute-done((bf16[2,3,32,1024]{3,2,1,0:T(8,128)(2,1)S(1)}, bf16[2,3,32,1024]{3,2,1,0:T(8,128)(2,1)S(1)}, u32[]{:S(2)}, u32[]{:S(2)}) %collective-permute-start.1) | collective-permute-done | bytes 393248 | tf_op jit(solution)/shard_map/ppermute | solution.py:24
  30.6 1.7 collective-permute-done.35.x.refs_2_
  32.2 9.8 %collective-permute-done.36.g.refs_6_ = bf16[256,1024]{1,0:T(8,128)(2,1)S(1)} collective-permute-done((bf16[256,1024]{1,0:T(8,128)(2,1)S(1)}, bf16[256,1024]{1,0:T(8,128)(2,1)S(1)}, u32[]{:S(2)}, u32[]{:S(2)}) %collective-permute-start.36) | collective-permute-done | bytes 524320 | tf_op jit(solution)/shard_map/ppermute | solution.py:29
  42.0 5.5 %forward.6 = (bf16[2,3,32,1024]{3,2,1,0:T(8,128)(2,1)S(1)}, bf16[2,3,32,1024]{3,2,1,0:T(8,128)(2,1)S(1)}, f32[2,3,32,1024]{3,2,1,0:T(8,128)S(1)}, f32[2,3,32,1024]{3,2,1,0:T(8,128)S(1)}) custom-call(s32[3]{0:T(128)S(1)} %pad_add_fusion.idx, bf16[256,1024]{1,0:T(8,128)(2,1)S(1)} %collective-permute-done.35.x.refs_2_, ...), custom_call_target="tpu_custom_call" | custom-call | flops 1610612736 | bytes 11534336 | tf_op jit(solution)/shard_map/forward/pallas_call | solution.py:65
  47.9 1.6 collective-permute-start.2
  51.3 5.5 %collective-permute-done.2.last_minus = bf16[3,32,1024]{2,1,0:T(8,128)(2,1)S(1)} collective-permute-done((bf16[3,32,1024]{2,1,0:T(8,128)(2,1)S(1)}, bf16[3,32,1024]{2,1,0:T(8,128)(2,1)S(1)}, u32[]{:S(2)}, u32[]{:S(2)}) %collective-permute-start.2) | collective-permute-done | bytes 196640 | tf_op jit(solution)/shard_map/ppermute | solution.py:24
  56.8 5.5 %forward.5 = (bf16[2,3,32,1024]{3,2,1,0:T(8,128)(2,1)S(1)}, bf16[2,3,32,1024]{3,2,1,0:T(8,128)(2,1)S(1)}, f32[2,3,32,1024]{3,2,1,0:T(8,128)S(1)}, f32[2,3,32,1024]{3,2,1,0:T(8,128)S(1)}) custom-call(s32[3]{0:T(128)S(1)} %pad_add_fusion.idx, bf16[256,1024]{1,0:T(8,128)(2,1)S(1)} %collective-permute-done.16.x.refs_1_, ...), custom_call_target="tpu_custom_call" | custom-call | flops 1610612736 | bytes 11534336 | tf_op jit(solution)/shard_map/forward/pallas_call | solution.py:65
  62.4 2.0 collective-permute-start.19
  64.6 1.7 collective-permute-start.5
  66.4 7.5 %collective-permute-done.18.from_plus = bf16[2,3,32,1024]{3,2,1,0:T(8,128)(2,1)S(1)} collective-permute-done((bf16[2,3,32,1024]{3,2,1,0:T(8,128)(2,1)S(1)}, bf16[2,3,32,1024]{3,2,1,0:T(8,128)(2,1)S(1)}, u32[]{:S(2)}, u32[]{:S(2)}) %collective-permute-start.18) | collective-permute-done | bytes 393248 | tf_op jit(solution)/shard_map/ppermute | solution.py:24
  76.5 2.7 %collective-permute-start.40 = (bf16[3,32,1024]{2,1,0:T(8,128)(2,1)S(1)}, bf16[3,32,1024]{2,1,0:T(8,128)(2,1)S(1)}, u32[]{:S(2)}, u32[]{:S(2)}) collective-permute-start(bf16[3,32,1024]{2,1,0:T(8,128)(2,1)S(1)} %get-tuple-element.88), channel_id=1, source_target_pairs={{0,24},{4,28},{8,0},{12,4},{16,8},{20,12},{24,16},{28,20},{1,25},{... | collective-permute-start | bytes 589832 | tf_op jit(solution)/shard_map/ppermute | solution.py:24
  79.2 5.5 %forward.7 = (bf16[2,3,32,1024]{3,2,1,0:T(8,128)(2,1)S(1)}, bf16[2,3,32,1024]{3,2,1,0:T(8,128)(2,1)S(1)}, f32[2,3,32,1024]{3,2,1,0:T(8,128)S(1)}, f32[2,3,32,1024]{3,2,1,0:T(8,128)S(1)}) custom-call(s32[3]{0:T(128)S(1)} %pad_add_fusion.idx, bf16[256,1024]{1,0:T(8,128)(2,1)S(1)} %collective-permute-done.54.x.refs_3_, ...), custom_call_target="tpu_custom_call" | custom-call | flops 1610612736 | bytes 11534336 | tf_op jit(solution)/shard_map/forward/pallas_call | solution.py:65
  87.3 2.9 %collective-permute-start.21 = (bf16[3,32,1024]{2,1,0:T(8,128)(2,1)S(1)}, bf16[3,32,1024]{2,1,0:T(8,128)(2,1)S(1)}, u32[]{:S(2)}, u32[]{:S(2)}) collective-permute-start(bf16[3,32,1024]{2,1,0:T(8,128)(2,1)S(1)} %get-tuple-element.76), channel_id=1, source_target_pairs={{0,24},{4,28},{8,0},{12,4},{16,8},{20,12},{24,16},{28,20},{1,25},{... | collective-permute-start | bytes 589832 | tf_op jit(solution)/shard_map/ppermute | solution.py:24
  91.7 9.5 %collective-permute-done.20.last_minus = bf16[3,32,1024]{2,1,0:T(8,128)(2,1)S(1)} collective-permute-done((bf16[3,32,1024]{2,1,0:T(8,128)(2,1)S(1)}, bf16[3,32,1024]{2,1,0:T(8,128)(2,1)S(1)}, u32[]{:S(2)}, u32[]{:S(2)}) %collective-permute-start.20) | collective-permute-done | bytes 196640 | tf_op jit(solution)/shard_map/ppermute | solution.py:24
  101.2 1.6 collective-permute-start.41
  102.9 3.2 %collective-permute-start.10 = (bf16[3,32,1024]{2,1,0:T(8,128)(2,1)S(1)}, bf16[3,32,1024]{2,1,0:T(8,128)(2,1)S(1)}, u32[]{:S(2)}, u32[]{:S(2)}) collective-permute-start(bf16[3,32,1024]{2,1,0:T(8,128)(2,1)S(1)} %collective-permute-done.7.refs_3_), channel_id=1, source_target_pairs={{0,24},{4,28},{8,0},{12,4},{16,8},{20,12},{24,16},{28,20},{1,25},{... | collective-permute-start | bytes 589832 | tf_op jit(solution)/shard_map/ppermute | solution.py:24
  106.3 1.6 collective-permute-start.22
  108.0 1.7 collective-permute-start.59
  110.7 1.7 collective-permute-done.11.refs_7_
  112.8 1.6 collective-permute-start.45
  114.4 4.5 %input_grad.4 = (bf16[2,32,1024]{2,1,0:T(8,128)(2,1)S(1)}, bf16[2,32,1024]{2,1,0:T(8,128)(2,1)S(1)}, f32[2,32,1024]{2,1,0:T(8,128)S(1)}, f32[2,32,1024]{2,1,0:T(8,128)S(1)}, bf16[3,256,1024]{2,1,0:T(8,128)(2,1)S(1)}) custom-call(s32[3]{0:T(128)S(1)} %pad_add_fusion.idx, bf16[3,32,1024]{2,1,0:T(8,128)(2,1)S(1)} %gate.4.refs_0_, ...), custom_call_target="tpu_custom_call" | custom-call | flops 1073741824 | bytes 8388608 | tf_op jit(solution)/shard_map/input_grad/pallas_call | solution.py:175
  118.9 1.6 collective-permute-start.12
  123.9 2.3 %collective-permute-start.24 = (bf16[3,32,1024]{2,1,0:T(8,128)(2,1)S(1)}, bf16[3,32,1024]{2,1,0:T(8,128)(2,1)S(1)}, u32[]{:S(2)}, u32[]{:S(2)}) collective-permute-start(bf16[3,32,1024]{2,1,0:T(8,128)(2,1)S(1)} %gate.5.refs_0_), channel_id=1, source_target_pairs={{0,24},{4,28},{8,0},{12,4},{16,8},{20,12},{24,16},{28,20},{1,25},{... | collective-permute-start | bytes 589832 | tf_op jit(solution)/shard_map/ppermute | solution.py:24
  126.2 3.3 %collective-permute-done.58.last_minus = bf16[3,32,1024]{2,1,0:T(8,128)(2,1)S(1)} collective-permute-done((bf16[3,32,1024]{2,1,0:T(8,128)(2,1)S(1)}, bf16[3,32,1024]{2,1,0:T(8,128)(2,1)S(1)}, u32[]{:S(2)}, u32[]{:S(2)}) %collective-permute-start.58) | collective-permute-done | bytes 196640 | tf_op jit(solution)/shard_map/ppermute | solution.py:24
  132.1 2.9 %collective-permute-start.25 = (bf16[3,32,1024]{2,1,0:T(8,128)(2,1)S(1)}, bf16[3,32,1024]{2,1,0:T(8,128)(2,1)S(1)}, u32[]{:S(2)}, u32[]{:S(2)}) collective-permute-start(bf16[3,32,1024]{2,1,0:T(8,128)(2,1)S(1)} %collective-permute-done.23.refs_1_), channel_id=1, source_target_pairs={{0,24},{4,28},{8,0},{12,4},{16,8},{20,12},{24,16},{28,20},{1,25},{... | collective-permute-start | bytes 589832 | tf_op jit(solution)/shard_map/ppermute | solution.py:24
  135.7 3.8 %collective-permute-done.46.refs_4_ = bf16[3,32,1024]{2,1,0:T(8,128)(2,1)S(1)} collective-permute-done((bf16[3,32,1024]{2,1,0:T(8,128)(2,1)S(1)}, bf16[3,32,1024]{2,1,0:T(8,128)(2,1)S(1)}, u32[]{:S(2)}, u32[]{:S(2)}) %collective-permute-start.46) | collective-permute-done | bytes 196640 | tf_op jit(solution)/shard_map/ppermute | solution.py:24
  139.5 4.2 %collective-permute-done.48.refs_7_ = bf16[3,32,1024]{2,1,0:T(8,128)(2,1)S(1)} collective-permute-done((bf16[3,32,1024]{2,1,0:T(8,128)(2,1)S(1)}, bf16[3,32,1024]{2,1,0:T(8,128)(2,1)S(1)}, u32[]{:S(2)}, u32[]{:S(2)}) %collective-permute-start.48) | collective-permute-done | bytes 196640 | tf_op jit(solution)/shard_map/ppermute | solution.py:24
  143.7 2.0 collective-permute-start.64
  147.8 4.2 %collective-permute-done.29.refs_7_ = bf16[3,32,1024]{2,1,0:T(8,128)(2,1)S(1)} collective-permute-done((bf16[3,32,1024]{2,1,0:T(8,128)(2,1)S(1)}, bf16[3,32,1024]{2,1,0:T(8,128)(2,1)S(1)}, u32[]{:S(2)}, u32[]{:S(2)}) %collective-permute-start.29) | collective-permute-done | bytes 196640 | tf_op jit(solution)/shard_map/ppermute | solution.py:24
  152.0 2.0 collective-permute-start.67
  154.0 2.1 collective-permute-done.64.refs_6_
  156.1 3.2 %collective-permute-start.66 = (bf16[3,32,1024]{2,1,0:T(8,128)(2,1)S(1)}, bf16[3,32,1024]{2,1,0:T(8,128)(2,1)S(1)}, u32[]{:S(2)}, u32[]{:S(2)}) collective-permute-start(bf16[3,32,1024]{2,1,0:T(8,128)(2,1)S(1)} %collective-permute-done.63.refs_3_), channel_id=1, source_target_pairs={{0,24},{4,28},{8,0},{12,4},{16,8},{20,12},{24,16},{28,20},{1,25},{... | collective-permute-start | bytes 589832 | tf_op jit(solution)/shard_map/ppermute | solution.py:24
  159.3 4.5 %input_grad.6 = (bf16[2,32,1024]{2,1,0:T(8,128)(2,1)S(1)}, bf16[2,32,1024]{2,1,0:T(8,128)(2,1)S(1)}, f32[2,32,1024]{2,1,0:T(8,128)S(1)}, f32[2,32,1024]{2,1,0:T(8,128)S(1)}, bf16[3,256,1024]{2,1,0:T(8,128)(2,1)S(1)}) custom-call(s32[3]{0:T(128)S(1)} %pad_add_fusion.idx, bf16[3,32,1024]{2,1,0:T(8,128)(2,1)S(1)} %gate.6.refs_0_, ...), custom_call_target="tpu_custom_call" | custom-call | flops 1073741824 | bytes 8388608 | tf_op jit(solution)/shard_map/input_grad/pallas_call | solution.py:175
  166.9 4.5 %input_grad.5 = (bf16[2,32,1024]{2,1,0:T(8,128)(2,1)S(1)}, bf16[2,32,1024]{2,1,0:T(8,128)(2,1)S(1)}, f32[2,32,1024]{2,1,0:T(8,128)S(1)}, f32[2,32,1024]{2,1,0:T(8,128)S(1)}, bf16[3,256,1024]{2,1,0:T(8,128)(2,1)S(1)}) custom-call(s32[3]{0:T(128)S(1)} %pad_add_fusion.idx, bf16[3,32,1024]{2,1,0:T(8,128)(2,1)S(1)} %gate.5.refs_0_, ...), custom_call_target="tpu_custom_call" | custom-call | flops 1073741824 | bytes 8388608 | tf_op jit(solution)/shard_map/input_grad/pallas_call | solution.py:175
  172.6 2.7 %collective-permute-start.50 = (bf16[2,32,1024]{2,1,0:T(8,128)(2,1)S(1)}, bf16[2,32,1024]{2,1,0:T(8,128)(2,1)S(1)}, u32[]{:S(2)}, u32[]{:S(2)}) collective-permute-start(bf16[2,32,1024]{2,1,0:T(8,128)(2,1)S(1)} %get-tuple-element.91), channel_id=1, source_target_pairs={{0,3},{1,0},{2,1},{3,2},{4,7},{5,4},{6,5},{7,6},{8,11},{9,8},{10,9... | collective-permute-start | bytes 393224 | tf_op jit(solution)/shard_map/ppermute | solution.py:33
  175.3 3.2 %collective-permute-start.31 = (bf16[2,32,1024]{2,1,0:T(8,128)(2,1)S(1)}, bf16[2,32,1024]{2,1,0:T(8,128)(2,1)S(1)}, u32[]{:S(2)}, u32[]{:S(2)}) collective-permute-start(bf16[2,32,1024]{2,1,0:T(8,128)(2,1)S(1)} %get-tuple-element.79), channel_id=1, source_target_pairs={{0,3},{1,0},{2,1},{3,2},{4,7},{5,4},{6,5},{7,6},{8,11},{9,8},{10,9... | collective-permute-start | bytes 393224 | tf_op jit(solution)/shard_map/ppermute | solution.py:33
  178.5 4.5 %input_grad.7 = (bf16[2,32,1024]{2,1,0:T(8,128)(2,1)S(1)}, bf16[2,32,1024]{2,1,0:T(8,128)(2,1)S(1)}, f32[2,32,1024]{2,1,0:T(8,128)S(1)}, f32[2,32,1024]{2,1,0:T(8,128)S(1)}, bf16[3,256,1024]{2,1,0:T(8,128)(2,1)S(1)}) custom-call(s32[3]{0:T(128)S(1)} %pad_add_fusion.idx, bf16[3,32,1024]{2,1,0:T(8,128)(2,1)S(1)} %gate.7.refs_0_, ...), custom_call_target="tpu_custom_call" | custom-call | flops 1073741824 | bytes 8388608 | tf_op jit(solution)/shard_map/input_grad/pallas_call | solution.py:175
  183.1 3.2 %collective-permute-start.69 = (bf16[2,32,1024]{2,1,0:T(8,128)(2,1)S(1)}, bf16[2,32,1024]{2,1,0:T(8,128)(2,1)S(1)}, u32[]{:S(2)}, u32[]{:S(2)}) collective-permute-start(bf16[2,32,1024]{2,1,0:T(8,128)(2,1)S(1)} %get-tuple-element.103), channel_id=1, source_target_pairs={{0,3},{1,0},{2,1},{3,2},{4,7},{5,4},{6,5},{7,6},{8,11},{9,8},{10,9... | collective-permute-start | bytes 393224 | tf_op jit(solution)/shard_map/ppermute | solution.py:33
  186.5 3.3 %collective-permute-start.15 = (bf16[32,1024]{1,0:T(8,128)(2,1)S(1)}, bf16[32,1024]{1,0:T(8,128)(2,1)S(1)}, u32[]{:S(2)}, u32[]{:S(2)}) collective-permute-start(bf16[32,1024]{1,0:T(8,128)(2,1)S(1)} %get-tuple-element.70), channel_id=1, source_target_pairs={{0,3},{1,0},{2,1},{3,2},{4,7},{5,4},{6,5},{7,6},{8,11},{9,8},{10,9... | collective-permute-start | bytes 196616 | tf_op jit(solution)/shard_map/ppermute | solution.py:33
  189.9 3.2 %collective-permute-start.52 = (bf16[32,1024]{1,0:T(8,128)(2,1)S(1)}, bf16[32,1024]{1,0:T(8,128)(2,1)S(1)}, u32[]{:S(2)}, u32[]{:S(2)}) collective-permute-start(bf16[32,1024]{1,0:T(8,128)(2,1)S(1)} %get-tuple-element.94), channel_id=1, source_target_pairs={{0,3},{1,0},{2,1},{3,2},{4,7},{5,4},{6,5},{7,6},{8,11},{9,8},{10,9... | collective-permute-start | bytes 196616 | tf_op jit(solution)/shard_map/ppermute | solution.py:33
  193.2 3.3 %collective-permute-start.33 = (bf16[32,1024]{1,0:T(8,128)(2,1)S(1)}, bf16[32,1024]{1,0:T(8,128)(2,1)S(1)}, u32[]{:S(2)}, u32[]{:S(2)}) collective-permute-start(bf16[32,1024]{1,0:T(8,128)(2,1)S(1)} %get-tuple-element.82), channel_id=1, source_target_pairs={{0,3},{1,0},{2,1},{3,2},{4,7},{5,4},{6,5},{7,6},{8,11},{9,8},{10,9... | collective-permute-start | bytes 196616 | tf_op jit(solution)/shard_map/ppermute | solution.py:33
  196.5 3.2 %collective-permute-start.71 = (bf16[32,1024]{1,0:T(8,128)(2,1)S(1)}, bf16[32,1024]{1,0:T(8,128)(2,1)S(1)}, u32[]{:S(2)}, u32[]{:S(2)}) collective-permute-start(bf16[32,1024]{1,0:T(8,128)(2,1)S(1)} %get-tuple-element.106), channel_id=1, source_target_pairs={{0,3},{1,0},{2,1},{3,2},{4,7},{5,4},{6,5},{7,6},{8,11},{9,8},{10,9... | collective-permute-start | bytes 196616 | tf_op jit(solution)/shard_map/ppermute | solution.py:33
  199.8 2.5 %collective-permute-start.53 = (bf16[2,32,1024]{2,1,0:T(8,128)(2,1)S(1)}, bf16[2,32,1024]{2,1,0:T(8,128)(2,1)S(1)}, u32[]{:S(2)}, u32[]{:S(2)}) collective-permute-start(bf16[2,32,1024]{2,1,0:T(8,128)(2,1)S(1)} %owned.6), channel_id=1, source_target_pairs={{0,64},{32,96},{64,0},{96,32},{1,65},{33,97},{65,1},{97,33},{2,66}... | collective-permute-start | bytes 393224 | tf_op jit(solution)/shard_map/ppermute | solution.py:29
  203.8 10.3 %weight_grad.1 = (bf16[1024,1024]{1,0:T(8,128)(2,1)}, bf16[1024,1024]{1,0:T(8,128)(2,1)}, bf16[1024,1024]{1,0:T(8,128)(2,1)}) custom-call(bf16[256,1024]{1,0:T(8,128)(2,1)} %refs_0_.1, bf16[256,1024]{1,0:T(8,128)(2,1)S(1)} %collective-permute-done.16.x.refs_1_, bf16[256,1024]{1,0:T(8,128)(2,1)S(1)} %collective-permute-done.35.x.refs_2_, ...), custom_call_target="tpu_custom_call" | custom-call | flops 6442450944 | bytes 16777216 | tf_op jit(solution)/shard_map/weight_grad/pallas_call | solution.py:237
  (150 shorter events, 32.5 us)
Async XLA Ops:
  11.5 12.6 %collective-permute-start = (bf16[2,3,32,1024]{3,2,1,0:T(8,128)(2,1)S(1)}, bf16[2,3,32,1024]{3,2,1,0:T(8,128)(2,1)S(1)}, u32[]{:S(2)}, u32[]{:S(2)}) collective-permute-start(bf16[2,3,32,1024]{3,2,1,0:T(8,128)(2,1)S(1)} %get-tuple-element.60), channel_id=1, source_target_pairs={{0,24},{4,28},{8,0},{12,4},{16,8},{20,12},{24,16},{28,20},{1,25},{... | collective-permute-start | bytes 1179656 | tf_op jit(solution)/shard_map/ppermute | solution.py:24
  15.7 16.6 %collective-permute-start.35 = (bf16[256,1024]{1,0:T(8,128)(2,1)}, bf16[256,1024]{1,0:T(8,128)(2,1)S(1)}, u32[]{:S(2)}, u32[]{:S(2)}) collective-permute-start(bf16[256,1024]{1,0:T(8,128)(2,1)} %refs_0_.1), channel_id=1, source_target_pairs={{0,64},{32,96},{64,0},{96,32},{1,65},{33,97},{65,1},{97,33},{2,66}... | collective-permute-start | bytes 1572872 | tf_op jit(solution)/shard_map/ppermute | solution.py:29
  18.7 23.3 %collective-permute-start.36 = (bf16[256,1024]{1,0:T(8,128)(2,1)S(1)}, bf16[256,1024]{1,0:T(8,128)(2,1)S(1)}, u32[]{:S(2)}, u32[]{:S(2)}) collective-permute-start(bf16[256,1024]{1,0:T(8,128)(2,1)S(1)} %multiply_convert_fusion.g.refs_4_), channel_id=1, source_target_pairs={{0,64},{32,96},{64,0},{96,32},{1,65},{33,97},{65,1},{97,33},{2,66}... | collective-permute-start | bytes 1572872 | tf_op jit(solution)/shard_map/ppermute | solution.py:29
  19.2 11.2 %collective-permute-start.1 = (bf16[2,3,32,1024]{3,2,1,0:T(8,128)(2,1)S(1)}, bf16[2,3,32,1024]{3,2,1,0:T(8,128)(2,1)S(1)}, u32[]{:S(2)}, u32[]{:S(2)}) collective-permute-start(bf16[2,3,32,1024]{3,2,1,0:T(8,128)(2,1)S(1)} %get-tuple-element.62), channel_id=1, source_target_pairs={{0,8},{4,12},{8,16},{12,20},{16,24},{20,28},{24,0},{28,4},{1,9},{5... | collective-permute-start | bytes 1179656 | tf_op jit(solution)/shard_map/ppermute | solution.py:24
  19.2 32.0 %collective-permute-start.16 = (bf16[256,1024]{1,0:T(8,128)(2,1)}, bf16[256,1024]{1,0:T(8,128)(2,1)S(1)}, u32[]{:S(2)}, u32[]{:S(2)}) collective-permute-start(bf16[256,1024]{1,0:T(8,128)(2,1)} %refs_0_.1), channel_id=1, source_target_pairs={{0,32},{32,0},{64,96},{96,64},{1,33},{33,1},{65,97},{97,65},{2,34}... | collective-permute-start | bytes 1572872 | tf_op jit(solution)/shard_map/ppermute | solution.py:29
  24.0 27.2 %collective-permute-start.17 = (bf16[256,1024]{1,0:T(8,128)(2,1)S(1)}, bf16[256,1024]{1,0:T(8,128)(2,1)S(1)}, u32[]{:S(2)}, u32[]{:S(2)}) collective-permute-start(bf16[256,1024]{1,0:T(8,128)(2,1)S(1)} %multiply_convert_fusion.g.refs_4_), channel_id=1, source_target_pairs={{0,32},{32,0},{64,96},{96,64},{1,33},{33,1},{65,97},{97,65},{2,34}... | collective-permute-start | bytes 1572872 | tf_op jit(solution)/shard_map/ppermute | solution.py:29
  30.5 19.1 %collective-permute-start.3 = (bf16[3,32,1024]{2,1,0:T(8,128)(2,1)S(1)}, bf16[3,32,1024]{2,1,0:T(8,128)(2,1)S(1)}, u32[]{:S(2)}, u32[]{:S(2)}) collective-permute-start(bf16[3,32,1024]{2,1,0:T(8,128)(2,1)S(1)} %get-tuple-element.64), channel_id=1, source_target_pairs={{0,24},{4,28},{8,0},{12,4},{16,8},{20,12},{24,16},{28,20},{1,25},{... | collective-permute-start | bytes 589832 | tf_op jit(solution)/shard_map/ppermute | solution.py:24
  47.5 14.9 %collective-permute-start.37 = (bf16[2,3,32,1024]{3,2,1,0:T(8,128)(2,1)S(1)}, bf16[2,3,32,1024]{3,2,1,0:T(8,128)(2,1)S(1)}, u32[]{:S(2)}, u32[]{:S(2)}) collective-permute-start(bf16[2,3,32,1024]{3,2,1,0:T(8,128)(2,1)S(1)} %get-tuple-element.84), channel_id=1, source_target_pairs={{0,24},{4,28},{8,0},{12,4},{16,8},{20,12},{24,16},{28,20},{1,25},{... | collective-permute-start | bytes 1179656 | tf_op jit(solution)/shard_map/ppermute | solution.py:24
  49.6 12.7 %collective-permute-start.4 = (bf16[3,32,1024]{2,1,0:T(8,128)(2,1)S(1)}, bf16[3,32,1024]{2,1,0:T(8,128)(2,1)S(1)}, u32[]{:S(2)}, u32[]{:S(2)}) collective-permute-start(bf16[3,32,1024]{2,1,0:T(8,128)(2,1)S(1)} %other_half.4), channel_id=1, source_target_pairs={{0,4},{4,0},{8,12},{12,8},{16,20},{20,16},{24,28},{28,24},{1,5},{5... | collective-permute-start | bytes 589832 | tf_op jit(solution)/shard_map/ppermute | solution.py:24
  51.2 13.3 %collective-permute-start.38 = (bf16[2,3,32,1024]{3,2,1,0:T(8,128)(2,1)S(1)}, bf16[2,3,32,1024]{3,2,1,0:T(8,128)(2,1)S(1)}, u32[]{:S(2)}, u32[]{:S(2)}) collective-permute-start(bf16[2,3,32,1024]{3,2,1,0:T(8,128)(2,1)S(1)} %get-tuple-element.86), channel_id=1, source_target_pairs={{0,8},{4,12},{8,16},{12,20},{16,24},{20,28},{24,0},{28,4},{1,9},{5... | collective-permute-start | bytes 1179656 | tf_op jit(solution)/shard_map/ppermute | solution.py:24
  51.2 24.7 %collective-permute-start.54 = (bf16[256,1024]{1,0:T(8,128)(2,1)S(1)}, bf16[256,1024]{1,0:T(8,128)(2,1)S(1)}, u32[]{:S(2)}, u32[]{:S(2)}) collective-permute-start(bf16[256,1024]{1,0:T(8,128)(2,1)S(1)} %collective-permute-done.35.x.refs_2_), channel_id=1, source_target_pairs={{0,32},{32,0},{64,96},{96,64},{1,33},{33,1},{65,97},{97,65},{2,34}... | collective-permute-start | bytes 1572872 | tf_op jit(solution)/shard_map/ppermute | solution.py:29
  56.8 19.7 %collective-permute-start.55 = (bf16[256,1024]{1,0:T(8,128)(2,1)S(1)}, bf16[256,1024]{1,0:T(8,128)(2,1)S(1)}, u32[]{:S(2)}, u32[]{:S(2)}) collective-permute-start(bf16[256,1024]{1,0:T(8,128)(2,1)S(1)} %collective-permute-done.36.g.refs_6_), channel_id=1, source_target_pairs={{0,32},{32,0},{64,96},{96,64},{1,33},{33,1},{65,97},{97,65},{2,34}... | collective-permute-start | bytes 1572872 | tf_op jit(solution)/shard_map/ppermute | solution.py:29
  62.3 11.6 %collective-permute-start.18 = (bf16[2,3,32,1024]{3,2,1,0:T(8,128)(2,1)S(1)}, bf16[2,3,32,1024]{3,2,1,0:T(8,128)(2,1)S(1)}, u32[]{:S(2)}, u32[]{:S(2)}) collective-permute-start(bf16[2,3,32,1024]{3,2,1,0:T(8,128)(2,1)S(1)} %get-tuple-element.72), channel_id=1, source_target_pairs={{0,24},{4,28},{8,0},{12,4},{16,8},{20,12},{24,16},{28,20},{1,25},{... | collective-permute-start | bytes 1179656 | tf_op jit(solution)/shard_map/ppermute | solution.py:24
  62.4 13.0 %collective-permute-start.19 = (bf16[2,3,32,1024]{3,2,1,0:T(8,128)(2,1)S(1)}, bf16[2,3,32,1024]{3,2,1,0:T(8,128)(2,1)S(1)}, u32[]{:S(2)}, u32[]{:S(2)}) collective-permute-start(bf16[2,3,32,1024]{3,2,1,0:T(8,128)(2,1)S(1)} %get-tuple-element.74), channel_id=1, source_target_pairs={{0,8},{4,12},{8,16},{12,20},{16,24},{20,28},{24,0},{28,4},{1,9},{5... | collective-permute-start | bytes 1179656 | tf_op jit(solution)/shard_map/ppermute | solution.py:24
  64.6 20.1 %collective-permute-start.5 = (bf16[3,32,1024]{2,1,0:T(8,128)(2,1)S(1)}, bf16[3,32,1024]{2,1,0:T(8,128)(2,1)S(1)}, u32[]{:S(2)}, u32[]{:S(2)}) collective-permute-start(bf16[3,32,1024]{2,1,0:T(8,128)(2,1)S(1)} %gate.4.refs_0_), channel_id=1, source_target_pairs={{0,4},{4,0},{8,12},{12,8},{16,20},{20,16},{24,28},{28,24},{1,5},{5... | collective-permute-start | bytes 589832 | tf_op jit(solution)/shard_map/ppermute | solution.py:24
  73.9 12.3 %collective-permute-start.6 = (bf16[3,32,1024]{2,1,0:T(8,128)(2,1)S(1)}, bf16[3,32,1024]{2,1,0:T(8,128)(2,1)S(1)}, u32[]{:S(2)}, u32[]{:S(2)}) collective-permute-start(bf16[3,32,1024]{2,1,0:T(8,128)(2,1)S(1)} %gate.4.refs_0_), channel_id=1, source_target_pairs={{0,24},{4,28},{8,0},{12,4},{16,8},{20,12},{24,16},{28,20},{1,25},{... | collective-permute-start | bytes 589832 | tf_op jit(solution)/shard_map/ppermute | solution.py:24
  75.4 11.4 %collective-permute-start.8 = (bf16[3,32,1024]{2,1,0:T(8,128)(2,1)S(1)}, bf16[3,32,1024]{2,1,0:T(8,128)(2,1)S(1)}, u32[]{:S(2)}, u32[]{:S(2)}) collective-permute-start(bf16[3,32,1024]{2,1,0:T(8,128)(2,1)S(1)} %gate.4.refs_0_), channel_id=1, source_target_pairs={{0,8},{4,12},{8,16},{12,20},{16,24},{20,28},{24,0},{28,4},{1,9},{5... | collective-permute-start | bytes 589832 | tf_op jit(solution)/shard_map/ppermute | solution.py:24
  75.9 11.4 %collective-permute-start.39 = (bf16[3,32,1024]{2,1,0:T(8,128)(2,1)S(1)}, bf16[3,32,1024]{2,1,0:T(8,128)(2,1)S(1)}, u32[]{:S(2)}, u32[]{:S(2)}) collective-permute-start(bf16[3,32,1024]{2,1,0:T(8,128)(2,1)S(1)} %get-tuple-element.87), channel_id=1, source_target_pairs={{0,8},{4,12},{8,16},{12,20},{16,24},{20,28},{24,0},{28,4},{1,9},{5... | collective-permute-start | bytes 589832 | tf_op jit(solution)/shard_map/ppermute | solution.py:24
  76.5 13.6 %collective-permute-start.40 = (bf16[3,32,1024]{2,1,0:T(8,128)(2,1)S(1)}, bf16[3,32,1024]{2,1,0:T(8,128)(2,1)S(1)}, u32[]{:S(2)}, u32[]{:S(2)}) collective-permute-start(bf16[3,32,1024]{2,1,0:T(8,128)(2,1)S(1)} %get-tuple-element.88), channel_id=1, source_target_pairs={{0,24},{4,28},{8,0},{12,4},{16,8},{20,12},{24,16},{28,20},{1,25},{... | collective-permute-start | bytes 589832 | tf_op jit(solution)/shard_map/ppermute | solution.py:24
  84.6 18.3 %collective-permute-start.56 = (bf16[2,3,32,1024]{3,2,1,0:T(8,128)(2,1)S(1)}, bf16[2,3,32,1024]{3,2,1,0:T(8,128)(2,1)S(1)}, u32[]{:S(2)}, u32[]{:S(2)}) collective-permute-start(bf16[2,3,32,1024]{3,2,1,0:T(8,128)(2,1)S(1)} %get-tuple-element.96), channel_id=1, source_target_pairs={{0,24},{4,28},{8,0},{12,4},{16,8},{20,12},{24,16},{28,20},{1,25},{... | collective-permute-start | bytes 1179656 | tf_op jit(solution)/shard_map/ppermute | solution.py:24
  86.2 20.0 %collective-permute-start.57 = (bf16[2,3,32,1024]{3,2,1,0:T(8,128)(2,1)S(1)}, bf16[2,3,32,1024]{3,2,1,0:T(8,128)(2,1)S(1)}, u32[]{:S(2)}, u32[]{:S(2)}) collective-permute-start(bf16[2,3,32,1024]{3,2,1,0:T(8,128)(2,1)S(1)} %get-tuple-element.98), channel_id=1, source_target_pairs={{0,8},{4,12},{8,16},{12,20},{16,24},{20,28},{24,0},{28,4},{1,9},{5... | collective-permute-start | bytes 1179656 | tf_op jit(solution)/shard_map/ppermute | solution.py:24
  86.8 14.4 %collective-permute-start.20 = (bf16[3,32,1024]{2,1,0:T(8,128)(2,1)S(1)}, bf16[3,32,1024]{2,1,0:T(8,128)(2,1)S(1)}, u32[]{:S(2)}, u32[]{:S(2)}) collective-permute-start(bf16[3,32,1024]{2,1,0:T(8,128)(2,1)S(1)} %get-tuple-element.75), channel_id=1, source_target_pairs={{0,8},{4,12},{8,16},{12,20},{16,24},{20,28},{24,0},{28,4},{1,9},{5... | collective-permute-start | bytes 589832 | tf_op jit(solution)/shard_map/ppermute | solution.py:24
  87.3 15.6 %collective-permute-start.21 = (bf16[3,32,1024]{2,1,0:T(8,128)(2,1)S(1)}, bf16[3,32,1024]{2,1,0:T(8,128)(2,1)S(1)}, u32[]{:S(2)}, u32[]{:S(2)}) collective-permute-start(bf16[3,32,1024]{2,1,0:T(8,128)(2,1)S(1)} %get-tuple-element.76), channel_id=1, source_target_pairs={{0,24},{4,28},{8,0},{12,4},{16,8},{20,12},{24,16},{28,20},{1,25},{... | collective-permute-start | bytes 589832 | tf_op jit(solution)/shard_map/ppermute | solution.py:24
  90.1 12.7 %collective-permute-start.7 = (bf16[3,32,1024]{2,1,0:T(8,128)(2,1)S(1)}, bf16[3,32,1024]{2,1,0:T(8,128)(2,1)S(1)}, u32[]{:S(2)}, u32[]{:S(2)}) collective-permute-start(bf16[3,32,1024]{2,1,0:T(8,128)(2,1)S(1)} %collective-permute-done.5.refs_1_), channel_id=1, source_target_pairs={{0,24},{4,28},{8,0},{12,4},{16,8},{20,12},{24,16},{28,20},{1,25},{... | collective-permute-start | bytes 589832 | tf_op jit(solution)/shard_map/ppermute | solution.py:24
  106.3 12.6 %collective-permute-start.22 = (bf16[3,32,1024]{2,1,0:T(8,128)(2,1)S(1)}, bf16[3,32,1024]{2,1,0:T(8,128)(2,1)S(1)}, u32[]{:S(2)}, u32[]{:S(2)}) collective-permute-start(bf16[3,32,1024]{2,1,0:T(8,128)(2,1)S(1)} %other_half.5), channel_id=1, source_target_pairs={{0,4},{4,0},{8,12},{12,8},{16,20},{20,16},{24,28},{28,24},{1,5},{5... | collective-permute-start | bytes 589832 | tf_op jit(solution)/shard_map/ppermute | solution.py:24
  108.0 12.6 %collective-permute-start.59 = (bf16[3,32,1024]{2,1,0:T(8,128)(2,1)S(1)}, bf16[3,32,1024]{2,1,0:T(8,128)(2,1)S(1)}, u32[]{:S(2)}, u32[]{:S(2)}) collective-permute-start(bf16[3,32,1024]{2,1,0:T(8,128)(2,1)S(1)} %get-tuple-element.100), channel_id=1, source_target_pairs={{0,24},{4,28},{8,0},{12,4},{16,8},{20,12},{24,16},{28,20},{1,25},{... | collective-permute-start | bytes 589832 | tf_op jit(solution)/shard_map/ppermute | solution.py:24
  110.3 11.3 %collective-permute-start.42 = (bf16[3,32,1024]{2,1,0:T(8,128)(2,1)S(1)}, bf16[3,32,1024]{2,1,0:T(8,128)(2,1)S(1)}, u32[]{:S(2)}, u32[]{:S(2)}) collective-permute-start(bf16[3,32,1024]{2,1,0:T(8,128)(2,1)S(1)} %gate.6.refs_0_), channel_id=1, source_target_pairs={{0,4},{4,0},{8,12},{12,8},{16,20},{20,16},{24,28},{28,24},{1,5},{5... | collective-permute-start | bytes 589832 | tf_op jit(solution)/shard_map/ppermute | solution.py:24
  112.4 10.6 %collective-permute-start.43 = (bf16[3,32,1024]{2,1,0:T(8,128)(2,1)S(1)}, bf16[3,32,1024]{2,1,0:T(8,128)(2,1)S(1)}, u32[]{:S(2)}, u32[]{:S(2)}) collective-permute-start(bf16[3,32,1024]{2,1,0:T(8,128)(2,1)S(1)} %gate.6.refs_0_), channel_id=1, source_target_pairs={{0,24},{4,28},{8,0},{12,4},{16,8},{20,12},{24,16},{28,20},{1,25},{... | collective-permute-start | bytes 589832 | tf_op jit(solution)/shard_map/ppermute | solution.py:24
  112.8 11.1 %collective-permute-start.45 = (bf16[3,32,1024]{2,1,0:T(8,128)(2,1)S(1)}, bf16[3,32,1024]{2,1,0:T(8,128)(2,1)S(1)}, u32[]{:S(2)}, u32[]{:S(2)}) collective-permute-start(bf16[3,32,1024]{2,1,0:T(8,128)(2,1)S(1)} %gate.6.refs_0_), channel_id=1, source_target_pairs={{0,8},{4,12},{8,16},{12,20},{16,24},{20,28},{24,0},{28,4},{1,9},{5... | collective-permute-start | bytes 589832 | tf_op jit(solution)/shard_map/ppermute | solution.py:24
  131.7 12.0 %collective-permute-start.48 = (bf16[3,32,1024]{2,1,0:T(8,128)(2,1)S(1)}, bf16[3,32,1024]{2,1,0:T(8,128)(2,1)S(1)}, u32[]{:S(2)}, u32[]{:S(2)}) collective-permute-start(bf16[3,32,1024]{2,1,0:T(8,128)(2,1)S(1)} %collective-permute-done.42.refs_1_), channel_id=1, source_target_pairs={{0,8},{4,12},{8,16},{12,20},{16,24},{20,28},{24,0},{28,4},{1,9},{5... | collective-permute-start | bytes 589832 | tf_op jit(solution)/shard_map/ppermute | solution.py:24
  132.1 11.6 %collective-permute-start.25 = (bf16[3,32,1024]{2,1,0:T(8,128)(2,1)S(1)}, bf16[3,32,1024]{2,1,0:T(8,128)(2,1)S(1)}, u32[]{:S(2)}, u32[]{:S(2)}) collective-permute-start(bf16[3,32,1024]{2,1,0:T(8,128)(2,1)S(1)} %collective-permute-done.23.refs_1_), channel_id=1, source_target_pairs={{0,24},{4,28},{8,0},{12,4},{16,8},{20,12},{24,16},{28,20},{1,25},{... | collective-permute-start | bytes 589832 | tf_op jit(solution)/shard_map/ppermute | solution.py:24
  135.3 10.5 %collective-permute-start.61 = (bf16[3,32,1024]{2,1,0:T(8,128)(2,1)S(1)}, bf16[3,32,1024]{2,1,0:T(8,128)(2,1)S(1)}, u32[]{:S(2)}, u32[]{:S(2)}) collective-permute-start(bf16[3,32,1024]{2,1,0:T(8,128)(2,1)S(1)} %gate.7.refs_0_), channel_id=1, source_target_pairs={{0,4},{4,0},{8,12},{12,8},{16,20},{20,16},{24,28},{28,24},{1,5},{5... | collective-permute-start | bytes 589832 | tf_op jit(solution)/shard_map/ppermute | solution.py:24
  135.7 12.1 %collective-permute-start.27 = (bf16[3,32,1024]{2,1,0:T(8,128)(2,1)S(1)}, bf16[3,32,1024]{2,1,0:T(8,128)(2,1)S(1)}, u32[]{:S(2)}, u32[]{:S(2)}) collective-permute-start(bf16[3,32,1024]{2,1,0:T(8,128)(2,1)S(1)} %collective-permute-done.26.refs_6_), channel_id=1, source_target_pairs={{0,8},{4,12},{8,16},{12,20},{16,24},{20,28},{24,0},{28,4},{1,9},{5... | collective-permute-start | bytes 589832 | tf_op jit(solution)/shard_map/ppermute | solution.py:24
  139.5 12.5 %collective-permute-start.29 = (bf16[3,32,1024]{2,1,0:T(8,128)(2,1)S(1)}, bf16[3,32,1024]{2,1,0:T(8,128)(2,1)S(1)}, u32[]{:S(2)}, u32[]{:S(2)}) collective-permute-start(bf16[3,32,1024]{2,1,0:T(8,128)(2,1)S(1)} %collective-permute-done.23.refs_1_), channel_id=1, source_target_pairs={{0,8},{4,12},{8,16},{12,20},{16,24},{20,28},{24,0},{28,4},{1,9},{5... | collective-permute-start | bytes 589832 | tf_op jit(solution)/shard_map/ppermute | solution.py:24
  143.7 12.4 %collective-permute-start.64 = (bf16[3,32,1024]{2,1,0:T(8,128)(2,1)S(1)}, bf16[3,32,1024]{2,1,0:T(8,128)(2,1)S(1)}, u32[]{:S(2)}, u32[]{:S(2)}) collective-permute-start(bf16[3,32,1024]{2,1,0:T(8,128)(2,1)S(1)} %gate.7.refs_0_), channel_id=1, source_target_pairs={{0,8},{4,12},{8,16},{12,20},{16,24},{20,28},{24,0},{28,4},{1,9},{5... | collective-permute-start | bytes 589832 | tf_op jit(solution)/shard_map/ppermute | solution.py:24
  147.8 17.2 %collective-permute-start.28 = (bf16[3,32,1024]{2,1,0:T(8,128)(2,1)S(1)}, bf16[3,32,1024]{2,1,0:T(8,128)(2,1)S(1)}, u32[]{:S(2)}, u32[]{:S(2)}) collective-permute-start(bf16[3,32,1024]{2,1,0:T(8,128)(2,1)S(1)} %collective-permute-done.25.refs_3_), channel_id=1, source_target_pairs={{0,24},{4,28},{8,0},{12,4},{16,8},{20,12},{24,16},{28,20},{1,25},{... | collective-permute-start | bytes 589832 | tf_op jit(solution)/shard_map/ppermute | solution.py:24
  152.0 14.4 %collective-permute-start.62 = (bf16[3,32,1024]{2,1,0:T(8,128)(2,1)S(1)}, bf16[3,32,1024]{2,1,0:T(8,128)(2,1)S(1)}, u32[]{:S(2)}, u32[]{:S(2)}) collective-permute-start(bf16[3,32,1024]{2,1,0:T(8,128)(2,1)S(1)} %gate.7.refs_0_), channel_id=1, source_target_pairs={{0,24},{4,28},{8,0},{12,4},{16,8},{20,12},{24,16},{28,20},{1,25},{... | collective-permute-start | bytes 589832 | tf_op jit(solution)/shard_map/ppermute | solution.py:24
  152.0 23.3 %collective-permute-start.67 = (bf16[3,32,1024]{2,1,0:T(8,128)(2,1)S(1)}, bf16[3,32,1024]{2,1,0:T(8,128)(2,1)S(1)}, u32[]{:S(2)}, u32[]{:S(2)}) collective-permute-start(bf16[3,32,1024]{2,1,0:T(8,128)(2,1)S(1)} %collective-permute-done.61.refs_1_), channel_id=1, source_target_pairs={{0,8},{4,12},{8,16},{12,20},{16,24},{20,28},{24,0},{28,4},{1,9},{5... | collective-permute-start | bytes 589832 | tf_op jit(solution)/shard_map/ppermute | solution.py:24
  156.1 16.5 %collective-permute-start.65 = (bf16[3,32,1024]{2,1,0:T(8,128)(2,1)S(1)}, bf16[3,32,1024]{2,1,0:T(8,128)(2,1)S(1)}, u32[]{:S(2)}, u32[]{:S(2)}) collective-permute-start(bf16[3,32,1024]{2,1,0:T(8,128)(2,1)S(1)} %collective-permute-done.64.refs_6_), channel_id=1, source_target_pairs={{0,8},{4,12},{8,16},{12,20},{16,24},{20,28},{24,0},{28,4},{1,9},{5... | collective-permute-start | bytes 589832 | tf_op jit(solution)/shard_map/ppermute | solution.py:24
  156.1 19.2 %collective-permute-start.66 = (bf16[3,32,1024]{2,1,0:T(8,128)(2,1)S(1)}, bf16[3,32,1024]{2,1,0:T(8,128)(2,1)S(1)}, u32[]{:S(2)}, u32[]{:S(2)}) collective-permute-start(bf16[3,32,1024]{2,1,0:T(8,128)(2,1)S(1)} %collective-permute-done.63.refs_3_), channel_id=1, source_target_pairs={{0,24},{4,28},{8,0},{12,4},{16,8},{20,12},{24,16},{28,20},{1,25},{... | collective-permute-start | bytes 589832 | tf_op jit(solution)/shard_map/ppermute | solution.py:24
  164.9 18.1 %collective-permute-start.13 = (bf16[2,32,1024]{2,1,0:T(8,128)(2,1)S(1)}, bf16[2,32,1024]{2,1,0:T(8,128)(2,1)S(1)}, u32[]{:S(2)}, u32[]{:S(2)}) collective-permute-start(bf16[2,32,1024]{2,1,0:T(8,128)(2,1)S(1)} %get-tuple-element.67), channel_id=1, source_target_pairs={{0,3},{1,0},{2,1},{3,2},{4,7},{5,4},{6,5},{7,6},{8,11},{9,8},{10,9... | collective-permute-start | bytes 393224 | tf_op jit(solution)/shard_map/ppermute | solution.py:33
  166.4 16.7 %collective-permute-start.49 = (bf16[2,32,1024]{2,1,0:T(8,128)(2,1)S(1)}, bf16[2,32,1024]{2,1,0:T(8,128)(2,1)S(1)}, u32[]{:S(2)}, u32[]{:S(2)}) collective-permute-start(bf16[2,32,1024]{2,1,0:T(8,128)(2,1)S(1)} %get-tuple-element.90), channel_id=1, source_target_pairs={{0,1},{1,2},{2,3},{3,0},{4,5},{5,6},{6,7},{7,4},{8,9},{9,10},{10,1... | collective-permute-start | bytes 393224 | tf_op jit(solution)/shard_map/ppermute | solution.py:33
  172.6 13.8 %collective-permute-start.50 = (bf16[2,32,1024]{2,1,0:T(8,128)(2,1)S(1)}, bf16[2,32,1024]{2,1,0:T(8,128)(2,1)S(1)}, u32[]{:S(2)}, u32[]{:S(2)}) collective-permute-start(bf16[2,32,1024]{2,1,0:T(8,128)(2,1)S(1)} %get-tuple-element.91), channel_id=1, source_target_pairs={{0,3},{1,0},{2,1},{3,2},{4,7},{5,4},{6,5},{7,6},{8,11},{9,8},{10,9... | collective-permute-start | bytes 393224 | tf_op jit(solution)/shard_map/ppermute | solution.py:33
  175.3 11.2 %collective-permute-start.30 = (bf16[2,32,1024]{2,1,0:T(8,128)(2,1)S(1)}, bf16[2,32,1024]{2,1,0:T(8,128)(2,1)S(1)}, u32[]{:S(2)}, u32[]{:S(2)}) collective-permute-start(bf16[2,32,1024]{2,1,0:T(8,128)(2,1)S(1)} %get-tuple-element.78), channel_id=1, source_target_pairs={{0,1},{1,2},{2,3},{3,0},{4,5},{5,6},{6,7},{7,4},{8,9},{9,10},{10,1... | collective-permute-start | bytes 393224 | tf_op jit(solution)/shard_map/ppermute | solution.py:33
  175.3 14.5 %collective-permute-start.31 = (bf16[2,32,1024]{2,1,0:T(8,128)(2,1)S(1)}, bf16[2,32,1024]{2,1,0:T(8,128)(2,1)S(1)}, u32[]{:S(2)}, u32[]{:S(2)}) collective-permute-start(bf16[2,32,1024]{2,1,0:T(8,128)(2,1)S(1)} %get-tuple-element.79), channel_id=1, source_target_pairs={{0,3},{1,0},{2,1},{3,2},{4,7},{5,4},{6,5},{7,6},{8,11},{9,8},{10,9... | collective-permute-start | bytes 393224 | tf_op jit(solution)/shard_map/ppermute | solution.py:33
  199.8 14.4 %collective-permute-start.53 = (bf16[2,32,1024]{2,1,0:T(8,128)(2,1)S(1)}, bf16[2,32,1024]{2,1,0:T(8,128)(2,1)S(1)}, u32[]{:S(2)}, u32[]{:S(2)}) collective-permute-start(bf16[2,32,1024]{2,1,0:T(8,128)(2,1)S(1)} %owned.6), channel_id=1, source_target_pairs={{0,64},{32,96},{64,0},{96,32},{1,65},{33,97},{65,1},{97,33},{2,66}... | collective-permute-start | bytes 393224 | tf_op jit(solution)/shard_map/ppermute | solution.py:29
  202.4 11.8 %collective-permute-start.34 = (bf16[2,32,1024]{2,1,0:T(8,128)(2,1)S(1)}, bf16[2,32,1024]{2,1,0:T(8,128)(2,1)S(1)}, u32[]{:S(2)}, u32[]{:S(2)}) collective-permute-start(bf16[2,32,1024]{2,1,0:T(8,128)(2,1)S(1)} %owned.5), channel_id=1, source_target_pairs={{0,32},{32,0},{64,96},{96,64},{1,33},{33,1},{65,97},{97,65},{2,34}... | collective-permute-start | bytes 393224 | tf_op jit(solution)/shard_map/ppermute | solution.py:29
  202.6 11.6 %collective-permute-start.72 = (bf16[2,32,1024]{2,1,0:T(8,128)(2,1)S(1)}, bf16[2,32,1024]{2,1,0:T(8,128)(2,1)S(1)}, u32[]{:S(2)}, u32[]{:S(2)}) collective-permute-start(bf16[2,32,1024]{2,1,0:T(8,128)(2,1)S(1)} %owned.7), channel_id=1, source_target_pairs={{0,96},{32,64},{64,32},{96,0},{1,97},{33,65},{65,33},{97,1},{2,98}... | collective-permute-start | bytes 393224 | tf_op jit(solution)/shard_map/ppermute | solution.py:29
  (32 other events, 294.5 us)

commit v2 on v1

v2 whole, which is shorter than its diff:
```python
import jax
import jax.numpy as jnp
from jax import lax
from jax.experimental import pallas as pl
from jax.experimental.pallas import tpu as pltpu
from jax.sharding import PartitionSpec as P

BF = jnp.bfloat16
F32 = jnp.float32
NT = (((1,), (1,)), ((), ()))
VMEM_LIMIT = 40 * 1024 * 1024


def params():
    return pltpu.CompilerParams(vmem_limit_bytes=VMEM_LIMIT)


def cost(flops, nbytes):
    return pl.CostEstimate(flops=flops, bytes_accessed=nbytes, transcendentals=0)


def fin_perm(x, dz, dx):
    pairs = [(z * 2 + l, ((z + dz) % 4) * 2 + (l ^ dx)) for z in range(4) for l in range(2)]
    return lax.ppermute(x, "fin", pairs)


def tok_perm(x, dh, dc):
    pairs = [(h * 2 + c, (h ^ dh) * 2 + (c ^ dc)) for h in range(2) for c in range(2)]
    return lax.ppermute(x, "tok", pairs)


def y_perm(x, dy):
    return lax.ppermute(x, "fout", [(y, (y + dy) % 4) for y in range(4)])


def row_start(z, lo, r, s):
    return pl.multiple_of((lax.rem(z + r, 4) * 2 + lax.bitwise_xor(lo, s)) * 32, 32)


def scale_kernel(margin, x, up, weight, ids, out):
    tokens = x.shape[0]
    out[0] = x[...]
    pair = ids[...] // 2
    picked = jnp.zeros(pair.shape, F32)
    for p in range(margin.shape[0]):
        picked = jnp.where(pair == p, margin[p], picked)
    side = jnp.where(ids[...] % 2 == 0, -1.0, 1.0)
    row = weight[...].astype(F32) * (side * jax.nn.sigmoid(-picked))
    at = lax.broadcasted_iota(jnp.int32, (tokens, tokens), 0)
    to = lax.broadcasted_iota(jnp.int32, (tokens, tokens), 1)
    column = jnp.sum(jnp.where(at == to, row, 0.0), axis=1, keepdims=True)
    out[1] = (column * up[...].astype(F32)).astype(BF)


def scaled(inputs, upstream, loss_weight, pair_ids, margin):
    tokens, depth = inputs.shape
    vmem = pl.BlockSpec(memory_space=pltpu.VMEM)
    return pl.pallas_call(
        scale_kernel,
        in_specs=[pl.BlockSpec(memory_space=pltpu.SMEM)] + [vmem] * 4,
        out_specs=vmem,
        out_shape=jax.ShapeDtypeStruct((2, tokens, depth), BF),
        compiler_params=params(),
        cost_estimate=cost(4 * tokens * depth, 8 * tokens * depth),
        name="scaled",
    )(margin, inputs, upstream, loss_weight.reshape(1, -1), pair_ids.reshape(1, -1))


def forward_kernel(idx, a, b, wg, wu, wd, plus, minus, keep, own, rows, acc):
    z, lo = idx[0], idx[1]
    tokens = a.shape[1]

    @pl.when(pl.program_id(0) == 0)
    def _():
        rows[:, :tokens] = a[...]
        rows[:, tokens:] = b[...]

    acc[0] = jnp.dot(rows[0], wg[...], preferred_element_type=F32)
    acc[1] = jnp.dot(rows[0], wu[...], preferred_element_type=F32)
    acc[2] = lax.dot_general(rows[1], wd[...], NT, preferred_element_type=F32)

    def put(out, k, r, s):
        start = row_start(z, lo, r, s)
        for t in range(2):
            out[k, :, t] = acc[:, pl.ds(t * tokens + start, 32), :].astype(out.dtype)

    put(plus, 0, 2, 0)
    put(plus, 1, 1, 1)
    put(minus, 0, 2, 1)
    put(minus, 1, 3, 0)
    put(keep, 0, 1, 0)
    put(keep, 1, 3, 1)
    put(own, 0, 0, 0)
    put(own, 1, 0, 1)


def forward(idx, a, b, wg, wu, wd):
    _, tokens, depth = a.shape
    width = wg.shape[1]
    tile = 256
    full = pl.BlockSpec((2, tokens, depth), lambda i, s: (0, 0, 0))
    part = pl.BlockSpec((2, 3, 2, 32, tile), lambda i, s: (0, 0, 0, 0, i))
    shape = (2, 3, 2, 32, width)
    return pl.pallas_call(
        forward_kernel,
        grid_spec=pltpu.PrefetchScalarGridSpec(
            num_scalar_prefetch=1,
            grid=(width // tile,),
            in_specs=[
                full,
                full,
                pl.BlockSpec((depth, tile), lambda i, s: (0, i)),
                pl.BlockSpec((depth, tile), lambda i, s: (0, i)),
                pl.BlockSpec((tile, depth), lambda i, s: (i, 0)),
            ],
            out_specs=[part] * 4,
            scratch_shapes=[
                pltpu.VMEM((2, 2 * tokens, depth), BF),
                pltpu.VMEM((3, 2 * tokens, tile), F32),
            ],
        ),
        out_shape=[
            jax.ShapeDtypeStruct(shape, BF),
            jax.ShapeDtypeStruct(shape, BF),
            jax.ShapeDtypeStruct(shape, F32),
            jax.ShapeDtypeStruct(shape, F32),
        ],
        compiler_params=params(),
        cost_estimate=cost(12 * tokens * depth * width, 6 * depth * width + 8 * 2**20),
        name="forward",
    )(idx, a, b, wg, wu, wd)


def pass_on_kernel(keep, from_minus, from_plus, plus, minus):
    plus[...] = (keep[0] + from_minus[0].astype(F32)).astype(BF)
    minus[...] = (keep[1] + from_plus[0].astype(F32)).astype(BF)


def pass_on(keep, from_minus, from_plus):
    shape = jax.ShapeDtypeStruct(keep.shape[1:], BF)
    return pl.pallas_call(
        pass_on_kernel,
        out_shape=[shape, shape],
        compiler_params=params(),
        cost_estimate=cost(keep.size, keep.size * 8),
        name="pass_on",
    )(keep, from_minus, from_plus)


def other_kernel(own, from_minus, last_plus, out):
    out[...] = (own[1] + from_minus[1].astype(F32) + last_plus[...].astype(F32)).astype(BF)


def other_half(own, from_minus, last_plus):
    return pl.pallas_call(
        other_kernel,
        out_shape=jax.ShapeDtypeStruct(own.shape[1:], BF),
        compiler_params=params(),
        cost_estimate=cost(own.size, own.size * 4),
        name="other_half",
    )(own, from_minus, last_plus)


def gate_kernel(own, from_plus, last_minus, across, out):
    total = own[0] + from_plus[1].astype(F32) + last_minus[...].astype(F32) + across[...].astype(F32)
    pre_gate, pre_up, grad_hidden = total[0], total[1], total[2]
    s = jax.nn.sigmoid(pre_gate)
    activated = pre_gate * s
    out[0] = (activated * pre_up).astype(BF)
    out[1] = (grad_hidden * pre_up * s * (1.0 + pre_gate * (1.0 - s))).astype(BF)
    out[2] = (grad_hidden * activated).astype(BF)


def gate(own, from_plus, last_minus, across):
    return pl.pallas_call(
        gate_kernel,
        out_shape=jax.ShapeDtypeStruct(own.shape[1:], BF),
        compiler_params=params(),
        cost_estimate=cost(own.size * 8, own.size * 5),
        name="gate",
    )(own, from_plus, last_minus, across)


def input_grad_kernel(idx, here, plus1, far_a, far_b, minus1, wg, wu, own, to1, to2, to3, acts, acc):
    z, lo, y = idx[0], idx[1], idx[2]
    tokens = acts.shape[1] // 2

    @pl.when(pl.program_id(0) == 0)
    def _():
        for r, s, block in (
            (0, 0, here.at[0]),
            (0, 1, here.at[1]),
            (1, 0, plus1.at[0]),
            (1, 1, plus1.at[1]),
            (2, 0, far_a),
            (2, 1, far_b),
            (3, 0, minus1.at[0]),
            (3, 1, minus1.at[1]),
        ):
            start = row_start(z, lo, r, s)
            for t in range(2):
                acts[:, pl.ds(t * tokens + start, 32), :] = block[:, t]

    acc[...] = lax.dot_general(acts[1], wg[...], NT, preferred_element_type=F32) + lax.dot_general(
        acts[2], wu[...], NT, preferred_element_type=F32
    )
    for r, out in enumerate((own, to1, to2, to3)):
        start = pl.multiple_of(lax.rem(y + r, 4) * 64, 64)
        for t in range(2):
            out[t] = acc[pl.ds(t * tokens + start, 64), :].astype(out.dtype)


def input_grad(idx, here, plus1, far_a, far_b, minus1, wg, wu):
    depth, width = wg.shape
    tokens = 256
    tile = 256
    part = pl.BlockSpec((2, 64, tile), lambda i, s: (0, 0, i))
    one = pl.BlockSpec((3, 2, 32, width), lambda i, s: (0, 0, 0, 0))
    two = pl.BlockSpec((2, 3, 2, 32, width), lambda i, s: (0, 0, 0, 0, 0))
    weight = pl.BlockSpec((tile, width), lambda i, s: (i, 0))
    return pl.pallas_call(
        input_grad_kernel,
        grid_spec=pltpu.PrefetchScalarGridSpec(
            num_scalar_prefetch=1,
            grid=(depth // tile,),
            in_specs=[two, two, one, one, two, weight, weight],
            out_specs=[part] * 4 + [pl.BlockSpec((3, 2 * tokens, width), lambda i, s: (0, 0, 0))],
            scratch_shapes=[pltpu.VMEM((2 * tokens, tile), F32)],
        ),
        out_shape=[
            jax.ShapeDtypeStruct((2, 64, depth), F32),
            jax.ShapeDtypeStruct((2, 64, depth), BF),
            jax.ShapeDtypeStruct((2, 64, depth), BF),
            jax.ShapeDtypeStruct((2, 64, depth), BF),
            jax.ShapeDtypeStruct((3, 2 * tokens, width), BF),
        ],
        compiler_params=params(),
        cost_estimate=cost(8 * tokens * depth * width, 4 * depth * width + 8 * 2**20),
        name="input_grad",
    )(idx, here, plus1, far_a, far_b, minus1, wg, wu)


def owned_kernel(own, a, b, c, mine, theirs):
    total = own[...] + a[...].astype(F32) + b[...].astype(F32) + c[...].astype(F32)
    mine[...] = total[0].astype(mine.dtype)
    theirs[...] = total[1].astype(BF)


def owned(own, a, b, c, dtype):
    return pl.pallas_call(
        owned_kernel,
        out_shape=[
            jax.ShapeDtypeStruct(own.shape[1:], dtype),
            jax.ShapeDtypeStruct(own.shape[1:], BF),
        ],
        compiler_params=params(),
        cost_estimate=cost(own.size * 4, own.size * 10),
        name="owned",
    )(own, a, b, c)


def weight_grad_kernel(*refs):
    rows, acts = refs[:4], refs[4:6]
    gate_out, up_out, down_out, xt, g = refs[6:]

    @pl.when(pl.program_id(0) == 0)
    def _():
        for k in range(4):
            xt[:, k * 256 : (k + 1) * 256] = rows[k][0].T
            g[k * 256 : (k + 1) * 256, :] = rows[k][1]

    hidden = jnp.concatenate([r[0] for r in acts], axis=0)
    grad_gate = jnp.concatenate([r[1] for r in acts], axis=0)
    grad_up = jnp.concatenate([r[2] for r in acts], axis=0)
    gate_out[...] = jnp.dot(xt[...], grad_gate, preferred_element_type=F32).astype(BF)
    up_out[...] = jnp.dot(xt[...], grad_up, preferred_element_type=F32).astype(BF)
    down_out[...] = jnp.dot(hidden.T, g[...], preferred_element_type=F32).astype(BF)


def weight_grad(rows, acts):
    _, tokens, depth = rows[0].shape
    width = acts[0].shape[2]
    tile = 256
    full = pl.BlockSpec((2, tokens, depth), lambda i: (0, 0, 0))
    return pl.pallas_call(
        weight_grad_kernel,
        grid=(width // tile,),
        in_specs=[full] * 4 + [pl.BlockSpec((3, 2 * tokens, tile), lambda i: (0, 0, i))] * 2,
        out_specs=[
            pl.BlockSpec((depth, tile), lambda i: (0, i)),
            pl.BlockSpec((depth, tile), lambda i: (0, i)),
            pl.BlockSpec((tile, depth), lambda i: (i, 0)),
        ],
        out_shape=[
            jax.ShapeDtypeStruct((depth, width), BF),
            jax.ShapeDtypeStruct((depth, width), BF),
            jax.ShapeDtypeStruct((width, depth), BF),
        ],
        scratch_shapes=[pltpu.VMEM((depth, 4 * tokens), BF), pltpu.VMEM((4 * tokens, depth), BF)],
        compiler_params=params(),
        cost_estimate=cost(24 * tokens * depth * width, 16 * 2**20),
        name="weight_grad",
    )(*rows, *acts)


def body(inputs, upstream, loss_weight, pair_ids, margin, w_gate, w_up, w_down):
    fin = lax.axis_index("fin")
    idx = jnp.stack([fin // 2, fin % 2, lax.axis_index("fout")]).astype(jnp.int32)

    m0 = scaled(inputs, upstream, loss_weight, pair_ids, margin)
    m1 = tok_perm(m0, 0, 1)
    m2 = tok_perm(m0, 1, 0)
    m3 = tok_perm(m2, 0, 1)

    acts, sums = [], []
    for k, (a, b) in enumerate(((m0, m1), (m2, m3))):
        plus, minus, keep, own = forward(idx, a, b, w_gate, w_up, w_down)
        from_minus, from_plus = fin_perm(plus, 1, 0), fin_perm(minus, 3, 0)
        plus, minus = pass_on(keep, from_minus, from_plus)
        last_minus, last_plus = fin_perm(plus, 1, 0), fin_perm(minus, 3, 0)
        across = fin_perm(other_half(own, from_minus, last_plus), 0, 1)
        mine = gate(own, from_plus, last_minus, across)

        here = jnp.stack([mine, fin_perm(mine, 0, 1)])
        minus1, plus1 = fin_perm(here, 1, 0), fin_perm(here, 3, 0)
        far_a, far_b = fin_perm(minus1[0], 1, 0), fin_perm(plus1[1], 3, 0)

        own, to1, to2, to3, act = input_grad(idx, here, plus1, far_a, far_b, minus1, w_gate, w_up)
        acts.append(act)
        a, b, c = y_perm(to1, 1), y_perm(to2, 2), y_perm(to3, 3)
        mine, theirs = owned(own, a, b, c, BF if k else F32)
        sums.append(tok_perm(mine, 1, 0) if k else mine)
        sums.append(tok_perm(theirs, k, 1))
    grad_gate, grad_up, grad_down = weight_grad((m0, m1, m2, m3), acts)
    total = sums[0] + sums[1].astype(F32) + sums[2].astype(F32) + sums[3].astype(F32)
    return (total.astype(BF), grad_gate, grad_up, grad_down)


def solution(mesh):
    placed = (
        P("tok", "fin"),
        P("tok", "fin"),
        P("tok"),
        P("tok"),
        P(),
        P("fin", ("tok", "fout")),
        P("fin", ("tok", "fout")),
        P(("tok", "fout"), "fin"),
    )
    return jax.shard_map(
        body,
        mesh=mesh,
        in_specs=placed,
        out_specs=(
            P(("tok", "fout"), "fin"),
            P("fin", ("tok", "fout")),
            P("fin", ("tok", "fout")),
            P(("tok", "fout"), "fin"),
        ),
        check_vma=False,
    )
```

time: 217 us -> 215 us (level)
  waiting for transfers between devices: 66.5 us -> 115 us
  starting transfers between devices: 87.4 us -> 46.8 us
  Pallas kernels: 51.6 us -> 36.7 us
  local copies, waits for them, and re-layouts: 4.06 us -> 12.8 us
  other arithmetic: 4.12 us -> 0.94 us
    ppermute x48 -> x20, waiting for transfers between devices: 54.9 us -> 83.6 us  [fin_perm(): return lax.ppermute(x, 'fin', pairs)]
    ppermute x48 -> x20, starting transfers between devices: 54 us -> 31.1 us  [fin_perm(): return lax.ppermute(x, 'fin', pairs)]
    ppermute x16 -> x6, starting transfers between devices: 26 us -> 9.24 us  [y_perm(): return lax.ppermute(x, 'fout', [(y, (y + dy) % 4) for y in range(4)])]
    ppermute x9 -> x6, waiting for transfers between devices: 11.4 us -> 23.3 us  [tok_perm(): return lax.ppermute(x, 'tok', pairs)]
    pallas_call x4 -> x2, Pallas kernels: 17.8 us -> 8.31 us  [input_grad(): pl.pallas_call(input_grad_kernel, grid_spec=pltpu.PrefetchScalarGridSpec(...]
    unnamed x14 -> x30, local copies, waits for them, and re-layouts: 3.88 us -> 12.7 us
    ppermute x16 -> x6, waiting for transfers between devices: 0.16 us -> 8.47 us  [y_perm(): return lax.ppermute(x, 'fout', [(y, (y + dy) % 4) for y in range(4)])]
    pallas_call x4 -> x2, Pallas kernels: 22 us -> 15 us  [forward(): pl.pallas_call(forward_kernel, grid_spec=pltpu.PrefetchScalarGridSpec(num...]
  transfers between devices with their start and end apart: 73 -> 32, of which waited for: 18 -> 16; matrix products, arithmetic and copies ran while one was open for 0% -> 0% of each run, Pallas kernels for 21% -> 17%
where the time goes in v2:
time: 215 us; the launch traced here: 214 us
  waiting for transfers between devices  115 us (53%)
  starting transfers between devices  46.8 us (22%)
  Pallas kernels  36.7 us (17%)
  local copies, waits for them, and re-layouts  12.8 us (6%)
    ppermute x20, waiting for transfers between devices, fin_perm(): return lax.ppermute(x, 'fin', pairs)  83.6 us
    ppermute x20, starting transfers between devices, fin_perm(): return lax.ppermute(x, 'fin', pairs)  31.1 us
    ppermute x6, waiting for transfers between devices, tok_perm(): return lax.ppermute(x, 'tok', pairs)  23.3 us
    pallas_call x2, Pallas kernels, forward(): pl.pallas_call(forward_kernel, grid_spec=pltpu.PrefetchScalarGridSpec(num...  15 us
    unnamed x30, local copies, waits for them, and re-layouts  12.7 us
    pallas_call x1, Pallas kernels, weight_grad(): pl.pallas_call(weight_grad_kernel, grid=(width // tile,), in_specs=[full]...  11.3 us
    ppermute x6, starting transfers between devices, y_perm(): return lax.ppermute(x, 'fout', [(y, (y + dy) % 4) for y in range(4)])  9.24 us
    ppermute x6, waiting for transfers between devices, y_perm(): return lax.ppermute(x, 'fout', [(y, (y + dy) % 4) for y in range(4)])  8.47 us
  transfers between devices with their start and end apart: 32, of which 16 were waited for; matrix products, arithmetic and copies ran while one was open for 0% of the time, Pallas kernels for 17%

profile of v2, /device:TPU:0, one launch (start us, length us, event | category | flops | bytes accessed | tf_op | source)
XLA Modules:
  0.0 213.6 jit_solution(1238197126807877713)
XLA Ops:
  0.6 1.0 copy-done
  1.7 1.0 copy-done.1
  4.7 0.7 scaled.1.a.refs_0_
  5.5 3.2 %collective-permute-start.15 = (bf16[2,256,1024]{2,1,0:T(8,128)(2,1)S(1)}, bf16[2,256,1024]{2,1,0:T(8,128)(2,1)}, u32[]{:S(2)}, u32[]{:S(2)}) collective-permute-start(bf16[2,256,1024]{2,1,0:T(8,128)(2,1)S(1)} %scaled.1.a.refs_0_), channel_id=1, source_target_pairs={{0,64},{32,96},{64,0},{96,32},{1,65},{33,97},{65,1},{97,33},{2,66}... | collective-permute-start | bytes 3145736 | tf_op jit(solution)/shard_map/ppermute | solution.py:29
  8.7 23.3 %collective-permute-done.15.a.refs_2_ = bf16[2,256,1024]{2,1,0:T(8,128)(2,1)} collective-permute-done((bf16[2,256,1024]{2,1,0:T(8,128)(2,1)S(1)}, bf16[2,256,1024]{2,1,0:T(8,128)(2,1)}, u32[]{:S(2)}, u32[]{:S(2)}) %collective-permute-start.15) | collective-permute-done | bytes 1048608 | tf_op jit(solution)/shard_map/ppermute | solution.py:29
  32.0 1.6 copy-done.6
  33.6 1.6 copy-done.8
  35.2 7.5 %forward.2 = (bf16[2,3,2,32,1024]{4,3,2,1,0:T(8,128)(2,1)S(1)}, bf16[2,3,2,32,1024]{4,3,2,1,0:T(8,128)(2,1)S(1)}, f32[2,3,2,32,1024]{4,3,2,1,0:T(8,128)S(1)}, f32[2,3,2,32,1024]{4,3,2,1,0:T(8,128)S(1)}) custom-call(s32[3]{0:T(128)S(1)} %pad_add_fusion.idx, bf16[2,256,1024]{2,1,0:T(8,128)(2,1)S(1)} %scaled.1.a.refs_0_, ...), custom_call_target="tpu_custom_call" | custom-call | flops 3221225472 | bytes 14680064 | tf_op jit(solution)/shard_map/forward/pallas_call | solution.py:104
  42.7 4.3 %collective-permute-start.1 = (bf16[2,3,2,32,1024]{4,3,2,1,0:T(8,128)(2,1)S(1)}, bf16[2,3,2,32,1024]{4,3,2,1,0:T(8,128)(2,1)S(1)}, u32[]{:S(2)}, u32[]{:S(2)}) collective-permute-start(bf16[2,3,2,32,1024]{4,3,2,1,0:T(8,128)(2,1)S(1)} %get-tuple-element.34), channel_id=1, source_target_pairs={{0,24},{4,28},{8,0},{12,4},{16,8},{20,12},{24,16},{28,20},{1,25},{... | collective-permute-start | bytes 2359304 | tf_op jit(solution)/shard_map/ppermute | solution.py:24
  47.0 7.5 %forward.3 = (bf16[2,3,2,32,1024]{4,3,2,1,0:T(8,128)(2,1)S(1)}, bf16[2,3,2,32,1024]{4,3,2,1,0:T(8,128)(2,1)S(1)}, f32[2,3,2,32,1024]{4,3,2,1,0:T(8,128)S(1)}, f32[2,3,2,32,1024]{4,3,2,1,0:T(8,128)S(1)}) custom-call(s32[3]{0:T(128)S(1)} %pad_add_fusion.idx, bf16[2,256,1024]{2,1,0:T(8,128)(2,1)} %collective-permute-done.15.a.refs_2_, ...), custom_call_target="tpu_custom_call" | custom-call | flops 3221225472 | bytes 14680064 | tf_op jit(solution)/shard_map/forward/pallas_call | solution.py:104
  54.5 3.3 %collective-permute-start.17 = (bf16[2,3,2,32,1024]{4,3,2,1,0:T(8,128)(2,1)S(1)}, bf16[2,3,2,32,1024]{4,3,2,1,0:T(8,128)(2,1)S(1)}, u32[]{:S(2)}, u32[]{:S(2)}) collective-permute-start(bf16[2,3,2,32,1024]{4,3,2,1,0:T(8,128)(2,1)S(1)} %get-tuple-element.46), channel_id=1, source_target_pairs={{0,24},{4,28},{8,0},{12,4},{16,8},{20,12},{24,16},{28,20},{1,25},{... | collective-permute-start | bytes 2359304 | tf_op jit(solution)/shard_map/ppermute | solution.py:24
  57.8 7.1 %collective-permute-done.1.from_plus = bf16[2,3,2,32,1024]{4,3,2,1,0:T(8,128)(2,1)S(1)} collective-permute-done((bf16[2,3,2,32,1024]{4,3,2,1,0:T(8,128)(2,1)S(1)}, bf16[2,3,2,32,1024]{4,3,2,1,0:T(8,128)(2,1)S(1)}, u32[]{:S(2)}, u32[]{:S(2)}) %collective-permute-start.1) | collective-permute-done | bytes 786464 | tf_op jit(solution)/shard_map/ppermute | solution.py:24
  64.9 3.7 %collective-permute-done.2.from_minus = bf16[2,3,2,32,1024]{4,3,2,1,0:T(8,128)(2,1)S(1)} collective-permute-done((bf16[2,3,2,32,1024]{4,3,2,1,0:T(8,128)(2,1)S(1)}, bf16[2,3,2,32,1024]{4,3,2,1,0:T(8,128)(2,1)S(1)}, u32[]{:S(2)}, u32[]{:S(2)}) %collective-permute-start.2) | collective-permute-done | bytes 786464 | tf_op jit(solution)/shard_map/ppermute | solution.py:24
  68.8 12.9 %collective-permute-done.17.from_plus = bf16[2,3,2,32,1024]{4,3,2,1,0:T(8,128)(2,1)S(1)} collective-permute-done((bf16[2,3,2,32,1024]{4,3,2,1,0:T(8,128)(2,1)S(1)}, bf16[2,3,2,32,1024]{4,3,2,1,0:T(8,128)(2,1)S(1)}, u32[]{:S(2)}, u32[]{:S(2)}) %collective-permute-start.17) | collective-permute-done | bytes 786464 | tf_op jit(solution)/shard_map/ppermute | solution.py:24
  81.7 3.0 %collective-permute-done.18.from_minus = bf16[2,3,2,32,1024]{4,3,2,1,0:T(8,128)(2,1)S(1)} collective-permute-done((bf16[2,3,2,32,1024]{4,3,2,1,0:T(8,128)(2,1)S(1)}, bf16[2,3,2,32,1024]{4,3,2,1,0:T(8,128)(2,1)S(1)}, u32[]{:S(2)}, u32[]{:S(2)}) %collective-permute-start.18) | collective-permute-done | bytes 786464 | tf_op jit(solution)/shard_map/ppermute | solution.py:24
  84.9 0.7 collective-permute-start.20
  85.7 1.4 collective-permute-start.3
  87.0 3.1 %collective-permute-done.4.last_plus = bf16[3,2,32,1024]{3,2,1,0:T(8,128)(2,1)S(1)} collective-permute-done((bf16[3,2,32,1024]{3,2,1,0:T(8,128)(2,1)S(1)}, bf16[3,2,32,1024]{3,2,1,0:T(8,128)(2,1)S(1)}, u32[]{:S(2)}, u32[]{:S(2)}) %collective-permute-start.4) | collective-permute-done | bytes 393248 | tf_op jit(solution)/shard_map/ppermute | solution.py:24
  90.3 1.6 collective-permute-start.5
  92.3 5.9 %collective-permute-done.20.last_plus = bf16[3,2,32,1024]{3,2,1,0:T(8,128)(2,1)S(1)} collective-permute-done((bf16[3,2,32,1024]{3,2,1,0:T(8,128)(2,1)S(1)}, bf16[3,2,32,1024]{3,2,1,0:T(8,128)(2,1)S(1)}, u32[]{:S(2)}, u32[]{:S(2)}) %collective-permute-start.20) | collective-permute-done | bytes 393248 | tf_op jit(solution)/shard_map/ppermute | solution.py:24
  98.3 1.6 collective-permute-start.21
  99.9 0.8 collective-permute-done.5.across
  101.0 1.6 collective-permute-start.6
  102.6 2.8 %collective-permute-done.19.last_minus = bf16[3,2,32,1024]{3,2,1,0:T(8,128)(2,1)S(1)} collective-permute-done((bf16[3,2,32,1024]{3,2,1,0:T(8,128)(2,1)S(1)}, bf16[3,2,32,1024]{3,2,1,0:T(8,128)(2,1)S(1)}, u32[]{:S(2)}, u32[]{:S(2)}) %collective-permute-start.19) | collective-permute-done | bytes 393248 | tf_op jit(solution)/shard_map/ppermute | solution.py:24
  105.4 5.1 %collective-permute-done.21.across = bf16[3,2,32,1024]{3,2,1,0:T(8,128)(2,1)S(1)} collective-permute-done((bf16[3,2,32,1024]{3,2,1,0:T(8,128)(2,1)S(1)}, bf16[3,2,32,1024]{3,2,1,0:T(8,128)(2,1)S(1)}, u32[]{:S(2)}, u32[]{:S(2)}) %collective-permute-start.21) | collective-permute-done | bytes 393248 | tf_op jit(solution)/shard_map/ppermute | solution.py:24
  110.7 1.6 collective-permute-start.22
  112.3 6.6 %collective-permute-done.6 = bf16[3,2,32,1024]{3,2,1,0:T(8,128)(2,1)S(1)} collective-permute-done((bf16[3,2,32,1024]{3,2,1,0:T(8,128)(2,1)S(1)}, bf16[3,2,32,1024]{3,2,1,0:T(8,128)(2,1)S(1)}, u32[]{:S(2)}, u32[]{:S(2)}) %collective-permute-start.6) | collective-permute-done | bytes 393248 | tf_op jit(solution)/shard_map/ppermute | solution.py:24
  119.5 3.2 %collective-permute-start.7 = (bf16[2,3,2,32,1024]{4,3,2,1,0:T(8,128)(2,1)S(1)}, bf16[2,3,2,32,1024]{4,3,2,1,0:T(8,128)(2,1)S(1)}, u32[]{:S(2)}, u32[]{:S(2)}) collective-permute-start(bf16[2,3,2,32,1024]{4,3,2,1,0:T(8,128)(2,1)S(1)} %pad_maximum_fusion.here), channel_id=1, source_target_pairs={{0,24},{4,28},{8,0},{12,4},{16,8},{20,12},{24,16},{28,20},{1,25},{... | collective-permute-start | bytes 2359304 | tf_op jit(solution)/shard_map/ppermute | solution.py:24
  122.8 3.2 %collective-permute-done.22 = bf16[3,2,32,1024]{3,2,1,0:T(8,128)(2,1)S(1)} collective-permute-done((bf16[3,2,32,1024]{3,2,1,0:T(8,128)(2,1)S(1)}, bf16[3,2,32,1024]{3,2,1,0:T(8,128)(2,1)S(1)}, u32[]{:S(2)}, u32[]{:S(2)}) %collective-permute-start.22) | collective-permute-done | bytes 393248 | tf_op jit(solution)/shard_map/ppermute | solution.py:24
  126.8 3.1 %collective-permute-start.23 = (bf16[2,3,2,32,1024]{4,3,2,1,0:T(8,128)(2,1)S(1)}, bf16[2,3,2,32,1024]{4,3,2,1,0:T(8,128)(2,1)S(1)}, u32[]{:S(2)}, u32[]{:S(2)}) collective-permute-start(bf16[2,3,2,32,1024]{4,3,2,1,0:T(8,128)(2,1)S(1)} %pad_maximum_fusion.1.here), channel_id=1, source_target_pairs={{0,24},{4,28},{8,0},{12,4},{16,8},{20,12},{24,16},{28,20},{1,25},{... | collective-permute-start | bytes 2359304 | tf_op jit(solution)/shard_map/ppermute | solution.py:24
  129.9 11.2 %collective-permute-done.8.minus1 = bf16[2,3,2,32,1024]{4,3,2,1,0:T(8,128)(2,1)S(1)} collective-permute-done((bf16[2,3,2,32,1024]{4,3,2,1,0:T(8,128)(2,1)S(1)}, bf16[2,3,2,32,1024]{4,3,2,1,0:T(8,128)(2,1)S(1)}, u32[]{:S(2)}, u32[]{:S(2)}) %collective-permute-start.8) | collective-permute-done | bytes 786464 | tf_op jit(solution)/shard_map/ppermute | solution.py:24
  141.3 3.3 %collective-permute-start.10 = (bf16[3,2,32,1024]{3,2,1,0:T(8,128)(2,1)S(1)}, bf16[3,2,32,1024]{3,2,1,0:T(8,128)(2,1)S(1)}, u32[]{:S(2)}, u32[]{:S(2)}) collective-permute-start(bf16[3,2,32,1024]{3,2,1,0:T(8,128)(2,1)S(1)} %slice_bitcast_fusion.2), channel_id=1, source_target_pairs={{0,24},{4,28},{8,0},{12,4},{16,8},{20,12},{24,16},{28,20},{1,25},{... | collective-permute-start | bytes 1179656 | tf_op jit(solution)/shard_map/ppermute | solution.py:24
  144.6 13.4 %collective-permute-done.24.minus1 = bf16[2,3,2,32,1024]{4,3,2,1,0:T(8,128)(2,1)S(1)} collective-permute-done((bf16[2,3,2,32,1024]{4,3,2,1,0:T(8,128)(2,1)S(1)}, bf16[2,3,2,32,1024]{4,3,2,1,0:T(8,128)(2,1)S(1)}, u32[]{:S(2)}, u32[]{:S(2)}) %collective-permute-start.24) | collective-permute-done | bytes 786464 | tf_op jit(solution)/shard_map/ppermute | solution.py:24
  158.2 3.5 %collective-permute-start.26 = (bf16[3,2,32,1024]{3,2,1,0:T(8,128)(2,1)S(1)}, bf16[3,2,32,1024]{3,2,1,0:T(8,128)(2,1)S(1)}, u32[]{:S(2)}, u32[]{:S(2)}) collective-permute-start(bf16[3,2,32,1024]{3,2,1,0:T(8,128)(2,1)S(1)} %slice_bitcast_fusion), channel_id=1, source_target_pairs={{0,24},{4,28},{8,0},{12,4},{16,8},{20,12},{24,16},{28,20},{1,25},{... | collective-permute-start | bytes 1179656 | tf_op jit(solution)/shard_map/ppermute | solution.py:24
  161.6 4.8 %collective-permute-done.9.far_a = bf16[3,2,32,1024]{3,2,1,0:T(8,128)(2,1)S(1)} collective-permute-done((bf16[3,2,32,1024]{3,2,1,0:T(8,128)(2,1)S(1)}, bf16[3,2,32,1024]{3,2,1,0:T(8,128)(2,1)S(1)}, u32[]{:S(2)}, u32[]{:S(2)}) %collective-permute-start.9) | collective-permute-done | bytes 393248 | tf_op jit(solution)/shard_map/ppermute | solution.py:24
  166.4 4.2 %input_grad.2 = (f32[2,64,1024]{2,1,0:T(8,128)S(1)}, bf16[2,64,1024]{2,1,0:T(8,128)(2,1)S(1)}, bf16[2,64,1024]{2,1,0:T(8,128)(2,1)S(1)}, bf16[2,64,1024]{2,1,0:T(8,128)(2,1)S(1)}, bf16[3,512,1024]{2,1,0:T(8,128)(2,1)S(1)}) custom-call(s32[3]{0:T(128)S(1)} %pad_add_fusion.idx, bf16[2,3,2,32,1024]{4,3,2,1,0:T(8,128)(2,1)S(1)} %pad_maximum_fusion.here, ...), custom_call_target="tpu_custom_call" | custom-call | flops 2147483648 | bytes 12582912 | tf_op jit(solution)/shard_map/input_grad/pallas_call | solution.py:221
  170.6 1.6 collective-permute-start.11
  172.3 2.9 %collective-permute-start.12 = (bf16[2,64,1024]{2,1,0:T(8,128)(2,1)S(1)}, bf16[2,64,1024]{2,1,0:T(8,128)(2,1)S(1)}, u32[]{:S(2)}, u32[]{:S(2)}) collective-permute-start(bf16[2,64,1024]{2,1,0:T(8,128)(2,1)S(1)} %get-tuple-element.41), channel_id=1, source_target_pairs={{0,2},{1,3},{2,0},{3,1},{4,6},{5,7},{6,4},{7,5},{8,10},{9,11},{10,... | collective-permute-start | bytes 786440 | tf_op jit(solution)/shard_map/ppermute | solution.py:33
  175.2 1.3 collective-permute-start.13
  176.5 4.2 %input_grad.3 = (f32[2,64,1024]{2,1,0:T(8,128)S(1)}, bf16[2,64,1024]{2,1,0:T(8,128)(2,1)S(1)}, bf16[2,64,1024]{2,1,0:T(8,128)(2,1)S(1)}, bf16[2,64,1024]{2,1,0:T(8,128)(2,1)S(1)}, bf16[3,512,1024]{2,1,0:T(8,128)(2,1)S(1)}) custom-call(s32[3]{0:T(128)S(1)} %pad_add_fusion.idx, bf16[2,3,2,32,1024]{4,3,2,1,0:T(8,128)(2,1)S(1)} %pad_maximum_fusion.1.here, ...), custom_call_target="tpu_custom_call" | custom-call | flops 2147483648 | bytes 12582912 | tf_op jit(solution)/shard_map/input_grad/pallas_call | solution.py:221
  180.7 1.7 copy-done.13
  183.1 0.8 collective-permute-start.28
  183.9 1.9 collective-permute-start.29
  185.9 8.5 %collective-permute-done.27.a = bf16[2,64,1024]{2,1,0:T(8,128)(2,1)S(1)} collective-permute-done((bf16[2,64,1024]{2,1,0:T(8,128)(2,1)S(1)}, bf16[2,64,1024]{2,1,0:T(8,128)(2,1)S(1)}, u32[]{:S(2)}, u32[]{:S(2)}) %collective-permute-start.27) | collective-permute-done | bytes 262176 | tf_op jit(solution)/shard_map/ppermute | solution.py:33
  194.7 3.1 %collective-permute-start.30 = (bf16[64,1024]{1,0:T(8,128)(2,1)S(1)}, bf16[64,1024]{1,0:T(8,128)(2,1)S(1)}, u32[]{:S(2)}, u32[]{:S(2)}) collective-permute-start(bf16[64,1024]{1,0:T(8,128)(2,1)S(1)} %get-tuple-element.55), channel_id=1, source_target_pairs={{0,64},{32,96},{64,0},{96,32},{1,65},{33,97},{65,1},{97,33},{2,66}... | collective-permute-start | bytes 393224 | tf_op jit(solution)/shard_map/ppermute | solution.py:29
  197.8 1.9 copy-done.12
  199.7 1.9 copy-done.14
  201.5 11.3 %weight_grad.1 = (bf16[1024,1024]{1,0:T(8,128)(2,1)}, bf16[1024,1024]{1,0:T(8,128)(2,1)}, bf16[1024,1024]{1,0:T(8,128)(2,1)}) custom-call(bf16[2,256,1024]{2,1,0:T(8,128)(2,1)S(1)} %scaled.1.a.refs_0_, bf16[2,256,1024]{2,1,0:T(8,128)(2,1)} %collective-permute-done.b.refs_1_, bf16[2,256,1024]{2,1,0:T(8,128)(2,1)} %collective-permute-done.15.a.refs_2_, ...), custom_call_target="tpu_custom_call" | custom-call | flops 6442450944 | bytes 16777216 | tf_op jit(solution)/shard_map/weight_grad/pallas_call | solution.py:285
  (68 shorter events, 7.4 us)
Async XLA Ops:
  0.6 1.0 copy-start
  1.7 1.0 copy-start.1
  2.7 0.7 copy-start.2
  3.4 0.7 copy-start.3
  4.1 0.7 copy-start.4
  4.7 27.3 %copy-start.5 = (bf16[1024,1024]{1,0:T(8,128)(2,1)S(1)}, bf16[1024,1024]{1,0:T(8,128)(2,1)}, u32[]{:S(2)}) copy-start(bf16[1024,1024]{1,0:T(8,128)(2,1)} %wd.3) | copy-start | bytes 6291460
  5.5 26.5 %collective-permute-start.15 = (bf16[2,256,1024]{2,1,0:T(8,128)(2,1)S(1)}, bf16[2,256,1024]{2,1,0:T(8,128)(2,1)}, u32[]{:S(2)}, u32[]{:S(2)}) collective-permute-start(bf16[2,256,1024]{2,1,0:T(8,128)(2,1)S(1)} %scaled.1.a.refs_0_), channel_id=1, source_target_pairs={{0,64},{32,96},{64,0},{96,32},{1,65},{33,97},{65,1},{97,33},{2,66}... | collective-permute-start | bytes 3145736 | tf_op jit(solution)/shard_map/ppermute | solution.py:29
  8.7 23.3 %collective-permute-start = (bf16[2,256,1024]{2,1,0:T(8,128)(2,1)S(1)}, bf16[2,256,1024]{2,1,0:T(8,128)(2,1)}, u32[]{:S(2)}, u32[]{:S(2)}) collective-permute-start(bf16[2,256,1024]{2,1,0:T(8,128)(2,1)S(1)} %scaled.1.a.refs_0_), channel_id=1, source_target_pairs={{0,32},{32,0},{64,96},{96,64},{1,33},{33,1},{65,97},{97,65},{2,34}... | collective-permute-start | bytes 3145736 | tf_op jit(solution)/shard_map/ppermute | solution.py:29
  31.9 15.1 %collective-permute-start.16 = (bf16[2,256,1024]{2,1,0:T(8,128)(2,1)}, bf16[2,256,1024]{2,1,0:T(8,128)(2,1)}, u32[]{:S(2)}, u32[]{:S(2)}) collective-permute-start(bf16[2,256,1024]{2,1,0:T(8,128)(2,1)} %collective-permute-done.15.a.refs_2_), channel_id=1, source_target_pairs={{0,32},{32,0},{64,96},{96,64},{1,33},{33,1},{65,97},{97,65},{2,34}... | collective-permute-start | bytes 3145736 | tf_op jit(solution)/shard_map/ppermute | solution.py:29
  32.0 1.6 copy-start.6
  33.6 1.6 copy-start.8
  35.2 11.8 %copy-start.7 = (bf16[1024,1024]{1,0:T(8,128)(2,1)S(1)}, bf16[1024,1024]{1,0:T(8,128)(2,1)}, u32[]{:S(2)}) copy-start(bf16[1024,1024]{1,0:T(8,128)(2,1)} %wg.7) | copy-start | bytes 6291460
  35.2 11.8 %copy-start.9 = (bf16[1024,1024]{1,0:T(8,128)(2,1)S(1)}, bf16[1024,1024]{1,0:T(8,128)(2,1)}, u32[]{:S(2)}) copy-start(bf16[1024,1024]{1,0:T(8,128)(2,1)} %wu.7) | copy-start | bytes 6291460
  42.7 22.2 %collective-permute-start.1 = (bf16[2,3,2,32,1024]{4,3,2,1,0:T(8,128)(2,1)S(1)}, bf16[2,3,2,32,1024]{4,3,2,1,0:T(8,128)(2,1)S(1)}, u32[]{:S(2)}, u32[]{:S(2)}) collective-permute-start(bf16[2,3,2,32,1024]{4,3,2,1,0:T(8,128)(2,1)S(1)} %get-tuple-element.34), channel_id=1, source_target_pairs={{0,24},{4,28},{8,0},{12,4},{16,8},{20,12},{24,16},{28,20},{1,25},{... | collective-permute-start | bytes 2359304 | tf_op jit(solution)/shard_map/ppermute | solution.py:24
  47.0 21.6 %collective-permute-start.2 = (bf16[2,3,2,32,1024]{4,3,2,1,0:T(8,128)(2,1)S(1)}, bf16[2,3,2,32,1024]{4,3,2,1,0:T(8,128)(2,1)S(1)}, u32[]{:S(2)}, u32[]{:S(2)}) collective-permute-start(bf16[2,3,2,32,1024]{4,3,2,1,0:T(8,128)(2,1)S(1)} %get-tuple-element.36), channel_id=1, source_target_pairs={{0,8},{4,12},{8,16},{12,20},{16,24},{20,28},{24,0},{28,4},{1,9},{5... | collective-permute-start | bytes 2359304 | tf_op jit(solution)/shard_map/ppermute | solution.py:24
  54.5 27.2 %collective-permute-start.17 = (bf16[2,3,2,32,1024]{4,3,2,1,0:T(8,128)(2,1)S(1)}, bf16[2,3,2,32,1024]{4,3,2,1,0:T(8,128)(2,1)S(1)}, u32[]{:S(2)}, u32[]{:S(2)}) collective-permute-start(bf16[2,3,2,32,1024]{4,3,2,1,0:T(8,128)(2,1)S(1)} %get-tuple-element.46), channel_id=1, source_target_pairs={{0,24},{4,28},{8,0},{12,4},{16,8},{20,12},{24,16},{28,20},{1,25},{... | collective-permute-start | bytes 2359304 | tf_op jit(solution)/shard_map/ppermute | solution.py:24
  57.8 26.9 %collective-permute-start.18 = (bf16[2,3,2,32,1024]{4,3,2,1,0:T(8,128)(2,1)S(1)}, bf16[2,3,2,32,1024]{4,3,2,1,0:T(8,128)(2,1)S(1)}, u32[]{:S(2)}, u32[]{:S(2)}) collective-permute-start(bf16[2,3,2,32,1024]{4,3,2,1,0:T(8,128)(2,1)S(1)} %get-tuple-element.48), channel_id=1, source_target_pairs={{0,8},{4,12},{8,16},{12,20},{16,24},{20,28},{24,0},{28,4},{1,9},{5... | collective-permute-start | bytes 2359304 | tf_op jit(solution)/shard_map/ppermute | solution.py:24
  68.7 21.4 %collective-permute-start.4 = (bf16[3,2,32,1024]{3,2,1,0:T(8,128)(2,1)S(1)}, bf16[3,2,32,1024]{3,2,1,0:T(8,128)(2,1)S(1)}, u32[]{:S(2)}, u32[]{:S(2)}) collective-permute-start(bf16[3,2,32,1024]{3,2,1,0:T(8,128)(2,1)S(1)} %get-tuple-element.38), channel_id=1, source_target_pairs={{0,24},{4,28},{8,0},{12,4},{16,8},{20,12},{24,16},{28,20},{1,25},{... | collective-permute-start | bytes 1179656 | tf_op jit(solution)/shard_map/ppermute | solution.py:24
  84.9 13.3 %collective-permute-start.20 = (bf16[3,2,32,1024]{3,2,1,0:T(8,128)(2,1)S(1)}, bf16[3,2,32,1024]{3,2,1,0:T(8,128)(2,1)S(1)}, u32[]{:S(2)}, u32[]{:S(2)}) collective-permute-start(bf16[3,2,32,1024]{3,2,1,0:T(8,128)(2,1)S(1)} %get-tuple-element.50), channel_id=1, source_target_pairs={{0,24},{4,28},{8,0},{12,4},{16,8},{20,12},{24,16},{28,20},{1,25},{... | collective-permute-start | bytes 1179656 | tf_op jit(solution)/shard_map/ppermute | solution.py:24
  85.7 14.3 %collective-permute-start.3 = (bf16[3,2,32,1024]{3,2,1,0:T(8,128)(2,1)S(1)}, bf16[3,2,32,1024]{3,2,1,0:T(8,128)(2,1)S(1)}, u32[]{:S(2)}, u32[]{:S(2)}) collective-permute-start(bf16[3,2,32,1024]{3,2,1,0:T(8,128)(2,1)S(1)} %get-tuple-element.37), channel_id=1, source_target_pairs={{0,8},{4,12},{8,16},{12,20},{16,24},{20,28},{24,0},{28,4},{1,9},{5... | collective-permute-start | bytes 1179656 | tf_op jit(solution)/shard_map/ppermute | solution.py:24
  90.3 10.4 %collective-permute-start.5 = (bf16[3,2,32,1024]{3,2,1,0:T(8,128)(2,1)S(1)}, bf16[3,2,32,1024]{3,2,1,0:T(8,128)(2,1)S(1)}, u32[]{:S(2)}, u32[]{:S(2)}) collective-permute-start(bf16[3,2,32,1024]{3,2,1,0:T(8,128)(2,1)S(1)} %other_half.2), channel_id=1, source_target_pairs={{0,4},{4,0},{8,12},{12,8},{16,20},{20,16},{24,28},{28,24},{1,5},{5... | collective-permute-start | bytes 1179656 | tf_op jit(solution)/shard_map/ppermute | solution.py:24
  91.9 13.5 %collective-permute-start.19 = (bf16[3,2,32,1024]{3,2,1,0:T(8,128)(2,1)S(1)}, bf16[3,2,32,1024]{3,2,1,0:T(8,128)(2,1)S(1)}, u32[]{:S(2)}, u32[]{:S(2)}) collective-permute-start(bf16[3,2,32,1024]{3,2,1,0:T(8,128)(2,1)S(1)} %get-tuple-element.49), channel_id=1, source_target_pairs={{0,8},{4,12},{8,16},{12,20},{16,24},{20,28},{24,0},{28,4},{1,9},{5... | collective-permute-start | bytes 1179656 | tf_op jit(solution)/shard_map/ppermute | solution.py:24
  98.3 12.1 %collective-permute-start.21 = (bf16[3,2,32,1024]{3,2,1,0:T(8,128)(2,1)S(1)}, bf16[3,2,32,1024]{3,2,1,0:T(8,128)(2,1)S(1)}, u32[]{:S(2)}, u32[]{:S(2)}) collective-permute-start(bf16[3,2,32,1024]{3,2,1,0:T(8,128)(2,1)S(1)} %other_half.3), channel_id=1, source_target_pairs={{0,4},{4,0},{8,12},{12,8},{16,20},{20,16},{24,28},{28,24},{1,5},{5... | collective-permute-start | bytes 1179656 | tf_op jit(solution)/shard_map/ppermute | solution.py:24
  101.0 17.8 %collective-permute-start.6 = (bf16[3,2,32,1024]{3,2,1,0:T(8,128)(2,1)S(1)}, bf16[3,2,32,1024]{3,2,1,0:T(8,128)(2,1)S(1)}, u32[]{:S(2)}, u32[]{:S(2)}) collective-permute-start(bf16[3,2,32,1024]{3,2,1,0:T(8,128)(2,1)S(1)} %gate.2), channel_id=1, source_target_pairs={{0,4},{4,0},{8,12},{12,8},{16,20},{20,16},{24,28},{28,24},{1,5},{5... | collective-permute-start | bytes 1179656 | tf_op jit(solution)/shard_map/ppermute | solution.py:24
  110.7 15.3 %collective-permute-start.22 = (bf16[3,2,32,1024]{3,2,1,0:T(8,128)(2,1)S(1)}, bf16[3,2,32,1024]{3,2,1,0:T(8,128)(2,1)S(1)}, u32[]{:S(2)}, u32[]{:S(2)}) collective-permute-start(bf16[3,2,32,1024]{3,2,1,0:T(8,128)(2,1)S(1)} %gate.3), channel_id=1, source_target_pairs={{0,4},{4,0},{8,12},{12,8},{16,20},{20,16},{24,28},{28,24},{1,5},{5... | collective-permute-start | bytes 1179656 | tf_op jit(solution)/shard_map/ppermute | solution.py:24
  118.9 22.2 %collective-permute-start.8 = (bf16[2,3,2,32,1024]{4,3,2,1,0:T(8,128)(2,1)S(1)}, bf16[2,3,2,32,1024]{4,3,2,1,0:T(8,128)(2,1)S(1)}, u32[]{:S(2)}, u32[]{:S(2)}) collective-permute-start(bf16[2,3,2,32,1024]{4,3,2,1,0:T(8,128)(2,1)S(1)} %pad_maximum_fusion.here), channel_id=1, source_target_pairs={{0,8},{4,12},{8,16},{12,20},{16,24},{20,28},{24,0},{28,4},{1,9},{5... | collective-permute-start | bytes 2359304 | tf_op jit(solution)/shard_map/ppermute | solution.py:24
  119.5 21.7 %collective-permute-start.7 = (bf16[2,3,2,32,1024]{4,3,2,1,0:T(8,128)(2,1)S(1)}, bf16[2,3,2,32,1024]{4,3,2,1,0:T(8,128)(2,1)S(1)}, u32[]{:S(2)}, u32[]{:S(2)}) collective-permute-start(bf16[2,3,2,32,1024]{4,3,2,1,0:T(8,128)(2,1)S(1)} %pad_maximum_fusion.here), channel_id=1, source_target_pairs={{0,24},{4,28},{8,0},{12,4},{16,8},{20,12},{24,16},{28,20},{1,25},{... | collective-permute-start | bytes 2359304 | tf_op jit(solution)/shard_map/ppermute | solution.py:24
  126.0 40.4 %copy-start.10 = (bf16[1024,1024]{1,0:T(8,128)(2,1)S(1)}, bf16[1024,1024]{1,0:T(8,128)(2,1)}, u32[]{:S(2)}) copy-start(bf16[1024,1024]{1,0:T(8,128)(2,1)} %wu.7) | copy-start | bytes 6291460
  126.1 31.9 %collective-permute-start.24 = (bf16[2,3,2,32,1024]{4,3,2,1,0:T(8,128)(2,1)S(1)}, bf16[2,3,2,32,1024]{4,3,2,1,0:T(8,128)(2,1)S(1)}, u32[]{:S(2)}, u32[]{:S(2)}) collective-permute-start(bf16[2,3,2,32,1024]{4,3,2,1,0:T(8,128)(2,1)S(1)} %pad_maximum_fusion.1.here), channel_id=1, source_target_pairs={{0,8},{4,12},{8,16},{12,20},{16,24},{20,28},{24,0},{28,4},{1,9},{5... | collective-permute-start | bytes 2359304 | tf_op jit(solution)/shard_map/ppermute | solution.py:24
  126.8 31.3 %collective-permute-start.23 = (bf16[2,3,2,32,1024]{4,3,2,1,0:T(8,128)(2,1)S(1)}, bf16[2,3,2,32,1024]{4,3,2,1,0:T(8,128)(2,1)S(1)}, u32[]{:S(2)}, u32[]{:S(2)}) collective-permute-start(bf16[2,3,2,32,1024]{4,3,2,1,0:T(8,128)(2,1)S(1)} %pad_maximum_fusion.1.here), channel_id=1, source_target_pairs={{0,24},{4,28},{8,0},{12,4},{16,8},{20,12},{24,16},{28,20},{1,25},{... | collective-permute-start | bytes 2359304 | tf_op jit(solution)/shard_map/ppermute | solution.py:24
  141.2 25.2 %collective-permute-start.9 = (bf16[3,2,32,1024]{3,2,1,0:T(8,128)(2,1)S(1)}, bf16[3,2,32,1024]{3,2,1,0:T(8,128)(2,1)S(1)}, u32[]{:S(2)}, u32[]{:S(2)}) collective-permute-start(bf16[3,2,32,1024]{3,2,1,0:T(8,128)(2,1)S(1)} %slice_bitcast_fusion.3), channel_id=1, source_target_pairs={{0,8},{4,12},{8,16},{12,20},{16,24},{20,28},{24,0},{28,4},{1,9},{5... | collective-permute-start | bytes 1179656 | tf_op jit(solution)/shard_map/ppermute | solution.py:24
  141.3 25.1 %collective-permute-start.10 = (bf16[3,2,32,1024]{3,2,1,0:T(8,128)(2,1)S(1)}, bf16[3,2,32,1024]{3,2,1,0:T(8,128)(2,1)S(1)}, u32[]{:S(2)}, u32[]{:S(2)}) collective-permute-start(bf16[3,2,32,1024]{3,2,1,0:T(8,128)(2,1)S(1)} %slice_bitcast_fusion.2), channel_id=1, source_target_pairs={{0,24},{4,28},{8,0},{12,4},{16,8},{20,12},{24,16},{28,20},{1,25},{... | collective-permute-start | bytes 1179656 | tf_op jit(solution)/shard_map/ppermute | solution.py:24
  158.0 18.5 %collective-permute-start.25 = (bf16[3,2,32,1024]{3,2,1,0:T(8,128)(2,1)S(1)}, bf16[3,2,32,1024]{3,2,1,0:T(8,128)(2,1)S(1)}, u32[]{:S(2)}, u32[]{:S(2)}) collective-permute-start(bf16[3,2,32,1024]{3,2,1,0:T(8,128)(2,1)S(1)} %slice_bitcast_fusion.1), channel_id=1, source_target_pairs={{0,8},{4,12},{8,16},{12,20},{16,24},{20,28},{24,0},{28,4},{1,9},{5... | collective-permute-start | bytes 1179656 | tf_op jit(solution)/shard_map/ppermute | solution.py:24
  158.2 18.3 %collective-permute-start.26 = (bf16[3,2,32,1024]{3,2,1,0:T(8,128)(2,1)S(1)}, bf16[3,2,32,1024]{3,2,1,0:T(8,128)(2,1)S(1)}, u32[]{:S(2)}, u32[]{:S(2)}) collective-permute-start(bf16[3,2,32,1024]{3,2,1,0:T(8,128)(2,1)S(1)} %slice_bitcast_fusion), channel_id=1, source_target_pairs={{0,24},{4,28},{8,0},{12,4},{16,8},{20,12},{24,16},{28,20},{1,25},{... | collective-permute-start | bytes 1179656 | tf_op jit(solution)/shard_map/ppermute | solution.py:24
  170.6 10.1 %copy-start.11 = (bf16[3,512,1024]{2,1,0:T(8,128)(2,1)}, bf16[3,512,1024]{2,1,0:T(8,128)(2,1)S(1)}, u32[]{:S(2)}) copy-start(bf16[3,512,1024]{2,1,0:T(8,128)(2,1)S(1)} %get-tuple-element.57.refs_4_) | copy-start | bytes 9437188
  170.6 13.2 %collective-permute-start.11 = (bf16[2,64,1024]{2,1,0:T(8,128)(2,1)S(1)}, bf16[2,64,1024]{2,1,0:T(8,128)(2,1)S(1)}, u32[]{:S(2)}, u32[]{:S(2)}) collective-permute-start(bf16[2,64,1024]{2,1,0:T(8,128)(2,1)S(1)} %get-tuple-element.40), channel_id=1, source_target_pairs={{0,1},{1,2},{2,3},{3,0},{4,5},{5,6},{6,7},{7,4},{8,9},{9,10},{10,1... | collective-permute-start | bytes 786440 | tf_op jit(solution)/shard_map/ppermute | solution.py:33
  172.3 13.5 %collective-permute-start.12 = (bf16[2,64,1024]{2,1,0:T(8,128)(2,1)S(1)}, bf16[2,64,1024]{2,1,0:T(8,128)(2,1)S(1)}, u32[]{:S(2)}, u32[]{:S(2)}) collective-permute-start(bf16[2,64,1024]{2,1,0:T(8,128)(2,1)S(1)} %get-tuple-element.41), channel_id=1, source_target_pairs={{0,2},{1,3},{2,0},{3,1},{4,6},{5,7},{6,4},{7,5},{8,10},{9,11},{10,... | collective-permute-start | bytes 786440 | tf_op jit(solution)/shard_map/ppermute | solution.py:33
  175.2 10.6 %collective-permute-start.13 = (bf16[2,64,1024]{2,1,0:T(8,128)(2,1)S(1)}, bf16[2,64,1024]{2,1,0:T(8,128)(2,1)S(1)}, u32[]{:S(2)}, u32[]{:S(2)}) collective-permute-start(bf16[2,64,1024]{2,1,0:T(8,128)(2,1)S(1)} %get-tuple-element.42), channel_id=1, source_target_pairs={{0,3},{1,0},{2,1},{3,2},{4,7},{5,4},{6,5},{7,6},{8,11},{9,8},{10,9... | collective-permute-start | bytes 786440 | tf_op jit(solution)/shard_map/ppermute | solution.py:33
  180.7 1.7 copy-start.13
  182.4 12.0 %collective-permute-start.27 = (bf16[2,64,1024]{2,1,0:T(8,128)(2,1)S(1)}, bf16[2,64,1024]{2,1,0:T(8,128)(2,1)S(1)}, u32[]{:S(2)}, u32[]{:S(2)}) collective-permute-start(bf16[2,64,1024]{2,1,0:T(8,128)(2,1)S(1)} %get-tuple-element.52), channel_id=1, source_target_pairs={{0,1},{1,2},{2,3},{3,0},{4,5},{5,6},{6,7},{7,4},{8,9},{9,10},{10,1... | collective-permute-start | bytes 786440 | tf_op jit(solution)/shard_map/ppermute | solution.py:33
  183.1 11.4 %collective-permute-start.28 = (bf16[2,64,1024]{2,1,0:T(8,128)(2,1)S(1)}, bf16[2,64,1024]{2,1,0:T(8,128)(2,1)S(1)}, u32[]{:S(2)}, u32[]{:S(2)}) collective-permute-start(bf16[2,64,1024]{2,1,0:T(8,128)(2,1)S(1)} %get-tuple-element.53), channel_id=1, source_target_pairs={{0,2},{1,3},{2,0},{3,1},{4,6},{5,7},{6,4},{7,5},{8,10},{9,11},{10,... | collective-permute-start | bytes 786440 | tf_op jit(solution)/shard_map/ppermute | solution.py:33
  183.9 10.6 %collective-permute-start.29 = (bf16[2,64,1024]{2,1,0:T(8,128)(2,1)S(1)}, bf16[2,64,1024]{2,1,0:T(8,128)(2,1)S(1)}, u32[]{:S(2)}, u32[]{:S(2)}) collective-permute-start(bf16[2,64,1024]{2,1,0:T(8,128)(2,1)S(1)} %get-tuple-element.54), channel_id=1, source_target_pairs={{0,3},{1,0},{2,1},{3,2},{4,7},{5,4},{6,5},{7,6},{8,11},{9,8},{10,9... | collective-permute-start | bytes 786440 | tf_op jit(solution)/shard_map/ppermute | solution.py:33
  185.9 27.0 %collective-permute-start.14 = (bf16[64,1024]{1,0:T(8,128)(2,1)S(1)}, bf16[64,1024]{1,0:T(8,128)(2,1)S(1)}, u32[]{:S(2)}, u32[]{:S(2)}) collective-permute-start(bf16[64,1024]{1,0:T(8,128)(2,1)S(1)} %get-tuple-element.44), channel_id=1, source_target_pairs={{0,32},{32,0},{64,96},{96,64},{1,33},{33,1},{65,97},{97,65},{2,34}... | collective-permute-start | bytes 393224 | tf_op jit(solution)/shard_map/ppermute | solution.py:29
  194.6 18.3 %collective-permute-start.31 = (bf16[64,1024]{1,0:T(8,128)(2,1)S(1)}, bf16[64,1024]{1,0:T(8,128)(2,1)S(1)}, u32[]{:S(2)}, u32[]{:S(2)}) collective-permute-start(bf16[64,1024]{1,0:T(8,128)(2,1)S(1)} %get-tuple-element.56), channel_id=1, source_target_pairs={{0,96},{32,64},{64,32},{96,0},{1,97},{33,65},{65,33},{97,1},{2,98}... | collective-permute-start | bytes 393224 | tf_op jit(solution)/shard_map/ppermute | solution.py:29
  194.7 18.2 %collective-permute-start.30 = (bf16[64,1024]{1,0:T(8,128)(2,1)S(1)}, bf16[64,1024]{1,0:T(8,128)(2,1)S(1)}, u32[]{:S(2)}, u32[]{:S(2)}) collective-permute-start(bf16[64,1024]{1,0:T(8,128)(2,1)S(1)} %get-tuple-element.55), channel_id=1, source_target_pairs={{0,64},{32,96},{64,0},{96,32},{1,65},{33,97},{65,1},{97,33},{2,66}... | collective-permute-start | bytes 393224 | tf_op jit(solution)/shard_map/ppermute | solution.py:29
  197.8 1.9 copy-start.12
  199.6 1.9 copy-start.14

commit v3 on v0

v3 whole, which is shorter than its diff:
```python
import jax
import jax.numpy as jnp
from jax import lax
from jax.experimental import pallas as pl
from jax.experimental.pallas import tpu as pltpu
from jax.sharding import PartitionSpec as P

BF = jnp.bfloat16
F32 = jnp.float32
NT = (((1,), (1,)), ((), ()))
VMEM_LIMIT = 16 * 1024 * 1024
PIPE_LIMIT = 24 * 1024 * 1024
SMEM = pl.BlockSpec(memory_space=pltpu.SMEM)
VMEM = pl.BlockSpec(memory_space=pltpu.VMEM)
WIDE_LIMIT = 56 * 1024 * 1024


def params(limit=VMEM_LIMIT):
    return pltpu.CompilerParams(vmem_limit_bytes=limit)


def cost(flops, nbytes):
    return pl.CostEstimate(flops=flops, bytes_accessed=nbytes, transcendentals=0)


def fin_perm(x, dz, dx):
    pairs = [(z * 2 + l, ((z + dz) % 4) * 2 + (l ^ dx)) for z in range(4) for l in range(2)]
    return lax.ppermute(x, "fin", pairs)


def tok_perm(x, dh, dc):
    pairs = [(h * 2 + c, (h ^ dh) * 2 + (c ^ dc)) for h in range(2) for c in range(2)]
    return lax.ppermute(x, "tok", pairs)


def y_perm(x, dy):
    return lax.ppermute(x, "fout", [(y, (y + dy) % 4) for y in range(4)])


def after(x, *done):
    n = len(x)
    return lax.optimization_barrier((*x, *done))[:n]


def row_start(z, lo, r, s):
    return pl.multiple_of((lax.rem(z + r, 4) * 2 + lax.bitwise_xor(lo, s)) * 32, 32)


def scale_kernel(margin, x, up, weight, ids, out):
    tokens = x.shape[0]
    out[0] = x[...]
    pair = ids[...] // 2
    picked = jnp.zeros(pair.shape, F32)
    for p in range(margin.shape[0]):
        picked = jnp.where(pair == p, margin[p], picked)
    side = jnp.where(ids[...] % 2 == 0, -1.0, 1.0)
    row = weight[...].astype(F32) * (side * jax.nn.sigmoid(-picked))
    at = lax.broadcasted_iota(jnp.int32, (tokens, tokens), 0)
    to = lax.broadcasted_iota(jnp.int32, (tokens, tokens), 1)
    column = jnp.sum(jnp.where(at == to, row, 0.0), axis=1, keepdims=True)
    out[1] = (column * up[...].astype(F32)).astype(BF)


def scaled(inputs, upstream, loss_weight, pair_ids, margin):
    tokens, depth = inputs.shape
    tile = depth // 2
    wide = pl.BlockSpec((tokens, tile), lambda i: (0, i))
    row = pl.BlockSpec((1, tokens), lambda i: (0, 0))
    return pl.pallas_call(
        scale_kernel,
        grid=(depth // tile,),
        in_specs=[pl.BlockSpec(memory_space=pltpu.SMEM), wide, wide, row, row],
        out_specs=pl.BlockSpec((2, tokens, tile), lambda i: (0, 0, i)),
        out_shape=jax.ShapeDtypeStruct((2, tokens, depth), BF),
        compiler_params=params(WIDE_LIMIT),
        cost_estimate=cost(4 * tokens * depth, 8 * tokens * depth),
        name="scaled",
    )(margin, inputs, upstream, loss_weight.reshape(1, -1), pair_ids.reshape(1, -1))


def forward_kernel(idx, m, wg, wu, wd, plus, minus, keep, own, acc):
    z, lo = idx[0], idx[1]
    tile = acc.shape[2]

    @pl.loop(0, wg.shape[1] // tile)
    def _(i):
        at = pl.ds(pl.multiple_of(i * tile, tile), tile)
        acc[0] = jnp.dot(m[0], wg[:, at], preferred_element_type=F32)
        acc[1] = jnp.dot(m[0], wu[:, at], preferred_element_type=F32)
        acc[2] = lax.dot_general(m[1], wd[at, :], NT, preferred_element_type=F32)

        def block(r, s):
            return acc[:, pl.ds(row_start(z, lo, r, s), 32), :]

        plus[0, :, :, at] = block(2, 0).astype(BF)
        plus[1, :, :, at] = block(1, 1).astype(BF)
        minus[0, :, :, at] = block(2, 1).astype(BF)
        minus[1, :, :, at] = block(3, 0).astype(BF)
        keep[0, :, :, at] = block(1, 0)
        keep[1, :, :, at] = block(3, 1)
        own[0, :, :, at] = block(0, 0)
        own[1, :, :, at] = block(0, 1)


def forward(idx, m, wg, wu, wd):
    _, tokens, depth = m.shape
    width = wg.shape[1]
    tile = 256
    shape = (2, 3, 32, width)
    return pl.pallas_call(
        forward_kernel,
        in_specs=[SMEM] + [VMEM] * 4,
        out_specs=[VMEM] * 4,
        out_shape=[
            jax.ShapeDtypeStruct(shape, BF),
            jax.ShapeDtypeStruct(shape, BF),
            jax.ShapeDtypeStruct(shape, F32),
            jax.ShapeDtypeStruct(shape, F32),
        ],
        scratch_shapes=[pltpu.VMEM((3, tokens, tile), F32)],
        compiler_params=params(),
        cost_estimate=cost(6 * tokens * depth * width, 5 * 2**20),
        name="forward",
    )(idx, m, wg, wu, wd)


def pass_on_kernel(*refs):
    plus, minus = refs[6:]
    for t in range(2):
        keep, from_minus, from_plus = refs[3 * t : 3 * t + 3]
        plus[:, t] = (keep[0] + from_minus[0].astype(F32)).astype(BF)
        minus[:, t] = (keep[1] + from_plus[0].astype(F32)).astype(BF)


def pass_on(keeps, nears):
    _, three, rows, width = keeps[0].shape
    shape = jax.ShapeDtypeStruct((three, 2, rows, width), BF)
    size = 2 * keeps[0].size
    return pl.pallas_call(
        pass_on_kernel,
        out_shape=[shape, shape],
        compiler_params=params(),
        cost_estimate=cost(size, size * 8),
        name="pass_on",
    )(keeps[0], *nears[:2], keeps[1], *nears[2:])


def ring_sum_kernel(*refs):
    last_minus, last_plus, held, sent = refs[6:]
    for t in range(2):
        own, from_minus, from_plus = refs[3 * t : 3 * t + 3]
        held[0, :, t] = own[0] + from_plus[1].astype(F32) + last_minus[:, t].astype(F32)
        held[1, :, t] = own[1] + from_minus[1].astype(F32) + last_plus[:, t].astype(F32)
    sent[...] = held[...].astype(BF)


def ring_sum(owns, nears, last_minus, last_plus):
    _, three, rows, width = owns[0].shape
    shape = (2, three, 2, rows, width)
    size = 2 * owns[0].size
    return pl.pallas_call(
        ring_sum_kernel,
        out_shape=[jax.ShapeDtypeStruct(shape, F32), jax.ShapeDtypeStruct(shape, BF)],
        compiler_params=params(),
        cost_estimate=cost(size * 4, size * 14),
        name="ring_sum",
    )(owns[0], *nears[:2], owns[1], *nears[2:], last_minus, last_plus)


def gate_kernel(held, across, out):
    for half in range(2):
        pre_gate, pre_up, grad_hidden = (
            held[half, i] + across[1 - half, i].astype(F32) for i in range(3)
        )
        s = jax.nn.sigmoid(pre_gate)
        activated = pre_gate * s
        out[half, 2] = (activated * pre_up).astype(BF)
        out[half, 0] = (grad_hidden * pre_up * s * (1.0 + pre_gate * (1.0 - s))).astype(BF)
        out[half, 1] = (grad_hidden * activated).astype(BF)


def gate(held, across):
    return pl.pallas_call(
        gate_kernel,
        out_shape=jax.ShapeDtypeStruct(held.shape, BF),
        compiler_params=params(),
        cost_estimate=cost(held.size * 8, held.size * 8),
        name="gate",
    )(held, across)


def input_grad_kernel(idx, here, plus1, far_a, far_b, minus1, wg, wu, own, to1, to2, to3, acts, acc):
    z, lo, y = idx[0], idx[1], idx[2]
    tokens = acts.shape[1] // 2
    tile = acc.shape[1]
    for r, s, block in (
        (0, 0, here.at[0]),
        (0, 1, here.at[1]),
        (1, 0, plus1.at[0]),
        (1, 1, plus1.at[1]),
        (2, 0, far_a),
        (2, 1, far_b),
        (3, 0, minus1.at[0]),
        (3, 1, minus1.at[1]),
    ):
        start = row_start(z, lo, r, s)
        for t in range(2):
            acts[:, pl.ds(t * tokens + start, 32), :] = block[:, t]

    @pl.loop(0, wg.shape[0] // tile)
    def _(i):
        at = pl.ds(pl.multiple_of(i * tile, tile), tile)
        acc[...] = lax.dot_general(acts[0], wg[at, :], NT, preferred_element_type=F32)
        acc[...] += lax.dot_general(acts[1], wu[at, :], NT, preferred_element_type=F32)
        for r, out in enumerate((own, to1, to2, to3)):
            start = pl.multiple_of(lax.rem(y + r, 4) * 64, 64)
            for t in range(2):
                out[t, :, at] = acc[pl.ds(t * tokens + start, 64), :].astype(out.dtype)


def input_grad(idx, here, plus1, far_a, far_b, minus1, wg, wu):
    depth, width = wg.shape
    tokens = 256
    tile = 256
    return pl.pallas_call(
        input_grad_kernel,
        in_specs=[SMEM] + [VMEM] * 7,
        out_specs=[VMEM] * 5,
        out_shape=[
            jax.ShapeDtypeStruct((2, 64, depth), F32),
            jax.ShapeDtypeStruct((2, 64, depth), BF),
            jax.ShapeDtypeStruct((2, 64, depth), BF),
            jax.ShapeDtypeStruct((2, 64, depth), BF),
            jax.ShapeDtypeStruct((3, 2 * tokens, width), BF),
        ],
        scratch_shapes=[pltpu.VMEM((2 * tokens, tile), F32)],
        compiler_params=params(),
        cost_estimate=cost(8 * tokens * depth * width, 10 * 2**20),
        name="input_grad",
    )(idx, here, plus1, far_a, far_b, minus1, wg, wu)


def owned_kernel(own0, a0, b0, c0, own1, a1, b1, c1, mine, core, far, cross):
    first = own0[...] + a0[...].astype(F32) + b0[...].astype(F32) + c0[...].astype(F32)
    last = own1[...] + a1[...].astype(F32) + b1[...].astype(F32) + c1[...].astype(F32)
    mine[...] = first[0]
    core[...] = first[1].astype(BF)
    far[...] = last[0].astype(BF)
    cross[...] = last[1].astype(BF)


def owned(first, last):
    shape = first[0].shape[1:]
    small = jax.ShapeDtypeStruct(shape, BF)
    return pl.pallas_call(
        owned_kernel,
        out_shape=[jax.ShapeDtypeStruct(shape, F32), small, small, small],
        compiler_params=params(),
        cost_estimate=cost(first[0].size * 8, first[0].size * 20),
        name="owned",
    )(*first, *last)


def in_grads_kernel(*refs):
    rows, acts, before, (gate_out, up_out, xt) = refs[:2], refs[2], refs[3:-3], refs[-3:]

    @pl.when(pl.program_id(0) == 0)
    def _():
        for k in range(2):
            xt[:, k * 256 : (k + 1) * 256] = rows[k][0].T

    for k, out in enumerate((gate_out, up_out)):
        total = jnp.dot(xt[...], acts[k], preferred_element_type=F32)
        if before:
            total += before[k][...]
        out[...] = total.astype(out.dtype)


def in_grads(rows, acts, before, dtype):
    _, tokens, depth = rows[0].shape
    width = acts.shape[2]
    tile = 256
    full = pl.BlockSpec((1, tokens, depth), lambda i: (0, 0, 0))
    part = pl.BlockSpec((depth, tile), lambda i: (0, i))
    out = jax.ShapeDtypeStruct((depth, width), dtype)
    return pl.pallas_call(
        in_grads_kernel,
        grid=(width // tile,),
        in_specs=[full] * 2
        + [pl.BlockSpec((2, 2 * tokens, tile), lambda i: (0, 0, i))]
        + [part] * len(before),
        out_specs=[part] * 2,
        out_shape=[out, out],
        scratch_shapes=[pltpu.VMEM((depth, 2 * tokens), BF)],
        compiler_params=params(PIPE_LIMIT),
        cost_estimate=cost(8 * tokens * depth * width, 12 * 2**20),
        name="in_grads",
    )(*rows, acts, *before)


def down_grad_kernel(*refs):
    rows, acts = refs[:4], refs[4:6]
    out, g = refs[6:]

    @pl.when(pl.program_id(0) == 0)
    def _():
        for k in range(4):
            g[k * 256 : (k + 1) * 256, :] = rows[k][0]

    hidden = jnp.concatenate([r[0] for r in acts], axis=0)
    out[...] = jnp.dot(hidden.T, g[...], preferred_element_type=F32).astype(BF)


def down_grad(rows, acts):
    _, tokens, depth = rows[0].shape
    width = acts[0].shape[2]
    tile = 256
    full = pl.BlockSpec((1, tokens, depth), lambda i: (1, 0, 0))
    return pl.pallas_call(
        down_grad_kernel,
        grid=(width // tile,),
        in_specs=[full] * 4 + [pl.BlockSpec((1, 2 * tokens, tile), lambda i: (2, 0, i))] * 2,
        out_specs=pl.BlockSpec((tile, depth), lambda i: (i, 0)),
        out_shape=jax.ShapeDtypeStruct((width, depth), BF),
        scratch_shapes=[pltpu.VMEM((4 * tokens, depth), BF)],
        compiler_params=params(PIPE_LIMIT),
        cost_estimate=cost(8 * tokens * depth * width, 6 * 2**20),
        name="down_grad",
    )(*rows, *acts)


def body(inputs, upstream, loss_weight, pair_ids, margin, w_gate, w_up, w_down):
    fin = lax.axis_index("fin")
    idx = jnp.stack([fin // 2, fin % 2, lax.axis_index("fout")]).astype(jnp.int32)

    m0 = scaled(inputs, upstream, loss_weight, pair_ids, margin)
    m1 = tok_perm(m0, 0, 1)
    m2 = tok_perm(m0, 1, 0)

    def ring(plus, minus):
        return fin_perm(plus, 1, 0), fin_perm(minus, 3, 0)

    def over_y(own, to1, to2, to3):
        return own, y_perm(to1, 1), y_perm(to2, 2), y_perm(to3, 3)

    weights = w_gate, w_up, w_down
    *out, keep_a, own_a = forward(idx, m0, *weights)
    near_a = ring(*out)
    (m1,) = after((m1,), *out)
    *out, keep_b, own_b = forward(idx, m1, *weights)
    near0 = *near_a, *ring(*out)
    owns0 = own_a, own_b
    step0 = pass_on((keep_a, keep_b), near0)
    last0 = ring(*step0)

    (m2,) = after((m2,), *step0)
    m3 = tok_perm(m2, 0, 1)
    *out, keep_a, own_a = forward(idx, m2, *weights)
    near_a = ring(*out)
    last0 = after(last0, *out)
    held0, sent0 = ring_sum(owns0, near0, *last0)
    across0 = fin_perm(sent0, 0, 1)
    (m3,) = after((m3,), sent0)
    *out, keep_b, own_b = forward(idx, m3, *weights)
    near1 = *near_a, *ring(*out)
    step1 = pass_on((keep_a, keep_b), near1)
    last1 = ring(*step1)

    (across0,) = after((across0,), *step1)
    here0 = gate(held0, across0)
    last1 = after(last1, here0)
    held1, sent1 = ring_sum((own_a, own_b), near1, *last1)
    across1 = fin_perm(sent1, 0, 1)

    (ready,) = after((here0,), sent1)
    minus1, plus1 = ring(ready, ready)
    on_plus, on_minus = minus1[0], plus1[1]
    far0 = ring(on_plus, on_minus)
    (across1,) = after((across1,), on_plus, on_minus)
    here1 = gate(held1, across1)
    side1 = ring(here1, here1)

    far0 = after(far0, here1)
    *grad0, act0 = input_grad(idx, here0, plus1, *far0, minus1, w_gate, w_up)
    first = over_y(*grad0)
    before = in_grads((m0, m1), act0, (), F32)

    minus1, plus1 = after(side1, *before)
    far1 = ring(minus1[0], plus1[1])
    *grad1, act1 = input_grad(idx, here1, plus1, *far1, minus1, w_gate, w_up)
    last = over_y(*grad1)

    grad_gate, grad_up = in_grads((m2, m3), act1, before, BF)
    rows = after((m0, m1, m2, m3), grad_gate)
    grad_down = down_grad(rows, (act0, act1))
    parts = after((*first, *last), grad_down)
    mine, core, far_part, cross = owned(parts[:4], parts[4:])
    others = (tok_perm(core, 0, 1), tok_perm(far_part, 1, 0), tok_perm(cross, 1, 1))
    total = mine + sum(r.astype(F32) for r in others)
    return (total.astype(BF), grad_gate, grad_up, grad_down)


def solution(mesh):
    placed = (
        P("tok", "fin"),
        P("tok", "fin"),
        P("tok"),
        P("tok"),
        P(),
        P("fin", ("tok", "fout")),
        P("fin", ("tok", "fout")),
        P(("tok", "fout"), "fin"),
    )
    return jax.shard_map(
        body,
        mesh=mesh,
        in_specs=placed,
        out_specs=(
            P(("tok", "fout"), "fin"),
            P("fin", ("tok", "fout")),
            P("fin", ("tok", "fout")),
            P(("tok", "fout"), "fin"),
        ),
        check_vma=False,
    )
```

time: 675 us -> 162 us (0.24)
  waiting for transfers between devices: 596 us -> 60.5 us
  starting transfers between devices: 0.34 us -> 53.1 us
  matrix products: 44 us -> 0 us
  Pallas kernels: 0 us -> 40.8 us
  between operations: 13.8 us -> 0.91 us
  other arithmetic: 11.6 us -> 0.8 us
    psum x1 -> x0, waiting for transfers between devices: 498 us -> none  [body(): lax.psum((part_gate, part_up, part_hidden), 'fin')]
    ppermute x0 -> x34, waiting for transfers between devices: none -> 60.5 us  [the longest x22 55.9 us: fin_perm(): return lax.ppermute(x, 'fin', pairs)]
    reduce_scatter x1 -> x0, waiting for transfers between devices: 53.3 us -> none  [body(): lax.psum_scatter(first + second, ('tok', 'fout'), scatter_dimension=0, ti...]
    ppermute x0 -> x34, starting transfers between devices: none -> 53.1 us  [the longest x22 34.9 us: fin_perm(): return lax.ppermute(x, 'fin', pairs)]
    all_gather x2 -> x0, waiting for transfers between devices: 44.5 us -> none  [the longest x1 26.5 us: body(): lax.all_gather(inputs, 'tok', axis=0, tiled=True)]
    dot_general x8 -> x0, matrix products: 44 us -> none  [the longest x1 8.38 us: body(): lax.dot_general(hidden, all_grad_out, (((0,), (0,)), ((), ())), preferred...]
    pallas_call x0 -> x17, Pallas kernels: none -> 40.8 us  [the longest x4 13.4 us: forward(): pl.pallas_call(forward_kernel, in_specs=[SMEM] + [VMEM] * 4, out_specs=[V...]
    convert_element_type x3 -> x1, other arithmetic: 9.51 us -> 0.73 us  [body(): return (total.astype(BF), grad_gate, grad_up, grad_down)]
  transfers between devices with their start and end apart: 4 -> 34, of which waited for: 4 -> 13; matrix products, arithmetic and copies ran while one was open for 6% -> 0% of each run, Pallas kernels for 0% -> 24%
where the time goes in v3:
time: 162 us; the launch traced here: 161 us
  waiting for transfers between devices  60.5 us (37%)
  starting transfers between devices  53.1 us (33%)
  Pallas kernels  40.8 us (25%)
  local copies, waits for them, and re-layouts  4.54 us (3%)
    ppermute x22, waiting for transfers between devices, fin_perm(): return lax.ppermute(x, 'fin', pairs)  55.9 us
    ppermute x22, starting transfers between devices, fin_perm(): return lax.ppermute(x, 'fin', pairs)  34.9 us
    pallas_call x4, Pallas kernels, forward(): pl.pallas_call(forward_kernel, in_specs=[SMEM] + [VMEM] * 4, out_specs=[V...  13.4 us
    ppermute x6, starting transfers between devices, y_perm(): return lax.ppermute(x, 'fout', [(y, (y + dy) % 4) for y in range(4)])  11.5 us
    pallas_call x2, Pallas kernels, in_grads(): pl.pallas_call(in_grads_kernel, grid=(width // tile,), in_specs=[full] *...  10.2 us
    pallas_call x2, Pallas kernels, input_grad(): pl.pallas_call(input_grad_kernel, in_specs=[SMEM] + [VMEM] * 7, out_specs...  7.73 us
    ppermute x6, starting transfers between devices, tok_perm(): return lax.ppermute(x, 'tok', pairs)  6.65 us
    pallas_call x1, Pallas kernels, down_grad(): pl.pallas_call(down_grad_kernel, grid=(width // tile,), in_specs=[full] *...  5.19 us
  transfers between devices with their start and end apart: 34, of which 13 were waited for; matrix products, arithmetic and copies ran while one was open for 0% of the time, Pallas kernels for 24%

profile of v3, /device:TPU:0, one launch (start us, length us, event | category | flops | bytes accessed | tf_op | source)
XLA Modules:
  0.0 160.6 jit_solution(4459581630034750038)
XLA Ops:
  0.6 2.3 %scaled.1.m.refs_0_ = bf16[2,256,1024]{2,1,0:T(8,128)(2,1)} custom-call(f32[16]{0:T(128)} %margin.1, bf16[256,1024]{1,0:T(8,128)(2,1)} %x.1, bf16[256,1024]{1,0:T(8,128)(2,1)} %up.1, s32[1,256]{1,0:T(1,128)} %bitcast.13, s32[1,256]{1,0:T(1,128)} %bitcast.14), custom_call_target="tpu_custom_call" | custom-call | flops 1048576 | bytes 2097152 | tf_op jit(solution)/shard_map/scaled/pallas_call | solution.py:69
  3.0 3.1 %collective-permute-start.7 = (bf16[2,256,1024]{2,1,0:T(8,128)(2,1)}, bf16[2,256,1024]{2,1,0:T(8,128)(2,1)S(1)}, u32[]{:S(2)}, u32[]{:S(2)}) collective-permute-start(bf16[2,256,1024]{2,1,0:T(8,128)(2,1)} %scaled.1.m.refs_0_), channel_id=1, source_target_pairs={{0,64},{32,96},{64,0},{96,32},{1,65},{33,97},{65,1},{97,33},{2,66}... | collective-permute-start | bytes 3145736 | tf_op jit(solution)/shard_map/ppermute | solution.py:33
  6.2 1.6 copy-done.1
  7.8 1.6 copy-done.3
  9.4 1.2 copy-done.5
  10.6 3.2 %forward.4 = (bf16[2,3,32,1024]{3,2,1,0:T(8,128)(2,1)S(1)}, bf16[2,3,32,1024]{3,2,1,0:T(8,128)(2,1)S(1)}, f32[2,3,32,1024]{3,2,1,0:T(8,128)S(1)}, f32[2,3,32,1024]{3,2,1,0:T(8,128)S(1)}) custom-call(s32[3]{0:T(128)S(1)} %pad_add_fusion.idx, bf16[2,256,1024]{2,1,0:T(8,128)(2,1)S(1)} %copy-done.5, bf16[1024,1024]{1,0:T(8,128)(2,1)S(1)} %copy-done.1, ...), custom_call_target="tpu_custom_call" | custom-call | flops 1610612736 | bytes 5242880 | tf_op jit(solution)/shard_map/forward/pallas_call | solution.py:110
  13.8 2.0 %collective-permute-start = (bf16[2,3,32,1024]{3,2,1,0:T(8,128)(2,1)S(1)}, bf16[2,3,32,1024]{3,2,1,0:T(8,128)(2,1)S(1)}, u32[]{:S(2)}, u32[]{:S(2)}) collective-permute-start(bf16[2,3,32,1024]{3,2,1,0:T(8,128)(2,1)S(1)} %get-tuple-element.73), channel_id=1, source_target_pairs={{0,8},{4,12},{8,16},{12,20},{16,24},{20,28},{24,0},{28,4},{1,9},{5... | collective-permute-start | bytes 1179656 | tf_op jit(solution)/shard_map/ppermute | solution.py:28
  15.8 2.2 %collective-permute-start.1 = (bf16[2,3,32,1024]{3,2,1,0:T(8,128)(2,1)S(1)}, bf16[2,3,32,1024]{3,2,1,0:T(8,128)(2,1)S(1)}, u32[]{:S(2)}, u32[]{:S(2)}) collective-permute-start(bf16[2,3,32,1024]{3,2,1,0:T(8,128)(2,1)S(1)} %get-tuple-element.74), channel_id=1, source_target_pairs={{0,24},{4,28},{8,0},{12,4},{16,8},{20,12},{24,16},{28,20},{1,25},{... | collective-permute-start | bytes 1179656 | tf_op jit(solution)/shard_map/ppermute | solution.py:28
  18.0 3.9 %forward.5 = (bf16[2,3,32,1024]{3,2,1,0:T(8,128)(2,1)S(1)}, bf16[2,3,32,1024]{3,2,1,0:T(8,128)(2,1)S(1)}, f32[2,3,32,1024]{3,2,1,0:T(8,128)S(1)}, f32[2,3,32,1024]{3,2,1,0:T(8,128)S(1)}) custom-call(s32[3]{0:T(128)S(1)} %pad_add_fusion.idx, bf16[2,256,1024]{2,1,0:T(8,128)(2,1)} %collective-permute-done.2.m.refs_1_, bf16[1024,1024]{1,0:T(8,128)(2,1)S(1)} %copy-done.2, ...), custom_call_target="tpu_custom_call" | custom-call | flops 1610612736 | bytes 5242880 | tf_op jit(solution)/shard_map/forward/pallas_call | solution.py:110
  21.9 3.2 %collective-permute-start.4 = (bf16[2,3,32,1024]{3,2,1,0:T(8,128)(2,1)S(1)}, bf16[2,3,32,1024]{3,2,1,0:T(8,128)(2,1)S(1)}, u32[]{:S(2)}, u32[]{:S(2)}) collective-permute-start(bf16[2,3,32,1024]{3,2,1,0:T(8,128)(2,1)S(1)} %get-tuple-element.78), channel_id=1, source_target_pairs={{0,24},{4,28},{8,0},{12,4},{16,8},{20,12},{24,16},{28,20},{1,25},{... | collective-permute-start | bytes 1179656 | tf_op jit(solution)/shard_map/ppermute | solution.py:28
  25.2 2.6 %collective-permute-done.refs_1_ = bf16[2,3,32,1024]{3,2,1,0:T(8,128)(2,1)S(1)} collective-permute-done((bf16[2,3,32,1024]{3,2,1,0:T(8,128)(2,1)S(1)}, bf16[2,3,32,1024]{3,2,1,0:T(8,128)(2,1)S(1)}, u32[]{:S(2)}, u32[]{:S(2)}) %collective-permute-start) | collective-permute-done | bytes 393248 | tf_op jit(solution)/shard_map/ppermute | solution.py:28
  27.8 8.0 %collective-permute-done.3.refs_4_ = bf16[2,3,32,1024]{3,2,1,0:T(8,128)(2,1)S(1)} collective-permute-done((bf16[2,3,32,1024]{3,2,1,0:T(8,128)(2,1)S(1)}, bf16[2,3,32,1024]{3,2,1,0:T(8,128)(2,1)S(1)}, u32[]{:S(2)}, u32[]{:S(2)}) %collective-permute-start.3) | collective-permute-done | bytes 393248 | tf_op jit(solution)/shard_map/ppermute | solution.py:28
  36.1 1.3 collective-permute-start.5
  37.4 2.0 %collective-permute-start.6 = (bf16[3,2,32,1024]{3,2,1,0:T(8,128)(2,1)S(1)}, bf16[3,2,32,1024]{3,2,1,0:T(8,128)(2,1)S(1)}, u32[]{:S(2)}, u32[]{:S(2)}) collective-permute-start(bf16[3,2,32,1024]{3,2,1,0:T(8,128)(2,1)S(1)} %get-tuple-element.82), channel_id=1, source_target_pairs={{0,24},{4,28},{8,0},{12,4},{16,8},{20,12},{24,16},{28,20},{1,25},{... | collective-permute-start | bytes 1179656 | tf_op jit(solution)/shard_map/ppermute | solution.py:28
  39.4 3.2 %forward.6 = (bf16[2,3,32,1024]{3,2,1,0:T(8,128)(2,1)S(1)}, bf16[2,3,32,1024]{3,2,1,0:T(8,128)(2,1)S(1)}, f32[2,3,32,1024]{3,2,1,0:T(8,128)S(1)}, f32[2,3,32,1024]{3,2,1,0:T(8,128)S(1)}) custom-call(s32[3]{0:T(128)S(1)} %pad_add_fusion.idx, bf16[2,256,1024]{2,1,0:T(8,128)(2,1)S(1)} %collective-permute-done.7.m.refs_0_.refs_2_, ...), custom_call_target="tpu_custom_call" | custom-call | flops 1610612736 | bytes 5242880 | tf_op jit(solution)/shard_map/forward/pallas_call | solution.py:110
  42.7 3.2 %collective-permute-start.10 = (bf16[2,3,32,1024]{3,2,1,0:T(8,128)(2,1)S(1)}, bf16[2,3,32,1024]{3,2,1,0:T(8,128)(2,1)S(1)}, u32[]{:S(2)}, u32[]{:S(2)}) collective-permute-start(bf16[2,3,32,1024]{3,2,1,0:T(8,128)(2,1)S(1)} %get-tuple-element.85), channel_id=1, source_target_pairs={{0,24},{4,28},{8,0},{12,4},{16,8},{20,12},{24,16},{28,20},{1,25},{... | collective-permute-start | bytes 1179656 | tf_op jit(solution)/shard_map/ppermute | solution.py:28
  45.8 3.4 %collective-permute-done.5.refs_6_ = bf16[3,2,32,1024]{3,2,1,0:T(8,128)(2,1)S(1)} collective-permute-done((bf16[3,2,32,1024]{3,2,1,0:T(8,128)(2,1)S(1)}, bf16[3,2,32,1024]{3,2,1,0:T(8,128)(2,1)S(1)}, u32[]{:S(2)}, u32[]{:S(2)}) %collective-permute-start.5) | collective-permute-done | bytes 393248 | tf_op jit(solution)/shard_map/ppermute | solution.py:28
  50.4 3.2 %forward.7 = (bf16[2,3,32,1024]{3,2,1,0:T(8,128)(2,1)S(1)}, bf16[2,3,32,1024]{3,2,1,0:T(8,128)(2,1)S(1)}, f32[2,3,32,1024]{3,2,1,0:T(8,128)S(1)}, f32[2,3,32,1024]{3,2,1,0:T(8,128)S(1)}) custom-call(s32[3]{0:T(128)S(1)} %pad_add_fusion.idx, bf16[2,256,1024]{2,1,0:T(8,128)(2,1)S(1)} %collective-permute-done.11.m.refs_1_.refs_3_, ...), custom_call_target="tpu_custom_call" | custom-call | flops 1610612736 | bytes 5242880 | tf_op jit(solution)/shard_map/forward/pallas_call | solution.py:110
  53.6 1.7 %collective-permute-start.12 = (bf16[2,3,32,1024]{3,2,1,0:T(8,128)(2,1)S(1)}, bf16[2,3,32,1024]{3,2,1,0:T(8,128)(2,1)S(1)}, u32[]{:S(2)}, u32[]{:S(2)}) collective-permute-start(bf16[2,3,32,1024]{3,2,1,0:T(8,128)(2,1)S(1)} %get-tuple-element.93), channel_id=1, source_target_pairs={{0,8},{4,12},{8,16},{12,20},{16,24},{20,28},{24,0},{28,4},{1,9},{5... | collective-permute-start | bytes 1179656 | tf_op jit(solution)/shard_map/ppermute | solution.py:28
  55.2 1.6 %collective-permute-start.13 = (bf16[2,3,32,1024]{3,2,1,0:T(8,128)(2,1)S(1)}, bf16[2,3,32,1024]{3,2,1,0:T(8,128)(2,1)S(1)}, u32[]{:S(2)}, u32[]{:S(2)}) collective-permute-start(bf16[2,3,32,1024]{3,2,1,0:T(8,128)(2,1)S(1)} %get-tuple-element.94), channel_id=1, source_target_pairs={{0,24},{4,28},{8,0},{12,4},{16,8},{20,12},{24,16},{28,20},{1,25},{... | collective-permute-start | bytes 1179656 | tf_op jit(solution)/shard_map/ppermute | solution.py:28
  56.9 0.8 collective-permute-done.9.refs_1_
  57.8 8.0 %collective-permute-done.12.refs_4_ = bf16[2,3,32,1024]{3,2,1,0:T(8,128)(2,1)S(1)} collective-permute-done((bf16[2,3,32,1024]{3,2,1,0:T(8,128)(2,1)S(1)}, bf16[2,3,32,1024]{3,2,1,0:T(8,128)(2,1)S(1)}, u32[]{:S(2)}, u32[]{:S(2)}) %collective-permute-start.12) | collective-permute-done | bytes 393248 | tf_op jit(solution)/shard_map/ppermute | solution.py:28
  65.8 1.4 collective-permute-start.14
  67.2 1.9 %collective-permute-start.15 = (bf16[3,2,32,1024]{3,2,1,0:T(8,128)(2,1)S(1)}, bf16[3,2,32,1024]{3,2,1,0:T(8,128)(2,1)S(1)}, u32[]{:S(2)}, u32[]{:S(2)}) collective-permute-start(bf16[3,2,32,1024]{3,2,1,0:T(8,128)(2,1)S(1)} %get-tuple-element.96), channel_id=1, source_target_pairs={{0,24},{4,28},{8,0},{12,4},{16,8},{20,12},{24,16},{28,20},{1,25},{... | collective-permute-start | bytes 1179656 | tf_op jit(solution)/shard_map/ppermute | solution.py:28
  69.5 7.5 %collective-permute-done.14.refs_6_ = bf16[3,2,32,1024]{3,2,1,0:T(8,128)(2,1)S(1)} collective-permute-done((bf16[3,2,32,1024]{3,2,1,0:T(8,128)(2,1)S(1)}, bf16[3,2,32,1024]{3,2,1,0:T(8,128)(2,1)S(1)}, u32[]{:S(2)}, u32[]{:S(2)}) %collective-permute-start.14) | collective-permute-done | bytes 393248 | tf_op jit(solution)/shard_map/ppermute | solution.py:28
  77.4 1.0 collective-permute-start.17
  78.4 2.3 %collective-permute-start.16 = (bf16[2,3,2,32,1024]{4,3,2,1,0:T(8,128)(2,1)S(1)}, bf16[2,3,2,32,1024]{4,3,2,1,0:T(8,128)(2,1)S(1)}, u32[]{:S(2)}, u32[]{:S(2)}) collective-permute-start(bf16[2,3,2,32,1024]{4,3,2,1,0:T(8,128)(2,1)S(1)} %gate.2.here), channel_id=1, source_target_pairs={{0,24},{4,28},{8,0},{12,4},{16,8},{20,12},{24,16},{28,20},{1,25},{... | collective-permute-start | bytes 2359304 | tf_op jit(solution)/shard_map/ppermute | solution.py:28
  80.8 15.4 %collective-permute-done.17.minus1 = bf16[2,3,2,32,1024]{4,3,2,1,0:T(8,128)(2,1)S(1)} collective-permute-done((bf16[2,3,2,32,1024]{4,3,2,1,0:T(8,128)(2,1)S(1)}, bf16[2,3,2,32,1024]{4,3,2,1,0:T(8,128)(2,1)S(1)}, u32[]{:S(2)}, u32[]{:S(2)}) %collective-permute-start.17) | collective-permute-done | bytes 786464 | tf_op jit(solution)/shard_map/ppermute | solution.py:28
  96.3 3.3 %collective-permute-start.19 = (bf16[3,2,32,1024]{3,2,1,0:T(8,128)(2,1)S(1)}, bf16[3,2,32,1024]{3,2,1,0:T(8,128)(2,1)S(1)}, u32[]{:S(2)}, u32[]{:S(2)}) collective-permute-start(bf16[3,2,32,1024]{3,2,1,0:T(8,128)(2,1)S(1)} %slice_bitcast_fusion), channel_id=1, source_target_pairs={{0,24},{4,28},{8,0},{12,4},{16,8},{20,12},{24,16},{28,20},{1,25},{... | collective-permute-start | bytes 1179656 | tf_op jit(solution)/shard_map/ppermute | solution.py:28
  100.3 3.2 %collective-permute-start.25 = (bf16[2,3,2,32,1024]{4,3,2,1,0:T(8,128)(2,1)S(1)}, bf16[2,3,2,32,1024]{4,3,2,1,0:T(8,128)(2,1)S(1)}, u32[]{:S(2)}, u32[]{:S(2)}) collective-permute-start(bf16[2,3,2,32,1024]{4,3,2,1,0:T(8,128)(2,1)S(1)} %gate.3.here), channel_id=1, source_target_pairs={{0,24},{4,28},{8,0},{12,4},{16,8},{20,12},{24,16},{28,20},{1,25},{... | collective-permute-start | bytes 2359304 | tf_op jit(solution)/shard_map/ppermute | solution.py:28
  103.5 6.0 %collective-permute-done.18.far_a = bf16[3,2,32,1024]{3,2,1,0:T(8,128)(2,1)S(1)} collective-permute-done((bf16[3,2,32,1024]{3,2,1,0:T(8,128)(2,1)S(1)}, bf16[3,2,32,1024]{3,2,1,0:T(8,128)(2,1)S(1)}, u32[]{:S(2)}, u32[]{:S(2)}) %collective-permute-start.18) | collective-permute-done | bytes 393248 | tf_op jit(solution)/shard_map/ppermute | solution.py:28
  109.5 3.9 %input_grad.2 = (f32[2,64,1024]{2,1,0:T(8,128)S(1)}, bf16[2,64,1024]{2,1,0:T(8,128)(2,1)S(1)}, bf16[2,64,1024]{2,1,0:T(8,128)(2,1)S(1)}, bf16[2,64,1024]{2,1,0:T(8,128)(2,1)S(1)}, bf16[3,512,1024]{2,1,0:T(8,128)(2,1)S(1)}) custom-call(s32[3]{0:T(128)S(1)} %pad_add_fusion.idx, bf16[2,3,2,32,1024]{4,3,2,1,0:T(8,128)(2,1)S(1)} %gate.2.here, ...), custom_call_target="tpu_custom_call" | custom-call | flops 2147483648 | bytes 10485760 | tf_op jit(solution)/shard_map/input_grad/pallas_call | solution.py:225
  113.4 5.1 %in_grads.2 = (f32[1024,1024]{1,0:T(8,128)S(1)}, f32[1024,1024]{1,0:T(8,128)S(1)}) custom-call(bf16[2,256,1024]{2,1,0:T(8,128)(2,1)S(1)} %copy-done.6, bf16[2,256,1024]{2,1,0:T(8,128)(2,1)} %collective-permute-done.2.m.refs_1_, bf16[3,512,1024]{2,1,0:T(8,128)(2,1)S(1)} %get-tuple-element.112.refs_2_.refs_4_), custom_call_target="tpu_custom_call" | custom-call | flops 2147483648 | bytes 12582912 | tf_op jit(solution)/shard_map/in_grads/pallas_call | solution.py:286
  118.5 3.9 %collective-permute-done.24.minus1 = bf16[2,3,2,32,1024]{4,3,2,1,0:T(8,128)(2,1)S(1)} collective-permute-done((bf16[2,3,2,32,1024]{4,3,2,1,0:T(8,128)(2,1)S(1)}, bf16[2,3,2,32,1024]{4,3,2,1,0:T(8,128)(2,1)S(1)}, u32[]{:S(2)}, u32[]{:S(2)}) %collective-permute-start.24) | collective-permute-done | bytes 786464 | tf_op jit(solution)/shard_map/ppermute | solution.py:28
  122.6 3.3 %collective-permute-start.27 = (bf16[3,2,32,1024]{3,2,1,0:T(8,128)(2,1)S(1)}, bf16[3,2,32,1024]{3,2,1,0:T(8,128)(2,1)S(1)}, u32[]{:S(2)}, u32[]{:S(2)}) collective-permute-start(bf16[3,2,32,1024]{3,2,1,0:T(8,128)(2,1)S(1)} %slice_bitcast_fusion.2), channel_id=1, source_target_pairs={{0,24},{4,28},{8,0},{12,4},{16,8},{20,12},{24,16},{28,20},{1,25},{... | collective-permute-start | bytes 1179656 | tf_op jit(solution)/shard_map/ppermute | solution.py:28
  125.9 1.6 collective-permute-start.21
  127.5 2.9 %collective-permute-start.22 = (bf16[2,64,1024]{2,1,0:T(8,128)(2,1)S(1)}, bf16[2,64,1024]{2,1,0:T(8,128)(2,1)S(1)}, u32[]{:S(2)}, u32[]{:S(2)}) collective-permute-start(bf16[2,64,1024]{2,1,0:T(8,128)(2,1)S(1)} %get-tuple-element.110), channel_id=1, source_target_pairs={{0,2},{1,3},{2,0},{3,1},{4,6},{5,7},{6,4},{7,5},{8,10},{9,11},{10,... | collective-permute-start | bytes 786440 | tf_op jit(solution)/shard_map/ppermute | solution.py:37
  130.3 1.3 collective-permute-start.23
  131.7 3.9 %input_grad.3 = (f32[2,64,1024]{2,1,0:T(8,128)S(1)}, bf16[2,64,1024]{2,1,0:T(8,128)(2,1)S(1)}, bf16[2,64,1024]{2,1,0:T(8,128)(2,1)S(1)}, bf16[2,64,1024]{2,1,0:T(8,128)(2,1)S(1)}, bf16[3,512,1024]{2,1,0:T(8,128)(2,1)S(1)}) custom-call(s32[3]{0:T(128)S(1)} %pad_add_fusion.idx, bf16[2,3,2,32,1024]{4,3,2,1,0:T(8,128)(2,1)S(1)} %gate.3.here, ...), custom_call_target="tpu_custom_call" | custom-call | flops 2147483648 | bytes 10485760 | tf_op jit(solution)/shard_map/input_grad/pallas_call | solution.py:225
  135.6 1.5 collective-permute-start.28
  137.0 2.9 %collective-permute-start.29 = (bf16[2,64,1024]{2,1,0:T(8,128)(2,1)S(1)}, bf16[2,64,1024]{2,1,0:T(8,128)(2,1)S(1)}, u32[]{:S(2)}, u32[]{:S(2)}) collective-permute-start(bf16[2,64,1024]{2,1,0:T(8,128)(2,1)S(1)} %get-tuple-element.119), channel_id=1, source_target_pairs={{0,2},{1,3},{2,0},{3,1},{4,6},{5,7},{6,4},{7,5},{8,10},{9,11},{10,... | collective-permute-start | bytes 786440 | tf_op jit(solution)/shard_map/ppermute | solution.py:37
  139.9 1.4 collective-permute-start.30
  141.3 5.1 %in_grads.3 = (bf16[1024,1024]{1,0:T(8,128)(2,1)}, bf16[1024,1024]{1,0:T(8,128)(2,1)}) custom-call(bf16[2,256,1024]{2,1,0:T(8,128)(2,1)S(1)} %collective-permute-done.7.m.refs_0_.refs_2_, bf16[2,256,1024]{2,1,0:T(8,128)(2,1)S(1)} %collective-permute-done.11.m.refs_1_.refs_3_, bf16[3,512,1024]{2,1,0:T(8,128)(2,1)S(1)} %get-tuple-element.121.refs_2_.refs_5_, ...), custom_call_target="tpu_custom_call" | custom-call | flops 2147483648 | bytes 12582912 | tf_op jit(solution)/shard_map/in_grads/pallas_call | solution.py:286
  146.4 5.2 %down_grad.1 = bf16[1024,1024]{1,0:T(8,128)(2,1)} custom-call(bf16[2,256,1024]{2,1,0:T(8,128)(2,1)S(1)} %copy-done.6, bf16[2,256,1024]{2,1,0:T(8,128)(2,1)} %collective-permute-done.2.m.refs_1_, bf16[2,256,1024]{2,1,0:T(8,128)(2,1)S(1)} %collective-permute-done.7.m.refs_0_.refs_2_, bf16[2,256,1024]{2,1,0:T(8,128)(2,1)S(1)} %collective-permute-done.11.m.refs_1_.refs_3_, ...), custom_call_target="tpu_custom_call" | custom-call | flops 2147483648 | bytes 6291456 | tf_op jit(solution)/shard_map/down_grad/pallas_call | solution.py:319
  152.1 3.3 %collective-permute-start.31 = (bf16[64,1024]{1,0:T(8,128)(2,1)S(1)}, bf16[64,1024]{1,0:T(8,128)(2,1)S(1)}, u32[]{:S(2)}, u32[]{:S(2)}) collective-permute-start(bf16[64,1024]{1,0:T(8,128)(2,1)S(1)} %get-tuple-element.136), channel_id=1, source_target_pairs={{0,32},{32,0},{64,96},{96,64},{1,33},{33,1},{65,97},{97,65},{2,34}... | collective-permute-start | bytes 393224 | tf_op jit(solution)/shard_map/ppermute | solution.py:33
  155.3 3.3 %collective-permute-done.33 = bf16[64,1024]{1,0:T(8,128)(2,1)S(1)} collective-permute-done((bf16[64,1024]{1,0:T(8,128)(2,1)S(1)}, bf16[64,1024]{1,0:T(8,128)(2,1)S(1)}, u32[]{:S(2)}, u32[]{:S(2)}) %collective-permute-start.33) | collective-permute-done | bytes 131104 | tf_op jit(solution)/shard_map/ppermute | solution.py:33
  158.7 1.2 collective-permute-done.32
  159.9 0.7 add_convert_fusion
  (57 shorter events, 3.9 us)
Async XLA Ops:
  0.6 5.6 %copy-start = (bf16[1024,1024]{1,0:T(8,128)(2,1)S(1)}, bf16[1024,1024]{1,0:T(8,128)(2,1)}, u32[]{:S(2)}) copy-start(bf16[1024,1024]{1,0:T(8,128)(2,1)} %wd.7) | copy-start | bytes 6291460
  3.0 15.0 %collective-permute-start.2 = (bf16[2,256,1024]{2,1,0:T(8,128)(2,1)}, bf16[2,256,1024]{2,1,0:T(8,128)(2,1)}, u32[]{:S(2)}, u32[]{:S(2)}) collective-permute-start(bf16[2,256,1024]{2,1,0:T(8,128)(2,1)} %scaled.1.m.refs_0_), channel_id=1, source_target_pairs={{0,32},{32,0},{64,96},{96,64},{1,33},{33,1},{65,97},{97,65},{2,34}... | collective-permute-start | bytes 3145736 | tf_op jit(solution)/shard_map/ppermute | solution.py:33
  3.0 33.0 %collective-permute-start.7 = (bf16[2,256,1024]{2,1,0:T(8,128)(2,1)}, bf16[2,256,1024]{2,1,0:T(8,128)(2,1)S(1)}, u32[]{:S(2)}, u32[]{:S(2)}) collective-permute-start(bf16[2,256,1024]{2,1,0:T(8,128)(2,1)} %scaled.1.m.refs_0_), channel_id=1, source_target_pairs={{0,64},{32,96},{64,0},{96,32},{1,65},{33,97},{65,1},{97,33},{2,66}... | collective-permute-start | bytes 3145736 | tf_op jit(solution)/shard_map/ppermute | solution.py:33
  6.2 1.6 copy-start.1
  7.8 1.6 copy-start.3
  9.4 1.2 copy-start.5
  10.6 7.4 %copy-start.2 = (bf16[1024,1024]{1,0:T(8,128)(2,1)S(1)}, bf16[1024,1024]{1,0:T(8,128)(2,1)}, u32[]{:S(2)}) copy-start(bf16[1024,1024]{1,0:T(8,128)(2,1)} %wg.11) | copy-start | bytes 6291460
  13.8 14.0 %collective-permute-start = (bf16[2,3,32,1024]{3,2,1,0:T(8,128)(2,1)S(1)}, bf16[2,3,32,1024]{3,2,1,0:T(8,128)(2,1)S(1)}, u32[]{:S(2)}, u32[]{:S(2)}) collective-permute-start(bf16[2,3,32,1024]{3,2,1,0:T(8,128)(2,1)S(1)} %get-tuple-element.73), channel_id=1, source_target_pairs={{0,8},{4,12},{8,16},{12,20},{16,24},{20,28},{24,0},{28,4},{1,9},{5... | collective-permute-start | bytes 1179656 | tf_op jit(solution)/shard_map/ppermute | solution.py:28
  15.8 12.0 %collective-permute-start.1 = (bf16[2,3,32,1024]{3,2,1,0:T(8,128)(2,1)S(1)}, bf16[2,3,32,1024]{3,2,1,0:T(8,128)(2,1)S(1)}, u32[]{:S(2)}, u32[]{:S(2)}) collective-permute-start(bf16[2,3,32,1024]{3,2,1,0:T(8,128)(2,1)S(1)} %get-tuple-element.74), channel_id=1, source_target_pairs={{0,24},{4,28},{8,0},{12,4},{16,8},{20,12},{24,16},{28,20},{1,25},{... | collective-permute-start | bytes 1179656 | tf_op jit(solution)/shard_map/ppermute | solution.py:28
  21.8 17.5 %copy-start.4 = (bf16[1024,1024]{1,0:T(8,128)(2,1)S(1)}, bf16[1024,1024]{1,0:T(8,128)(2,1)}, u32[]{:S(2)}) copy-start(bf16[1024,1024]{1,0:T(8,128)(2,1)} %wu.11) | copy-start | bytes 6291460
  21.9 13.9 %collective-permute-start.3 = (bf16[2,3,32,1024]{3,2,1,0:T(8,128)(2,1)S(1)}, bf16[2,3,32,1024]{3,2,1,0:T(8,128)(2,1)S(1)}, u32[]{:S(2)}, u32[]{:S(2)}) collective-permute-start(bf16[2,3,32,1024]{3,2,1,0:T(8,128)(2,1)S(1)} %get-tuple-element.77), channel_id=1, source_target_pairs={{0,8},{4,12},{8,16},{12,20},{16,24},{20,28},{24,0},{28,4},{1,9},{5... | collective-permute-start | bytes 1179656 | tf_op jit(solution)/shard_map/ppermute | solution.py:28
  21.9 13.9 %collective-permute-start.4 = (bf16[2,3,32,1024]{3,2,1,0:T(8,128)(2,1)S(1)}, bf16[2,3,32,1024]{3,2,1,0:T(8,128)(2,1)S(1)}, u32[]{:S(2)}, u32[]{:S(2)}) collective-permute-start(bf16[2,3,32,1024]{3,2,1,0:T(8,128)(2,1)S(1)} %get-tuple-element.78), channel_id=1, source_target_pairs={{0,24},{4,28},{8,0},{12,4},{16,8},{20,12},{24,16},{28,20},{1,25},{... | collective-permute-start | bytes 1179656 | tf_op jit(solution)/shard_map/ppermute | solution.py:28
  36.0 14.4 %collective-permute-start.11 = (bf16[2,256,1024]{2,1,0:T(8,128)(2,1)S(1)}, bf16[2,256,1024]{2,1,0:T(8,128)(2,1)S(1)}, u32[]{:S(2)}, u32[]{:S(2)}) collective-permute-start(bf16[2,256,1024]{2,1,0:T(8,128)(2,1)S(1)} %collective-permute-done.7.m.refs_0_.refs_2_), channel_id=1, source_target_pairs={{0,32},{32,0},{64,96},{96,64},{1,33},{33,1},{65,97},{97,65},{2,34}... | collective-permute-start | bytes 3145736 | tf_op jit(solution)/shard_map/ppermute | solution.py:33
  36.1 13.2 %collective-permute-start.5 = (bf16[3,2,32,1024]{3,2,1,0:T(8,128)(2,1)S(1)}, bf16[3,2,32,1024]{3,2,1,0:T(8,128)(2,1)S(1)}, u32[]{:S(2)}, u32[]{:S(2)}) collective-permute-start(bf16[3,2,32,1024]{3,2,1,0:T(8,128)(2,1)S(1)} %get-tuple-element.81), channel_id=1, source_target_pairs={{0,8},{4,12},{8,16},{12,20},{16,24},{20,28},{24,0},{28,4},{1,9},{5... | collective-permute-start | bytes 1179656 | tf_op jit(solution)/shard_map/ppermute | solution.py:28
  37.4 12.0 %collective-permute-start.6 = (bf16[3,2,32,1024]{3,2,1,0:T(8,128)(2,1)S(1)}, bf16[3,2,32,1024]{3,2,1,0:T(8,128)(2,1)S(1)}, u32[]{:S(2)}, u32[]{:S(2)}) collective-permute-start(bf16[3,2,32,1024]{3,2,1,0:T(8,128)(2,1)S(1)} %get-tuple-element.82), channel_id=1, source_target_pairs={{0,24},{4,28},{8,0},{12,4},{16,8},{20,12},{24,16},{28,20},{1,25},{... | collective-permute-start | bytes 1179656 | tf_op jit(solution)/shard_map/ppermute | solution.py:28
  42.5 15.1 %collective-permute-start.9 = (bf16[2,3,32,1024]{3,2,1,0:T(8,128)(2,1)S(1)}, bf16[2,3,32,1024]{3,2,1,0:T(8,128)(2,1)S(1)}, u32[]{:S(2)}, u32[]{:S(2)}) collective-permute-start(bf16[2,3,32,1024]{3,2,1,0:T(8,128)(2,1)S(1)} %get-tuple-element.84), channel_id=1, source_target_pairs={{0,8},{4,12},{8,16},{12,20},{16,24},{20,28},{24,0},{28,4},{1,9},{5... | collective-permute-start | bytes 1179656 | tf_op jit(solution)/shard_map/ppermute | solution.py:28
  42.7 15.1 %collective-permute-start.10 = (bf16[2,3,32,1024]{3,2,1,0:T(8,128)(2,1)S(1)}, bf16[2,3,32,1024]{3,2,1,0:T(8,128)(2,1)S(1)}, u32[]{:S(2)}, u32[]{:S(2)}) collective-permute-start(bf16[2,3,32,1024]{3,2,1,0:T(8,128)(2,1)S(1)} %get-tuple-element.85), channel_id=1, source_target_pairs={{0,24},{4,28},{8,0},{12,4},{16,8},{20,12},{24,16},{28,20},{1,25},{... | collective-permute-start | bytes 1179656 | tf_op jit(solution)/shard_map/ppermute | solution.py:28
  49.7 19.5 %collective-permute-start.8 = (bf16[2,3,2,32,1024]{4,3,2,1,0:T(8,128)(2,1)S(1)}, bf16[2,3,2,32,1024]{4,3,2,1,0:T(8,128)(2,1)S(1)}, u32[]{:S(2)}, u32[]{:S(2)}) collective-permute-start(bf16[2,3,2,32,1024]{4,3,2,1,0:T(8,128)(2,1)S(1)} %get-tuple-element.89), channel_id=1, source_target_pairs={{0,4},{4,0},{8,12},{12,8},{16,20},{20,16},{24,28},{28,24},{1,5},{5... | collective-permute-start | bytes 2359304 | tf_op jit(solution)/shard_map/ppermute | solution.py:28
  53.6 12.1 %collective-permute-start.12 = (bf16[2,3,32,1024]{3,2,1,0:T(8,128)(2,1)S(1)}, bf16[2,3,32,1024]{3,2,1,0:T(8,128)(2,1)S(1)}, u32[]{:S(2)}, u32[]{:S(2)}) collective-permute-start(bf16[2,3,32,1024]{3,2,1,0:T(8,128)(2,1)S(1)} %get-tuple-element.93), channel_id=1, source_target_pairs={{0,8},{4,12},{8,16},{12,20},{16,24},{20,28},{24,0},{28,4},{1,9},{5... | collective-permute-start | bytes 1179656 | tf_op jit(solution)/shard_map/ppermute | solution.py:28
  55.2 10.5 %collective-permute-start.13 = (bf16[2,3,32,1024]{3,2,1,0:T(8,128)(2,1)S(1)}, bf16[2,3,32,1024]{3,2,1,0:T(8,128)(2,1)S(1)}, u32[]{:S(2)}, u32[]{:S(2)}) collective-permute-start(bf16[2,3,32,1024]{3,2,1,0:T(8,128)(2,1)S(1)} %get-tuple-element.94), channel_id=1, source_target_pairs={{0,24},{4,28},{8,0},{12,4},{16,8},{20,12},{24,16},{28,20},{1,25},{... | collective-permute-start | bytes 1179656 | tf_op jit(solution)/shard_map/ppermute | solution.py:28
  65.8 11.2 %collective-permute-start.14 = (bf16[3,2,32,1024]{3,2,1,0:T(8,128)(2,1)S(1)}, bf16[3,2,32,1024]{3,2,1,0:T(8,128)(2,1)S(1)}, u32[]{:S(2)}, u32[]{:S(2)}) collective-permute-start(bf16[3,2,32,1024]{3,2,1,0:T(8,128)(2,1)S(1)} %get-tuple-element.95), channel_id=1, source_target_pairs={{0,8},{4,12},{8,16},{12,20},{16,24},{20,28},{24,0},{28,4},{1,9},{5... | collective-permute-start | bytes 1179656 | tf_op jit(solution)/shard_map/ppermute | solution.py:28
  67.2 9.8 %collective-permute-start.15 = (bf16[3,2,32,1024]{3,2,1,0:T(8,128)(2,1)S(1)}, bf16[3,2,32,1024]{3,2,1,0:T(8,128)(2,1)S(1)}, u32[]{:S(2)}, u32[]{:S(2)}) collective-permute-start(bf16[3,2,32,1024]{3,2,1,0:T(8,128)(2,1)S(1)} %get-tuple-element.96), channel_id=1, source_target_pairs={{0,24},{4,28},{8,0},{12,4},{16,8},{20,12},{24,16},{28,20},{1,25},{... | collective-permute-start | bytes 1179656 | tf_op jit(solution)/shard_map/ppermute | solution.py:28
  77.4 18.7 %collective-permute-start.17 = (bf16[2,3,2,32,1024]{4,3,2,1,0:T(8,128)(2,1)S(1)}, bf16[2,3,2,32,1024]{4,3,2,1,0:T(8,128)(2,1)S(1)}, u32[]{:S(2)}, u32[]{:S(2)}) collective-permute-start(bf16[2,3,2,32,1024]{4,3,2,1,0:T(8,128)(2,1)S(1)} %gate.2.here), channel_id=1, source_target_pairs={{0,8},{4,12},{8,16},{12,20},{16,24},{20,28},{24,0},{28,4},{1,9},{5... | collective-permute-start | bytes 2359304 | tf_op jit(solution)/shard_map/ppermute | solution.py:28
  78.4 17.9 %collective-permute-start.16 = (bf16[2,3,2,32,1024]{4,3,2,1,0:T(8,128)(2,1)S(1)}, bf16[2,3,2,32,1024]{4,3,2,1,0:T(8,128)(2,1)S(1)}, u32[]{:S(2)}, u32[]{:S(2)}) collective-permute-start(bf16[2,3,2,32,1024]{4,3,2,1,0:T(8,128)(2,1)S(1)} %gate.2.here), channel_id=1, source_target_pairs={{0,24},{4,28},{8,0},{12,4},{16,8},{20,12},{24,16},{28,20},{1,25},{... | collective-permute-start | bytes 2359304 | tf_op jit(solution)/shard_map/ppermute | solution.py:28
  80.8 18.9 %collective-permute-start.20 = (bf16[2,3,2,32,1024]{4,3,2,1,0:T(8,128)(2,1)S(1)}, bf16[2,3,2,32,1024]{4,3,2,1,0:T(8,128)(2,1)S(1)}, u32[]{:S(2)}, u32[]{:S(2)}) collective-permute-start(bf16[2,3,2,32,1024]{4,3,2,1,0:T(8,128)(2,1)S(1)} %get-tuple-element.102), channel_id=1, source_target_pairs={{0,4},{4,0},{8,12},{12,8},{16,20},{20,16},{24,28},{28,24},{1,5},{5... | collective-permute-start | bytes 2359304 | tf_op jit(solution)/shard_map/ppermute | solution.py:28
  96.2 13.3 %collective-permute-start.18 = (bf16[3,2,32,1024]{3,2,1,0:T(8,128)(2,1)S(1)}, bf16[3,2,32,1024]{3,2,1,0:T(8,128)(2,1)S(1)}, u32[]{:S(2)}, u32[]{:S(2)}) collective-permute-start(bf16[3,2,32,1024]{3,2,1,0:T(8,128)(2,1)S(1)} %slice_bitcast_fusion.1), channel_id=1, source_target_pairs={{0,8},{4,12},{8,16},{12,20},{16,24},{20,28},{24,0},{28,4},{1,9},{5... | collective-permute-start | bytes 1179656 | tf_op jit(solution)/shard_map/ppermute | solution.py:28
  96.3 13.2 %collective-permute-start.19 = (bf16[3,2,32,1024]{3,2,1,0:T(8,128)(2,1)S(1)}, bf16[3,2,32,1024]{3,2,1,0:T(8,128)(2,1)S(1)}, u32[]{:S(2)}, u32[]{:S(2)}) collective-permute-start(bf16[3,2,32,1024]{3,2,1,0:T(8,128)(2,1)S(1)} %slice_bitcast_fusion), channel_id=1, source_target_pairs={{0,24},{4,28},{8,0},{12,4},{16,8},{20,12},{24,16},{28,20},{1,25},{... | collective-permute-start | bytes 1179656 | tf_op jit(solution)/shard_map/ppermute | solution.py:28
  100.0 13.4 %copy-start.6 = (bf16[2,256,1024]{2,1,0:T(8,128)(2,1)S(1)}, bf16[2,256,1024]{2,1,0:T(8,128)(2,1)}, u32[]{:S(2)}) copy-start(bf16[2,256,1024]{2,1,0:T(8,128)(2,1)} %scaled.1.m.refs_0_) | copy-start | bytes 3145732
  100.0 22.4 %collective-permute-start.24 = (bf16[2,3,2,32,1024]{4,3,2,1,0:T(8,128)(2,1)S(1)}, bf16[2,3,2,32,1024]{4,3,2,1,0:T(8,128)(2,1)S(1)}, u32[]{:S(2)}, u32[]{:S(2)}) collective-permute-start(bf16[2,3,2,32,1024]{4,3,2,1,0:T(8,128)(2,1)S(1)} %gate.3.here), channel_id=1, source_target_pairs={{0,8},{4,12},{8,16},{12,20},{16,24},{20,28},{24,0},{28,4},{1,9},{5... | collective-permute-start | bytes 2359304 | tf_op jit(solution)/shard_map/ppermute | solution.py:28
  100.3 22.2 %collective-permute-start.25 = (bf16[2,3,2,32,1024]{4,3,2,1,0:T(8,128)(2,1)S(1)}, bf16[2,3,2,32,1024]{4,3,2,1,0:T(8,128)(2,1)S(1)}, u32[]{:S(2)}, u32[]{:S(2)}) collective-permute-start(bf16[2,3,2,32,1024]{4,3,2,1,0:T(8,128)(2,1)S(1)} %gate.3.here), channel_id=1, source_target_pairs={{0,24},{4,28},{8,0},{12,4},{16,8},{20,12},{24,16},{28,20},{1,25},{... | collective-permute-start | bytes 2359304 | tf_op jit(solution)/shard_map/ppermute | solution.py:28
  122.5 9.2 %collective-permute-start.26 = (bf16[3,2,32,1024]{3,2,1,0:T(8,128)(2,1)S(1)}, bf16[3,2,32,1024]{3,2,1,0:T(8,128)(2,1)S(1)}, u32[]{:S(2)}, u32[]{:S(2)}) collective-permute-start(bf16[3,2,32,1024]{3,2,1,0:T(8,128)(2,1)S(1)} %slice_bitcast_fusion.3), channel_id=1, source_target_pairs={{0,8},{4,12},{8,16},{12,20},{16,24},{20,28},{24,0},{28,4},{1,9},{5... | collective-permute-start | bytes 1179656 | tf_op jit(solution)/shard_map/ppermute | solution.py:28
  122.6 9.1 %collective-permute-start.27 = (bf16[3,2,32,1024]{3,2,1,0:T(8,128)(2,1)S(1)}, bf16[3,2,32,1024]{3,2,1,0:T(8,128)(2,1)S(1)}, u32[]{:S(2)}, u32[]{:S(2)}) collective-permute-start(bf16[3,2,32,1024]{3,2,1,0:T(8,128)(2,1)S(1)} %slice_bitcast_fusion.2), channel_id=1, source_target_pairs={{0,24},{4,28},{8,0},{12,4},{16,8},{20,12},{24,16},{28,20},{1,25},{... | collective-permute-start | bytes 1179656 | tf_op jit(solution)/shard_map/ppermute | solution.py:28
  125.9 14.1 %collective-permute-start.21 = (bf16[2,64,1024]{2,1,0:T(8,128)(2,1)S(1)}, bf16[2,64,1024]{2,1,0:T(8,128)(2,1)S(1)}, u32[]{:S(2)}, u32[]{:S(2)}) collective-permute-start(bf16[2,64,1024]{2,1,0:T(8,128)(2,1)S(1)} %get-tuple-element.109), channel_id=1, source_target_pairs={{0,1},{1,2},{2,3},{3,0},{4,5},{5,6},{6,7},{7,4},{8,9},{9,10},{10,1... | collective-permute-start | bytes 786440 | tf_op jit(solution)/shard_map/ppermute | solution.py:37
  127.5 24.2 %collective-permute-start.22 = (bf16[2,64,1024]{2,1,0:T(8,128)(2,1)S(1)}, bf16[2,64,1024]{2,1,0:T(8,128)(2,1)S(1)}, u32[]{:S(2)}, u32[]{:S(2)}) collective-permute-start(bf16[2,64,1024]{2,1,0:T(8,128)(2,1)S(1)} %get-tuple-element.110), channel_id=1, source_target_pairs={{0,2},{1,3},{2,0},{3,1},{4,6},{5,7},{6,4},{7,5},{8,10},{9,11},{10,... | collective-permute-start | bytes 786440 | tf_op jit(solution)/shard_map/ppermute | solution.py:37
  130.3 21.3 %collective-permute-start.23 = (bf16[2,64,1024]{2,1,0:T(8,128)(2,1)S(1)}, bf16[2,64,1024]{2,1,0:T(8,128)(2,1)S(1)}, u32[]{:S(2)}, u32[]{:S(2)}) collective-permute-start(bf16[2,64,1024]{2,1,0:T(8,128)(2,1)S(1)} %get-tuple-element.111), channel_id=1, source_target_pairs={{0,3},{1,0},{2,1},{3,2},{4,7},{5,4},{6,5},{7,6},{8,11},{9,8},{10,9... | collective-permute-start | bytes 786440 | tf_op jit(solution)/shard_map/ppermute | solution.py:37
  135.6 16.1 %collective-permute-start.28 = (bf16[2,64,1024]{2,1,0:T(8,128)(2,1)S(1)}, bf16[2,64,1024]{2,1,0:T(8,128)(2,1)S(1)}, u32[]{:S(2)}, u32[]{:S(2)}) collective-permute-start(bf16[2,64,1024]{2,1,0:T(8,128)(2,1)S(1)} %get-tuple-element.118), channel_id=1, source_target_pairs={{0,1},{1,2},{2,3},{3,0},{4,5},{5,6},{6,7},{7,4},{8,9},{9,10},{10,1... | collective-permute-start | bytes 786440 | tf_op jit(solution)/shard_map/ppermute | solution.py:37
  137.0 14.6 %collective-permute-start.29 = (bf16[2,64,1024]{2,1,0:T(8,128)(2,1)S(1)}, bf16[2,64,1024]{2,1,0:T(8,128)(2,1)S(1)}, u32[]{:S(2)}, u32[]{:S(2)}) collective-permute-start(bf16[2,64,1024]{2,1,0:T(8,128)(2,1)S(1)} %get-tuple-element.119), channel_id=1, source_target_pairs={{0,2},{1,3},{2,0},{3,1},{4,6},{5,7},{6,4},{7,5},{8,10},{9,11},{10,... | collective-permute-start | bytes 786440 | tf_op jit(solution)/shard_map/ppermute | solution.py:37
  139.9 11.7 %collective-permute-start.30 = (bf16[2,64,1024]{2,1,0:T(8,128)(2,1)S(1)}, bf16[2,64,1024]{2,1,0:T(8,128)(2,1)S(1)}, u32[]{:S(2)}, u32[]{:S(2)}) collective-permute-start(bf16[2,64,1024]{2,1,0:T(8,128)(2,1)S(1)} %get-tuple-element.120), channel_id=1, source_target_pairs={{0,3},{1,0},{2,1},{3,2},{4,7},{5,4},{6,5},{7,6},{8,11},{9,8},{10,9... | collective-permute-start | bytes 786440 | tf_op jit(solution)/shard_map/ppermute | solution.py:37
  151.9 6.8 %collective-permute-start.33 = (bf16[64,1024]{1,0:T(8,128)(2,1)S(1)}, bf16[64,1024]{1,0:T(8,128)(2,1)S(1)}, u32[]{:S(2)}, u32[]{:S(2)}) collective-permute-start(bf16[64,1024]{1,0:T(8,128)(2,1)S(1)} %get-tuple-element.138), channel_id=1, source_target_pairs={{0,96},{32,64},{64,32},{96,0},{1,97},{33,65},{65,33},{97,1},{2,98}... | collective-permute-start | bytes 393224 | tf_op jit(solution)/shard_map/ppermute | solution.py:33
  152.0 7.9 %collective-permute-start.32 = (bf16[64,1024]{1,0:T(8,128)(2,1)S(1)}, bf16[64,1024]{1,0:T(8,128)(2,1)S(1)}, u32[]{:S(2)}, u32[]{:S(2)}) collective-permute-start(bf16[64,1024]{1,0:T(8,128)(2,1)S(1)} %get-tuple-element.137), channel_id=1, source_target_pairs={{0,64},{32,96},{64,0},{96,32},{1,65},{33,97},{65,1},{97,33},{2,66}... | collective-permute-start | bytes 393224 | tf_op jit(solution)/shard_map/ppermute | solution.py:33
  152.1 7.8 %collective-permute-start.31 = (bf16[64,1024]{1,0:T(8,128)(2,1)S(1)}, bf16[64,1024]{1,0:T(8,128)(2,1)S(1)}, u32[]{:S(2)}, u32[]{:S(2)}) collective-permute-start(bf16[64,1024]{1,0:T(8,128)(2,1)S(1)} %get-tuple-element.136), channel_id=1, source_target_pairs={{0,32},{32,0},{64,96},{96,64},{1,33},{33,1},{65,97},{97,65},{2,34}... | collective-permute-start | bytes 393224 | tf_op jit(solution)/shard_map/ppermute | solution.py:33

commit v4 on v3

--- a/solution.py
+++ b/solution.py
@@ -9,10 +9,9 @@
 F32 = jnp.float32
 NT = (((1,), (1,)), ((), ()))
 VMEM_LIMIT = 16 * 1024 * 1024
-PIPE_LIMIT = 24 * 1024 * 1024
+FIRST_LIMIT = 56 * 1024 * 1024
 SMEM = pl.BlockSpec(memory_space=pltpu.SMEM)
 VMEM = pl.BlockSpec(memory_space=pltpu.VMEM)
-WIDE_LIMIT = 56 * 1024 * 1024
 
 
 def params(limit=VMEM_LIMIT):
@@ -72,7 +71,7 @@
         in_specs=[pl.BlockSpec(memory_space=pltpu.SMEM), wide, wide, row, row],
         out_specs=pl.BlockSpec((2, tokens, tile), lambda i: (0, 0, i)),
         out_shape=jax.ShapeDtypeStruct((2, tokens, depth), BF),
-        compiler_params=params(WIDE_LIMIT),
+        compiler_params=params(FIRST_LIMIT),
         cost_estimate=cost(4 * tokens * depth, 8 * tokens * depth),
         name="scaled",
     )(margin, inputs, upstream, loss_weight.reshape(1, -1), pair_ids.reshape(1, -1))
@@ -167,55 +166,71 @@
     )(owns[0], *nears[:2], owns[1], *nears[2:], last_minus, last_plus)
 
 
-def gate_kernel(held, across, out):
+def gate_kernel(held, across, out, other):
     for half in range(2):
         pre_gate, pre_up, grad_hidden = (
             held[half, i] + across[1 - half, i].astype(F32) for i in range(3)
         )
         s = jax.nn.sigmoid(pre_gate)
         activated = pre_gate * s
-        out[half, 2] = (activated * pre_up).astype(BF)
-        out[half, 0] = (grad_hidden * pre_up * s * (1.0 + pre_gate * (1.0 - s))).astype(BF)
-        out[half, 1] = (grad_hidden * activated).astype(BF)
+        first = 6 * half
+        out[first : first + 2] = (
+            grad_hidden * pre_up * s * (1.0 + pre_gate * (1.0 - s))
+        ).astype(BF)
+        out[first + 2 : first + 4] = (grad_hidden * activated).astype(BF)
+        hidden = (activated * pre_up).astype(BF)
+        if half:
+            other[...] = hidden
+        else:
+            out[4:6] = hidden
 
 
 def gate(held, across):
+    _, _, two, rows, width = held.shape
     return pl.pallas_call(
         gate_kernel,
-        out_shape=jax.ShapeDtypeStruct(held.shape, BF),
+        in_specs=[VMEM] * 2,
+        out_specs=[VMEM] * 2,
+        out_shape=[
+            jax.ShapeDtypeStruct((10, rows, width), BF),
+            jax.ShapeDtypeStruct((two, rows, width), BF),
+        ],
         compiler_params=params(),
         cost_estimate=cost(held.size * 8, held.size * 8),
         name="gate",
     )(held, across)
 
 
-def input_grad_kernel(idx, here, plus1, far_a, far_b, minus1, wg, wu, own, to1, to2, to3, acts, acc):
-    z, lo, y = idx[0], idx[1], idx[2]
+def input_grad_kernel(idx, here, plus1, far_a, far_b, minus1, wg, wu, mine, theirs, acts, hidden, acc):
+    z, lo = idx[0], idx[1]
     tokens = acts.shape[1] // 2
     tile = acc.shape[1]
     for r, s, block in (
-        (0, 0, here.at[0]),
-        (0, 1, here.at[1]),
-        (1, 0, plus1.at[0]),
-        (1, 1, plus1.at[1]),
-        (2, 0, far_a),
-        (2, 1, far_b),
-        (3, 0, minus1.at[0]),
-        (3, 1, minus1.at[1]),
+        (0, 0, here.at[:4]),
+        (0, 1, here.at[6:]),
+        (1, 0, plus1.at[:4]),
+        (1, 1, plus1.at[6:]),
+        (2, 0, far_a.at[:4]),
+        (2, 1, far_b.at[1:]),
+        (3, 0, minus1.at[:4]),
+        (3, 1, minus1.at[6:]),
     ):
         start = row_start(z, lo, r, s)
-        for t in range(2):
-            acts[:, pl.ds(t * tokens + start, 32), :] = block[:, t]
+        for i in range(2):
+            for t in range(2):
+                acts[i, pl.ds(t * tokens + start, 32), :] = block[2 * i + t]
+    hidden[0] = plus1[4:6]
+    hidden[1, 0] = far_a[4]
+    hidden[1, 1] = far_b[0]
+    hidden[2] = minus1[4:6]
 
     @pl.loop(0, wg.shape[0] // tile)
     def _(i):
         at = pl.ds(pl.multiple_of(i * tile, tile), tile)
         acc[...] = lax.dot_general(acts[0], wg[at, :], NT, preferred_element_type=F32)
         acc[...] += lax.dot_general(acts[1], wu[at, :], NT, preferred_element_type=F32)
-        for r, out in enumerate((own, to1, to2, to3)):
-            start = pl.multiple_of(lax.rem(y + r, 4) * 64, 64)
-            for t in range(2):
-                out[t, :, at] = acc[pl.ds(t * tokens + start, 64), :].astype(out.dtype)
+        mine[:, at] = acc[:tokens]
+        theirs[:, at] = acc[tokens:].astype(BF)
 
 
 def input_grad(idx, here, plus1, far_a, far_b, minus1, wg, wu):
@@ -225,13 +240,12 @@
     return pl.pallas_call(
         input_grad_kernel,
         in_specs=[SMEM] + [VMEM] * 7,
-        out_specs=[VMEM] * 5,
+        out_specs=[VMEM] * 4,
         out_shape=[
-            jax.ShapeDtypeStruct((2, 64, depth), F32),
-            jax.ShapeDtypeStruct((2, 64, depth), BF),
-            jax.ShapeDtypeStruct((2, 64, depth), BF),
-            jax.ShapeDtypeStruct((2, 64, depth), BF),
-            jax.ShapeDtypeStruct((3, 2 * tokens, width), BF),
+            jax.ShapeDtypeStruct((tokens, depth), F32),
+            jax.ShapeDtypeStruct((tokens, depth), BF),
+            jax.ShapeDtypeStruct((2, 2 * tokens, width), BF),
+            jax.ShapeDtypeStruct((3, 2, 32, width), BF),
         ],
         scratch_shapes=[pltpu.VMEM((2 * tokens, tile), F32)],
         compiler_params=params(),
@@ -240,99 +254,156 @@
     )(idx, here, plus1, far_a, far_b, minus1, wg, wu)
 
 
-def owned_kernel(own0, a0, b0, c0, own1, a1, b1, c1, mine, core, far, cross):
-    first = own0[...] + a0[...].astype(F32) + b0[...].astype(F32) + c0[...].astype(F32)
-    last = own1[...] + a1[...].astype(F32) + b1[...].astype(F32) + c1[...].astype(F32)
-    mine[...] = first[0]
-    core[...] = first[1].astype(BF)
-    far[...] = last[0].astype(BF)
-    cross[...] = last[1].astype(BF)
-
-
-def owned(first, last):
-    shape = first[0].shape[1:]
-    small = jax.ShapeDtypeStruct(shape, BF)
+def split_kernel(idx, mine, across, *outs):
+    for r, out in enumerate(outs):
+        at = pl.ds(pl.multiple_of(lax.rem(idx[2] + r, 4) * 64, 64), 64)
+        out[...] = (mine[at, :] + across[at, :].astype(F32)).astype(out.dtype)
+
+
+def split(idx, mine, across):
+    shape = (64, mine.shape[1])
+    return pl.pallas_call(
+        split_kernel,
+        in_specs=[SMEM, VMEM, VMEM],
+        out_specs=[VMEM] * 4,
+        out_shape=[jax.ShapeDtypeStruct(shape, F32)] + [jax.ShapeDtypeStruct(shape, BF)] * 3,
+        compiler_params=params(),
+        cost_estimate=cost(mine.size, mine.size * 9),
+        name="split",
+    )(idx, mine, across)
+
+
+def owned_kernel(own, a, b, c, out):
+    total = own[...] + a[...].astype(F32) + b[...].astype(F32) + c[...].astype(F32)
+    out[...] = total.astype(out.dtype)
+
+
+def owned(own, a, b, c, dtype):
     return pl.pallas_call(
         owned_kernel,
-        out_shape=[jax.ShapeDtypeStruct(shape, F32), small, small, small],
-        compiler_params=params(),
-        cost_estimate=cost(first[0].size * 8, first[0].size * 20),
+        in_specs=[VMEM] * 4,
+        out_specs=VMEM,
+        out_shape=jax.ShapeDtypeStruct(own.shape, dtype),
+        compiler_params=params(),
+        cost_estimate=cost(own.size * 4, own.size * 12),
         name="owned",
-    )(*first, *last)
-
-
-def in_grads_kernel(*refs):
-    rows, acts, before, (gate_out, up_out, xt) = refs[:2], refs[2], refs[3:-3], refs[-3:]
-
-    @pl.when(pl.program_id(0) == 0)
+    )(own, a, b, c)
+
+
+def part_grads_kernel(m0, m1, acts, gate_out, up_out, xt):
+    tokens = m0.shape[1]
+    for k, m in enumerate((m0, m1)):
+        xt[:, k * tokens : (k + 1) * tokens] = m[0].T
+    tile = 256
+
+    @pl.loop(0, acts.shape[2] // tile)
+    def _(i):
+        at = pl.ds(pl.multiple_of(i * tile, tile), tile)
+        gate_out[:, at] = jnp.dot(xt[...], acts[0, :, at], preferred_element_type=F32)
+        up_out[:, at] = jnp.dot(xt[...], acts[1, :, at], preferred_element_type=F32)
+
+
+def part_grads(m0, m1, acts):
+    _, tokens, depth = m0.shape
+    width = acts.shape[2]
+    out = jax.ShapeDtypeStruct((depth, width), F32)
+    return pl.pallas_call(
+        part_grads_kernel,
+        in_specs=[VMEM] * 3,
+        out_specs=[VMEM] * 2,
+        out_shape=[out, out],
+        scratch_shapes=[pltpu.VMEM((depth, 2 * tokens), BF)],
+        compiler_params=params(),
+        cost_estimate=cost(8 * tokens * depth * width, 8 * 2**20),
+        name="part_grads",
+    )(m0, m1, acts)
+
+
+def in_grads_kernel(m0, m1, acts, gate_part, up_part, gate_out, up_out, xt):
+    tokens = m0.shape[1]
+    tile = gate_out.shape[1]
+    i = pl.program_id(0)
+
+    @pl.when(i == 0)
+    def _():
+        for k, m in enumerate((m0, m1)):
+            xt[:, k * tokens : (k + 1) * tokens] = m[0].T
+
+    at = pl.ds(pl.multiple_of(i * tile, tile), tile)
+    total = gate_part[:, at] + jnp.dot(xt[...], acts[0, :, at], preferred_element_type=F32)
+    gate_out[...] = total.astype(BF)
+    total = up_part[:, at] + jnp.dot(xt[...], acts[1, :, at], preferred_element_type=F32)
+    up_out[...] = total.astype(BF)
+
+
+def in_grads(m0, m1, acts, gate_part, up_part):
+    _, tokens, depth = m0.shape
+    width = acts.shape[2]
+    tile = 256
+    out = jax.ShapeDtypeStruct((depth, width), BF)
+    return pl.pallas_call(
+        in_grads_kernel,
+        grid=(width // tile,),
+        in_specs=[VMEM] * 5,
+        out_specs=[pl.BlockSpec((depth, tile), lambda i: (0, i))] * 2,
+        out_shape=[out, out],
+        scratch_shapes=[pltpu.VMEM((depth, 2 * tokens), BF)],
+        compiler_params=params(),
+        cost_estimate=cost(8 * tokens * depth * width, 8 * 2**20),
+        name="in_grads",
+    )(m0, m1, acts, gate_part, up_part)
+
+
+def gather_hidden(idx, here, other, near, across, out, base):
+    for r in range(4):
+        for s in range(2):
+            start = row_start(idx[0], idx[1], r, s)
+            for t in range(2):
+                if r:
+                    block = (across if s else near)[r - 1, t]
+                else:
+                    block = other[t] if s else here[4 + t]
+                out[pl.ds(base + t * 256 + start, 32), :] = block
+
+
+def down_grad_kernel(idx, *refs):
+    rows, blocks, (out, hidden) = refs[:4], refs[4:12], refs[12:]
+    tile = out.shape[0]
+    i = pl.program_id(0)
+
+    @pl.when(i == 0)
     def _():
         for k in range(2):
-            xt[:, k * 256 : (k + 1) * 256] = rows[k][0].T
-
-    for k, out in enumerate((gate_out, up_out)):
-        total = jnp.dot(xt[...], acts[k], preferred_element_type=F32)
-        if before:
-            total += before[k][...]
-        out[...] = total.astype(out.dtype)
-
-
-def in_grads(rows, acts, before, dtype):
+            gather_hidden(idx, *blocks[4 * k : 4 * k + 4], hidden, k * 512)
+
+    at = pl.ds(pl.multiple_of(i * tile, tile), tile)
+    g = jnp.concatenate([m[1] for m in rows], axis=0)
+    total = jnp.dot(hidden[:, at].T, g, preferred_element_type=F32)
+    out[...] = total.astype(BF)
+
+
+def down_grad(idx, rows, blocks0, blocks1):
     _, tokens, depth = rows[0].shape
-    width = acts.shape[2]
+    width = blocks0[0].shape[2]
     tile = 256
-    full = pl.BlockSpec((1, tokens, depth), lambda i: (0, 0, 0))
-    part = pl.BlockSpec((depth, tile), lambda i: (0, i))
-    out = jax.ShapeDtypeStruct((depth, width), dtype)
-    return pl.pallas_call(
-        in_grads_kernel,
-        grid=(width // tile,),
-        in_specs=[full] * 2
-        + [pl.BlockSpec((2, 2 * tokens, tile), lambda i: (0, 0, i))]
-        + [part] * len(before),
-        out_specs=[part] * 2,
-        out_shape=[out, out],
-        scratch_shapes=[pltpu.VMEM((depth, 2 * tokens), BF)],
-        compiler_params=params(PIPE_LIMIT),
-        cost_estimate=cost(8 * tokens * depth * width, 12 * 2**20),
-        name="in_grads",
-    )(*rows, acts, *before)
-
-
-def down_grad_kernel(*refs):
-    rows, acts = refs[:4], refs[4:6]
-    out, g = refs[6:]
-
-    @pl.when(pl.program_id(0) == 0)
-    def _():
-        for k in range(4):
-            g[k * 256 : (k + 1) * 256, :] = rows[k][0]
-
-    hidden = jnp.concatenate([r[0] for r in acts], axis=0)
-    out[...] = jnp.dot(hidden.T, g[...], preferred_element_type=F32).astype(BF)
-
-
-def down_grad(rows, acts):
-    _, tokens, depth = rows[0].shape
-    width = acts[0].shape[2]
-    tile = 256
-    full = pl.BlockSpec((1, tokens, depth), lambda i: (1, 0, 0))
     return pl.pallas_call(
         down_grad_kernel,
         grid=(width // tile,),
-        in_specs=[full] * 4 + [pl.BlockSpec((1, 2 * tokens, tile), lambda i: (2, 0, i))] * 2,
+        in_specs=[SMEM] + [VMEM] * 12,
         out_specs=pl.BlockSpec((tile, depth), lambda i: (i, 0)),
         out_shape=jax.ShapeDtypeStruct((width, depth), BF),
-        scratch_shapes=[pltpu.VMEM((4 * tokens, depth), BF)],
-        compiler_params=params(PIPE_LIMIT),
-        cost_estimate=cost(8 * tokens * depth * width, 6 * 2**20),
+        scratch_shapes=[pltpu.VMEM((4 * tokens, width), BF)],
+        compiler_params=params(),
+        cost_estimate=cost(8 * tokens * depth * width, 4 * 2**20),
         name="down_grad",
-    )(*rows, *acts)
+    )(idx, *rows, *blocks0, *blocks1)
 
 
 def body(inputs, upstream, loss_weight, pair_ids, margin, w_gate, w_up, w_down):
     fin = lax.axis_index("fin")
     idx = jnp.stack([fin // 2, fin % 2, lax.axis_index("fout")]).astype(jnp.int32)
 
+    weights = w_gate, w_up, w_down
     m0 = scaled(inputs, upstream, loss_weight, pair_ids, margin)
     m1 = tok_perm(m0, 0, 1)
     m2 = tok_perm(m0, 1, 0)
@@ -343,7 +414,6 @@
     def over_y(own, to1, to2, to3):
         return own, y_perm(to1, 1), y_perm(to2, 2), y_perm(to3, 3)
 
-    weights = w_gate, w_up, w_down
     *out, keep_a, own_a = forward(idx, m0, *weights)
     near_a = ring(*out)
     (m1,) = after((m1,), *out)
@@ -367,36 +437,46 @@
     last1 = ring(*step1)
 
     (across0,) = after((across0,), *step1)
-    here0 = gate(held0, across0)
+    here0, other0 = gate(held0, across0)
     last1 = after(last1, here0)
     held1, sent1 = ring_sum((own_a, own_b), near1, *last1)
     across1 = fin_perm(sent1, 0, 1)
 
     (ready,) = after((here0,), sent1)
     minus1, plus1 = ring(ready, ready)
-    on_plus, on_minus = minus1[0], plus1[1]
+    on_plus, on_minus = minus1[:5], plus1[5:]
     far0 = ring(on_plus, on_minus)
     (across1,) = after((across1,), on_plus, on_minus)
-    here1 = gate(held1, across1)
+    here1, other1 = gate(held1, across1)
     side1 = ring(here1, here1)
 
     far0 = after(far0, here1)
-    *grad0, act0 = input_grad(idx, here0, plus1, *far0, minus1, w_gate, w_up)
-    first = over_y(*grad0)
-    before = in_grads((m0, m1), act0, (), F32)
-
-    minus1, plus1 = after(side1, *before)
-    far1 = ring(minus1[0], plus1[1])
-    *grad1, act1 = input_grad(idx, here1, plus1, *far1, minus1, w_gate, w_up)
-    last = over_y(*grad1)
-
-    grad_gate, grad_up = in_grads((m2, m3), act1, before, BF)
-    rows = after((m0, m1, m2, m3), grad_gate)
-    grad_down = down_grad(rows, (act0, act1))
-    parts = after((*first, *last), grad_down)
-    mine, core, far_part, cross = owned(parts[:4], parts[4:])
-    others = (tok_perm(core, 0, 1), tok_perm(far_part, 1, 0), tok_perm(cross, 1, 1))
-    total = mine + sum(r.astype(F32) for r in others)
+    mine0, theirs0, act0, near = input_grad(idx, here0, plus1, *far0, minus1, *weights[:2])
+    core0 = tok_perm(theirs0, 0, 1)
+    blocks0 = here0, other0, near, fin_perm(near, 0, 1)
+    gate_part, up_part = part_grads(m0, m1, act0)
+    (core0,) = after((core0,), gate_part)
+    parts0 = split(idx, mine0, core0)
+    sums0 = over_y(*parts0)
+    side1 = after(side1, parts0[0])
+    far1 = ring(side1[0][:5], side1[1][5:])
+
+    far1 = after(far1, *sums0[1:], blocks0[3])
+    mine1, theirs1, act1, near = input_grad(idx, here1, side1[1], *far1, side1[0], *weights[:2])
+    core1 = tok_perm(theirs1, 0, 1)
+    blocks1 = here1, other1, near, fin_perm(near, 0, 1)
+    total0 = owned(*after(sums0, act1), F32)
+    (core1,) = after((core1,), total0)
+    parts1 = split(idx, mine1, core1)
+    sums1 = over_y(*parts1)
+    (act1,) = after((act1,), parts1[0])
+    grad_gate, grad_up = in_grads(m2, m3, act1, gate_part, up_part)
+    far = owned(*after(sums1, grad_gate), BF)
+    blocks1 = after(blocks1, far)
+    far = tok_perm(far, 1, 0)
+    grad_down = down_grad(idx, (m0, m1, m2, m3), blocks0, blocks1)
+    (far,) = after((far,), grad_down)
+    total = total0 + far.astype(F32)
     return (total.astype(BF), grad_gate, grad_up, grad_down)
 
 

time: 162 us -> 155 us (0.957)
  waiting for transfers between devices: 60.5 us -> 53.9 us
    ppermute x22 -> x24, waiting for transfers between devices: 55.9 us -> 49.2 us  [fin_perm(): return lax.ppermute(x, 'fin', pairs)]
    ppermute x6, waiting for transfers between devices: 0.02 us -> 4.46 us  [y_perm(): return lax.ppermute(x, 'fout', [(y, (y + dy) % 4) for y in range(4)])]
    ppermute x6, waiting for transfers between devices: 4.56 us -> 0.17 us  [tok_perm(): return lax.ppermute(x, 'tok', pairs)]
    ppermute x22 -> x24, starting transfers between devices: 34.9 us -> 36.8 us  [fin_perm(): return lax.ppermute(x, 'fin', pairs)]
    pallas_call x6 -> x9, Pallas kernels: 16.3 us -> 16.3 us  [the longest x1 5.3 us: down_grad(): pl.pallas_call(down_grad_kernel, grid=(width // tile,), in_specs=[SMEM] +...]
  transfers between devices with their start and end apart: 34 -> 36, of which waited for: 13 -> 17; matrix products, arithmetic and copies ran while one was open for 0% -> 0% of each run, Pallas kernels for 24% -> 22%
where the time goes in v4:
time: 155 us; the launch traced here: 154 us
  waiting for transfers between devices  53.9 us (35%)
  starting transfers between devices  53.8 us (35%)
  Pallas kernels  40.4 us (26%)
  local copies, waits for them, and re-layouts  4.52 us (3%)
    ppermute x24, waiting for transfers between devices, fin_perm(): return lax.ppermute(x, 'fin', pairs)  49.2 us
    ppermute x24, starting transfers between devices, fin_perm(): return lax.ppermute(x, 'fin', pairs)  36.8 us
    pallas_call x4, Pallas kernels, forward(): pl.pallas_call(forward_kernel, in_specs=[SMEM] + [VMEM] * 4, out_specs=[V...  13.4 us
    ppermute x6, starting transfers between devices, y_perm(): return lax.ppermute(x, 'fout', [(y, (y + dy) % 4) for y in range(4)])  11 us
    pallas_call x2, Pallas kernels, input_grad(): pl.pallas_call(input_grad_kernel, in_specs=[SMEM] + [VMEM] * 7, out_specs...  7.43 us
    ppermute x6, starting transfers between devices, tok_perm(): return lax.ppermute(x, 'tok', pairs)  6.09 us
    pallas_call x1, Pallas kernels, down_grad(): pl.pallas_call(down_grad_kernel, grid=(width // tile,), in_specs=[SMEM] +...  5.3 us
    ppermute x6, waiting for transfers between devices, y_perm(): return lax.ppermute(x, 'fout', [(y, (y + dy) % 4) for y in range(4)])  4.46 us
  transfers between devices with their start and end apart: 36, of which 17 were waited for; matrix products, arithmetic and copies ran while one was open for 0% of the time, Pallas kernels for 22%

profile of v4, /device:TPU:0, one launch (start us, length us, event | category | flops | bytes accessed | tf_op | source)
XLA Modules:
  0.0 154.3 jit_solution(5953053053793079959)
XLA Ops:
  0.6 2.3 %scaled.1.m.m0.refs_0_ = bf16[2,256,1024]{2,1,0:T(8,128)(2,1)} custom-call(f32[16]{0:T(128)} %margin.1, bf16[256,1024]{1,0:T(8,128)(2,1)} %x.1, bf16[256,1024]{1,0:T(8,128)(2,1)} %up.1, s32[1,256]{1,0:T(1,128)} %bitcast.5, s32[1,256]{1,0:T(1,128)} %bitcast.6), custom_call_target="tpu_custom_call" | custom-call | flops 1048576 | bytes 2097152 | tf_op jit(solution)/shard_map/scaled/pallas_call | solution.py:68
  3.0 3.1 %collective-permute-start.7 = (bf16[2,256,1024]{2,1,0:T(8,128)(2,1)}, bf16[2,256,1024]{2,1,0:T(8,128)(2,1)S(1)}, u32[]{:S(2)}, u32[]{:S(2)}) collective-permute-start(bf16[2,256,1024]{2,1,0:T(8,128)(2,1)} %scaled.1.m.m0.refs_0_), channel_id=1, source_target_pairs={{0,64},{32,96},{64,0},{96,32},{1,65},{33,97},{65,1},{97,33},{2,66}... | collective-permute-start | bytes 3145736 | tf_op jit(solution)/shard_map/ppermute | solution.py:32
  6.2 1.6 %copy-done.1 = bf16[1024,1024]{1,0:T(8,128)(2,1)S(1)} copy-done((bf16[1024,1024]{1,0:T(8,128)(2,1)S(1)}, bf16[1024,1024]{1,0:T(8,128)(2,1)}, u32[]{:S(2)}) %copy-start.1) | copy-done | bytes 2097176
  7.8 1.6 %copy-done.3 = bf16[1024,1024]{1,0:T(8,128)(2,1)S(1)} copy-done((bf16[1024,1024]{1,0:T(8,128)(2,1)S(1)}, bf16[1024,1024]{1,0:T(8,128)(2,1)}, u32[]{:S(2)}) %copy-start.3) | copy-done | bytes 2097176
  9.4 1.2 copy-done.5
  10.6 3.2 %forward.4 = (bf16[2,3,32,1024]{3,2,1,0:T(8,128)(2,1)S(1)}, bf16[2,3,32,1024]{3,2,1,0:T(8,128)(2,1)S(1)}, f32[2,3,32,1024]{3,2,1,0:T(8,128)S(1)}, f32[2,3,32,1024]{3,2,1,0:T(8,128)S(1)}) custom-call(s32[3]{0:T(128)S(1)} %pad_add_fusion.idx, bf16[2,256,1024]{2,1,0:T(8,128)(2,1)S(1)} %copy-done.5, bf16[1024,1024]{1,0:T(8,128)(2,1)S(1)} %copy-done.1, ...), custom_call_target="tpu_custom_call" | custom-call | flops 1610612736 | bytes 5242880 | tf_op jit(solution)/shard_map/forward/pallas_call | solution.py:109
  13.8 2.0 %collective-permute-start = (bf16[2,3,32,1024]{3,2,1,0:T(8,128)(2,1)S(1)}, bf16[2,3,32,1024]{3,2,1,0:T(8,128)(2,1)S(1)}, u32[]{:S(2)}, u32[]{:S(2)}) collective-permute-start(bf16[2,3,32,1024]{3,2,1,0:T(8,128)(2,1)S(1)} %get-tuple-element.85), channel_id=1, source_target_pairs={{0,8},{4,12},{8,16},{12,20},{16,24},{20,28},{24,0},{28,4},{1,9},{5... | collective-permute-start | bytes 1179656 | tf_op jit(solution)/shard_map/ppermute | solution.py:27
  15.8 2.2 %collective-permute-start.1 = (bf16[2,3,32,1024]{3,2,1,0:T(8,128)(2,1)S(1)}, bf16[2,3,32,1024]{3,2,1,0:T(8,128)(2,1)S(1)}, u32[]{:S(2)}, u32[]{:S(2)}) collective-permute-start(bf16[2,3,32,1024]{3,2,1,0:T(8,128)(2,1)S(1)} %get-tuple-element.86), channel_id=1, source_target_pairs={{0,24},{4,28},{8,0},{12,4},{16,8},{20,12},{24,16},{28,20},{1,25},{... | collective-permute-start | bytes 1179656 | tf_op jit(solution)/shard_map/ppermute | solution.py:27
  18.0 3.9 %forward.5 = (bf16[2,3,32,1024]{3,2,1,0:T(8,128)(2,1)S(1)}, bf16[2,3,32,1024]{3,2,1,0:T(8,128)(2,1)S(1)}, f32[2,3,32,1024]{3,2,1,0:T(8,128)S(1)}, f32[2,3,32,1024]{3,2,1,0:T(8,128)S(1)}) custom-call(s32[3]{0:T(128)S(1)} %pad_add_fusion.idx, bf16[2,256,1024]{2,1,0:T(8,128)(2,1)} %collective-permute-done.2.m.m1.refs_1_, bf16[1024,1024]{1,0:T(8,128)(2,1)S(1)} %copy-done.2, ...), custom_call_target="tpu_custom_call" | custom-call | flops 1610612736 | bytes 5242880 | tf_op jit(solution)/shard_map/forward/pallas_call | solution.py:109
  21.9 3.2 %collective-permute-start.4 = (bf16[2,3,32,1024]{3,2,1,0:T(8,128)(2,1)S(1)}, bf16[2,3,32,1024]{3,2,1,0:T(8,128)(2,1)S(1)}, u32[]{:S(2)}, u32[]{:S(2)}) collective-permute-start(bf16[2,3,32,1024]{3,2,1,0:T(8,128)(2,1)S(1)} %get-tuple-element.90), channel_id=1, source_target_pairs={{0,24},{4,28},{8,0},{12,4},{16,8},{20,12},{24,16},{28,20},{1,25},{... | collective-permute-start | bytes 1179656 | tf_op jit(solution)/shard_map/ppermute | solution.py:27
  25.2 2.6 %collective-permute-done.refs_1_ = bf16[2,3,32,1024]{3,2,1,0:T(8,128)(2,1)S(1)} collective-permute-done((bf16[2,3,32,1024]{3,2,1,0:T(8,128)(2,1)S(1)}, bf16[2,3,32,1024]{3,2,1,0:T(8,128)(2,1)S(1)}, u32[]{:S(2)}, u32[]{:S(2)}) %collective-permute-start) | collective-permute-done | bytes 393248 | tf_op jit(solution)/shard_map/ppermute | solution.py:27
  27.8 8.0 %collective-permute-done.3.refs_4_ = bf16[2,3,32,1024]{3,2,1,0:T(8,128)(2,1)S(1)} collective-permute-done((bf16[2,3,32,1024]{3,2,1,0:T(8,128)(2,1)S(1)}, bf16[2,3,32,1024]{3,2,1,0:T(8,128)(2,1)S(1)}, u32[]{:S(2)}, u32[]{:S(2)}) %collective-permute-start.3) | collective-permute-done | bytes 393248 | tf_op jit(solution)/shard_map/ppermute | solution.py:27
  36.0 1.3 collective-permute-start.5
  37.4 2.0 %collective-permute-start.6 = (bf16[3,2,32,1024]{3,2,1,0:T(8,128)(2,1)S(1)}, bf16[3,2,32,1024]{3,2,1,0:T(8,128)(2,1)S(1)}, u32[]{:S(2)}, u32[]{:S(2)}) collective-permute-start(bf16[3,2,32,1024]{3,2,1,0:T(8,128)(2,1)S(1)} %get-tuple-element.94), channel_id=1, source_target_pairs={{0,24},{4,28},{8,0},{12,4},{16,8},{20,12},{24,16},{28,20},{1,25},{... | collective-permute-start | bytes 1179656 | tf_op jit(solution)/shard_map/ppermute | solution.py:27
  39.4 3.2 %forward.6 = (bf16[2,3,32,1024]{3,2,1,0:T(8,128)(2,1)S(1)}, bf16[2,3,32,1024]{3,2,1,0:T(8,128)(2,1)S(1)}, f32[2,3,32,1024]{3,2,1,0:T(8,128)S(1)}, f32[2,3,32,1024]{3,2,1,0:T(8,128)S(1)}) custom-call(s32[3]{0:T(128)S(1)} %pad_add_fusion.idx, bf16[2,256,1024]{2,1,0:T(8,128)(2,1)S(1)} %collective-permute-done.7.m.m0.refs_2_, bf16[1024,1024]{1,0:T(8,128)(2,1)S(1)} %copy-done.2, ...), custom_call_target="tpu_custom_call" | custom-call | flops 1610612736 | bytes 5242880 | tf_op jit(solution)/shard_map/forward/pallas_call | solution.py:109
  42.6 3.2 %collective-permute-start.10 = (bf16[2,3,32,1024]{3,2,1,0:T(8,128)(2,1)S(1)}, bf16[2,3,32,1024]{3,2,1,0:T(8,128)(2,1)S(1)}, u32[]{:S(2)}, u32[]{:S(2)}) collective-permute-start(bf16[2,3,32,1024]{3,2,1,0:T(8,128)(2,1)S(1)} %get-tuple-element.97), channel_id=1, source_target_pairs={{0,24},{4,28},{8,0},{12,4},{16,8},{20,12},{24,16},{28,20},{1,25},{... | collective-permute-start | bytes 1179656 | tf_op jit(solution)/shard_map/ppermute | solution.py:27
  45.8 3.4 %collective-permute-done.5.refs_6_ = bf16[3,2,32,1024]{3,2,1,0:T(8,128)(2,1)S(1)} collective-permute-done((bf16[3,2,32,1024]{3,2,1,0:T(8,128)(2,1)S(1)}, bf16[3,2,32,1024]{3,2,1,0:T(8,128)(2,1)S(1)}, u32[]{:S(2)}, u32[]{:S(2)}) %collective-permute-start.5) | collective-permute-done | bytes 393248 | tf_op jit(solution)/shard_map/ppermute | solution.py:27
  50.4 3.2 %forward.7 = (bf16[2,3,32,1024]{3,2,1,0:T(8,128)(2,1)S(1)}, bf16[2,3,32,1024]{3,2,1,0:T(8,128)(2,1)S(1)}, f32[2,3,32,1024]{3,2,1,0:T(8,128)S(1)}, f32[2,3,32,1024]{3,2,1,0:T(8,128)S(1)}) custom-call(s32[3]{0:T(128)S(1)} %pad_add_fusion.idx, bf16[2,256,1024]{2,1,0:T(8,128)(2,1)S(1)} %collective-permute-done.11.m.m1.refs_3_, bf16[1024,1024]{1,0:T(8,128)(2,1)S(1)} %copy-done.2, ...), custom_call_target="tpu_custom_call" | custom-call | flops 1610612736 | bytes 5242880 | tf_op jit(solution)/shard_map/forward/pallas_call | solution.py:109
  53.6 1.7 %collective-permute-start.12 = (bf16[2,3,32,1024]{3,2,1,0:T(8,128)(2,1)S(1)}, bf16[2,3,32,1024]{3,2,1,0:T(8,128)(2,1)S(1)}, u32[]{:S(2)}, u32[]{:S(2)}) collective-permute-start(bf16[2,3,32,1024]{3,2,1,0:T(8,128)(2,1)S(1)} %get-tuple-element.105), channel_id=1, source_target_pairs={{0,8},{4,12},{8,16},{12,20},{16,24},{20,28},{24,0},{28,4},{1,9},{5... | collective-permute-start | bytes 1179656 | tf_op jit(solution)/shard_map/ppermute | solution.py:27
  55.2 1.6 %collective-permute-start.13 = (bf16[2,3,32,1024]{3,2,1,0:T(8,128)(2,1)S(1)}, bf16[2,3,32,1024]{3,2,1,0:T(8,128)(2,1)S(1)}, u32[]{:S(2)}, u32[]{:S(2)}) collective-permute-start(bf16[2,3,32,1024]{3,2,1,0:T(8,128)(2,1)S(1)} %get-tuple-element.106), channel_id=1, source_target_pairs={{0,24},{4,28},{8,0},{12,4},{16,8},{20,12},{24,16},{28,20},{1,25},{... | collective-permute-start | bytes 1179656 | tf_op jit(solution)/shard_map/ppermute | solution.py:27
  57.8 7.9 %collective-permute-done.12.refs_4_ = bf16[2,3,32,1024]{3,2,1,0:T(8,128)(2,1)S(1)} collective-permute-done((bf16[2,3,32,1024]{3,2,1,0:T(8,128)(2,1)S(1)}, bf16[2,3,32,1024]{3,2,1,0:T(8,128)(2,1)S(1)}, u32[]{:S(2)}, u32[]{:S(2)}) %collective-permute-start.12) | collective-permute-done | bytes 393248 | tf_op jit(solution)/shard_map/ppermute | solution.py:27
  65.8 1.4 collective-permute-start.14
  67.2 1.9 %collective-permute-start.15 = (bf16[3,2,32,1024]{3,2,1,0:T(8,128)(2,1)S(1)}, bf16[3,2,32,1024]{3,2,1,0:T(8,128)(2,1)S(1)}, u32[]{:S(2)}, u32[]{:S(2)}) collective-permute-start(bf16[3,2,32,1024]{3,2,1,0:T(8,128)(2,1)S(1)} %get-tuple-element.108), channel_id=1, source_target_pairs={{0,24},{4,28},{8,0},{12,4},{16,8},{20,12},{24,16},{28,20},{1,25},{... | collective-permute-start | bytes 1179656 | tf_op jit(solution)/shard_map/ppermute | solution.py:27
  69.5 7.5 %collective-permute-done.14.refs_6_ = bf16[3,2,32,1024]{3,2,1,0:T(8,128)(2,1)S(1)} collective-permute-done((bf16[3,2,32,1024]{3,2,1,0:T(8,128)(2,1)S(1)}, bf16[3,2,32,1024]{3,2,1,0:T(8,128)(2,1)S(1)}, u32[]{:S(2)}, u32[]{:S(2)}) %collective-permute-start.14) | collective-permute-done | bytes 393248 | tf_op jit(solution)/shard_map/ppermute | solution.py:27
  77.5 1.0 collective-permute-start.17
  78.4 2.3 %collective-permute-start.16 = (bf16[10,32,1024]{2,1,0:T(8,128)(2,1)S(1)}, bf16[10,32,1024]{2,1,0:T(8,128)(2,1)S(1)}, u32[]{:S(2)}, u32[]{:S(2)}) collective-permute-start(bf16[10,32,1024]{2,1,0:T(8,128)(2,1)S(1)} %get-tuple-element.116.here.refs_4_), channel_id=1, source_target_pairs={{0,24},{4,28},{8,0},{12,4},{16,8},{20,12},{24,16},{28,20},{1,25},{... | collective-permute-start | bytes 1966088 | tf_op jit(solution)/shard_map/ppermute | solution.py:27
  80.8 12.6 %collective-permute-done.17.minus1 = bf16[10,32,1024]{2,1,0:T(8,128)(2,1)S(1)} collective-permute-done((bf16[10,32,1024]{2,1,0:T(8,128)(2,1)S(1)}, bf16[10,32,1024]{2,1,0:T(8,128)(2,1)S(1)}, u32[]{:S(2)}, u32[]{:S(2)}) %collective-permute-start.17) | collective-permute-done | bytes 655392 | tf_op jit(solution)/shard_map/ppermute | solution.py:27
  93.5 3.3 %collective-permute-start.19 = (bf16[5,32,1024]{2,1,0:T(8,128)(2,1)S(1)}, bf16[5,32,1024]{2,1,0:T(8,128)(2,1)S(1)}, u32[]{:S(2)}, u32[]{:S(2)}) collective-permute-start(bf16[5,32,1024]{2,1,0:T(8,128)(2,1)S(1)} %slice.17), channel_id=1, source_target_pairs={{0,24},{4,28},{8,0},{12,4},{16,8},{20,12},{24,16},{28,20},{1,25},{... | collective-permute-start | bytes 983048 | tf_op jit(solution)/shard_map/ppermute | solution.py:27
  96.8 0.8 collective-permute-done.20.across
  98.3 3.2 %collective-permute-start.26 = (bf16[10,32,1024]{2,1,0:T(8,128)(2,1)S(1)}, bf16[10,32,1024]{2,1,0:T(8,128)(2,1)S(1)}, u32[]{:S(2)}, u32[]{:S(2)}) collective-permute-start(bf16[10,32,1024]{2,1,0:T(8,128)(2,1)S(1)} %get-tuple-element.158.here.refs_8_), channel_id=1, source_target_pairs={{0,24},{4,28},{8,0},{12,4},{16,8},{20,12},{24,16},{28,20},{1,25},{... | collective-permute-start | bytes 1966088 | tf_op jit(solution)/shard_map/ppermute | solution.py:27
  101.5 3.4 %collective-permute-done.18.far_a = bf16[5,32,1024]{2,1,0:T(8,128)(2,1)S(1)} collective-permute-done((bf16[5,32,1024]{2,1,0:T(8,128)(2,1)S(1)}, bf16[5,32,1024]{2,1,0:T(8,128)(2,1)S(1)}, u32[]{:S(2)}, u32[]{:S(2)}) %collective-permute-start.18) | collective-permute-done | bytes 327712 | tf_op jit(solution)/shard_map/ppermute | solution.py:27
  104.9 3.7 %input_grad.2 = (f32[256,1024]{1,0:T(8,128)S(1)}, bf16[256,1024]{1,0:T(8,128)(2,1)S(1)}, bf16[2,512,1024]{2,1,0:T(8,128)(2,1)S(1)}, bf16[3,2,32,1024]{3,2,1,0:T(8,128)(2,1)S(1)}) custom-call(s32[3]{0:T(128)S(1)} %pad_add_fusion.idx, bf16[10,32,1024]{2,1,0:T(8,128)(2,1)S(1)} %get-tuple-element.116.here.refs_4_, ...), custom_call_target="tpu_custom_call" | custom-call | flops 2147483648 | bytes 10485760 | tf_op jit(solution)/shard_map/input_grad/pallas_call | solution.py:240
  108.8 4.4 %part_grads.1 = (f32[1024,1024]{1,0:T(8,128)S(1)}, f32[1024,1024]{1,0:T(8,128)S(1)}) custom-call(bf16[2,256,1024]{2,1,0:T(8,128)(2,1)S(1)} %copy-done.6, bf16[2,256,1024]{2,1,0:T(8,128)(2,1)} %collective-permute-done.2.m.m1.refs_1_, bf16[2,512,1024]{2,1,0:T(8,128)(2,1)S(1)} %get-tuple-element.124.acts), custom_call_target="tpu_custom_call" | custom-call | flops 2147483648 | bytes 8388608 | tf_op jit(solution)/shard_map/part_grads/pallas_call | solution.py:310
  113.9 1.9 %collective-permute-done.25.minus1 = bf16[10,32,1024]{2,1,0:T(8,128)(2,1)S(1)} collective-permute-done((bf16[10,32,1024]{2,1,0:T(8,128)(2,1)S(1)}, bf16[10,32,1024]{2,1,0:T(8,128)(2,1)S(1)}, u32[]{:S(2)}, u32[]{:S(2)}) %collective-permute-start.25) | collective-permute-done | bytes 655392 | tf_op jit(solution)/shard_map/ppermute | solution.py:27
  115.9 3.4 %collective-permute-start.28 = (bf16[5,32,1024]{2,1,0:T(8,128)(2,1)S(1)}, bf16[5,32,1024]{2,1,0:T(8,128)(2,1)S(1)}, u32[]{:S(2)}, u32[]{:S(2)}) collective-permute-start(bf16[5,32,1024]{2,1,0:T(8,128)(2,1)S(1)} %slice.15), channel_id=1, source_target_pairs={{0,24},{4,28},{8,0},{12,4},{16,8},{20,12},{24,16},{28,20},{1,25},{... | collective-permute-start | bytes 983048 | tf_op jit(solution)/shard_map/ppermute | solution.py:27
  119.3 1.6 %collective-permute-start.22 = (bf16[64,1024]{1,0:T(8,128)(2,1)S(1)}, bf16[64,1024]{1,0:T(8,128)(2,1)S(1)}, u32[]{:S(2)}, u32[]{:S(2)}) collective-permute-start(bf16[64,1024]{1,0:T(8,128)(2,1)S(1)} %get-tuple-element.128), channel_id=1, source_target_pairs={{0,1},{1,2},{2,3},{3,0},{4,5},{5,6},{6,7},{7,4},{8,9},{9,10},{10,1... | collective-permute-start | bytes 393224 | tf_op jit(solution)/shard_map/ppermute | solution.py:36
  120.9 2.9 %collective-permute-start.23 = (bf16[64,1024]{1,0:T(8,128)(2,1)S(1)}, bf16[64,1024]{1,0:T(8,128)(2,1)S(1)}, u32[]{:S(2)}, u32[]{:S(2)}) collective-permute-start(bf16[64,1024]{1,0:T(8,128)(2,1)S(1)} %get-tuple-element.129), channel_id=1, source_target_pairs={{0,2},{1,3},{2,0},{3,1},{4,6},{5,7},{6,4},{7,5},{8,10},{9,11},{10,... | collective-permute-start | bytes 393224 | tf_op jit(solution)/shard_map/ppermute | solution.py:36
  123.8 1.3 collective-permute-start.24
  125.1 1.8 %collective-permute-done.22.a = bf16[64,1024]{1,0:T(8,128)(2,1)S(1)} collective-permute-done((bf16[64,1024]{1,0:T(8,128)(2,1)S(1)}, bf16[64,1024]{1,0:T(8,128)(2,1)S(1)}, u32[]{:S(2)}, u32[]{:S(2)}) %collective-permute-start.22) | collective-permute-done | bytes 131104 | tf_op jit(solution)/shard_map/ppermute | solution.py:36
  126.9 1.7 %collective-permute-done.23.b = bf16[64,1024]{1,0:T(8,128)(2,1)S(1)} collective-permute-done((bf16[64,1024]{1,0:T(8,128)(2,1)S(1)}, bf16[64,1024]{1,0:T(8,128)(2,1)S(1)}, u32[]{:S(2)}, u32[]{:S(2)}) %collective-permute-start.23) | collective-permute-done | bytes 131104 | tf_op jit(solution)/shard_map/ppermute | solution.py:36
  128.8 3.7 %input_grad.3 = (f32[256,1024]{1,0:T(8,128)S(1)}, bf16[256,1024]{1,0:T(8,128)(2,1)S(1)}, bf16[2,512,1024]{2,1,0:T(8,128)(2,1)S(1)}, bf16[3,2,32,1024]{3,2,1,0:T(8,128)(2,1)S(1)}) custom-call(s32[3]{0:T(128)S(1)} %pad_add_fusion.idx, bf16[10,32,1024]{2,1,0:T(8,128)(2,1)S(1)} %get-tuple-element.158.here.refs_8_, ...), custom_call_target="tpu_custom_call" | custom-call | flops 2147483648 | bytes 10485760 | tf_op jit(solution)/shard_map/input_grad/pallas_call | solution.py:240
  132.6 1.7 %collective-permute-start.35 = (bf16[3,2,32,1024]{3,2,1,0:T(8,128)(2,1)S(1)}, bf16[3,2,32,1024]{3,2,1,0:T(8,128)(2,1)S(1)}, u32[]{:S(2)}, u32[]{:S(2)}) collective-permute-start(bf16[3,2,32,1024]{3,2,1,0:T(8,128)(2,1)S(1)} %get-tuple-element.160.refs_10_), channel_id=1, source_target_pairs={{0,4},{4,0},{8,12},{12,8},{16,20},{20,16},{24,28},{28,24},{1,5},{5... | collective-permute-start | bytes 1179656 | tf_op jit(solution)/shard_map/ppermute | solution.py:27
  135.1 1.1 collective-permute-start.31
  136.2 3.0 %collective-permute-start.32 = (bf16[64,1024]{1,0:T(8,128)(2,1)S(1)}, bf16[64,1024]{1,0:T(8,128)(2,1)S(1)}, u32[]{:S(2)}, u32[]{:S(2)}) collective-permute-start(bf16[64,1024]{1,0:T(8,128)(2,1)S(1)} %get-tuple-element.146), channel_id=1, source_target_pairs={{0,2},{1,3},{2,0},{3,1},{4,6},{5,7},{6,4},{7,5},{8,10},{9,11},{10,... | collective-permute-start | bytes 393224 | tf_op jit(solution)/shard_map/ppermute | solution.py:36
  139.2 1.1 collective-permute-start.33
  140.3 4.4 %in_grads.1 = (bf16[1024,1024]{1,0:T(8,128)(2,1)}, bf16[1024,1024]{1,0:T(8,128)(2,1)}) custom-call(bf16[2,256,1024]{2,1,0:T(8,128)(2,1)S(1)} %collective-permute-done.7.m.m0.refs_2_, bf16[2,256,1024]{2,1,0:T(8,128)(2,1)S(1)} %collective-permute-done.11.m.m1.refs_3_, bf16[2,512,1024]{2,1,0:T(8,128)(2,1)S(1)} %get-tuple-element.148.acts, ...), custom_call_target="tpu_custom_call" | custom-call | flops 2147483648 | bytes 8388608 | tf_op jit(solution)/shard_map/in_grads/pallas_call | solution.py:344
  145.6 2.7 %collective-permute-start.34 = (bf16[64,1024]{1,0:T(8,128)(2,1)S(1)}, bf16[64,1024]{1,0:T(8,128)(2,1)S(1)}, u32[]{:S(2)}, u32[]{:S(2)}) collective-permute-start(bf16[64,1024]{1,0:T(8,128)(2,1)S(1)} %owned.3), channel_id=1, source_target_pairs={{0,64},{32,96},{64,0},{96,32},{1,65},{33,97},{65,1},{97,33},{2,66}... | collective-permute-start | bytes 393224 | tf_op jit(solution)/shard_map/ppermute | solution.py:32
  148.3 5.3 %down_grad.1 = bf16[1024,1024]{1,0:T(8,128)(2,1)} custom-call(s32[3]{0:T(128)S(1)} %pad_add_fusion.idx, bf16[2,256,1024]{2,1,0:T(8,128)(2,1)S(1)} %copy-done.6, bf16[2,256,1024]{2,1,0:T(8,128)(2,1)} %collective-permute-done.2.m.m1.refs_1_, bf16[2,256,1024]{2,1,0:T(8,128)(2,1)S(1)} %collective-permute-done.7.m.m0.refs_2_, ...), custom_call_target="tpu_custom_call" | custom-call | flops 2147483648 | bytes 4194304 | tf_op jit(solution)/shard_map/down_grad/pallas_call | solution.py:389
  (64 shorter events, 7.7 us)
Async XLA Ops:
  0.6 5.6 %copy-start = (bf16[1024,1024]{1,0:T(8,128)(2,1)S(1)}, bf16[1024,1024]{1,0:T(8,128)(2,1)}, u32[]{:S(2)}) copy-start(bf16[1024,1024]{1,0:T(8,128)(2,1)} %wd.7) | copy-start | bytes 6291460
  3.0 15.0 %collective-permute-start.2 = (bf16[2,256,1024]{2,1,0:T(8,128)(2,1)}, bf16[2,256,1024]{2,1,0:T(8,128)(2,1)}, u32[]{:S(2)}, u32[]{:S(2)}) collective-permute-start(bf16[2,256,1024]{2,1,0:T(8,128)(2,1)} %scaled.1.m.m0.refs_0_), channel_id=1, source_target_pairs={{0,32},{32,0},{64,96},{96,64},{1,33},{33,1},{65,97},{97,65},{2,34}... | collective-permute-start | bytes 3145736 | tf_op jit(solution)/shard_map/ppermute | solution.py:32
  3.0 33.0 %collective-permute-start.7 = (bf16[2,256,1024]{2,1,0:T(8,128)(2,1)}, bf16[2,256,1024]{2,1,0:T(8,128)(2,1)S(1)}, u32[]{:S(2)}, u32[]{:S(2)}) collective-permute-start(bf16[2,256,1024]{2,1,0:T(8,128)(2,1)} %scaled.1.m.m0.refs_0_), channel_id=1, source_target_pairs={{0,64},{32,96},{64,0},{96,32},{1,65},{33,97},{65,1},{97,33},{2,66}... | collective-permute-start | bytes 3145736 | tf_op jit(solution)/shard_map/ppermute | solution.py:32
  6.2 1.6 %copy-start.1 = (bf16[1024,1024]{1,0:T(8,128)(2,1)S(1)}, bf16[1024,1024]{1,0:T(8,128)(2,1)}, u32[]{:S(2)}) copy-start(bf16[1024,1024]{1,0:T(8,128)(2,1)} %wg.11) | copy-start | bytes 6291460
  7.8 1.6 %copy-start.3 = (bf16[1024,1024]{1,0:T(8,128)(2,1)S(1)}, bf16[1024,1024]{1,0:T(8,128)(2,1)}, u32[]{:S(2)}) copy-start(bf16[1024,1024]{1,0:T(8,128)(2,1)} %wu.11) | copy-start | bytes 6291460
  9.4 1.2 copy-start.5
  10.6 7.4 %copy-start.2 = (bf16[1024,1024]{1,0:T(8,128)(2,1)S(1)}, bf16[1024,1024]{1,0:T(8,128)(2,1)}, u32[]{:S(2)}) copy-start(bf16[1024,1024]{1,0:T(8,128)(2,1)} %wg.11) | copy-start | bytes 6291460
  13.8 14.0 %collective-permute-start = (bf16[2,3,32,1024]{3,2,1,0:T(8,128)(2,1)S(1)}, bf16[2,3,32,1024]{3,2,1,0:T(8,128)(2,1)S(1)}, u32[]{:S(2)}, u32[]{:S(2)}) collective-permute-start(bf16[2,3,32,1024]{3,2,1,0:T(8,128)(2,1)S(1)} %get-tuple-element.85), channel_id=1, source_target_pairs={{0,8},{4,12},{8,16},{12,20},{16,24},{20,28},{24,0},{28,4},{1,9},{5... | collective-permute-start | bytes 1179656 | tf_op jit(solution)/shard_map/ppermute | solution.py:27
  15.8 12.0 %collective-permute-start.1 = (bf16[2,3,32,1024]{3,2,1,0:T(8,128)(2,1)S(1)}, bf16[2,3,32,1024]{3,2,1,0:T(8,128)(2,1)S(1)}, u32[]{:S(2)}, u32[]{:S(2)}) collective-permute-start(bf16[2,3,32,1024]{3,2,1,0:T(8,128)(2,1)S(1)} %get-tuple-element.86), channel_id=1, source_target_pairs={{0,24},{4,28},{8,0},{12,4},{16,8},{20,12},{24,16},{28,20},{1,25},{... | collective-permute-start | bytes 1179656 | tf_op jit(solution)/shard_map/ppermute | solution.py:27
  21.9 13.9 %collective-permute-start.3 = (bf16[2,3,32,1024]{3,2,1,0:T(8,128)(2,1)S(1)}, bf16[2,3,32,1024]{3,2,1,0:T(8,128)(2,1)S(1)}, u32[]{:S(2)}, u32[]{:S(2)}) collective-permute-start(bf16[2,3,32,1024]{3,2,1,0:T(8,128)(2,1)S(1)} %get-tuple-element.89), channel_id=1, source_target_pairs={{0,8},{4,12},{8,16},{12,20},{16,24},{20,28},{24,0},{28,4},{1,9},{5... | collective-permute-start | bytes 1179656 | tf_op jit(solution)/shard_map/ppermute | solution.py:27
  21.9 13.9 %collective-permute-start.4 = (bf16[2,3,32,1024]{3,2,1,0:T(8,128)(2,1)S(1)}, bf16[2,3,32,1024]{3,2,1,0:T(8,128)(2,1)S(1)}, u32[]{:S(2)}, u32[]{:S(2)}) collective-permute-start(bf16[2,3,32,1024]{3,2,1,0:T(8,128)(2,1)S(1)} %get-tuple-element.90), channel_id=1, source_target_pairs={{0,24},{4,28},{8,0},{12,4},{16,8},{20,12},{24,16},{28,20},{1,25},{... | collective-permute-start | bytes 1179656 | tf_op jit(solution)/shard_map/ppermute | solution.py:27
  36.0 14.4 %collective-permute-start.11 = (bf16[2,256,1024]{2,1,0:T(8,128)(2,1)S(1)}, bf16[2,256,1024]{2,1,0:T(8,128)(2,1)S(1)}, u32[]{:S(2)}, u32[]{:S(2)}) collective-permute-start(bf16[2,256,1024]{2,1,0:T(8,128)(2,1)S(1)} %collective-permute-done.7.m.m0.refs_2_), channel_id=1, source_target_pairs={{0,32},{32,0},{64,96},{96,64},{1,33},{33,1},{65,97},{97,65},{2,34}... | collective-permute-start | bytes 3145736 | tf_op jit(solution)/shard_map/ppermute | solution.py:32
  36.0 13.2 %collective-permute-start.5 = (bf16[3,2,32,1024]{3,2,1,0:T(8,128)(2,1)S(1)}, bf16[3,2,32,1024]{3,2,1,0:T(8,128)(2,1)S(1)}, u32[]{:S(2)}, u32[]{:S(2)}) collective-permute-start(bf16[3,2,32,1024]{3,2,1,0:T(8,128)(2,1)S(1)} %get-tuple-element.93), channel_id=1, source_target_pairs={{0,8},{4,12},{8,16},{12,20},{16,24},{20,28},{24,0},{28,4},{1,9},{5... | collective-permute-start | bytes 1179656 | tf_op jit(solution)/shard_map/ppermute | solution.py:27
  37.4 12.0 %collective-permute-start.6 = (bf16[3,2,32,1024]{3,2,1,0:T(8,128)(2,1)S(1)}, bf16[3,2,32,1024]{3,2,1,0:T(8,128)(2,1)S(1)}, u32[]{:S(2)}, u32[]{:S(2)}) collective-permute-start(bf16[3,2,32,1024]{3,2,1,0:T(8,128)(2,1)S(1)} %get-tuple-element.94), channel_id=1, source_target_pairs={{0,24},{4,28},{8,0},{12,4},{16,8},{20,12},{24,16},{28,20},{1,25},{... | collective-permute-start | bytes 1179656 | tf_op jit(solution)/shard_map/ppermute | solution.py:27
  42.5 15.1 %collective-permute-start.9 = (bf16[2,3,32,1024]{3,2,1,0:T(8,128)(2,1)S(1)}, bf16[2,3,32,1024]{3,2,1,0:T(8,128)(2,1)S(1)}, u32[]{:S(2)}, u32[]{:S(2)}) collective-permute-start(bf16[2,3,32,1024]{3,2,1,0:T(8,128)(2,1)S(1)} %get-tuple-element.96), channel_id=1, source_target_pairs={{0,8},{4,12},{8,16},{12,20},{16,24},{20,28},{24,0},{28,4},{1,9},{5... | collective-permute-start | bytes 1179656 | tf_op jit(solution)/shard_map/ppermute | solution.py:27
  42.6 15.1 %collective-permute-start.10 = (bf16[2,3,32,1024]{3,2,1,0:T(8,128)(2,1)S(1)}, bf16[2,3,32,1024]{3,2,1,0:T(8,128)(2,1)S(1)}, u32[]{:S(2)}, u32[]{:S(2)}) collective-permute-start(bf16[2,3,32,1024]{3,2,1,0:T(8,128)(2,1)S(1)} %get-tuple-element.97), channel_id=1, source_target_pairs={{0,24},{4,28},{8,0},{12,4},{16,8},{20,12},{24,16},{28,20},{1,25},{... | collective-permute-start | bytes 1179656 | tf_op jit(solution)/shard_map/ppermute | solution.py:27
  49.7 19.4 %collective-permute-start.8 = (bf16[2,3,2,32,1024]{4,3,2,1,0:T(8,128)(2,1)S(1)}, bf16[2,3,2,32,1024]{4,3,2,1,0:T(8,128)(2,1)S(1)}, u32[]{:S(2)}, u32[]{:S(2)}) collective-permute-start(bf16[2,3,2,32,1024]{4,3,2,1,0:T(8,128)(2,1)S(1)} %get-tuple-element.101), channel_id=1, source_target_pairs={{0,4},{4,0},{8,12},{12,8},{16,20},{20,16},{24,28},{28,24},{1,5},{5... | collective-permute-start | bytes 2359304 | tf_op jit(solution)/shard_map/ppermute | solution.py:27
  53.6 12.1 %collective-permute-start.12 = (bf16[2,3,32,1024]{3,2,1,0:T(8,128)(2,1)S(1)}, bf16[2,3,32,1024]{3,2,1,0:T(8,128)(2,1)S(1)}, u32[]{:S(2)}, u32[]{:S(2)}) collective-permute-start(bf16[2,3,32,1024]{3,2,1,0:T(8,128)(2,1)S(1)} %get-tuple-element.105), channel_id=1, source_target_pairs={{0,8},{4,12},{8,16},{12,20},{16,24},{20,28},{24,0},{28,4},{1,9},{5... | collective-permute-start | bytes 1179656 | tf_op jit(solution)/shard_map/ppermute | solution.py:27
  55.2 10.5 %collective-permute-start.13 = (bf16[2,3,32,1024]{3,2,1,0:T(8,128)(2,1)S(1)}, bf16[2,3,32,1024]{3,2,1,0:T(8,128)(2,1)S(1)}, u32[]{:S(2)}, u32[]{:S(2)}) collective-permute-start(bf16[2,3,32,1024]{3,2,1,0:T(8,128)(2,1)S(1)} %get-tuple-element.106), channel_id=1, source_target_pairs={{0,24},{4,28},{8,0},{12,4},{16,8},{20,12},{24,16},{28,20},{1,25},{... | collective-permute-start | bytes 1179656 | tf_op jit(solution)/shard_map/ppermute | solution.py:27
  65.8 11.2 %collective-permute-start.14 = (bf16[3,2,32,1024]{3,2,1,0:T(8,128)(2,1)S(1)}, bf16[3,2,32,1024]{3,2,1,0:T(8,128)(2,1)S(1)}, u32[]{:S(2)}, u32[]{:S(2)}) collective-permute-start(bf16[3,2,32,1024]{3,2,1,0:T(8,128)(2,1)S(1)} %get-tuple-element.107), channel_id=1, source_target_pairs={{0,8},{4,12},{8,16},{12,20},{16,24},{20,28},{24,0},{28,4},{1,9},{5... | collective-permute-start | bytes 1179656 | tf_op jit(solution)/shard_map/ppermute | solution.py:27
  67.2 9.8 %collective-permute-start.15 = (bf16[3,2,32,1024]{3,2,1,0:T(8,128)(2,1)S(1)}, bf16[3,2,32,1024]{3,2,1,0:T(8,128)(2,1)S(1)}, u32[]{:S(2)}, u32[]{:S(2)}) collective-permute-start(bf16[3,2,32,1024]{3,2,1,0:T(8,128)(2,1)S(1)} %get-tuple-element.108), channel_id=1, source_target_pairs={{0,24},{4,28},{8,0},{12,4},{16,8},{20,12},{24,16},{28,20},{1,25},{... | collective-permute-start | bytes 1179656 | tf_op jit(solution)/shard_map/ppermute | solution.py:27
  77.4 27.5 %copy-start.4 = (bf16[1024,1024]{1,0:T(8,128)(2,1)S(1)}, bf16[1024,1024]{1,0:T(8,128)(2,1)}, u32[]{:S(2)}) copy-start(bf16[1024,1024]{1,0:T(8,128)(2,1)} %wu.11) | copy-start | bytes 6291460
  77.5 15.9 %collective-permute-start.17 = (bf16[10,32,1024]{2,1,0:T(8,128)(2,1)S(1)}, bf16[10,32,1024]{2,1,0:T(8,128)(2,1)S(1)}, u32[]{:S(2)}, u32[]{:S(2)}) collective-permute-start(bf16[10,32,1024]{2,1,0:T(8,128)(2,1)S(1)} %get-tuple-element.116.here.refs_4_), channel_id=1, source_target_pairs={{0,8},{4,12},{8,16},{12,20},{16,24},{20,28},{24,0},{28,4},{1,9},{5... | collective-permute-start | bytes 1966088 | tf_op jit(solution)/shard_map/ppermute | solution.py:27
  78.4 15.0 %collective-permute-start.16 = (bf16[10,32,1024]{2,1,0:T(8,128)(2,1)S(1)}, bf16[10,32,1024]{2,1,0:T(8,128)(2,1)S(1)}, u32[]{:S(2)}, u32[]{:S(2)}) collective-permute-start(bf16[10,32,1024]{2,1,0:T(8,128)(2,1)S(1)} %get-tuple-element.116.here.refs_4_), channel_id=1, source_target_pairs={{0,24},{4,28},{8,0},{12,4},{16,8},{20,12},{24,16},{28,20},{1,25},{... | collective-permute-start | bytes 1966088 | tf_op jit(solution)/shard_map/ppermute | solution.py:27
  80.8 16.9 %collective-permute-start.20 = (bf16[2,3,2,32,1024]{4,3,2,1,0:T(8,128)(2,1)S(1)}, bf16[2,3,2,32,1024]{4,3,2,1,0:T(8,128)(2,1)S(1)}, u32[]{:S(2)}, u32[]{:S(2)}) collective-permute-start(bf16[2,3,2,32,1024]{4,3,2,1,0:T(8,128)(2,1)S(1)} %get-tuple-element.115), channel_id=1, source_target_pairs={{0,4},{4,0},{8,12},{12,8},{16,20},{20,16},{24,28},{28,24},{1,5},{5... | collective-permute-start | bytes 2359304 | tf_op jit(solution)/shard_map/ppermute | solution.py:27
  93.4 11.5 %collective-permute-start.18 = (bf16[5,32,1024]{2,1,0:T(8,128)(2,1)S(1)}, bf16[5,32,1024]{2,1,0:T(8,128)(2,1)S(1)}, u32[]{:S(2)}, u32[]{:S(2)}) collective-permute-start(bf16[5,32,1024]{2,1,0:T(8,128)(2,1)S(1)} %slice.16), channel_id=1, source_target_pairs={{0,8},{4,12},{8,16},{12,20},{16,24},{20,28},{24,0},{28,4},{1,9},{5... | collective-permute-start | bytes 983048 | tf_op jit(solution)/shard_map/ppermute | solution.py:27
  93.5 11.4 %collective-permute-start.19 = (bf16[5,32,1024]{2,1,0:T(8,128)(2,1)S(1)}, bf16[5,32,1024]{2,1,0:T(8,128)(2,1)S(1)}, u32[]{:S(2)}, u32[]{:S(2)}) collective-permute-start(bf16[5,32,1024]{2,1,0:T(8,128)(2,1)S(1)} %slice.17), channel_id=1, source_target_pairs={{0,24},{4,28},{8,0},{12,4},{16,8},{20,12},{24,16},{28,20},{1,25},{... | collective-permute-start | bytes 983048 | tf_op jit(solution)/shard_map/ppermute | solution.py:27
  98.0 10.8 %copy-start.6 = (bf16[2,256,1024]{2,1,0:T(8,128)(2,1)S(1)}, bf16[2,256,1024]{2,1,0:T(8,128)(2,1)}, u32[]{:S(2)}) copy-start(bf16[2,256,1024]{2,1,0:T(8,128)(2,1)} %scaled.1.m.m0.refs_0_) | copy-start | bytes 3145732
  98.0 17.8 %collective-permute-start.25 = (bf16[10,32,1024]{2,1,0:T(8,128)(2,1)S(1)}, bf16[10,32,1024]{2,1,0:T(8,128)(2,1)S(1)}, u32[]{:S(2)}, u32[]{:S(2)}) collective-permute-start(bf16[10,32,1024]{2,1,0:T(8,128)(2,1)S(1)} %get-tuple-element.158.here.refs_8_), channel_id=1, source_target_pairs={{0,8},{4,12},{8,16},{12,20},{16,24},{20,28},{24,0},{28,4},{1,9},{5... | collective-permute-start | bytes 1966088 | tf_op jit(solution)/shard_map/ppermute | solution.py:27
  98.3 17.5 %collective-permute-start.26 = (bf16[10,32,1024]{2,1,0:T(8,128)(2,1)S(1)}, bf16[10,32,1024]{2,1,0:T(8,128)(2,1)S(1)}, u32[]{:S(2)}, u32[]{:S(2)}) collective-permute-start(bf16[10,32,1024]{2,1,0:T(8,128)(2,1)S(1)} %get-tuple-element.158.here.refs_8_), channel_id=1, source_target_pairs={{0,24},{4,28},{8,0},{12,4},{16,8},{20,12},{24,16},{28,20},{1,25},{... | collective-permute-start | bytes 1966088 | tf_op jit(solution)/shard_map/ppermute | solution.py:27
  108.6 4.6 %collective-permute-start.21 = (bf16[256,1024]{1,0:T(8,128)(2,1)S(1)}, bf16[256,1024]{1,0:T(8,128)(2,1)S(1)}, u32[]{:S(2)}, u32[]{:S(2)}) collective-permute-start(bf16[256,1024]{1,0:T(8,128)(2,1)S(1)} %get-tuple-element.123), channel_id=1, source_target_pairs={{0,32},{32,0},{64,96},{96,64},{1,33},{33,1},{65,97},{97,65},{2,34}... | collective-permute-start | bytes 1572872 | tf_op jit(solution)/shard_map/ppermute | solution.py:32
  108.7 15.0 %collective-permute-start.29 = (bf16[3,2,32,1024]{3,2,1,0:T(8,128)(2,1)S(1)}, bf16[3,2,32,1024]{3,2,1,0:T(8,128)(2,1)S(1)}, u32[]{:S(2)}, u32[]{:S(2)}) collective-permute-start(bf16[3,2,32,1024]{3,2,1,0:T(8,128)(2,1)S(1)} %get-tuple-element.133.refs_6_), channel_id=1, source_target_pairs={{0,4},{4,0},{8,12},{12,8},{16,20},{20,16},{24,28},{28,24},{1,5},{5... | collective-permute-start | bytes 1179656 | tf_op jit(solution)/shard_map/ppermute | solution.py:27
  115.8 12.9 %collective-permute-start.27 = (bf16[5,32,1024]{2,1,0:T(8,128)(2,1)S(1)}, bf16[5,32,1024]{2,1,0:T(8,128)(2,1)S(1)}, u32[]{:S(2)}, u32[]{:S(2)}) collective-permute-start(bf16[5,32,1024]{2,1,0:T(8,128)(2,1)S(1)} %slice.14), channel_id=1, source_target_pairs={{0,8},{4,12},{8,16},{12,20},{16,24},{20,28},{24,0},{28,4},{1,9},{5... | collective-permute-start | bytes 983048 | tf_op jit(solution)/shard_map/ppermute | solution.py:27
  115.9 12.8 %collective-permute-start.28 = (bf16[5,32,1024]{2,1,0:T(8,128)(2,1)S(1)}, bf16[5,32,1024]{2,1,0:T(8,128)(2,1)S(1)}, u32[]{:S(2)}, u32[]{:S(2)}) collective-permute-start(bf16[5,32,1024]{2,1,0:T(8,128)(2,1)S(1)} %slice.15), channel_id=1, source_target_pairs={{0,24},{4,28},{8,0},{12,4},{16,8},{20,12},{24,16},{28,20},{1,25},{... | collective-permute-start | bytes 983048 | tf_op jit(solution)/shard_map/ppermute | solution.py:27
  119.3 7.6 %collective-permute-start.22 = (bf16[64,1024]{1,0:T(8,128)(2,1)S(1)}, bf16[64,1024]{1,0:T(8,128)(2,1)S(1)}, u32[]{:S(2)}, u32[]{:S(2)}) collective-permute-start(bf16[64,1024]{1,0:T(8,128)(2,1)S(1)} %get-tuple-element.128), channel_id=1, source_target_pairs={{0,1},{1,2},{2,3},{3,0},{4,5},{5,6},{6,7},{7,4},{8,9},{9,10},{10,1... | collective-permute-start | bytes 393224 | tf_op jit(solution)/shard_map/ppermute | solution.py:36
  120.9 7.7 %collective-permute-start.23 = (bf16[64,1024]{1,0:T(8,128)(2,1)S(1)}, bf16[64,1024]{1,0:T(8,128)(2,1)S(1)}, u32[]{:S(2)}, u32[]{:S(2)}) collective-permute-start(bf16[64,1024]{1,0:T(8,128)(2,1)S(1)} %get-tuple-element.129), channel_id=1, source_target_pairs={{0,2},{1,3},{2,0},{3,1},{4,6},{5,7},{6,4},{7,5},{8,10},{9,11},{10,... | collective-permute-start | bytes 393224 | tf_op jit(solution)/shard_map/ppermute | solution.py:36
  123.8 5.0 %collective-permute-start.24 = (bf16[64,1024]{1,0:T(8,128)(2,1)S(1)}, bf16[64,1024]{1,0:T(8,128)(2,1)S(1)}, u32[]{:S(2)}, u32[]{:S(2)}) collective-permute-start(bf16[64,1024]{1,0:T(8,128)(2,1)S(1)} %get-tuple-element.130), channel_id=1, source_target_pairs={{0,3},{1,0},{2,1},{3,2},{4,7},{5,4},{6,5},{7,6},{8,11},{9,8},{10,9... | collective-permute-start | bytes 393224 | tf_op jit(solution)/shard_map/ppermute | solution.py:36
  132.5 2.0 %collective-permute-start.30 = (bf16[256,1024]{1,0:T(8,128)(2,1)S(1)}, bf16[256,1024]{1,0:T(8,128)(2,1)S(1)}, u32[]{:S(2)}, u32[]{:S(2)}) collective-permute-start(bf16[256,1024]{1,0:T(8,128)(2,1)S(1)} %get-tuple-element.142), channel_id=1, source_target_pairs={{0,32},{32,0},{64,96},{96,64},{1,33},{33,1},{65,97},{97,65},{2,34}... | collective-permute-start | bytes 1572872 | tf_op jit(solution)/shard_map/ppermute | solution.py:32
  132.6 15.7 %collective-permute-start.35 = (bf16[3,2,32,1024]{3,2,1,0:T(8,128)(2,1)S(1)}, bf16[3,2,32,1024]{3,2,1,0:T(8,128)(2,1)S(1)}, u32[]{:S(2)}, u32[]{:S(2)}) collective-permute-start(bf16[3,2,32,1024]{3,2,1,0:T(8,128)(2,1)S(1)} %get-tuple-element.160.refs_10_), channel_id=1, source_target_pairs={{0,4},{4,0},{8,12},{12,8},{16,20},{20,16},{24,28},{28,24},{1,5},{5... | collective-permute-start | bytes 1179656 | tf_op jit(solution)/shard_map/ppermute | solution.py:27
  135.1 9.6 %collective-permute-start.31 = (bf16[64,1024]{1,0:T(8,128)(2,1)S(1)}, bf16[64,1024]{1,0:T(8,128)(2,1)S(1)}, u32[]{:S(2)}, u32[]{:S(2)}) collective-permute-start(bf16[64,1024]{1,0:T(8,128)(2,1)S(1)} %get-tuple-element.145), channel_id=1, source_target_pairs={{0,1},{1,2},{2,3},{3,0},{4,5},{5,6},{6,7},{7,4},{8,9},{9,10},{10,1... | collective-permute-start | bytes 393224 | tf_op jit(solution)/shard_map/ppermute | solution.py:36
  136.2 9.3 %collective-permute-start.32 = (bf16[64,1024]{1,0:T(8,128)(2,1)S(1)}, bf16[64,1024]{1,0:T(8,128)(2,1)S(1)}, u32[]{:S(2)}, u32[]{:S(2)}) collective-permute-start(bf16[64,1024]{1,0:T(8,128)(2,1)S(1)} %get-tuple-element.146), channel_id=1, source_target_pairs={{0,2},{1,3},{2,0},{3,1},{4,6},{5,7},{6,4},{7,5},{8,10},{9,11},{10,... | collective-permute-start | bytes 393224 | tf_op jit(solution)/shard_map/ppermute | solution.py:36
  139.2 6.3 %collective-permute-start.33 = (bf16[64,1024]{1,0:T(8,128)(2,1)S(1)}, bf16[64,1024]{1,0:T(8,128)(2,1)S(1)}, u32[]{:S(2)}, u32[]{:S(2)}) collective-permute-start(bf16[64,1024]{1,0:T(8,128)(2,1)S(1)} %get-tuple-element.147), channel_id=1, source_target_pairs={{0,3},{1,0},{2,1},{3,2},{4,7},{5,4},{6,5},{7,6},{8,11},{9,8},{10,9... | collective-permute-start | bytes 393224 | tf_op jit(solution)/shard_map/ppermute | solution.py:36
  145.6 8.0 %collective-permute-start.34 = (bf16[64,1024]{1,0:T(8,128)(2,1)S(1)}, bf16[64,1024]{1,0:T(8,128)(2,1)S(1)}, u32[]{:S(2)}, u32[]{:S(2)}) collective-permute-start(bf16[64,1024]{1,0:T(8,128)(2,1)S(1)} %owned.3), channel_id=1, source_target_pairs={{0,64},{32,96},{64,0},{96,32},{1,65},{33,97},{65,1},{97,33},{2,66}... | collective-permute-start | bytes 393224 | tf_op jit(solution)/shard_map/ppermute | solution.py:32

commit v5 on v4

--- a/solution.py
+++ b/solution.py
@@ -123,6 +123,67 @@
     )(idx, m, wg, wu, wd)
 
 
+def own_forward_kernel(idx, m, wg, wu, wd, plus, minus, keep, own, hg, hu, acc, sems):
+    z, lo = idx[0], idx[1]
+    piece = 256
+    order = [(k, i) for i in range(wg.shape[0] // piece) for k in range(2)]
+    places = (wg, hg), (wu, hu)
+    copies = []
+    for n, (k, i) in enumerate(order):
+        src, dst = places[k]
+        at = pl.ds(i * piece, piece)
+        copies.append(pltpu.make_async_copy(src.at[at], dst.at[at], sems.at[n]))
+    ahead = 4
+    for copy in copies[:ahead]:
+        copy.start()
+    acc[2] = lax.dot_general(m[1], wd[...], NT, preferred_element_type=F32)
+    for n, (k, i) in enumerate(order):
+        copies[n].wait()
+        if n + ahead < len(copies):
+            copies[n + ahead].start()
+        at = slice(i * piece, (i + 1) * piece)
+        part = jnp.dot(m[0, :, at], places[k][1][at, :], preferred_element_type=F32)
+        acc[k] = acc[k] + part if i else part
+
+    def block(r, s):
+        return acc[:, pl.ds(row_start(z, lo, r, s), 32), :]
+
+    plus[0] = block(2, 0).astype(BF)
+    plus[1] = block(1, 1).astype(BF)
+    minus[0] = block(2, 1).astype(BF)
+    minus[1] = block(3, 0).astype(BF)
+    keep[0] = block(1, 0)
+    keep[1] = block(3, 1)
+    own[0] = block(0, 0)
+    own[1] = block(0, 1)
+
+
+def own_forward(idx, m, wg, wu, wd):
+    _, tokens, depth = m.shape
+    width = wg.shape[1]
+    shape = (2, 3, 32, width)
+    return pl.pallas_call(
+        own_forward_kernel,
+        in_specs=[SMEM, VMEM] + [pl.BlockSpec(memory_space=pl.ANY)] * 2 + [VMEM],
+        out_specs=[VMEM] * 4,
+        out_shape=[
+            jax.ShapeDtypeStruct(shape, BF),
+            jax.ShapeDtypeStruct(shape, BF),
+            jax.ShapeDtypeStruct(shape, F32),
+            jax.ShapeDtypeStruct(shape, F32),
+        ],
+        scratch_shapes=[
+            pltpu.VMEM(wg.shape, BF),
+            pltpu.VMEM(wu.shape, BF),
+            pltpu.VMEM((3, tokens, width), F32),
+            pltpu.SemaphoreType.DMA((8,)),
+        ],
+        compiler_params=params(50 * 2**20),
+        cost_estimate=cost(6 * tokens * depth * width, 11 * 2**20),
+        name="own_forward",
+    )(idx, m, wg, wu, wd)
+
+
 def pass_on_kernel(*refs):
     plus, minus = refs[6:]
     for t in range(2):
@@ -166,23 +227,194 @@
     )(owns[0], *nears[:2], owns[1], *nears[2:], last_minus, last_plus)
 
 
+def cross_forward_kernel(idx, m, wg, wu, wd, plus, minus, keep, own, cross, stay, acc):
+    z, lo = idx[0], idx[1]
+    tile = acc.shape[2]
+
+    @pl.loop(0, wg.shape[1] // tile)
+    def _(i):
+        at = pl.ds(pl.multiple_of(i * tile, tile), tile)
+        acc[0] = jnp.dot(m[0], wg[:, at], preferred_element_type=F32)
+        acc[1] = jnp.dot(m[0], wu[:, at], preferred_element_type=F32)
+        acc[2] = lax.dot_general(m[1], wd[at, :], NT, preferred_element_type=F32)
+
+        def block(r, s):
+            return acc[:2, pl.ds(row_start(z, lo, r, s), 32), :]
+
+        plus[0, :, :, at] = block(2, 0).astype(BF)
+        plus[1, :, :, at] = block(1, 1).astype(BF)
+        minus[0, :, :, at] = block(2, 1).astype(BF)
+        minus[1, :, :, at] = block(3, 0).astype(BF)
+        keep[0, :, :, at] = block(1, 0)
+        keep[1, :, :, at] = block(3, 1)
+        own[0, :, :, at] = block(0, 0)
+        own[1, :, :, at] = block(0, 1)
+        for r in range(4):
+            stay[r, :, at] = acc[2, pl.ds(row_start(z, lo, r, 0), 32), :]
+            cross[r, :, at] = acc[2, pl.ds(row_start(z, lo, r, 1), 32), :].astype(BF)
+
+
+def cross_forward(idx, m, wg, wu, wd):
+    _, tokens, depth = m.shape
+    width = wg.shape[1]
+    tile = 256
+    shape = (2, 2, 32, width)
+    return pl.pallas_call(
+        cross_forward_kernel,
+        in_specs=[SMEM] + [VMEM] * 4,
+        out_specs=[VMEM] * 6,
+        out_shape=[
+            jax.ShapeDtypeStruct(shape, BF),
+            jax.ShapeDtypeStruct(shape, BF),
+            jax.ShapeDtypeStruct(shape, F32),
+            jax.ShapeDtypeStruct(shape, F32),
+            jax.ShapeDtypeStruct((4, 32, width), BF),
+            jax.ShapeDtypeStruct((4, 32, width), F32),
+        ],
+        scratch_shapes=[pltpu.VMEM((3, tokens, tile), F32)],
+        compiler_params=params(),
+        cost_estimate=cost(6 * tokens * depth * width, 5 * 2**20),
+        name="cross_forward",
+    )(idx, m, wg, wu, wd)
+
+
+def cross_sum_kernel(stay0, got0, stay1, got1, plus, minus, keep, own):
+    def total(t, r):
+        stay, got = (stay0, got0) if t == 0 else (stay1, got1)
+        return stay[r] + got[r].astype(F32)
+
+    plus[0] = total(0, 2).astype(BF)
+    plus[1] = total(1, 1).astype(BF)
+    minus[0] = total(1, 2).astype(BF)
+    minus[1] = total(0, 3).astype(BF)
+    keep[0] = total(0, 1)
+    keep[1] = total(1, 3)
+    own[0] = total(0, 0)
+    own[1] = total(1, 0)
+
+
+def cross_sum(stay0, got0, stay1, got1):
+    shape = (2, *stay0.shape[1:])
+    return pl.pallas_call(
+        cross_sum_kernel,
+        in_specs=[VMEM] * 4,
+        out_specs=[VMEM] * 4,
+        out_shape=[
+            jax.ShapeDtypeStruct(shape, BF),
+            jax.ShapeDtypeStruct(shape, BF),
+            jax.ShapeDtypeStruct(shape, F32),
+            jax.ShapeDtypeStruct(shape, F32),
+        ],
+        compiler_params=params(),
+        cost_estimate=cost(stay0.size * 2, stay0.size * 18),
+        name="cross_sum",
+    )(stay0, got0, stay1, got1)
+
+
+def cross_pass_on_kernel(*refs):
+    (keep, from_minus, from_plus), (plus, minus) = refs[6:9], refs[9:]
+    plus[4] = (keep[0] + from_minus[0].astype(F32)).astype(BF)
+    minus[4] = (keep[1] + from_plus[0].astype(F32)).astype(BF)
+    for t in range(2):
+        keep, from_minus, from_plus = refs[3 * t : 3 * t + 3]
+        for i in range(2):
+            plus[2 * i + t] = (keep[0, i] + from_minus[0, i].astype(F32)).astype(BF)
+            minus[2 * i + t] = (keep[1, i] + from_plus[0, i].astype(F32)).astype(BF)
+
+
+def cross_pass_on(keeps, nears):
+    _, _, rows, width = keeps[0].shape
+    shape = jax.ShapeDtypeStruct((5, rows, width), BF)
+    size = 10 * rows * width
+    return pl.pallas_call(
+        cross_pass_on_kernel,
+        in_specs=[VMEM] * 9,
+        out_specs=[VMEM] * 2,
+        out_shape=[shape, shape],
+        compiler_params=params(),
+        cost_estimate=cost(size, size * 8),
+        name="cross_pass_on",
+    )(keeps[0], *nears[:2], keeps[1], *nears[2:4], keeps[2], *nears[4:])
+
+
+def cross_ring_sum_kernel(*refs):
+    (own_g, minus_g, plus_g), (last_minus, last_plus, held, held_g, sent) = refs[6:9], refs[9:]
+    for t in range(2):
+        own, from_minus, from_plus = refs[3 * t : 3 * t + 3]
+        for i in range(2):
+            k = 2 * i + t
+            held[k] = own[0, i] + from_plus[1, i].astype(F32) + last_minus[k].astype(F32)
+            held[4 + k] = own[1, i] + from_minus[1, i].astype(F32) + last_plus[k].astype(F32)
+    held_g[0] = own_g[0] + plus_g[1].astype(F32) + last_minus[4].astype(F32)
+    held_g[1] = own_g[1] + minus_g[1].astype(F32) + last_plus[4].astype(F32)
+    sent[:8] = held[...].astype(BF)
+    sent[8:] = held_g[...].astype(BF)
+
+
+def cross_ring_sum(owns, nears, last_minus, last_plus):
+    _, _, rows, width = owns[0].shape
+    size = 10 * rows * width
+    return pl.pallas_call(
+        cross_ring_sum_kernel,
+        in_specs=[VMEM] * 11,
+        out_specs=[VMEM] * 3,
+        out_shape=[
+            jax.ShapeDtypeStruct((8, rows, width), F32),
+            jax.ShapeDtypeStruct((2, rows, width), F32),
+            jax.ShapeDtypeStruct((10, rows, width), BF),
+        ],
+        compiler_params=params(),
+        cost_estimate=cost(size * 4, size * 14),
+        name="cross_ring_sum",
+    )(owns[0], *nears[:2], owns[1], *nears[2:4], owns[2], *nears[4:], last_minus, last_plus)
+
+
+def cross_gate_kernel(held, held_g, across, out, other):
+    for half in range(2):
+        mine, theirs = 4 * half, 4 * (1 - half)
+        pre_gate = held[mine : mine + 2] + across[theirs : theirs + 2].astype(F32)
+        pre_up = held[mine + 2 : mine + 4] + across[theirs + 2 : theirs + 4].astype(F32)
+        grad_hidden = across[8:].astype(F32) if half else held_g[...]
+        put_gate(half, pre_gate, pre_up, grad_hidden, out, other)
+
+
+def cross_gate(held, held_g, across):
+    _, rows, width = held.shape
+    return pl.pallas_call(
+        cross_gate_kernel,
+        in_specs=[VMEM] * 3,
+        out_specs=[VMEM] * 2,
+        out_shape=[
+            jax.ShapeDtypeStruct((10, rows, width), BF),
+            jax.ShapeDtypeStruct((2, rows, width), BF),
+        ],
+        compiler_params=params(),
+        cost_estimate=cost(held.size * 8, held.size * 8),
+        name="cross_gate",
+    )(held, held_g, across)
+
+
+def put_gate(half, pre_gate, pre_up, grad_hidden, out, other):
+    s = jax.nn.sigmoid(pre_gate)
+    activated = pre_gate * s
+    first = 6 * half
+    out[first : first + 2] = (
+        grad_hidden * pre_up * s * (1.0 + pre_gate * (1.0 - s))
+    ).astype(BF)
+    out[first + 2 : first + 4] = (grad_hidden * activated).astype(BF)
+    hidden = (activated * pre_up).astype(BF)
+    if half:
+        other[...] = hidden
+    else:
+        out[4:6] = hidden
+
+
 def gate_kernel(held, across, out, other):
     for half in range(2):
         pre_gate, pre_up, grad_hidden = (
             held[half, i] + across[1 - half, i].astype(F32) for i in range(3)
         )
-        s = jax.nn.sigmoid(pre_gate)
-        activated = pre_gate * s
-        first = 6 * half
-        out[first : first + 2] = (
-            grad_hidden * pre_up * s * (1.0 + pre_gate * (1.0 - s))
-        ).astype(BF)
-        out[first + 2 : first + 4] = (grad_hidden * activated).astype(BF)
-        hidden = (activated * pre_up).astype(BF)
-        if half:
-            other[...] = hidden
-        else:
-            out[4:6] = hidden
+        put_gate(half, pre_gate, pre_up, grad_hidden, out, other)
 
 
 def gate(held, across):
@@ -201,10 +433,9 @@
     )(held, across)
 
 
-def input_grad_kernel(idx, here, plus1, far_a, far_b, minus1, wg, wu, mine, theirs, acts, hidden, acc):
+def their_grad_kernel(idx, here, plus1, far_a, far_b, minus1, wg, wu, theirs, acts, hidden):
     z, lo = idx[0], idx[1]
     tokens = acts.shape[1] // 2
-    tile = acc.shape[1]
     for r, s, block in (
         (0, 0, here.at[:4]),
         (0, 1, here.at[6:]),
@@ -224,34 +455,58 @@
     hidden[1, 1] = far_b[0]
     hidden[2] = minus1[4:6]
 
+    rows_grad(acts, tokens, wg, wu, theirs)
+
+
+def rows_grad(acts, first, wg, wu, out):
+    rows, tile = out.shape[0], 256
+
     @pl.loop(0, wg.shape[0] // tile)
     def _(i):
         at = pl.ds(pl.multiple_of(i * tile, tile), tile)
-        acc[...] = lax.dot_general(acts[0], wg[at, :], NT, preferred_element_type=F32)
-        acc[...] += lax.dot_general(acts[1], wu[at, :], NT, preferred_element_type=F32)
-        mine[:, at] = acc[:tokens]
-        theirs[:, at] = acc[tokens:].astype(BF)
-
-
-def input_grad(idx, here, plus1, far_a, far_b, minus1, wg, wu):
+        total = lax.dot_general(
+            acts[0, first : first + rows], wg[at, :], NT, preferred_element_type=F32
+        )
+        total += lax.dot_general(
+            acts[1, first : first + rows], wu[at, :], NT, preferred_element_type=F32
+        )
+        out[:, at] = total.astype(out.dtype)
+
+
+def their_grad(idx, here, plus1, far_a, far_b, minus1, wg, wu):
     depth, width = wg.shape
     tokens = 256
-    tile = 256
-    return pl.pallas_call(
-        input_grad_kernel,
+    return pl.pallas_call(
+        their_grad_kernel,
         in_specs=[SMEM] + [VMEM] * 7,
-        out_specs=[VMEM] * 4,
+        out_specs=[VMEM] * 3,
         out_shape=[
-            jax.ShapeDtypeStruct((tokens, depth), F32),
             jax.ShapeDtypeStruct((tokens, depth), BF),
             jax.ShapeDtypeStruct((2, 2 * tokens, width), BF),
             jax.ShapeDtypeStruct((3, 2, 32, width), BF),
         ],
-        scratch_shapes=[pltpu.VMEM((2 * tokens, tile), F32)],
-        compiler_params=params(),
-        cost_estimate=cost(8 * tokens * depth * width, 10 * 2**20),
-        name="input_grad",
+        compiler_params=params(),
+        cost_estimate=cost(4 * tokens * depth * width, 10 * 2**20),
+        name="their_grad",
     )(idx, here, plus1, far_a, far_b, minus1, wg, wu)
+
+
+def my_grad_kernel(acts, wg, wu, mine):
+    rows_grad(acts, 0, wg, wu, mine)
+
+
+def my_grad(acts, wg, wu):
+    depth, width = wg.shape
+    tokens = acts.shape[1] // 2
+    return pl.pallas_call(
+        my_grad_kernel,
+        in_specs=[VMEM] * 3,
+        out_specs=VMEM,
+        out_shape=jax.ShapeDtypeStruct((tokens, depth), F32),
+        compiler_params=params(),
+        cost_estimate=cost(4 * tokens * depth * width, 10 * 2**20),
+        name="my_grad",
+    )(acts, wg, wu)
 
 
 def split_kernel(idx, mine, across, *outs):
@@ -412,9 +667,9 @@
         return fin_perm(plus, 1, 0), fin_perm(minus, 3, 0)
 
     def over_y(own, to1, to2, to3):
-        return own, y_perm(to1, 1), y_perm(to2, 2), y_perm(to3, 3)
-
-    *out, keep_a, own_a = forward(idx, m0, *weights)
+        return own, y_perm(to2, 2), y_perm(to1, 1), y_perm(to3, 3)
+
+    *out, keep_a, own_a = own_forward(idx, m0, *weights)
     near_a = ring(*out)
     (m1,) = after((m1,), *out)
     *out, keep_b, own_b = forward(idx, m1, *weights)
@@ -425,21 +680,27 @@
 
     (m2,) = after((m2,), *step0)
     m3 = tok_perm(m2, 0, 1)
-    *out, keep_a, own_a = forward(idx, m2, *weights)
+    *out, keep_a, own_a, cross, stay_a = cross_forward(idx, m2, *weights)
     near_a = ring(*out)
+    got_a = fin_perm(cross, 0, 1)
+    (m3,) = after((m3,), *out)
+    *out, keep_b, own_b, cross, stay_b = cross_forward(idx, m3, *weights)
+    near_b = ring(*out)
+    got_b = fin_perm(cross, 0, 1)
     last0 = after(last0, *out)
     held0, sent0 = ring_sum(owns0, near0, *last0)
     across0 = fin_perm(sent0, 0, 1)
-    (m3,) = after((m3,), sent0)
-    *out, keep_b, own_b = forward(idx, m3, *weights)
-    near1 = *near_a, *ring(*out)
-    step1 = pass_on((keep_a, keep_b), near1)
+    got_a, got_b = after((got_a, got_b), sent0)
+    *out, keep_c, own_c = cross_sum(stay_a, got_a, stay_b, got_b)
+    near1 = *after((*near_a, *near_b), *out), *ring(*out)
+    owns1 = own_a, own_b, own_c
+    step1 = cross_pass_on((keep_a, keep_b, keep_c), near1)
     last1 = ring(*step1)
 
     (across0,) = after((across0,), *step1)
     here0, other0 = gate(held0, across0)
     last1 = after(last1, here0)
-    held1, sent1 = ring_sum((own_a, own_b), near1, *last1)
+    held1, held_g, sent1 = cross_ring_sum(owns1, near1, *last1)
     across1 = fin_perm(sent1, 0, 1)
 
     (ready,) = after((here0,), sent1)
@@ -447,11 +708,12 @@
     on_plus, on_minus = minus1[:5], plus1[5:]
     far0 = ring(on_plus, on_minus)
     (across1,) = after((across1,), on_plus, on_minus)
-    here1, other1 = gate(held1, across1)
+    here1, other1 = cross_gate(held1, held_g, across1)
     side1 = ring(here1, here1)
 
     far0 = after(far0, here1)
-    mine0, theirs0, act0, near = input_grad(idx, here0, plus1, *far0, minus1, *weights[:2])
+    theirs0, act0, near = their_grad(idx, here0, plus1, *far0, minus1, *weights[:2])
+    mine0 = my_grad(act0, *weights[:2])
     core0 = tok_perm(theirs0, 0, 1)
     blocks0 = here0, other0, near, fin_perm(near, 0, 1)
     gate_part, up_part = part_grads(m0, m1, act0)
@@ -462,7 +724,8 @@
     far1 = ring(side1[0][:5], side1[1][5:])
 
     far1 = after(far1, *sums0[1:], blocks0[3])
-    mine1, theirs1, act1, near = input_grad(idx, here1, side1[1], *far1, side1[0], *weights[:2])
+    theirs1, act1, near = their_grad(idx, here1, side1[1], *far1, side1[0], *weights[:2])
+    mine1 = my_grad(act1, *weights[:2])
     core1 = tok_perm(theirs1, 0, 1)
     blocks1 = here1, other1, near, fin_perm(near, 0, 1)
     total0 = owned(*after(sums0, act1), F32)

time: 155 us -> 152 us (0.981)
  waiting for transfers between devices: 53.9 us -> 46.9 us
  starting transfers between devices: 53.8 us -> 59.8 us
  local copies, waits for them, and re-layouts: 4.52 us -> 1.33 us
  Pallas kernels: 40.4 us -> 42 us
    pallas_call x2 -> x11, Pallas kernels: 7.43 us -> 22.1 us  [the longest x2 6.32 us: cross_forward(): pl.pallas_call(cross_forward_kernel, in_specs=[SMEM] + [VMEM] * 4, out_sp...]
    pallas_call x4 -> x1, Pallas kernels: 13.4 us -> 3.17 us  [forward(): pl.pallas_call(forward_kernel, in_specs=[SMEM] + [VMEM] * 4, out_specs=[V...]
    ppermute x24 -> x28, waiting for transfers between devices: 49.2 us -> 42.4 us  [fin_perm(): return lax.ppermute(x, 'fin', pairs)]
    ppermute x24 -> x28, starting transfers between devices: 36.8 us -> 43.1 us  [fin_perm(): return lax.ppermute(x, 'fin', pairs)]
    unnamed x14 -> x8, local copies, waits for them, and re-layouts: 4.43 us -> 1.24 us
  transfers between devices with their start and end apart: 36 -> 40, of which waited for: 17 -> 16; matrix products, arithmetic and copies ran while one was open for 0% -> 0% of each run, Pallas kernels for 22% -> 24%
where the time goes in v5:
time: 152 us
  starting transfers between devices  59.8 us (39%)
  waiting for transfers between devices  46.9 us (31%)
  Pallas kernels  42 us (28%)
    ppermute x28, starting transfers between devices, fin_perm(): return lax.ppermute(x, 'fin', pairs)  43.1 us
    ppermute x28, waiting for transfers between devices, fin_perm(): return lax.ppermute(x, 'fin', pairs)  42.4 us
    ppermute x6, starting transfers between devices, y_perm(): return lax.ppermute(x, 'fout', [(y, (y + dy) % 4) for y in range(4)])  11.4 us
    pallas_call x2, Pallas kernels, cross_forward(): pl.pallas_call(cross_forward_kernel, in_specs=[SMEM] + [VMEM] * 4, out_sp...  6.32 us
    pallas_call x1, Pallas kernels, own_forward(): pl.pallas_call(own_forward_kernel, in_specs=[SMEM, VMEM] + [pl.BlockSpec(...  5.92 us
    ppermute x6, starting transfers between devices, tok_perm(): return lax.ppermute(x, 'tok', pairs)  5.24 us
    pallas_call x2, Pallas kernels, their_grad(): pl.pallas_call(their_grad_kernel, in_specs=[SMEM] + [VMEM] * 7, out_specs...  5.24 us
    pallas_call x1, Pallas kernels, down_grad(): pl.pallas_call(down_grad_kernel, grid=(width // tile,), in_specs=[SMEM] +...  4.63 us
  transfers between devices with their start and end apart: 40, of which 16 were waited for; matrix products, arithmetic and copies ran while one was open for 0% of the time, Pallas kernels for 24%

profile of v5, /device:TPU:0, one launch (start us, length us, event | category | flops | bytes accessed | tf_op | source)
XLA Modules:
  0.0 151.8 jit_solution(6586296185851365075)
XLA Ops:
  0.6 2.2 %scaled.1.m.m0.refs_0_ = bf16[2,256,1024]{2,1,0:T(8,128)(2,1)} custom-call(f32[16]{0:T(128)} %margin.1, bf16[256,1024]{1,0:T(8,128)(2,1)} %x.1, bf16[256,1024]{1,0:T(8,128)(2,1)} %up.1, s32[1,256]{1,0:T(1,128)} %bitcast.5, s32[1,256]{1,0:T(1,128)} %bitcast.6), custom_call_target="tpu_custom_call" | custom-call | flops 1048576 | bytes 2097152 | tf_op jit(solution)/shard_map/scaled/pallas_call | solution.py:68
  2.8 3.1 %collective-permute-start.7 = (bf16[2,256,1024]{2,1,0:T(8,128)(2,1)}, bf16[2,256,1024]{2,1,0:T(8,128)(2,1)S(1)}, u32[]{:S(2)}, u32[]{:S(2)}) collective-permute-start(bf16[2,256,1024]{2,1,0:T(8,128)(2,1)} %scaled.1.m.m0.refs_0_), channel_id=1, source_target_pairs={{0,64},{32,96},{64,0},{96,32},{1,65},{33,97},{65,1},{97,33},{2,66}... | collective-permute-start | bytes 3145736 | tf_op jit(solution)/shard_map/ppermute | solution.py:32
  6.0 1.2 copy-done.3
  7.3 5.9 %own_forward.1 = (bf16[2,3,32,1024]{3,2,1,0:T(8,128)(2,1)S(1)}, bf16[2,3,32,1024]{3,2,1,0:T(8,128)(2,1)S(1)}, f32[2,3,32,1024]{3,2,1,0:T(8,128)S(1)}, f32[2,3,32,1024]{3,2,1,0:T(8,128)S(1)}) custom-call(s32[3]{0:T(128)S(1)} %pad_add_fusion.idx, bf16[2,256,1024]{2,1,0:T(8,128)(2,1)S(1)} %copy-done.3, bf16[1024,1024]{1,0:T(8,128)(2,1)} %wg.15, ...), custom_call_target="tpu_custom_call" | custom-call | flops 1610612736 | bytes 11534336 | tf_op jit(solution)/shard_map/own_forward/pallas_call | solution.py:165
  13.2 2.0 %collective-permute-start = (bf16[2,3,32,1024]{3,2,1,0:T(8,128)(2,1)S(1)}, bf16[2,3,32,1024]{3,2,1,0:T(8,128)(2,1)S(1)}, u32[]{:S(2)}, u32[]{:S(2)}) collective-permute-start(bf16[2,3,32,1024]{3,2,1,0:T(8,128)(2,1)S(1)} %get-tuple-element.98), channel_id=1, source_target_pairs={{0,8},{4,12},{8,16},{12,20},{16,24},{20,28},{24,0},{28,4},{1,9},{5... | collective-permute-start | bytes 1179656 | tf_op jit(solution)/shard_map/ppermute | solution.py:27
  15.2 2.2 %collective-permute-start.1 = (bf16[2,3,32,1024]{3,2,1,0:T(8,128)(2,1)S(1)}, bf16[2,3,32,1024]{3,2,1,0:T(8,128)(2,1)S(1)}, u32[]{:S(2)}, u32[]{:S(2)}) collective-permute-start(bf16[2,3,32,1024]{3,2,1,0:T(8,128)(2,1)S(1)} %get-tuple-element.99), channel_id=1, source_target_pairs={{0,24},{4,28},{8,0},{12,4},{16,8},{20,12},{24,16},{28,20},{1,25},{... | collective-permute-start | bytes 1179656 | tf_op jit(solution)/shard_map/ppermute | solution.py:27
  17.4 3.2 %forward.1 = (bf16[2,3,32,1024]{3,2,1,0:T(8,128)(2,1)S(1)}, bf16[2,3,32,1024]{3,2,1,0:T(8,128)(2,1)S(1)}, f32[2,3,32,1024]{3,2,1,0:T(8,128)S(1)}, f32[2,3,32,1024]{3,2,1,0:T(8,128)S(1)}) custom-call(s32[3]{0:T(128)S(1)} %pad_add_fusion.idx, bf16[2,256,1024]{2,1,0:T(8,128)(2,1)S(1)} %collective-permute-done.2.m.m1.refs_1_, bf16[1024,1024]{1,0:T(8,128)(2,1)S(1)} %copy-done, ...), custom_call_target="tpu_custom_call" | custom-call | flops 1610612736 | bytes 5242880 | tf_op jit(solution)/shard_map/forward/pallas_call | solution.py:109
  20.7 3.2 %collective-permute-start.4 = (bf16[2,3,32,1024]{3,2,1,0:T(8,128)(2,1)S(1)}, bf16[2,3,32,1024]{3,2,1,0:T(8,128)(2,1)S(1)}, u32[]{:S(2)}, u32[]{:S(2)}) collective-permute-start(bf16[2,3,32,1024]{3,2,1,0:T(8,128)(2,1)S(1)} %get-tuple-element.103), channel_id=1, source_target_pairs={{0,24},{4,28},{8,0},{12,4},{16,8},{20,12},{24,16},{28,20},{1,25},{... | collective-permute-start | bytes 1179656 | tf_op jit(solution)/shard_map/ppermute | solution.py:27
  23.9 3.3 %collective-permute-done.refs_1_ = bf16[2,3,32,1024]{3,2,1,0:T(8,128)(2,1)S(1)} collective-permute-done((bf16[2,3,32,1024]{3,2,1,0:T(8,128)(2,1)S(1)}, bf16[2,3,32,1024]{3,2,1,0:T(8,128)(2,1)S(1)}, u32[]{:S(2)}, u32[]{:S(2)}) %collective-permute-start) | collective-permute-done | bytes 393248 | tf_op jit(solution)/shard_map/ppermute | solution.py:27
  27.2 8.0 %collective-permute-done.3.refs_4_ = bf16[2,3,32,1024]{3,2,1,0:T(8,128)(2,1)S(1)} collective-permute-done((bf16[2,3,32,1024]{3,2,1,0:T(8,128)(2,1)S(1)}, bf16[2,3,32,1024]{3,2,1,0:T(8,128)(2,1)S(1)}, u32[]{:S(2)}, u32[]{:S(2)}) %collective-permute-start.3) | collective-permute-done | bytes 393248 | tf_op jit(solution)/shard_map/ppermute | solution.py:27
  35.5 1.3 collective-permute-start.5
  36.8 2.0 %collective-permute-start.6 = (bf16[3,2,32,1024]{3,2,1,0:T(8,128)(2,1)S(1)}, bf16[3,2,32,1024]{3,2,1,0:T(8,128)(2,1)S(1)}, u32[]{:S(2)}, u32[]{:S(2)}) collective-permute-start(bf16[3,2,32,1024]{3,2,1,0:T(8,128)(2,1)S(1)} %get-tuple-element.107), channel_id=1, source_target_pairs={{0,24},{4,28},{8,0},{12,4},{16,8},{20,12},{24,16},{28,20},{1,25},{... | collective-permute-start | bytes 1179656 | tf_op jit(solution)/shard_map/ppermute | solution.py:27
  38.8 3.2 %cross_forward.2 = (bf16[2,2,32,1024]{3,2,1,0:T(8,128)(2,1)S(1)}, bf16[2,2,32,1024]{3,2,1,0:T(8,128)(2,1)S(1)}, f32[2,2,32,1024]{3,2,1,0:T(8,128)S(1)}, f32[2,2,...) custom-call(s32[3]{0:T(128)S(1)} %pad_add_fusion.idx, ...), custom_call_target="tpu_custom_call" | custom-call | flops 1610612736 | bytes 5242880 | tf_op jit(solution)/shard_map/cross_forward/pallas_call | solution.py:262
  42.6 3.2 %cross_forward.3 = (bf16[2,2,32,1024]{3,2,1,0:T(8,128)(2,1)S(1)}, bf16[2,2,32,1024]{3,2,1,0:T(8,128)(2,1)S(1)}, f32[2,2,32,1024]{3,2,1,0:T(8,128)S(1)}, f32[2,2,...) custom-call(s32[3]{0:T(128)S(1)} %pad_add_fusion.idx, ...), custom_call_target="tpu_custom_call" | custom-call | flops 1610612736 | bytes 5242880 | tf_op jit(solution)/shard_map/cross_forward/pallas_call | solution.py:262
  45.8 1.5 collective-permute-start.15
  49.3 1.3 collective-permute-start.10
  50.7 1.9 %collective-permute-start.11 = (bf16[2,2,32,1024]{3,2,1,0:T(8,128)(2,1)S(1)}, bf16[2,2,32,1024]{3,2,1,0:T(8,128)(2,1)S(1)}, u32[]{:S(2)}, u32[]{:S(2)}) collective-permute-start(bf16[2,2,32,1024]{3,2,1,0:T(8,128)(2,1)S(1)} %get-tuple-element.110), channel_id=1, source_target_pairs={{0,24},{4,28},{8,0},{12,4},{16,8},{20,12},{24,16},{28,20},{1,25},{... | collective-permute-start | bytes 786440 | tf_op jit(solution)/shard_map/ppermute | solution.py:27
  52.7 4.1 %collective-permute-done.15.got1 = bf16[4,32,1024]{2,1,0:T(8,128)(2,1)S(1)} collective-permute-done((bf16[4,32,1024]{2,1,0:T(8,128)(2,1)S(1)}, bf16[4,32,1024]{2,1,0:T(8,128)(2,1)S(1)}, u32[]{:S(2)}, u32[]{:S(2)}) %collective-permute-start.15) | collective-permute-done | bytes 262176 | tf_op jit(solution)/shard_map/ppermute | solution.py:27
  56.8 1.8 %collective-permute-start.13 = (bf16[2,2,32,1024]{3,2,1,0:T(8,128)(2,1)S(1)}, bf16[2,2,32,1024]{3,2,1,0:T(8,128)(2,1)S(1)}, u32[]{:S(2)}, u32[]{:S(2)}) collective-permute-start(bf16[2,2,32,1024]{3,2,1,0:T(8,128)(2,1)S(1)} %get-tuple-element.113), channel_id=1, source_target_pairs={{0,24},{4,28},{8,0},{12,4},{16,8},{20,12},{24,16},{28,20},{1,25},{... | collective-permute-start | bytes 786440 | tf_op jit(solution)/shard_map/ppermute | solution.py:27
  59.9 3.1 %collective-permute-start.17 = (bf16[2,32,1024]{2,1,0:T(8,128)(2,1)S(1)}, bf16[2,32,1024]{2,1,0:T(8,128)(2,1)S(1)}, u32[]{:S(2)}, u32[]{:S(2)}) collective-permute-start(bf16[2,32,1024]{2,1,0:T(8,128)(2,1)S(1)} %get-tuple-element.126), channel_id=1, source_target_pairs={{0,24},{4,28},{8,0},{12,4},{16,8},{20,12},{24,16},{28,20},{1,25},{... | collective-permute-start | bytes 393224 | tf_op jit(solution)/shard_map/ppermute | solution.py:27
  63.0 2.2 %collective-permute-done.12.refs_4_ = bf16[2,2,32,1024]{3,2,1,0:T(8,128)(2,1)S(1)} collective-permute-done((bf16[2,2,32,1024]{3,2,1,0:T(8,128)(2,1)S(1)}, bf16[2,2,32,1024]{3,2,1,0:T(8,128)(2,1)S(1)}, u32[]{:S(2)}, u32[]{:S(2)}) %collective-permute-start.12) | collective-permute-done | bytes 262176 | tf_op jit(solution)/shard_map/ppermute | solution.py:27
  65.2 1.4 collective-permute-done.16.refs_7_
  66.8 1.1 collective-permute-start.18
  67.8 2.2 %collective-permute-start.19 = (bf16[5,32,1024]{2,1,0:T(8,128)(2,1)S(1)}, bf16[5,32,1024]{2,1,0:T(8,128)(2,1)S(1)}, u32[]{:S(2)}, u32[]{:S(2)}) collective-permute-start(bf16[5,32,1024]{2,1,0:T(8,128)(2,1)S(1)} %get-tuple-element.134), channel_id=1, source_target_pairs={{0,24},{4,28},{8,0},{12,4},{16,8},{20,12},{24,16},{28,20},{1,25},{... | collective-permute-start | bytes 983048 | tf_op jit(solution)/shard_map/ppermute | solution.py:27
  70.1 2.6 %collective-permute-done.9.across = bf16[2,3,2,32,1024]{4,3,2,1,0:T(8,128)(2,1)S(1)} collective-permute-done((bf16[2,3,2,32,1024]{4,3,2,1,0:T(8,128)(2,1)S(1)}, bf16[2,3,2,32,1024]{4,3,2,1,0:T(8,128)(2,1)S(1)}, u32[]{:S(2)}, u32[]{:S(2)}) %collective-permute-start.9) | collective-permute-done | bytes 786464 | tf_op jit(solution)/shard_map/ppermute | solution.py:27
  73.0 3.2 %collective-permute-done.18.refs_9_ = bf16[5,32,1024]{2,1,0:T(8,128)(2,1)S(1)} collective-permute-done((bf16[5,32,1024]{2,1,0:T(8,128)(2,1)S(1)}, bf16[5,32,1024]{2,1,0:T(8,128)(2,1)S(1)}, u32[]{:S(2)}, u32[]{:S(2)}) %collective-permute-start.18) | collective-permute-done | bytes 327712 | tf_op jit(solution)/shard_map/ppermute | solution.py:27
  77.5 2.3 %collective-permute-start.20 = (bf16[10,32,1024]{2,1,0:T(8,128)(2,1)S(1)}, bf16[10,32,1024]{2,1,0:T(8,128)(2,1)S(1)}, u32[]{:S(2)}, u32[]{:S(2)}) collective-permute-start(bf16[10,32,1024]{2,1,0:T(8,128)(2,1)S(1)} %get-tuple-element.143.here.refs_4_), channel_id=1, source_target_pairs={{0,24},{4,28},{8,0},{12,4},{16,8},{20,12},{24,16},{28,20},{1,25},{... | collective-permute-start | bytes 1966088 | tf_op jit(solution)/shard_map/ppermute | solution.py:27
  79.8 1.5 %collective-permute-start.24 = (bf16[10,32,1024]{2,1,0:T(8,128)(2,1)S(1)}, bf16[10,32,1024]{2,1,0:T(8,128)(2,1)S(1)}, u32[]{:S(2)}, u32[]{:S(2)}) collective-permute-start(bf16[10,32,1024]{2,1,0:T(8,128)(2,1)S(1)} %get-tuple-element.142), channel_id=1, source_target_pairs={{0,4},{4,0},{8,12},{12,8},{16,20},{20,16},{24,28},{28,24},{1,5},{5... | collective-permute-start | bytes 1966088 | tf_op jit(solution)/shard_map/ppermute | solution.py:27
  81.3 10.7 %collective-permute-done.21.minus1 = bf16[10,32,1024]{2,1,0:T(8,128)(2,1)S(1)} collective-permute-done((bf16[10,32,1024]{2,1,0:T(8,128)(2,1)S(1)}, bf16[10,32,1024]{2,1,0:T(8,128)(2,1)S(1)}, u32[]{:S(2)}, u32[]{:S(2)}) %collective-permute-start.21) | collective-permute-done | bytes 655392 | tf_op jit(solution)/shard_map/ppermute | solution.py:27
  92.1 3.3 %collective-permute-start.23 = (bf16[5,32,1024]{2,1,0:T(8,128)(2,1)S(1)}, bf16[5,32,1024]{2,1,0:T(8,128)(2,1)S(1)}, u32[]{:S(2)}, u32[]{:S(2)}) collective-permute-start(bf16[5,32,1024]{2,1,0:T(8,128)(2,1)S(1)} %slice.17), channel_id=1, source_target_pairs={{0,24},{4,28},{8,0},{12,4},{16,8},{20,12},{24,16},{28,20},{1,25},{... | collective-permute-start | bytes 983048 | tf_op jit(solution)/shard_map/ppermute | solution.py:27
  95.8 3.2 %collective-permute-start.30 = (bf16[10,32,1024]{2,1,0:T(8,128)(2,1)S(1)}, bf16[10,32,1024]{2,1,0:T(8,128)(2,1)S(1)}, u32[]{:S(2)}, u32[]{:S(2)}) collective-permute-start(bf16[10,32,1024]{2,1,0:T(8,128)(2,1)S(1)} %get-tuple-element.184.here.refs_8_), channel_id=1, source_target_pairs={{0,24},{4,28},{8,0},{12,4},{16,8},{20,12},{24,16},{28,20},{1,25},{... | collective-permute-start | bytes 1966088 | tf_op jit(solution)/shard_map/ppermute | solution.py:27
  99.1 4.9 %collective-permute-done.22.far_a = bf16[5,32,1024]{2,1,0:T(8,128)(2,1)S(1)} collective-permute-done((bf16[5,32,1024]{2,1,0:T(8,128)(2,1)S(1)}, bf16[5,32,1024]{2,1,0:T(8,128)(2,1)S(1)}, u32[]{:S(2)}, u32[]{:S(2)}) %collective-permute-start.22) | collective-permute-done | bytes 327712 | tf_op jit(solution)/shard_map/ppermute | solution.py:27
  103.9 2.6 %their_grad.2 = (bf16[256,1024]{1,0:T(8,128)(2,1)S(1)}, bf16[2,512,1024]{2,1,0:T(8,128)(2,1)S(1)}, bf16[3,2,32,1024]{3,2,1,0:T(8,128)(2,1)S(1)}) custom-call(s32[3]{0:T(128)S(1)} %pad_add_fusion.idx, bf16[10,32,1024]{2,1,0:T(8,128)(2,1)S(1)} %get-tuple-element.143.here.refs_4_, bf16[10,32,1024]{2,1,0:T(8,128)(2,1)S(1)} %collective-permute-done.20.plus1, ...), custom_call_target="tpu_custom_call" | custom-call | flops 1073741824 | bytes 10485760 | tf_op jit(solution)/shard_map/their_grad/pallas_call | solution.py:479
  106.7 1.8 %collective-permute-start.33 = (bf16[3,2,32,1024]{3,2,1,0:T(8,128)(2,1)S(1)}, bf16[3,2,32,1024]{3,2,1,0:T(8,128)(2,1)S(1)}, u32[]{:S(2)}, u32[]{:S(2)}) collective-permute-start(bf16[3,2,32,1024]{3,2,1,0:T(8,128)(2,1)S(1)} %get-tuple-element.160.refs_6_), channel_id=1, source_target_pairs={{0,4},{4,0},{8,12},{12,8},{16,20},{20,16},{24,28},{28,24},{1,5},{5... | collective-permute-start | bytes 1179656 | tf_op jit(solution)/shard_map/ppermute | solution.py:27
  108.5 1.9 %my_grad.2.mine = f32[256,1024]{1,0:T(8,128)S(1)} custom-call(bf16[2,512,1024]{2,1,0:T(8,128)(2,1)S(1)} %get-tuple-element.150.acts, bf16[1024,1024]{1,0:T(8,128)(2,1)S(1)} %copy-done, bf16[1024,1024]{1,0:T(8,128)(2,1)S(1)} %copy-done.1), custom_call_target="tpu_custom_call" | custom-call | flops 1073741824 | bytes 10485760 | tf_op jit(solution)/shard_map/my_grad/pallas_call | solution.py:501
  110.4 3.2 %part_grads.1 = (f32[1024,1024]{1,0:T(8,128)S(1)}, f32[1024,1024]{1,0:T(8,128)S(1)}) custom-call(bf16[2,256,1024]{2,1,0:T(8,128)(2,1)S(1)} %copy-done.3, bf16[2,256,1024]{2,1,0:T(8,128)(2,1)S(1)} %collective-permute-done.2.m.m1.refs_1_, bf16[2,512,1024]{2,1,0:T(8,128)(2,1)S(1)} %get-tuple-element.150.acts), custom_call_target="tpu_custom_call" | custom-call | flops 2147483648 | bytes 8388608 | tf_op jit(solution)/shard_map/part_grads/pallas_call | solution.py:565
  115.2 2.6 %collective-permute-start.32 = (bf16[5,32,1024]{2,1,0:T(8,128)(2,1)S(1)}, bf16[5,32,1024]{2,1,0:T(8,128)(2,1)S(1)}, u32[]{:S(2)}, u32[]{:S(2)}) collective-permute-start(bf16[5,32,1024]{2,1,0:T(8,128)(2,1)S(1)} %slice.15), channel_id=1, source_target_pairs={{0,24},{4,28},{8,0},{12,4},{16,8},{20,12},{24,16},{28,20},{1,25},{... | collective-permute-start | bytes 983048 | tf_op jit(solution)/shard_map/ppermute | solution.py:27
  117.8 3.2 %collective-permute-start.26 = (bf16[64,1024]{1,0:T(8,128)(2,1)S(1)}, bf16[64,1024]{1,0:T(8,128)(2,1)S(1)}, u32[]{:S(2)}, u32[]{:S(2)}) collective-permute-start(bf16[64,1024]{1,0:T(8,128)(2,1)S(1)} %get-tuple-element.155), channel_id=1, source_target_pairs={{0,2},{1,3},{2,0},{3,1},{4,6},{5,7},{6,4},{7,5},{8,10},{9,11},{10,... | collective-permute-start | bytes 393224 | tf_op jit(solution)/shard_map/ppermute | solution.py:36
  121.7 2.6 %collective-permute-start.28 = (bf16[64,1024]{1,0:T(8,128)(2,1)S(1)}, bf16[64,1024]{1,0:T(8,128)(2,1)S(1)}, u32[]{:S(2)}, u32[]{:S(2)}) collective-permute-start(bf16[64,1024]{1,0:T(8,128)(2,1)S(1)} %get-tuple-element.157), channel_id=1, source_target_pairs={{0,3},{1,0},{2,1},{3,2},{4,7},{5,4},{6,5},{7,6},{8,11},{9,8},{10,9... | collective-permute-start | bytes 393224 | tf_op jit(solution)/shard_map/ppermute | solution.py:36
  124.2 1.3 collective-permute-done.26.a
  125.6 2.2 %collective-permute-done.27.b = bf16[64,1024]{1,0:T(8,128)(2,1)S(1)} collective-permute-done((bf16[64,1024]{1,0:T(8,128)(2,1)S(1)}, bf16[64,1024]{1,0:T(8,128)(2,1)S(1)}, u32[]{:S(2)}, u32[]{:S(2)}) %collective-permute-start.27) | collective-permute-done | bytes 131104 | tf_op jit(solution)/shard_map/ppermute | solution.py:36
  127.8 2.6 %their_grad.3 = (bf16[256,1024]{1,0:T(8,128)(2,1)S(1)}, bf16[2,512,1024]{2,1,0:T(8,128)(2,1)S(1)}, bf16[3,2,32,1024]{3,2,1,0:T(8,128)(2,1)S(1)}) custom-call(s32[3]{0:T(128)S(1)} %pad_add_fusion.idx, bf16[10,32,1024]{2,1,0:T(8,128)(2,1)S(1)} %get-tuple-element.184.here.refs_8_, bf16[10,32,1024]{2,1,0:T(8,128)(2,1)S(1)} %collective-permute-done.30.plus1, ...), custom_call_target="tpu_custom_call" | custom-call | flops 1073741824 | bytes 10485760 | tf_op jit(solution)/shard_map/their_grad/pallas_call | solution.py:479
  131.5 1.9 %my_grad.3.mine = f32[256,1024]{1,0:T(8,128)S(1)} custom-call(bf16[2,512,1024]{2,1,0:T(8,128)(2,1)S(1)} %get-tuple-element.174.acts, bf16[1024,1024]{1,0:T(8,128)(2,1)S(1)} %copy-done, bf16[1024,1024]{1,0:T(8,128)(2,1)S(1)} %copy-done.1), custom_call_target="tpu_custom_call" | custom-call | flops 1073741824 | bytes 10485760 | tf_op jit(solution)/shard_map/my_grad/pallas_call | solution.py:501
  134.1 1.8 %collective-permute-start.35 = (bf16[64,1024]{1,0:T(8,128)(2,1)S(1)}, bf16[64,1024]{1,0:T(8,128)(2,1)S(1)}, u32[]{:S(2)}, u32[]{:S(2)}) collective-permute-start(bf16[64,1024]{1,0:T(8,128)(2,1)S(1)} %get-tuple-element.171), channel_id=1, source_target_pairs={{0,2},{1,3},{2,0},{3,1},{4,6},{5,7},{6,4},{7,5},{8,10},{9,11},{10,... | collective-permute-start | bytes 393224 | tf_op jit(solution)/shard_map/ppermute | solution.py:36
  135.9 2.2 %collective-permute-start.36 = (bf16[64,1024]{1,0:T(8,128)(2,1)S(1)}, bf16[64,1024]{1,0:T(8,128)(2,1)S(1)}, u32[]{:S(2)}, u32[]{:S(2)}) collective-permute-start(bf16[64,1024]{1,0:T(8,128)(2,1)S(1)} %get-tuple-element.172), channel_id=1, source_target_pairs={{0,1},{1,2},{2,3},{3,0},{4,5},{5,6},{6,7},{7,4},{8,9},{9,10},{10,1... | collective-permute-start | bytes 393224 | tf_op jit(solution)/shard_map/ppermute | solution.py:36
  139.1 4.4 %in_grads.1 = (bf16[1024,1024]{1,0:T(8,128)(2,1)}, bf16[1024,1024]{1,0:T(8,128)(2,1)}) custom-call(bf16[2,256,1024]{2,1,0:T(8,128)(2,1)S(1)} %collective-permute-done.7.m.m0.refs_2_, bf16[2,256,1024]{2,1,0:T(8,128)(2,1)S(1)} %collective-permute-done.8.m.m1.refs_3_, bf16[2,512,1024]{2,1,0:T(8,128)(2,1)S(1)} %get-tuple-element.174.acts, ...), custom_call_target="tpu_custom_call" | custom-call | flops 2147483648 | bytes 8388608 | tf_op jit(solution)/shard_map/in_grads/pallas_call | solution.py:599
  144.5 1.9 %collective-permute-start.38 = (bf16[64,1024]{1,0:T(8,128)(2,1)S(1)}, bf16[64,1024]{1,0:T(8,128)(2,1)S(1)}, u32[]{:S(2)}, u32[]{:S(2)}) collective-permute-start(bf16[64,1024]{1,0:T(8,128)(2,1)S(1)} %owned.3), channel_id=1, source_target_pairs={{0,64},{32,96},{64,0},{96,32},{1,65},{33,97},{65,1},{97,33},{2,66}... | collective-permute-start | bytes 393224 | tf_op jit(solution)/shard_map/ppermute | solution.py:32
  146.3 4.6 %down_grad.1 = bf16[1024,1024]{1,0:T(8,128)(2,1)} custom-call(s32[3]{0:T(128)S(1)} %pad_add_fusion.idx, bf16[2,256,1024]{2,1,0:T(8,128)(2,1)S(1)} %copy-done.3, bf16[2,256,1024]{2,1,0:T(8,128)(2,1)S(1)} %collective-permute-done.2.m.m1.refs_1_, bf16[2,256,1024]{2,1,0:T(8,128)(2,1)S(1)} %collective-permute-done.7.m.m0.refs_2_, ...), custom_call_target="tpu_custom_call" | custom-call | flops 2147483648 | bytes 4194304 | tf_op jit(solution)/shard_map/down_grad/pallas_call | solution.py:644
  (69 shorter events, 13.7 us)
Async XLA Ops:
  2.8 14.6 %collective-permute-start.2 = (bf16[2,256,1024]{2,1,0:T(8,128)(2,1)}, bf16[2,256,1024]{2,1,0:T(8,128)(2,1)S(1)}, u32[]{:S(2)}, u32[]{:S(2)}) collective-permute-start(bf16[2,256,1024]{2,1,0:T(8,128)(2,1)} %scaled.1.m.m0.refs_0_), channel_id=1, source_target_pairs={{0,32},{32,0},{64,96},{96,64},{1,33},{33,1},{65,97},{97,65},{2,34}... | collective-permute-start | bytes 3145736 | tf_op jit(solution)/shard_map/ppermute | solution.py:32
  2.8 32.6 %collective-permute-start.7 = (bf16[2,256,1024]{2,1,0:T(8,128)(2,1)}, bf16[2,256,1024]{2,1,0:T(8,128)(2,1)S(1)}, u32[]{:S(2)}, u32[]{:S(2)}) collective-permute-start(bf16[2,256,1024]{2,1,0:T(8,128)(2,1)} %scaled.1.m.m0.refs_0_), channel_id=1, source_target_pairs={{0,64},{32,96},{64,0},{96,32},{1,65},{33,97},{65,1},{97,33},{2,66}... | collective-permute-start | bytes 3145736 | tf_op jit(solution)/shard_map/ppermute | solution.py:32
  6.0 1.2 copy-start.3
  7.3 10.1 %copy-start = (bf16[1024,1024]{1,0:T(8,128)(2,1)S(1)}, bf16[1024,1024]{1,0:T(8,128)(2,1)}, u32[]{:S(2)}) copy-start(bf16[1024,1024]{1,0:T(8,128)(2,1)} %wg.15) | copy-start | bytes 6291460
  7.3 10.1 %copy-start.1 = (bf16[1024,1024]{1,0:T(8,128)(2,1)S(1)}, bf16[1024,1024]{1,0:T(8,128)(2,1)}, u32[]{:S(2)}) copy-start(bf16[1024,1024]{1,0:T(8,128)(2,1)} %wu.15) | copy-start | bytes 6291460
  7.3 10.1 %copy-start.2 = (bf16[1024,1024]{1,0:T(8,128)(2,1)S(1)}, bf16[1024,1024]{1,0:T(8,128)(2,1)}, u32[]{:S(2)}) copy-start(bf16[1024,1024]{1,0:T(8,128)(2,1)} %wd.7) | copy-start | bytes 6291460
  13.2 14.0 %collective-permute-start = (bf16[2,3,32,1024]{3,2,1,0:T(8,128)(2,1)S(1)}, bf16[2,3,32,1024]{3,2,1,0:T(8,128)(2,1)S(1)}, u32[]{:S(2)}, u32[]{:S(2)}) collective-permute-start(bf16[2,3,32,1024]{3,2,1,0:T(8,128)(2,1)S(1)} %get-tuple-element.98), channel_id=1, source_target_pairs={{0,8},{4,12},{8,16},{12,20},{16,24},{20,28},{24,0},{28,4},{1,9},{5... | collective-permute-start | bytes 1179656 | tf_op jit(solution)/shard_map/ppermute | solution.py:27
  15.2 12.0 %collective-permute-start.1 = (bf16[2,3,32,1024]{3,2,1,0:T(8,128)(2,1)S(1)}, bf16[2,3,32,1024]{3,2,1,0:T(8,128)(2,1)S(1)}, u32[]{:S(2)}, u32[]{:S(2)}) collective-permute-start(bf16[2,3,32,1024]{3,2,1,0:T(8,128)(2,1)S(1)} %get-tuple-element.99), channel_id=1, source_target_pairs={{0,24},{4,28},{8,0},{12,4},{16,8},{20,12},{24,16},{28,20},{1,25},{... | collective-permute-start | bytes 1179656 | tf_op jit(solution)/shard_map/ppermute | solution.py:27
  20.6 14.6 %collective-permute-start.3 = (bf16[2,3,32,1024]{3,2,1,0:T(8,128)(2,1)S(1)}, bf16[2,3,32,1024]{3,2,1,0:T(8,128)(2,1)S(1)}, u32[]{:S(2)}, u32[]{:S(2)}) collective-permute-start(bf16[2,3,32,1024]{3,2,1,0:T(8,128)(2,1)S(1)} %get-tuple-element.102), channel_id=1, source_target_pairs={{0,8},{4,12},{8,16},{12,20},{16,24},{20,28},{24,0},{28,4},{1,9},{5... | collective-permute-start | bytes 1179656 | tf_op jit(solution)/shard_map/ppermute | solution.py:27
  20.7 14.5 %collective-permute-start.4 = (bf16[2,3,32,1024]{3,2,1,0:T(8,128)(2,1)S(1)}, bf16[2,3,32,1024]{3,2,1,0:T(8,128)(2,1)S(1)}, u32[]{:S(2)}, u32[]{:S(2)}) collective-permute-start(bf16[2,3,32,1024]{3,2,1,0:T(8,128)(2,1)S(1)} %get-tuple-element.103), channel_id=1, source_target_pairs={{0,24},{4,28},{8,0},{12,4},{16,8},{20,12},{24,16},{28,20},{1,25},{... | collective-permute-start | bytes 1179656 | tf_op jit(solution)/shard_map/ppermute | solution.py:27
  35.4 7.2 %collective-permute-start.8 = (bf16[2,256,1024]{2,1,0:T(8,128)(2,1)S(1)}, bf16[2,256,1024]{2,1,0:T(8,128)(2,1)S(1)}, u32[]{:S(2)}, u32[]{:S(2)}) collective-permute-start(bf16[2,256,1024]{2,1,0:T(8,128)(2,1)S(1)} %collective-permute-done.7.m.m0.refs_2_), channel_id=1, source_target_pairs={{0,32},{32,0},{64,96},{96,64},{1,33},{33,1},{65,97},{97,65},{2,34}... | collective-permute-start | bytes 3145736 | tf_op jit(solution)/shard_map/ppermute | solution.py:32
  35.5 12.8 %collective-permute-start.5 = (bf16[3,2,32,1024]{3,2,1,0:T(8,128)(2,1)S(1)}, bf16[3,2,32,1024]{3,2,1,0:T(8,128)(2,1)S(1)}, u32[]{:S(2)}, u32[]{:S(2)}) collective-permute-start(bf16[3,2,32,1024]{3,2,1,0:T(8,128)(2,1)S(1)} %get-tuple-element.106), channel_id=1, source_target_pairs={{0,8},{4,12},{8,16},{12,20},{16,24},{20,28},{24,0},{28,4},{1,9},{5... | collective-permute-start | bytes 1179656 | tf_op jit(solution)/shard_map/ppermute | solution.py:27
  36.8 11.5 %collective-permute-start.6 = (bf16[3,2,32,1024]{3,2,1,0:T(8,128)(2,1)S(1)}, bf16[3,2,32,1024]{3,2,1,0:T(8,128)(2,1)S(1)}, u32[]{:S(2)}, u32[]{:S(2)}) collective-permute-start(bf16[3,2,32,1024]{3,2,1,0:T(8,128)(2,1)S(1)} %get-tuple-element.107), channel_id=1, source_target_pairs={{0,24},{4,28},{8,0},{12,4},{16,8},{20,12},{24,16},{28,20},{1,25},{... | collective-permute-start | bytes 1179656 | tf_op jit(solution)/shard_map/ppermute | solution.py:27
  42.0 10.6 %collective-permute-start.14 = (bf16[4,32,1024]{2,1,0:T(8,128)(2,1)S(1)}, bf16[4,32,1024]{2,1,0:T(8,128)(2,1)S(1)}, u32[]{:S(2)}, u32[]{:S(2)}) collective-permute-start(bf16[4,32,1024]{2,1,0:T(8,128)(2,1)S(1)} %get-tuple-element.120), channel_id=1, source_target_pairs={{0,4},{4,0},{8,12},{12,8},{16,20},{20,16},{24,28},{28,24},{1,5},{5... | collective-permute-start | bytes 786440 | tf_op jit(solution)/shard_map/ppermute | solution.py:27
  45.8 11.0 %collective-permute-start.15 = (bf16[4,32,1024]{2,1,0:T(8,128)(2,1)S(1)}, bf16[4,32,1024]{2,1,0:T(8,128)(2,1)S(1)}, u32[]{:S(2)}, u32[]{:S(2)}) collective-permute-start(bf16[4,32,1024]{2,1,0:T(8,128)(2,1)S(1)} %get-tuple-element.121), channel_id=1, source_target_pairs={{0,4},{4,0},{8,12},{12,8},{16,20},{20,16},{24,28},{28,24},{1,5},{5... | collective-permute-start | bytes 786440 | tf_op jit(solution)/shard_map/ppermute | solution.py:27
  48.7 24.0 %collective-permute-start.9 = (bf16[2,3,2,32,1024]{4,3,2,1,0:T(8,128)(2,1)S(1)}, bf16[2,3,2,32,1024]{4,3,2,1,0:T(8,128)(2,1)S(1)}, u32[]{:S(2)}, u32[]{:S(2)}) collective-permute-start(bf16[2,3,2,32,1024]{4,3,2,1,0:T(8,128)(2,1)S(1)} %get-tuple-element.117), channel_id=1, source_target_pairs={{0,4},{4,0},{8,12},{12,8},{16,20},{20,16},{24,28},{28,24},{1,5},{5... | collective-permute-start | bytes 2359304 | tf_op jit(solution)/shard_map/ppermute | solution.py:27
  49.3 10.5 %collective-permute-start.10 = (bf16[2,2,32,1024]{3,2,1,0:T(8,128)(2,1)S(1)}, bf16[2,2,32,1024]{3,2,1,0:T(8,128)(2,1)S(1)}, u32[]{:S(2)}, u32[]{:S(2)}) collective-permute-start(bf16[2,2,32,1024]{3,2,1,0:T(8,128)(2,1)S(1)} %get-tuple-element.109), channel_id=1, source_target_pairs={{0,8},{4,12},{8,16},{12,20},{16,24},{20,28},{24,0},{28,4},{1,9},{5... | collective-permute-start | bytes 786440 | tf_op jit(solution)/shard_map/ppermute | solution.py:27
  50.7 9.2 %collective-permute-start.11 = (bf16[2,2,32,1024]{3,2,1,0:T(8,128)(2,1)S(1)}, bf16[2,2,32,1024]{3,2,1,0:T(8,128)(2,1)S(1)}, u32[]{:S(2)}, u32[]{:S(2)}) collective-permute-start(bf16[2,2,32,1024]{3,2,1,0:T(8,128)(2,1)S(1)} %get-tuple-element.110), channel_id=1, source_target_pairs={{0,24},{4,28},{8,0},{12,4},{16,8},{20,12},{24,16},{28,20},{1,25},{... | collective-permute-start | bytes 786440 | tf_op jit(solution)/shard_map/ppermute | solution.py:27
  52.6 12.6 %collective-permute-start.12 = (bf16[2,2,32,1024]{3,2,1,0:T(8,128)(2,1)S(1)}, bf16[2,2,32,1024]{3,2,1,0:T(8,128)(2,1)S(1)}, u32[]{:S(2)}, u32[]{:S(2)}) collective-permute-start(bf16[2,2,32,1024]{3,2,1,0:T(8,128)(2,1)S(1)} %get-tuple-element.112), channel_id=1, source_target_pairs={{0,8},{4,12},{8,16},{12,20},{16,24},{20,28},{24,0},{28,4},{1,9},{5... | collective-permute-start | bytes 786440 | tf_op jit(solution)/shard_map/ppermute | solution.py:27
  56.8 8.4 %collective-permute-start.13 = (bf16[2,2,32,1024]{3,2,1,0:T(8,128)(2,1)S(1)}, bf16[2,2,32,1024]{3,2,1,0:T(8,128)(2,1)S(1)}, u32[]{:S(2)}, u32[]{:S(2)}) collective-permute-start(bf16[2,2,32,1024]{3,2,1,0:T(8,128)(2,1)S(1)} %get-tuple-element.113), channel_id=1, source_target_pairs={{0,24},{4,28},{8,0},{12,4},{16,8},{20,12},{24,16},{28,20},{1,25},{... | collective-permute-start | bytes 786440 | tf_op jit(solution)/shard_map/ppermute | solution.py:27
  59.8 6.8 %collective-permute-start.16 = (bf16[2,32,1024]{2,1,0:T(8,128)(2,1)S(1)}, bf16[2,32,1024]{2,1,0:T(8,128)(2,1)S(1)}, u32[]{:S(2)}, u32[]{:S(2)}) collective-permute-start(bf16[2,32,1024]{2,1,0:T(8,128)(2,1)S(1)} %get-tuple-element.125), channel_id=1, source_target_pairs={{0,8},{4,12},{8,16},{12,20},{16,24},{20,28},{24,0},{28,4},{1,9},{5... | collective-permute-start | bytes 393224 | tf_op jit(solution)/shard_map/ppermute | solution.py:27
  59.9 6.7 %collective-permute-start.17 = (bf16[2,32,1024]{2,1,0:T(8,128)(2,1)S(1)}, bf16[2,32,1024]{2,1,0:T(8,128)(2,1)S(1)}, u32[]{:S(2)}, u32[]{:S(2)}) collective-permute-start(bf16[2,32,1024]{2,1,0:T(8,128)(2,1)S(1)} %get-tuple-element.126), channel_id=1, source_target_pairs={{0,24},{4,28},{8,0},{12,4},{16,8},{20,12},{24,16},{28,20},{1,25},{... | collective-permute-start | bytes 393224 | tf_op jit(solution)/shard_map/ppermute | solution.py:27
  66.8 9.4 %collective-permute-start.18 = (bf16[5,32,1024]{2,1,0:T(8,128)(2,1)S(1)}, bf16[5,32,1024]{2,1,0:T(8,128)(2,1)S(1)}, u32[]{:S(2)}, u32[]{:S(2)}) collective-permute-start(bf16[5,32,1024]{2,1,0:T(8,128)(2,1)S(1)} %get-tuple-element.133), channel_id=1, source_target_pairs={{0,8},{4,12},{8,16},{12,20},{16,24},{20,28},{24,0},{28,4},{1,9},{5... | collective-permute-start | bytes 983048 | tf_op jit(solution)/shard_map/ppermute | solution.py:27
  67.8 8.3 %collective-permute-start.19 = (bf16[5,32,1024]{2,1,0:T(8,128)(2,1)S(1)}, bf16[5,32,1024]{2,1,0:T(8,128)(2,1)S(1)}, u32[]{:S(2)}, u32[]{:S(2)}) collective-permute-start(bf16[5,32,1024]{2,1,0:T(8,128)(2,1)S(1)} %get-tuple-element.134), channel_id=1, source_target_pairs={{0,24},{4,28},{8,0},{12,4},{16,8},{20,12},{24,16},{28,20},{1,25},{... | collective-permute-start | bytes 983048 | tf_op jit(solution)/shard_map/ppermute | solution.py:27
  76.5 15.5 %collective-permute-start.21 = (bf16[10,32,1024]{2,1,0:T(8,128)(2,1)S(1)}, bf16[10,32,1024]{2,1,0:T(8,128)(2,1)S(1)}, u32[]{:S(2)}, u32[]{:S(2)}) collective-permute-start(bf16[10,32,1024]{2,1,0:T(8,128)(2,1)S(1)} %get-tuple-element.143.here.refs_4_), channel_id=1, source_target_pairs={{0,8},{4,12},{8,16},{12,20},{16,24},{20,28},{24,0},{28,4},{1,9},{5... | collective-permute-start | bytes 1966088 | tf_op jit(solution)/shard_map/ppermute | solution.py:27
  77.5 14.6 %collective-permute-start.20 = (bf16[10,32,1024]{2,1,0:T(8,128)(2,1)S(1)}, bf16[10,32,1024]{2,1,0:T(8,128)(2,1)S(1)}, u32[]{:S(2)}, u32[]{:S(2)}) collective-permute-start(bf16[10,32,1024]{2,1,0:T(8,128)(2,1)S(1)} %get-tuple-element.143.here.refs_4_), channel_id=1, source_target_pairs={{0,24},{4,28},{8,0},{12,4},{16,8},{20,12},{24,16},{28,20},{1,25},{... | collective-permute-start | bytes 1966088 | tf_op jit(solution)/shard_map/ppermute | solution.py:27
  79.8 15.6 %collective-permute-start.24 = (bf16[10,32,1024]{2,1,0:T(8,128)(2,1)S(1)}, bf16[10,32,1024]{2,1,0:T(8,128)(2,1)S(1)}, u32[]{:S(2)}, u32[]{:S(2)}) collective-permute-start(bf16[10,32,1024]{2,1,0:T(8,128)(2,1)S(1)} %get-tuple-element.142), channel_id=1, source_target_pairs={{0,4},{4,0},{8,12},{12,8},{16,20},{20,16},{24,28},{28,24},{1,5},{5... | collective-permute-start | bytes 1966088 | tf_op jit(solution)/shard_map/ppermute | solution.py:27
  92.0 11.9 %collective-permute-start.22 = (bf16[5,32,1024]{2,1,0:T(8,128)(2,1)S(1)}, bf16[5,32,1024]{2,1,0:T(8,128)(2,1)S(1)}, u32[]{:S(2)}, u32[]{:S(2)}) collective-permute-start(bf16[5,32,1024]{2,1,0:T(8,128)(2,1)S(1)} %slice.16), channel_id=1, source_target_pairs={{0,8},{4,12},{8,16},{12,20},{16,24},{20,28},{24,0},{28,4},{1,9},{5... | collective-permute-start | bytes 983048 | tf_op jit(solution)/shard_map/ppermute | solution.py:27
  92.1 11.8 %collective-permute-start.23 = (bf16[5,32,1024]{2,1,0:T(8,128)(2,1)S(1)}, bf16[5,32,1024]{2,1,0:T(8,128)(2,1)S(1)}, u32[]{:S(2)}, u32[]{:S(2)}) collective-permute-start(bf16[5,32,1024]{2,1,0:T(8,128)(2,1)S(1)} %slice.17), channel_id=1, source_target_pairs={{0,24},{4,28},{8,0},{12,4},{16,8},{20,12},{24,16},{28,20},{1,25},{... | collective-permute-start | bytes 983048 | tf_op jit(solution)/shard_map/ppermute | solution.py:27
  95.8 18.5 %collective-permute-start.29 = (bf16[10,32,1024]{2,1,0:T(8,128)(2,1)S(1)}, bf16[10,32,1024]{2,1,0:T(8,128)(2,1)S(1)}, u32[]{:S(2)}, u32[]{:S(2)}) collective-permute-start(bf16[10,32,1024]{2,1,0:T(8,128)(2,1)S(1)} %get-tuple-element.184.here.refs_8_), channel_id=1, source_target_pairs={{0,8},{4,12},{8,16},{12,20},{16,24},{20,28},{24,0},{28,4},{1,9},{5... | collective-permute-start | bytes 1966088 | tf_op jit(solution)/shard_map/ppermute | solution.py:27
  95.8 18.4 %collective-permute-start.30 = (bf16[10,32,1024]{2,1,0:T(8,128)(2,1)S(1)}, bf16[10,32,1024]{2,1,0:T(8,128)(2,1)S(1)}, u32[]{:S(2)}, u32[]{:S(2)}) collective-permute-start(bf16[10,32,1024]{2,1,0:T(8,128)(2,1)S(1)} %get-tuple-element.184.here.refs_8_), channel_id=1, source_target_pairs={{0,24},{4,28},{8,0},{12,4},{16,8},{20,12},{24,16},{28,20},{1,25},{... | collective-permute-start | bytes 1966088 | tf_op jit(solution)/shard_map/ppermute | solution.py:27
  106.6 7.0 %collective-permute-start.25 = (bf16[256,1024]{1,0:T(8,128)(2,1)S(1)}, bf16[256,1024]{1,0:T(8,128)(2,1)S(1)}, u32[]{:S(2)}, u32[]{:S(2)}) collective-permute-start(bf16[256,1024]{1,0:T(8,128)(2,1)S(1)} %get-tuple-element.151), channel_id=1, source_target_pairs={{0,32},{32,0},{64,96},{96,64},{1,33},{33,1},{65,97},{97,65},{2,34}... | collective-permute-start | bytes 1572872 | tf_op jit(solution)/shard_map/ppermute | solution.py:32
  106.7 15.0 %collective-permute-start.33 = (bf16[3,2,32,1024]{3,2,1,0:T(8,128)(2,1)S(1)}, bf16[3,2,32,1024]{3,2,1,0:T(8,128)(2,1)S(1)}, u32[]{:S(2)}, u32[]{:S(2)}) collective-permute-start(bf16[3,2,32,1024]{3,2,1,0:T(8,128)(2,1)S(1)} %get-tuple-element.160.refs_6_), channel_id=1, source_target_pairs={{0,4},{4,0},{8,12},{12,8},{16,20},{20,16},{24,28},{28,24},{1,5},{5... | collective-permute-start | bytes 1179656 | tf_op jit(solution)/shard_map/ppermute | solution.py:27
  114.3 13.5 %collective-permute-start.31 = (bf16[5,32,1024]{2,1,0:T(8,128)(2,1)S(1)}, bf16[5,32,1024]{2,1,0:T(8,128)(2,1)S(1)}, u32[]{:S(2)}, u32[]{:S(2)}) collective-permute-start(bf16[5,32,1024]{2,1,0:T(8,128)(2,1)S(1)} %slice.14), channel_id=1, source_target_pairs={{0,8},{4,12},{8,16},{12,20},{16,24},{20,28},{24,0},{28,4},{1,9},{5... | collective-permute-start | bytes 983048 | tf_op jit(solution)/shard_map/ppermute | solution.py:27
  115.2 12.6 %collective-permute-start.32 = (bf16[5,32,1024]{2,1,0:T(8,128)(2,1)S(1)}, bf16[5,32,1024]{2,1,0:T(8,128)(2,1)S(1)}, u32[]{:S(2)}, u32[]{:S(2)}) collective-permute-start(bf16[5,32,1024]{2,1,0:T(8,128)(2,1)S(1)} %slice.15), channel_id=1, source_target_pairs={{0,24},{4,28},{8,0},{12,4},{16,8},{20,12},{24,16},{28,20},{1,25},{... | collective-permute-start | bytes 983048 | tf_op jit(solution)/shard_map/ppermute | solution.py:27
  117.8 7.8 %collective-permute-start.26 = (bf16[64,1024]{1,0:T(8,128)(2,1)S(1)}, bf16[64,1024]{1,0:T(8,128)(2,1)S(1)}, u32[]{:S(2)}, u32[]{:S(2)}) collective-permute-start(bf16[64,1024]{1,0:T(8,128)(2,1)S(1)} %get-tuple-element.155), channel_id=1, source_target_pairs={{0,2},{1,3},{2,0},{3,1},{4,6},{5,7},{6,4},{7,5},{8,10},{9,11},{10,... | collective-permute-start | bytes 393224 | tf_op jit(solution)/shard_map/ppermute | solution.py:36
  121.0 6.8 %collective-permute-start.27 = (bf16[64,1024]{1,0:T(8,128)(2,1)S(1)}, bf16[64,1024]{1,0:T(8,128)(2,1)S(1)}, u32[]{:S(2)}, u32[]{:S(2)}) collective-permute-start(bf16[64,1024]{1,0:T(8,128)(2,1)S(1)} %get-tuple-element.156), channel_id=1, source_target_pairs={{0,1},{1,2},{2,3},{3,0},{4,5},{5,6},{6,7},{7,4},{8,9},{9,10},{10,1... | collective-permute-start | bytes 393224 | tf_op jit(solution)/shard_map/ppermute | solution.py:36
  121.7 6.1 %collective-permute-start.28 = (bf16[64,1024]{1,0:T(8,128)(2,1)S(1)}, bf16[64,1024]{1,0:T(8,128)(2,1)S(1)}, u32[]{:S(2)}, u32[]{:S(2)}) collective-permute-start(bf16[64,1024]{1,0:T(8,128)(2,1)S(1)} %get-tuple-element.157), channel_id=1, source_target_pairs={{0,3},{1,0},{2,1},{3,2},{4,7},{5,4},{6,5},{7,6},{8,11},{9,8},{10,9... | collective-permute-start | bytes 393224 | tf_op jit(solution)/shard_map/ppermute | solution.py:36
  130.4 3.0 %collective-permute-start.34 = (bf16[256,1024]{1,0:T(8,128)(2,1)S(1)}, bf16[256,1024]{1,0:T(8,128)(2,1)S(1)}, u32[]{:S(2)}, u32[]{:S(2)}) collective-permute-start(bf16[256,1024]{1,0:T(8,128)(2,1)S(1)} %get-tuple-element.168), channel_id=1, source_target_pairs={{0,32},{32,0},{64,96},{96,64},{1,33},{33,1},{65,97},{97,65},{2,34}... | collective-permute-start | bytes 1572872 | tf_op jit(solution)/shard_map/ppermute | solution.py:32
  130.5 15.8 %collective-permute-start.39 = (bf16[3,2,32,1024]{3,2,1,0:T(8,128)(2,1)S(1)}, bf16[3,2,32,1024]{3,2,1,0:T(8,128)(2,1)S(1)}, u32[]{:S(2)}, u32[]{:S(2)}) collective-permute-start(bf16[3,2,32,1024]{3,2,1,0:T(8,128)(2,1)S(1)} %get-tuple-element.186.refs_10_), channel_id=1, source_target_pairs={{0,4},{4,0},{8,12},{12,8},{16,20},{20,16},{24,28},{28,24},{1,5},{5... | collective-permute-start | bytes 1179656 | tf_op jit(solution)/shard_map/ppermute | solution.py:27
  134.1 9.5 %collective-permute-start.35 = (bf16[64,1024]{1,0:T(8,128)(2,1)S(1)}, bf16[64,1024]{1,0:T(8,128)(2,1)S(1)}, u32[]{:S(2)}, u32[]{:S(2)}) collective-permute-start(bf16[64,1024]{1,0:T(8,128)(2,1)S(1)} %get-tuple-element.171), channel_id=1, source_target_pairs={{0,2},{1,3},{2,0},{3,1},{4,6},{5,7},{6,4},{7,5},{8,10},{9,11},{10,... | collective-permute-start | bytes 393224 | tf_op jit(solution)/shard_map/ppermute | solution.py:36
  135.9 8.2 %collective-permute-start.36 = (bf16[64,1024]{1,0:T(8,128)(2,1)S(1)}, bf16[64,1024]{1,0:T(8,128)(2,1)S(1)}, u32[]{:S(2)}, u32[]{:S(2)}) collective-permute-start(bf16[64,1024]{1,0:T(8,128)(2,1)S(1)} %get-tuple-element.172), channel_id=1, source_target_pairs={{0,1},{1,2},{2,3},{3,0},{4,5},{5,6},{6,7},{7,4},{8,9},{9,10},{10,1... | collective-permute-start | bytes 393224 | tf_op jit(solution)/shard_map/ppermute | solution.py:36
  138.1 6.3 %collective-permute-start.37 = (bf16[64,1024]{1,0:T(8,128)(2,1)S(1)}, bf16[64,1024]{1,0:T(8,128)(2,1)S(1)}, u32[]{:S(2)}, u32[]{:S(2)}) collective-permute-start(bf16[64,1024]{1,0:T(8,128)(2,1)S(1)} %get-tuple-element.173), channel_id=1, source_target_pairs={{0,3},{1,0},{2,1},{3,2},{4,7},{5,4},{6,5},{7,6},{8,11},{9,8},{10,9... | collective-permute-start | bytes 393224 | tf_op jit(solution)/shard_map/ppermute | solution.py:36
  144.5 6.6 %collective-permute-start.38 = (bf16[64,1024]{1,0:T(8,128)(2,1)S(1)}, bf16[64,1024]{1,0:T(8,128)(2,1)S(1)}, u32[]{:S(2)}, u32[]{:S(2)}) collective-permute-start(bf16[64,1024]{1,0:T(8,128)(2,1)S(1)} %owned.3), channel_id=1, source_target_pairs={{0,64},{32,96},{64,0},{96,32},{1,65},{33,97},{65,1},{97,33},{2,66}... | collective-permute-start | bytes 393224 | tf_op jit(solution)/shard_map/ppermute | solution.py:32

commit v6 on v5

--- a/solution.py
+++ b/solution.py
@@ -703,7 +703,7 @@
     held1, held_g, sent1 = cross_ring_sum(owns1, near1, *last1)
     across1 = fin_perm(sent1, 0, 1)
 
-    (ready,) = after((here0,), sent1)
+    (ready,) = after((here0,), *last1)
     minus1, plus1 = ring(ready, ready)
     on_plus, on_minus = minus1[:5], plus1[5:]
     far0 = ring(on_plus, on_minus)

time: 152 us -> 151 us (level)
  transfers between devices with their start and end apart: 40 -> 40, of which waited for: 16 -> 15; matrix products, arithmetic and copies ran while one was open for 0% -> 0% of each run, Pallas kernels for 24% -> 25%
where the time goes in v6:
time: 151 us
  starting transfers between devices  59.7 us (40%)
  waiting for transfers between devices  46.4 us (31%)
  Pallas kernels  42.1 us (28%)
    ppermute x28, starting transfers between devices, fin_perm(): return lax.ppermute(x, 'fin', pairs)  42.7 us
    ppermute x28, waiting for transfers between devices, fin_perm(): return lax.ppermute(x, 'fin', pairs)  42.1 us
    ppermute x6, starting transfers between devices, y_perm(): return lax.ppermute(x, 'fout', [(y, (y + dy) % 4) for y in range(4)])  11.6 us
    pallas_call x2, Pallas kernels, cross_forward(): pl.pallas_call(cross_forward_kernel, in_specs=[SMEM] + [VMEM] * 4, out_sp...  6.32 us
    pallas_call x1, Pallas kernels, own_forward(): pl.pallas_call(own_forward_kernel, in_specs=[SMEM, VMEM] + [pl.BlockSpec(...  5.92 us
    ppermute x6, starting transfers between devices, tok_perm(): return lax.ppermute(x, 'tok', pairs)  5.42 us
    pallas_call x2, Pallas kernels, their_grad(): pl.pallas_call(their_grad_kernel, in_specs=[SMEM] + [VMEM] * 7, out_specs...  5.24 us
    pallas_call x1, Pallas kernels, down_grad(): pl.pallas_call(down_grad_kernel, grid=(width // tile,), in_specs=[SMEM] +...  4.62 us
  transfers between devices with their start and end apart: 40, of which 15 were waited for; matrix products, arithmetic and copies ran while one was open for 0% of the time, Pallas kernels for 25%

profile of v6, /device:TPU:0, one launch (start us, length us, event | category | flops | bytes accessed | tf_op | source)
XLA Modules:
  0.0 151.2 jit_solution(7673138571200391827)
XLA Ops:
  0.6 2.2 %scaled.1.m.m0.refs_0_ = bf16[2,256,1024]{2,1,0:T(8,128)(2,1)} custom-call(f32[16]{0:T(128)} %margin.1, bf16[256,1024]{1,0:T(8,128)(2,1)} %x.1, bf16[256,1024]{1,0:T(8,128)(2,1)} %up.1, s32[1,256]{1,0:T(1,128)} %bitcast.5, s32[1,256]{1,0:T(1,128)} %bitcast.6), custom_call_target="tpu_custom_call" | custom-call | flops 1048576 | bytes 2097152 | tf_op jit(solution)/shard_map/scaled/pallas_call | solution.py:68
  2.8 3.1 %collective-permute-start.7 = (bf16[2,256,1024]{2,1,0:T(8,128)(2,1)}, bf16[2,256,1024]{2,1,0:T(8,128)(2,1)S(1)}, u32[]{:S(2)}, u32[]{:S(2)}) collective-permute-start(bf16[2,256,1024]{2,1,0:T(8,128)(2,1)} %scaled.1.m.m0.refs_0_), channel_id=1, source_target_pairs={{0,64},{32,96},{64,0},{96,32},{1,65},{33,97},{65,1},{97,33},{2,66}... | collective-permute-start | bytes 3145736 | tf_op jit(solution)/shard_map/ppermute | solution.py:32
  6.0 1.2 copy-done.3
  7.3 5.9 %own_forward.1 = (bf16[2,3,32,1024]{3,2,1,0:T(8,128)(2,1)S(1)}, bf16[2,3,32,1024]{3,2,1,0:T(8,128)(2,1)S(1)}, f32[2,3,32,1024]{3,2,1,0:T(8,128)S(1)}, f32[2,3,32,1024]{3,2,1,0:T(8,128)S(1)}) custom-call(s32[3]{0:T(128)S(1)} %pad_add_fusion.idx, bf16[2,256,1024]{2,1,0:T(8,128)(2,1)S(1)} %copy-done.3, bf16[1024,1024]{1,0:T(8,128)(2,1)} %wg.15, ...), custom_call_target="tpu_custom_call" | custom-call | flops 1610612736 | bytes 11534336 | tf_op jit(solution)/shard_map/own_forward/pallas_call | solution.py:165
  13.2 2.0 %collective-permute-start = (bf16[2,3,32,1024]{3,2,1,0:T(8,128)(2,1)S(1)}, bf16[2,3,32,1024]{3,2,1,0:T(8,128)(2,1)S(1)}, u32[]{:S(2)}, u32[]{:S(2)}) collective-permute-start(bf16[2,3,32,1024]{3,2,1,0:T(8,128)(2,1)S(1)} %get-tuple-element.98), channel_id=1, source_target_pairs={{0,8},{4,12},{8,16},{12,20},{16,24},{20,28},{24,0},{28,4},{1,9},{5... | collective-permute-start | bytes 1179656 | tf_op jit(solution)/shard_map/ppermute | solution.py:27
  15.2 2.2 %collective-permute-start.1 = (bf16[2,3,32,1024]{3,2,1,0:T(8,128)(2,1)S(1)}, bf16[2,3,32,1024]{3,2,1,0:T(8,128)(2,1)S(1)}, u32[]{:S(2)}, u32[]{:S(2)}) collective-permute-start(bf16[2,3,32,1024]{3,2,1,0:T(8,128)(2,1)S(1)} %get-tuple-element.99), channel_id=1, source_target_pairs={{0,24},{4,28},{8,0},{12,4},{16,8},{20,12},{24,16},{28,20},{1,25},{... | collective-permute-start | bytes 1179656 | tf_op jit(solution)/shard_map/ppermute | solution.py:27
  17.4 3.2 %forward.1 = (bf16[2,3,32,1024]{3,2,1,0:T(8,128)(2,1)S(1)}, bf16[2,3,32,1024]{3,2,1,0:T(8,128)(2,1)S(1)}, f32[2,3,32,1024]{3,2,1,0:T(8,128)S(1)}, f32[2,3,32,1024]{3,2,1,0:T(8,128)S(1)}) custom-call(s32[3]{0:T(128)S(1)} %pad_add_fusion.idx, bf16[2,256,1024]{2,1,0:T(8,128)(2,1)S(1)} %collective-permute-done.2.m.m1.refs_1_, bf16[1024,1024]{1,0:T(8,128)(2,1)S(1)} %copy-done, ...), custom_call_target="tpu_custom_call" | custom-call | flops 1610612736 | bytes 5242880 | tf_op jit(solution)/shard_map/forward/pallas_call | solution.py:109
  20.7 3.2 %collective-permute-start.4 = (bf16[2,3,32,1024]{3,2,1,0:T(8,128)(2,1)S(1)}, bf16[2,3,32,1024]{3,2,1,0:T(8,128)(2,1)S(1)}, u32[]{:S(2)}, u32[]{:S(2)}) collective-permute-start(bf16[2,3,32,1024]{3,2,1,0:T(8,128)(2,1)S(1)} %get-tuple-element.103), channel_id=1, source_target_pairs={{0,24},{4,28},{8,0},{12,4},{16,8},{20,12},{24,16},{28,20},{1,25},{... | collective-permute-start | bytes 1179656 | tf_op jit(solution)/shard_map/ppermute | solution.py:27
  23.9 3.3 %collective-permute-done.refs_1_ = bf16[2,3,32,1024]{3,2,1,0:T(8,128)(2,1)S(1)} collective-permute-done((bf16[2,3,32,1024]{3,2,1,0:T(8,128)(2,1)S(1)}, bf16[2,3,32,1024]{3,2,1,0:T(8,128)(2,1)S(1)}, u32[]{:S(2)}, u32[]{:S(2)}) %collective-permute-start) | collective-permute-done | bytes 393248 | tf_op jit(solution)/shard_map/ppermute | solution.py:27
  27.2 8.0 %collective-permute-done.3.refs_4_ = bf16[2,3,32,1024]{3,2,1,0:T(8,128)(2,1)S(1)} collective-permute-done((bf16[2,3,32,1024]{3,2,1,0:T(8,128)(2,1)S(1)}, bf16[2,3,32,1024]{3,2,1,0:T(8,128)(2,1)S(1)}, u32[]{:S(2)}, u32[]{:S(2)}) %collective-permute-start.3) | collective-permute-done | bytes 393248 | tf_op jit(solution)/shard_map/ppermute | solution.py:27
  35.5 1.3 collective-permute-start.5
  36.8 2.0 %collective-permute-start.6 = (bf16[3,2,32,1024]{3,2,1,0:T(8,128)(2,1)S(1)}, bf16[3,2,32,1024]{3,2,1,0:T(8,128)(2,1)S(1)}, u32[]{:S(2)}, u32[]{:S(2)}) collective-permute-start(bf16[3,2,32,1024]{3,2,1,0:T(8,128)(2,1)S(1)} %get-tuple-element.107), channel_id=1, source_target_pairs={{0,24},{4,28},{8,0},{12,4},{16,8},{20,12},{24,16},{28,20},{1,25},{... | collective-permute-start | bytes 1179656 | tf_op jit(solution)/shard_map/ppermute | solution.py:27
  38.8 3.2 %cross_forward.2 = (bf16[2,2,32,1024]{3,2,1,0:T(8,128)(2,1)S(1)}, bf16[2,2,32,1024]{3,2,1,0:T(8,128)(2,1)S(1)}, f32[2,2,32,1024]{3,2,1,0:T(8,128)S(1)}, f32[2,2,...) custom-call(s32[3]{0:T(128)S(1)} %pad_add_fusion.idx, ...), custom_call_target="tpu_custom_call" | custom-call | flops 1610612736 | bytes 5242880 | tf_op jit(solution)/shard_map/cross_forward/pallas_call | solution.py:262
  42.6 3.2 %cross_forward.3 = (bf16[2,2,32,1024]{3,2,1,0:T(8,128)(2,1)S(1)}, bf16[2,2,32,1024]{3,2,1,0:T(8,128)(2,1)S(1)}, f32[2,2,32,1024]{3,2,1,0:T(8,128)S(1)}, f32[2,2,...) custom-call(s32[3]{0:T(128)S(1)} %pad_add_fusion.idx, ...), custom_call_target="tpu_custom_call" | custom-call | flops 1610612736 | bytes 5242880 | tf_op jit(solution)/shard_map/cross_forward/pallas_call | solution.py:262
  45.8 1.5 %collective-permute-start.15 = (bf16[4,32,1024]{2,1,0:T(8,128)(2,1)S(1)}, bf16[4,32,1024]{2,1,0:T(8,128)(2,1)S(1)}, u32[]{:S(2)}, u32[]{:S(2)}) collective-permute-start(bf16[4,32,1024]{2,1,0:T(8,128)(2,1)S(1)} %get-tuple-element.121), channel_id=1, source_target_pairs={{0,4},{4,0},{8,12},{12,8},{16,20},{20,16},{24,28},{28,24},{1,5},{5... | collective-permute-start | bytes 786440 | tf_op jit(solution)/shard_map/ppermute | solution.py:27
  49.3 1.3 collective-permute-start.10
  50.7 1.9 %collective-permute-start.11 = (bf16[2,2,32,1024]{3,2,1,0:T(8,128)(2,1)S(1)}, bf16[2,2,32,1024]{3,2,1,0:T(8,128)(2,1)S(1)}, u32[]{:S(2)}, u32[]{:S(2)}) collective-permute-start(bf16[2,2,32,1024]{3,2,1,0:T(8,128)(2,1)S(1)} %get-tuple-element.110), channel_id=1, source_target_pairs={{0,24},{4,28},{8,0},{12,4},{16,8},{20,12},{24,16},{28,20},{1,25},{... | collective-permute-start | bytes 786440 | tf_op jit(solution)/shard_map/ppermute | solution.py:27
  52.7 4.1 %collective-permute-done.15.got1 = bf16[4,32,1024]{2,1,0:T(8,128)(2,1)S(1)} collective-permute-done((bf16[4,32,1024]{2,1,0:T(8,128)(2,1)S(1)}, bf16[4,32,1024]{2,1,0:T(8,128)(2,1)S(1)}, u32[]{:S(2)}, u32[]{:S(2)}) %collective-permute-start.15) | collective-permute-done | bytes 262176 | tf_op jit(solution)/shard_map/ppermute | solution.py:27
  56.8 1.8 %collective-permute-start.13 = (bf16[2,2,32,1024]{3,2,1,0:T(8,128)(2,1)S(1)}, bf16[2,2,32,1024]{3,2,1,0:T(8,128)(2,1)S(1)}, u32[]{:S(2)}, u32[]{:S(2)}) collective-permute-start(bf16[2,2,32,1024]{3,2,1,0:T(8,128)(2,1)S(1)} %get-tuple-element.113), channel_id=1, source_target_pairs={{0,24},{4,28},{8,0},{12,4},{16,8},{20,12},{24,16},{28,20},{1,25},{... | collective-permute-start | bytes 786440 | tf_op jit(solution)/shard_map/ppermute | solution.py:27
  59.9 3.1 %collective-permute-start.17 = (bf16[2,32,1024]{2,1,0:T(8,128)(2,1)S(1)}, bf16[2,32,1024]{2,1,0:T(8,128)(2,1)S(1)}, u32[]{:S(2)}, u32[]{:S(2)}) collective-permute-start(bf16[2,32,1024]{2,1,0:T(8,128)(2,1)S(1)} %get-tuple-element.126), channel_id=1, source_target_pairs={{0,24},{4,28},{8,0},{12,4},{16,8},{20,12},{24,16},{28,20},{1,25},{... | collective-permute-start | bytes 393224 | tf_op jit(solution)/shard_map/ppermute | solution.py:27
  63.0 2.2 %collective-permute-done.12.refs_4_ = bf16[2,2,32,1024]{3,2,1,0:T(8,128)(2,1)S(1)} collective-permute-done((bf16[2,2,32,1024]{3,2,1,0:T(8,128)(2,1)S(1)}, bf16[2,2,32,1024]{3,2,1,0:T(8,128)(2,1)S(1)}, u32[]{:S(2)}, u32[]{:S(2)}) %collective-permute-start.12) | collective-permute-done | bytes 262176 | tf_op jit(solution)/shard_map/ppermute | solution.py:27
  65.2 1.4 collective-permute-done.16.refs_7_
  67.9 2.2 %collective-permute-start.19 = (bf16[5,32,1024]{2,1,0:T(8,128)(2,1)S(1)}, bf16[5,32,1024]{2,1,0:T(8,128)(2,1)S(1)}, u32[]{:S(2)}, u32[]{:S(2)}) collective-permute-start(bf16[5,32,1024]{2,1,0:T(8,128)(2,1)S(1)} %get-tuple-element.134), channel_id=1, source_target_pairs={{0,24},{4,28},{8,0},{12,4},{16,8},{20,12},{24,16},{28,20},{1,25},{... | collective-permute-start | bytes 983048 | tf_op jit(solution)/shard_map/ppermute | solution.py:27
  70.1 2.6 %collective-permute-done.9.across = bf16[2,3,2,32,1024]{4,3,2,1,0:T(8,128)(2,1)S(1)} collective-permute-done((bf16[2,3,2,32,1024]{4,3,2,1,0:T(8,128)(2,1)S(1)}, bf16[2,3,2,32,1024]{4,3,2,1,0:T(8,128)(2,1)S(1)}, u32[]{:S(2)}, u32[]{:S(2)}) %collective-permute-start.9) | collective-permute-done | bytes 786464 | tf_op jit(solution)/shard_map/ppermute | solution.py:27
  73.0 3.1 %collective-permute-done.18.refs_9_ = bf16[5,32,1024]{2,1,0:T(8,128)(2,1)S(1)} collective-permute-done((bf16[5,32,1024]{2,1,0:T(8,128)(2,1)S(1)}, bf16[5,32,1024]{2,1,0:T(8,128)(2,1)S(1)}, u32[]{:S(2)}, u32[]{:S(2)}) %collective-permute-start.18) | collective-permute-done | bytes 327712 | tf_op jit(solution)/shard_map/ppermute | solution.py:27
  77.2 2.3 %collective-permute-start.20 = (bf16[10,32,1024]{2,1,0:T(8,128)(2,1)S(1)}, bf16[10,32,1024]{2,1,0:T(8,128)(2,1)S(1)}, u32[]{:S(2)}, u32[]{:S(2)}) collective-permute-start(bf16[10,32,1024]{2,1,0:T(8,128)(2,1)S(1)} %get-tuple-element.139.here.refs_4_), channel_id=1, source_target_pairs={{0,24},{4,28},{8,0},{12,4},{16,8},{20,12},{24,16},{28,20},{1,25},{... | collective-permute-start | bytes 1966088 | tf_op jit(solution)/shard_map/ppermute | solution.py:27
  79.7 1.5 %collective-permute-start.24 = (bf16[10,32,1024]{2,1,0:T(8,128)(2,1)S(1)}, bf16[10,32,1024]{2,1,0:T(8,128)(2,1)S(1)}, u32[]{:S(2)}, u32[]{:S(2)}) collective-permute-start(bf16[10,32,1024]{2,1,0:T(8,128)(2,1)S(1)} %get-tuple-element.145), channel_id=1, source_target_pairs={{0,4},{4,0},{8,12},{12,8},{16,20},{20,16},{24,28},{28,24},{1,5},{5... | collective-permute-start | bytes 1966088 | tf_op jit(solution)/shard_map/ppermute | solution.py:27
  81.3 10.4 %collective-permute-done.21.minus1 = bf16[10,32,1024]{2,1,0:T(8,128)(2,1)S(1)} collective-permute-done((bf16[10,32,1024]{2,1,0:T(8,128)(2,1)S(1)}, bf16[10,32,1024]{2,1,0:T(8,128)(2,1)S(1)}, u32[]{:S(2)}, u32[]{:S(2)}) %collective-permute-start.21) | collective-permute-done | bytes 655392 | tf_op jit(solution)/shard_map/ppermute | solution.py:27
  91.8 3.3 %collective-permute-start.23 = (bf16[5,32,1024]{2,1,0:T(8,128)(2,1)S(1)}, bf16[5,32,1024]{2,1,0:T(8,128)(2,1)S(1)}, u32[]{:S(2)}, u32[]{:S(2)}) collective-permute-start(bf16[5,32,1024]{2,1,0:T(8,128)(2,1)S(1)} %slice.17), channel_id=1, source_target_pairs={{0,24},{4,28},{8,0},{12,4},{16,8},{20,12},{24,16},{28,20},{1,25},{... | collective-permute-start | bytes 983048 | tf_op jit(solution)/shard_map/ppermute | solution.py:27
  95.5 3.2 %collective-permute-start.30 = (bf16[10,32,1024]{2,1,0:T(8,128)(2,1)S(1)}, bf16[10,32,1024]{2,1,0:T(8,128)(2,1)S(1)}, u32[]{:S(2)}, u32[]{:S(2)}) collective-permute-start(bf16[10,32,1024]{2,1,0:T(8,128)(2,1)S(1)} %get-tuple-element.184.here.refs_8_), channel_id=1, source_target_pairs={{0,24},{4,28},{8,0},{12,4},{16,8},{20,12},{24,16},{28,20},{1,25},{... | collective-permute-start | bytes 1966088 | tf_op jit(solution)/shard_map/ppermute | solution.py:27
  98.7 4.9 %collective-permute-done.22.far_a = bf16[5,32,1024]{2,1,0:T(8,128)(2,1)S(1)} collective-permute-done((bf16[5,32,1024]{2,1,0:T(8,128)(2,1)S(1)}, bf16[5,32,1024]{2,1,0:T(8,128)(2,1)S(1)}, u32[]{:S(2)}, u32[]{:S(2)}) %collective-permute-start.22) | collective-permute-done | bytes 327712 | tf_op jit(solution)/shard_map/ppermute | solution.py:27
  103.6 2.6 %their_grad.2 = (bf16[256,1024]{1,0:T(8,128)(2,1)S(1)}, bf16[2,512,1024]{2,1,0:T(8,128)(2,1)S(1)}, bf16[3,2,32,1024]{3,2,1,0:T(8,128)(2,1)S(1)}) custom-call(s32[3]{0:T(128)S(1)} %pad_add_fusion.idx, bf16[10,32,1024]{2,1,0:T(8,128)(2,1)S(1)} %get-tuple-element.139.here.refs_4_, bf16[10,32,1024]{2,1,0:T(8,128)(2,1)S(1)} %collective-permute-done.20.plus1, ...), custom_call_target="tpu_custom_call" | custom-call | flops 1073741824 | bytes 10485760 | tf_op jit(solution)/shard_map/their_grad/pallas_call | solution.py:479
  106.3 1.6 %collective-permute-start.33 = (bf16[3,2,32,1024]{3,2,1,0:T(8,128)(2,1)S(1)}, bf16[3,2,32,1024]{3,2,1,0:T(8,128)(2,1)S(1)}, u32[]{:S(2)}, u32[]{:S(2)}) collective-permute-start(bf16[3,2,32,1024]{3,2,1,0:T(8,128)(2,1)S(1)} %get-tuple-element.160.refs_6_), channel_id=1, source_target_pairs={{0,4},{4,0},{8,12},{12,8},{16,20},{20,16},{24,28},{28,24},{1,5},{5... | collective-permute-start | bytes 1179656 | tf_op jit(solution)/shard_map/ppermute | solution.py:27
  107.9 1.9 %my_grad.2.mine = f32[256,1024]{1,0:T(8,128)S(1)} custom-call(bf16[2,512,1024]{2,1,0:T(8,128)(2,1)S(1)} %get-tuple-element.150.acts, bf16[1024,1024]{1,0:T(8,128)(2,1)S(1)} %copy-done, bf16[1024,1024]{1,0:T(8,128)(2,1)S(1)} %copy-done.1), custom_call_target="tpu_custom_call" | custom-call | flops 1073741824 | bytes 10485760 | tf_op jit(solution)/shard_map/my_grad/pallas_call | solution.py:501
  109.8 3.2 %part_grads.1 = (f32[1024,1024]{1,0:T(8,128)S(1)}, f32[1024,1024]{1,0:T(8,128)S(1)}) custom-call(bf16[2,256,1024]{2,1,0:T(8,128)(2,1)S(1)} %copy-done.3, bf16[2,256,1024]{2,1,0:T(8,128)(2,1)S(1)} %collective-permute-done.2.m.m1.refs_1_, bf16[2,512,1024]{2,1,0:T(8,128)(2,1)S(1)} %get-tuple-element.150.acts), custom_call_target="tpu_custom_call" | custom-call | flops 2147483648 | bytes 8388608 | tf_op jit(solution)/shard_map/part_grads/pallas_call | solution.py:565
  113.7 1.2 collective-permute-start.31
  114.9 2.3 %collective-permute-start.32 = (bf16[5,32,1024]{2,1,0:T(8,128)(2,1)S(1)}, bf16[5,32,1024]{2,1,0:T(8,128)(2,1)S(1)}, u32[]{:S(2)}, u32[]{:S(2)}) collective-permute-start(bf16[5,32,1024]{2,1,0:T(8,128)(2,1)S(1)} %slice.15), channel_id=1, source_target_pairs={{0,24},{4,28},{8,0},{12,4},{16,8},{20,12},{24,16},{28,20},{1,25},{... | collective-permute-start | bytes 983048 | tf_op jit(solution)/shard_map/ppermute | solution.py:27
  117.2 3.2 %collective-permute-start.26 = (bf16[64,1024]{1,0:T(8,128)(2,1)S(1)}, bf16[64,1024]{1,0:T(8,128)(2,1)S(1)}, u32[]{:S(2)}, u32[]{:S(2)}) collective-permute-start(bf16[64,1024]{1,0:T(8,128)(2,1)S(1)} %get-tuple-element.155), channel_id=1, source_target_pairs={{0,2},{1,3},{2,0},{3,1},{4,6},{5,7},{6,4},{7,5},{8,10},{9,11},{10,... | collective-permute-start | bytes 393224 | tf_op jit(solution)/shard_map/ppermute | solution.py:36
  121.1 2.6 %collective-permute-start.28 = (bf16[64,1024]{1,0:T(8,128)(2,1)S(1)}, bf16[64,1024]{1,0:T(8,128)(2,1)S(1)}, u32[]{:S(2)}, u32[]{:S(2)}) collective-permute-start(bf16[64,1024]{1,0:T(8,128)(2,1)S(1)} %get-tuple-element.157), channel_id=1, source_target_pairs={{0,3},{1,0},{2,1},{3,2},{4,7},{5,4},{6,5},{7,6},{8,11},{9,8},{10,9... | collective-permute-start | bytes 393224 | tf_op jit(solution)/shard_map/ppermute | solution.py:36
  123.7 1.3 collective-permute-done.26.a
  124.9 2.3 %collective-permute-done.27.b = bf16[64,1024]{1,0:T(8,128)(2,1)S(1)} collective-permute-done((bf16[64,1024]{1,0:T(8,128)(2,1)S(1)}, bf16[64,1024]{1,0:T(8,128)(2,1)S(1)}, u32[]{:S(2)}, u32[]{:S(2)}) %collective-permute-start.27) | collective-permute-done | bytes 131104 | tf_op jit(solution)/shard_map/ppermute | solution.py:36
  127.2 2.6 %their_grad.3 = (bf16[256,1024]{1,0:T(8,128)(2,1)S(1)}, bf16[2,512,1024]{2,1,0:T(8,128)(2,1)S(1)}, bf16[3,2,32,1024]{3,2,1,0:T(8,128)(2,1)S(1)}) custom-call(s32[3]{0:T(128)S(1)} %pad_add_fusion.idx, bf16[10,32,1024]{2,1,0:T(8,128)(2,1)S(1)} %get-tuple-element.184.here.refs_8_, bf16[10,32,1024]{2,1,0:T(8,128)(2,1)S(1)} %collective-permute-done.30.plus1, ...), custom_call_target="tpu_custom_call" | custom-call | flops 1073741824 | bytes 10485760 | tf_op jit(solution)/shard_map/their_grad/pallas_call | solution.py:479
  130.8 1.9 %my_grad.3.mine = f32[256,1024]{1,0:T(8,128)S(1)} custom-call(bf16[2,512,1024]{2,1,0:T(8,128)(2,1)S(1)} %get-tuple-element.174.acts, bf16[1024,1024]{1,0:T(8,128)(2,1)S(1)} %copy-done, bf16[1024,1024]{1,0:T(8,128)(2,1)S(1)} %copy-done.1), custom_call_target="tpu_custom_call" | custom-call | flops 1073741824 | bytes 10485760 | tf_op jit(solution)/shard_map/my_grad/pallas_call | solution.py:501
  133.3 1.9 %collective-permute-start.35 = (bf16[64,1024]{1,0:T(8,128)(2,1)S(1)}, bf16[64,1024]{1,0:T(8,128)(2,1)S(1)}, u32[]{:S(2)}, u32[]{:S(2)}) collective-permute-start(bf16[64,1024]{1,0:T(8,128)(2,1)S(1)} %get-tuple-element.171), channel_id=1, source_target_pairs={{0,2},{1,3},{2,0},{3,1},{4,6},{5,7},{6,4},{7,5},{8,10},{9,11},{10,... | collective-permute-start | bytes 393224 | tf_op jit(solution)/shard_map/ppermute | solution.py:36
  135.3 2.1 %collective-permute-start.36 = (bf16[64,1024]{1,0:T(8,128)(2,1)S(1)}, bf16[64,1024]{1,0:T(8,128)(2,1)S(1)}, u32[]{:S(2)}, u32[]{:S(2)}) collective-permute-start(bf16[64,1024]{1,0:T(8,128)(2,1)S(1)} %get-tuple-element.172), channel_id=1, source_target_pairs={{0,1},{1,2},{2,3},{3,0},{4,5},{5,6},{6,7},{7,4},{8,9},{9,10},{10,1... | collective-permute-start | bytes 393224 | tf_op jit(solution)/shard_map/ppermute | solution.py:36
  138.5 4.4 %in_grads.1 = (bf16[1024,1024]{1,0:T(8,128)(2,1)}, bf16[1024,1024]{1,0:T(8,128)(2,1)}) custom-call(bf16[2,256,1024]{2,1,0:T(8,128)(2,1)S(1)} %collective-permute-done.7.m.m0.refs_2_, bf16[2,256,1024]{2,1,0:T(8,128)(2,1)S(1)} %collective-permute-done.8.m.m1.refs_3_, bf16[2,512,1024]{2,1,0:T(8,128)(2,1)S(1)} %get-tuple-element.174.acts, ...), custom_call_target="tpu_custom_call" | custom-call | flops 2147483648 | bytes 8388608 | tf_op jit(solution)/shard_map/in_grads/pallas_call | solution.py:599
  143.8 2.0 %collective-permute-start.38 = (bf16[64,1024]{1,0:T(8,128)(2,1)S(1)}, bf16[64,1024]{1,0:T(8,128)(2,1)S(1)}, u32[]{:S(2)}, u32[]{:S(2)}) collective-permute-start(bf16[64,1024]{1,0:T(8,128)(2,1)S(1)} %owned.3), channel_id=1, source_target_pairs={{0,64},{32,96},{64,0},{96,32},{1,65},{33,97},{65,1},{97,33},{2,66}... | collective-permute-start | bytes 393224 | tf_op jit(solution)/shard_map/ppermute | solution.py:32
  145.8 4.6 %down_grad.1 = bf16[1024,1024]{1,0:T(8,128)(2,1)} custom-call(s32[3]{0:T(128)S(1)} %pad_add_fusion.idx, bf16[2,256,1024]{2,1,0:T(8,128)(2,1)S(1)} %copy-done.3, bf16[2,256,1024]{2,1,0:T(8,128)(2,1)S(1)} %collective-permute-done.2.m.m1.refs_1_, bf16[2,256,1024]{2,1,0:T(8,128)(2,1)S(1)} %collective-permute-done.7.m.m0.refs_2_, ...), custom_call_target="tpu_custom_call" | custom-call | flops 2147483648 | bytes 4194304 | tf_op jit(solution)/shard_map/down_grad/pallas_call | solution.py:644
  (69 shorter events, 13.6 us)
Async XLA Ops:
  2.8 14.6 %collective-permute-start.2 = (bf16[2,256,1024]{2,1,0:T(8,128)(2,1)}, bf16[2,256,1024]{2,1,0:T(8,128)(2,1)S(1)}, u32[]{:S(2)}, u32[]{:S(2)}) collective-permute-start(bf16[2,256,1024]{2,1,0:T(8,128)(2,1)} %scaled.1.m.m0.refs_0_), channel_id=1, source_target_pairs={{0,32},{32,0},{64,96},{96,64},{1,33},{33,1},{65,97},{97,65},{2,34}... | collective-permute-start | bytes 3145736 | tf_op jit(solution)/shard_map/ppermute | solution.py:32
  2.8 32.6 %collective-permute-start.7 = (bf16[2,256,1024]{2,1,0:T(8,128)(2,1)}, bf16[2,256,1024]{2,1,0:T(8,128)(2,1)S(1)}, u32[]{:S(2)}, u32[]{:S(2)}) collective-permute-start(bf16[2,256,1024]{2,1,0:T(8,128)(2,1)} %scaled.1.m.m0.refs_0_), channel_id=1, source_target_pairs={{0,64},{32,96},{64,0},{96,32},{1,65},{33,97},{65,1},{97,33},{2,66}... | collective-permute-start | bytes 3145736 | tf_op jit(solution)/shard_map/ppermute | solution.py:32
  6.0 1.2 copy-start.3
  7.3 10.1 %copy-start = (bf16[1024,1024]{1,0:T(8,128)(2,1)S(1)}, bf16[1024,1024]{1,0:T(8,128)(2,1)}, u32[]{:S(2)}) copy-start(bf16[1024,1024]{1,0:T(8,128)(2,1)} %wg.15) | copy-start | bytes 6291460
  7.3 10.1 %copy-start.1 = (bf16[1024,1024]{1,0:T(8,128)(2,1)S(1)}, bf16[1024,1024]{1,0:T(8,128)(2,1)}, u32[]{:S(2)}) copy-start(bf16[1024,1024]{1,0:T(8,128)(2,1)} %wu.15) | copy-start | bytes 6291460
  7.3 10.1 %copy-start.2 = (bf16[1024,1024]{1,0:T(8,128)(2,1)S(1)}, bf16[1024,1024]{1,0:T(8,128)(2,1)}, u32[]{:S(2)}) copy-start(bf16[1024,1024]{1,0:T(8,128)(2,1)} %wd.7) | copy-start | bytes 6291460
  13.2 14.0 %collective-permute-start = (bf16[2,3,32,1024]{3,2,1,0:T(8,128)(2,1)S(1)}, bf16[2,3,32,1024]{3,2,1,0:T(8,128)(2,1)S(1)}, u32[]{:S(2)}, u32[]{:S(2)}) collective-permute-start(bf16[2,3,32,1024]{3,2,1,0:T(8,128)(2,1)S(1)} %get-tuple-element.98), channel_id=1, source_target_pairs={{0,8},{4,12},{8,16},{12,20},{16,24},{20,28},{24,0},{28,4},{1,9},{5... | collective-permute-start | bytes 1179656 | tf_op jit(solution)/shard_map/ppermute | solution.py:27
  15.2 12.0 %collective-permute-start.1 = (bf16[2,3,32,1024]{3,2,1,0:T(8,128)(2,1)S(1)}, bf16[2,3,32,1024]{3,2,1,0:T(8,128)(2,1)S(1)}, u32[]{:S(2)}, u32[]{:S(2)}) collective-permute-start(bf16[2,3,32,1024]{3,2,1,0:T(8,128)(2,1)S(1)} %get-tuple-element.99), channel_id=1, source_target_pairs={{0,24},{4,28},{8,0},{12,4},{16,8},{20,12},{24,16},{28,20},{1,25},{... | collective-permute-start | bytes 1179656 | tf_op jit(solution)/shard_map/ppermute | solution.py:27
  20.6 14.6 %collective-permute-start.3 = (bf16[2,3,32,1024]{3,2,1,0:T(8,128)(2,1)S(1)}, bf16[2,3,32,1024]{3,2,1,0:T(8,128)(2,1)S(1)}, u32[]{:S(2)}, u32[]{:S(2)}) collective-permute-start(bf16[2,3,32,1024]{3,2,1,0:T(8,128)(2,1)S(1)} %get-tuple-element.102), channel_id=1, source_target_pairs={{0,8},{4,12},{8,16},{12,20},{16,24},{20,28},{24,0},{28,4},{1,9},{5... | collective-permute-start | bytes 1179656 | tf_op jit(solution)/shard_map/ppermute | solution.py:27
  20.7 14.5 %collective-permute-start.4 = (bf16[2,3,32,1024]{3,2,1,0:T(8,128)(2,1)S(1)}, bf16[2,3,32,1024]{3,2,1,0:T(8,128)(2,1)S(1)}, u32[]{:S(2)}, u32[]{:S(2)}) collective-permute-start(bf16[2,3,32,1024]{3,2,1,0:T(8,128)(2,1)S(1)} %get-tuple-element.103), channel_id=1, source_target_pairs={{0,24},{4,28},{8,0},{12,4},{16,8},{20,12},{24,16},{28,20},{1,25},{... | collective-permute-start | bytes 1179656 | tf_op jit(solution)/shard_map/ppermute | solution.py:27
  35.4 7.2 %collective-permute-start.8 = (bf16[2,256,1024]{2,1,0:T(8,128)(2,1)S(1)}, bf16[2,256,1024]{2,1,0:T(8,128)(2,1)S(1)}, u32[]{:S(2)}, u32[]{:S(2)}) collective-permute-start(bf16[2,256,1024]{2,1,0:T(8,128)(2,1)S(1)} %collective-permute-done.7.m.m0.refs_2_), channel_id=1, source_target_pairs={{0,32},{32,0},{64,96},{96,64},{1,33},{33,1},{65,97},{97,65},{2,34}... | collective-permute-start | bytes 3145736 | tf_op jit(solution)/shard_map/ppermute | solution.py:32
  35.5 12.8 %collective-permute-start.5 = (bf16[3,2,32,1024]{3,2,1,0:T(8,128)(2,1)S(1)}, bf16[3,2,32,1024]{3,2,1,0:T(8,128)(2,1)S(1)}, u32[]{:S(2)}, u32[]{:S(2)}) collective-permute-start(bf16[3,2,32,1024]{3,2,1,0:T(8,128)(2,1)S(1)} %get-tuple-element.106), channel_id=1, source_target_pairs={{0,8},{4,12},{8,16},{12,20},{16,24},{20,28},{24,0},{28,4},{1,9},{5... | collective-permute-start | bytes 1179656 | tf_op jit(solution)/shard_map/ppermute | solution.py:27
  36.8 11.5 %collective-permute-start.6 = (bf16[3,2,32,1024]{3,2,1,0:T(8,128)(2,1)S(1)}, bf16[3,2,32,1024]{3,2,1,0:T(8,128)(2,1)S(1)}, u32[]{:S(2)}, u32[]{:S(2)}) collective-permute-start(bf16[3,2,32,1024]{3,2,1,0:T(8,128)(2,1)S(1)} %get-tuple-element.107), channel_id=1, source_target_pairs={{0,24},{4,28},{8,0},{12,4},{16,8},{20,12},{24,16},{28,20},{1,25},{... | collective-permute-start | bytes 1179656 | tf_op jit(solution)/shard_map/ppermute | solution.py:27
  42.0 10.6 %collective-permute-start.14 = (bf16[4,32,1024]{2,1,0:T(8,128)(2,1)S(1)}, bf16[4,32,1024]{2,1,0:T(8,128)(2,1)S(1)}, u32[]{:S(2)}, u32[]{:S(2)}) collective-permute-start(bf16[4,32,1024]{2,1,0:T(8,128)(2,1)S(1)} %get-tuple-element.120), channel_id=1, source_target_pairs={{0,4},{4,0},{8,12},{12,8},{16,20},{20,16},{24,28},{28,24},{1,5},{5... | collective-permute-start | bytes 786440 | tf_op jit(solution)/shard_map/ppermute | solution.py:27
  45.8 11.0 %collective-permute-start.15 = (bf16[4,32,1024]{2,1,0:T(8,128)(2,1)S(1)}, bf16[4,32,1024]{2,1,0:T(8,128)(2,1)S(1)}, u32[]{:S(2)}, u32[]{:S(2)}) collective-permute-start(bf16[4,32,1024]{2,1,0:T(8,128)(2,1)S(1)} %get-tuple-element.121), channel_id=1, source_target_pairs={{0,4},{4,0},{8,12},{12,8},{16,20},{20,16},{24,28},{28,24},{1,5},{5... | collective-permute-start | bytes 786440 | tf_op jit(solution)/shard_map/ppermute | solution.py:27
  48.7 24.0 %collective-permute-start.9 = (bf16[2,3,2,32,1024]{4,3,2,1,0:T(8,128)(2,1)S(1)}, bf16[2,3,2,32,1024]{4,3,2,1,0:T(8,128)(2,1)S(1)}, u32[]{:S(2)}, u32[]{:S(2)}) collective-permute-start(bf16[2,3,2,32,1024]{4,3,2,1,0:T(8,128)(2,1)S(1)} %get-tuple-element.117), channel_id=1, source_target_pairs={{0,4},{4,0},{8,12},{12,8},{16,20},{20,16},{24,28},{28,24},{1,5},{5... | collective-permute-start | bytes 2359304 | tf_op jit(solution)/shard_map/ppermute | solution.py:27
  49.3 10.5 %collective-permute-start.10 = (bf16[2,2,32,1024]{3,2,1,0:T(8,128)(2,1)S(1)}, bf16[2,2,32,1024]{3,2,1,0:T(8,128)(2,1)S(1)}, u32[]{:S(2)}, u32[]{:S(2)}) collective-permute-start(bf16[2,2,32,1024]{3,2,1,0:T(8,128)(2,1)S(1)} %get-tuple-element.109), channel_id=1, source_target_pairs={{0,8},{4,12},{8,16},{12,20},{16,24},{20,28},{24,0},{28,4},{1,9},{5... | collective-permute-start | bytes 786440 | tf_op jit(solution)/shard_map/ppermute | solution.py:27
  50.7 9.2 %collective-permute-start.11 = (bf16[2,2,32,1024]{3,2,1,0:T(8,128)(2,1)S(1)}, bf16[2,2,32,1024]{3,2,1,0:T(8,128)(2,1)S(1)}, u32[]{:S(2)}, u32[]{:S(2)}) collective-permute-start(bf16[2,2,32,1024]{3,2,1,0:T(8,128)(2,1)S(1)} %get-tuple-element.110), channel_id=1, source_target_pairs={{0,24},{4,28},{8,0},{12,4},{16,8},{20,12},{24,16},{28,20},{1,25},{... | collective-permute-start | bytes 786440 | tf_op jit(solution)/shard_map/ppermute | solution.py:27
  52.6 12.6 %collective-permute-start.12 = (bf16[2,2,32,1024]{3,2,1,0:T(8,128)(2,1)S(1)}, bf16[2,2,32,1024]{3,2,1,0:T(8,128)(2,1)S(1)}, u32[]{:S(2)}, u32[]{:S(2)}) collective-permute-start(bf16[2,2,32,1024]{3,2,1,0:T(8,128)(2,1)S(1)} %get-tuple-element.112), channel_id=1, source_target_pairs={{0,8},{4,12},{8,16},{12,20},{16,24},{20,28},{24,0},{28,4},{1,9},{5... | collective-permute-start | bytes 786440 | tf_op jit(solution)/shard_map/ppermute | solution.py:27
  56.8 8.4 %collective-permute-start.13 = (bf16[2,2,32,1024]{3,2,1,0:T(8,128)(2,1)S(1)}, bf16[2,2,32,1024]{3,2,1,0:T(8,128)(2,1)S(1)}, u32[]{:S(2)}, u32[]{:S(2)}) collective-permute-start(bf16[2,2,32,1024]{3,2,1,0:T(8,128)(2,1)S(1)} %get-tuple-element.113), channel_id=1, source_target_pairs={{0,24},{4,28},{8,0},{12,4},{16,8},{20,12},{24,16},{28,20},{1,25},{... | collective-permute-start | bytes 786440 | tf_op jit(solution)/shard_map/ppermute | solution.py:27
  59.8 6.8 %collective-permute-start.16 = (bf16[2,32,1024]{2,1,0:T(8,128)(2,1)S(1)}, bf16[2,32,1024]{2,1,0:T(8,128)(2,1)S(1)}, u32[]{:S(2)}, u32[]{:S(2)}) collective-permute-start(bf16[2,32,1024]{2,1,0:T(8,128)(2,1)S(1)} %get-tuple-element.125), channel_id=1, source_target_pairs={{0,8},{4,12},{8,16},{12,20},{16,24},{20,28},{24,0},{28,4},{1,9},{5... | collective-permute-start | bytes 393224 | tf_op jit(solution)/shard_map/ppermute | solution.py:27
  59.9 6.7 %collective-permute-start.17 = (bf16[2,32,1024]{2,1,0:T(8,128)(2,1)S(1)}, bf16[2,32,1024]{2,1,0:T(8,128)(2,1)S(1)}, u32[]{:S(2)}, u32[]{:S(2)}) collective-permute-start(bf16[2,32,1024]{2,1,0:T(8,128)(2,1)S(1)} %get-tuple-element.126), channel_id=1, source_target_pairs={{0,24},{4,28},{8,0},{12,4},{16,8},{20,12},{24,16},{28,20},{1,25},{... | collective-permute-start | bytes 393224 | tf_op jit(solution)/shard_map/ppermute | solution.py:27
  66.8 9.4 %collective-permute-start.18 = (bf16[5,32,1024]{2,1,0:T(8,128)(2,1)S(1)}, bf16[5,32,1024]{2,1,0:T(8,128)(2,1)S(1)}, u32[]{:S(2)}, u32[]{:S(2)}) collective-permute-start(bf16[5,32,1024]{2,1,0:T(8,128)(2,1)S(1)} %get-tuple-element.133), channel_id=1, source_target_pairs={{0,8},{4,12},{8,16},{12,20},{16,24},{20,28},{24,0},{28,4},{1,9},{5... | collective-permute-start | bytes 983048 | tf_op jit(solution)/shard_map/ppermute | solution.py:27
  67.9 8.3 %collective-permute-start.19 = (bf16[5,32,1024]{2,1,0:T(8,128)(2,1)S(1)}, bf16[5,32,1024]{2,1,0:T(8,128)(2,1)S(1)}, u32[]{:S(2)}, u32[]{:S(2)}) collective-permute-start(bf16[5,32,1024]{2,1,0:T(8,128)(2,1)S(1)} %get-tuple-element.134), channel_id=1, source_target_pairs={{0,24},{4,28},{8,0},{12,4},{16,8},{20,12},{24,16},{28,20},{1,25},{... | collective-permute-start | bytes 983048 | tf_op jit(solution)/shard_map/ppermute | solution.py:27
  76.2 15.4 %collective-permute-start.21 = (bf16[10,32,1024]{2,1,0:T(8,128)(2,1)S(1)}, bf16[10,32,1024]{2,1,0:T(8,128)(2,1)S(1)}, u32[]{:S(2)}, u32[]{:S(2)}) collective-permute-start(bf16[10,32,1024]{2,1,0:T(8,128)(2,1)S(1)} %get-tuple-element.139.here.refs_4_), channel_id=1, source_target_pairs={{0,8},{4,12},{8,16},{12,20},{16,24},{20,28},{24,0},{28,4},{1,9},{5... | collective-permute-start | bytes 1966088 | tf_op jit(solution)/shard_map/ppermute | solution.py:27
  77.2 14.6 %collective-permute-start.20 = (bf16[10,32,1024]{2,1,0:T(8,128)(2,1)S(1)}, bf16[10,32,1024]{2,1,0:T(8,128)(2,1)S(1)}, u32[]{:S(2)}, u32[]{:S(2)}) collective-permute-start(bf16[10,32,1024]{2,1,0:T(8,128)(2,1)S(1)} %get-tuple-element.139.here.refs_4_), channel_id=1, source_target_pairs={{0,24},{4,28},{8,0},{12,4},{16,8},{20,12},{24,16},{28,20},{1,25},{... | collective-permute-start | bytes 1966088 | tf_op jit(solution)/shard_map/ppermute | solution.py:27
  79.7 15.4 %collective-permute-start.24 = (bf16[10,32,1024]{2,1,0:T(8,128)(2,1)S(1)}, bf16[10,32,1024]{2,1,0:T(8,128)(2,1)S(1)}, u32[]{:S(2)}, u32[]{:S(2)}) collective-permute-start(bf16[10,32,1024]{2,1,0:T(8,128)(2,1)S(1)} %get-tuple-element.145), channel_id=1, source_target_pairs={{0,4},{4,0},{8,12},{12,8},{16,20},{20,16},{24,28},{28,24},{1,5},{5... | collective-permute-start | bytes 1966088 | tf_op jit(solution)/shard_map/ppermute | solution.py:27
  91.7 11.9 %collective-permute-start.22 = (bf16[5,32,1024]{2,1,0:T(8,128)(2,1)S(1)}, bf16[5,32,1024]{2,1,0:T(8,128)(2,1)S(1)}, u32[]{:S(2)}, u32[]{:S(2)}) collective-permute-start(bf16[5,32,1024]{2,1,0:T(8,128)(2,1)S(1)} %slice.16), channel_id=1, source_target_pairs={{0,8},{4,12},{8,16},{12,20},{16,24},{20,28},{24,0},{28,4},{1,9},{5... | collective-permute-start | bytes 983048 | tf_op jit(solution)/shard_map/ppermute | solution.py:27
  91.8 11.8 %collective-permute-start.23 = (bf16[5,32,1024]{2,1,0:T(8,128)(2,1)S(1)}, bf16[5,32,1024]{2,1,0:T(8,128)(2,1)S(1)}, u32[]{:S(2)}, u32[]{:S(2)}) collective-permute-start(bf16[5,32,1024]{2,1,0:T(8,128)(2,1)S(1)} %slice.17), channel_id=1, source_target_pairs={{0,24},{4,28},{8,0},{12,4},{16,8},{20,12},{24,16},{28,20},{1,25},{... | collective-permute-start | bytes 983048 | tf_op jit(solution)/shard_map/ppermute | solution.py:27
  95.4 18.2 %collective-permute-start.29 = (bf16[10,32,1024]{2,1,0:T(8,128)(2,1)S(1)}, bf16[10,32,1024]{2,1,0:T(8,128)(2,1)S(1)}, u32[]{:S(2)}, u32[]{:S(2)}) collective-permute-start(bf16[10,32,1024]{2,1,0:T(8,128)(2,1)S(1)} %get-tuple-element.184.here.refs_8_), channel_id=1, source_target_pairs={{0,8},{4,12},{8,16},{12,20},{16,24},{20,28},{24,0},{28,4},{1,9},{5... | collective-permute-start | bytes 1966088 | tf_op jit(solution)/shard_map/ppermute | solution.py:27
  95.5 18.2 %collective-permute-start.30 = (bf16[10,32,1024]{2,1,0:T(8,128)(2,1)S(1)}, bf16[10,32,1024]{2,1,0:T(8,128)(2,1)S(1)}, u32[]{:S(2)}, u32[]{:S(2)}) collective-permute-start(bf16[10,32,1024]{2,1,0:T(8,128)(2,1)S(1)} %get-tuple-element.184.here.refs_8_), channel_id=1, source_target_pairs={{0,24},{4,28},{8,0},{12,4},{16,8},{20,12},{24,16},{28,20},{1,25},{... | collective-permute-start | bytes 1966088 | tf_op jit(solution)/shard_map/ppermute | solution.py:27
  106.2 6.8 %collective-permute-start.25 = (bf16[256,1024]{1,0:T(8,128)(2,1)S(1)}, bf16[256,1024]{1,0:T(8,128)(2,1)S(1)}, u32[]{:S(2)}, u32[]{:S(2)}) collective-permute-start(bf16[256,1024]{1,0:T(8,128)(2,1)S(1)} %get-tuple-element.151), channel_id=1, source_target_pairs={{0,32},{32,0},{64,96},{96,64},{1,33},{33,1},{65,97},{97,65},{2,34}... | collective-permute-start | bytes 1572872 | tf_op jit(solution)/shard_map/ppermute | solution.py:32
  106.3 14.8 %collective-permute-start.33 = (bf16[3,2,32,1024]{3,2,1,0:T(8,128)(2,1)S(1)}, bf16[3,2,32,1024]{3,2,1,0:T(8,128)(2,1)S(1)}, u32[]{:S(2)}, u32[]{:S(2)}) collective-permute-start(bf16[3,2,32,1024]{3,2,1,0:T(8,128)(2,1)S(1)} %get-tuple-element.160.refs_6_), channel_id=1, source_target_pairs={{0,4},{4,0},{8,12},{12,8},{16,20},{20,16},{24,28},{28,24},{1,5},{5... | collective-permute-start | bytes 1179656 | tf_op jit(solution)/shard_map/ppermute | solution.py:27
  113.7 13.5 %collective-permute-start.31 = (bf16[5,32,1024]{2,1,0:T(8,128)(2,1)S(1)}, bf16[5,32,1024]{2,1,0:T(8,128)(2,1)S(1)}, u32[]{:S(2)}, u32[]{:S(2)}) collective-permute-start(bf16[5,32,1024]{2,1,0:T(8,128)(2,1)S(1)} %slice.14), channel_id=1, source_target_pairs={{0,8},{4,12},{8,16},{12,20},{16,24},{20,28},{24,0},{28,4},{1,9},{5... | collective-permute-start | bytes 983048 | tf_op jit(solution)/shard_map/ppermute | solution.py:27
  114.9 12.3 %collective-permute-start.32 = (bf16[5,32,1024]{2,1,0:T(8,128)(2,1)S(1)}, bf16[5,32,1024]{2,1,0:T(8,128)(2,1)S(1)}, u32[]{:S(2)}, u32[]{:S(2)}) collective-permute-start(bf16[5,32,1024]{2,1,0:T(8,128)(2,1)S(1)} %slice.15), channel_id=1, source_target_pairs={{0,24},{4,28},{8,0},{12,4},{16,8},{20,12},{24,16},{28,20},{1,25},{... | collective-permute-start | bytes 983048 | tf_op jit(solution)/shard_map/ppermute | solution.py:27
  117.2 7.7 %collective-permute-start.26 = (bf16[64,1024]{1,0:T(8,128)(2,1)S(1)}, bf16[64,1024]{1,0:T(8,128)(2,1)S(1)}, u32[]{:S(2)}, u32[]{:S(2)}) collective-permute-start(bf16[64,1024]{1,0:T(8,128)(2,1)S(1)} %get-tuple-element.155), channel_id=1, source_target_pairs={{0,2},{1,3},{2,0},{3,1},{4,6},{5,7},{6,4},{7,5},{8,10},{9,11},{10,... | collective-permute-start | bytes 393224 | tf_op jit(solution)/shard_map/ppermute | solution.py:36
  120.4 6.8 %collective-permute-start.27 = (bf16[64,1024]{1,0:T(8,128)(2,1)S(1)}, bf16[64,1024]{1,0:T(8,128)(2,1)S(1)}, u32[]{:S(2)}, u32[]{:S(2)}) collective-permute-start(bf16[64,1024]{1,0:T(8,128)(2,1)S(1)} %get-tuple-element.156), channel_id=1, source_target_pairs={{0,1},{1,2},{2,3},{3,0},{4,5},{5,6},{6,7},{7,4},{8,9},{9,10},{10,1... | collective-permute-start | bytes 393224 | tf_op jit(solution)/shard_map/ppermute | solution.py:36
  121.1 6.1 %collective-permute-start.28 = (bf16[64,1024]{1,0:T(8,128)(2,1)S(1)}, bf16[64,1024]{1,0:T(8,128)(2,1)S(1)}, u32[]{:S(2)}, u32[]{:S(2)}) collective-permute-start(bf16[64,1024]{1,0:T(8,128)(2,1)S(1)} %get-tuple-element.157), channel_id=1, source_target_pairs={{0,3},{1,0},{2,1},{3,2},{4,7},{5,4},{6,5},{7,6},{8,11},{9,8},{10,9... | collective-permute-start | bytes 393224 | tf_op jit(solution)/shard_map/ppermute | solution.py:36
  129.8 2.9 %collective-permute-start.34 = (bf16[256,1024]{1,0:T(8,128)(2,1)S(1)}, bf16[256,1024]{1,0:T(8,128)(2,1)S(1)}, u32[]{:S(2)}, u32[]{:S(2)}) collective-permute-start(bf16[256,1024]{1,0:T(8,128)(2,1)S(1)} %get-tuple-element.168), channel_id=1, source_target_pairs={{0,32},{32,0},{64,96},{96,64},{1,33},{33,1},{65,97},{97,65},{2,34}... | collective-permute-start | bytes 1572872 | tf_op jit(solution)/shard_map/ppermute | solution.py:32
  129.9 15.9 %collective-permute-start.39 = (bf16[3,2,32,1024]{3,2,1,0:T(8,128)(2,1)S(1)}, bf16[3,2,32,1024]{3,2,1,0:T(8,128)(2,1)S(1)}, u32[]{:S(2)}, u32[]{:S(2)}) collective-permute-start(bf16[3,2,32,1024]{3,2,1,0:T(8,128)(2,1)S(1)} %get-tuple-element.186.refs_10_), channel_id=1, source_target_pairs={{0,4},{4,0},{8,12},{12,8},{16,20},{20,16},{24,28},{28,24},{1,5},{5... | collective-permute-start | bytes 1179656 | tf_op jit(solution)/shard_map/ppermute | solution.py:27
  133.3 9.6 %collective-permute-start.35 = (bf16[64,1024]{1,0:T(8,128)(2,1)S(1)}, bf16[64,1024]{1,0:T(8,128)(2,1)S(1)}, u32[]{:S(2)}, u32[]{:S(2)}) collective-permute-start(bf16[64,1024]{1,0:T(8,128)(2,1)S(1)} %get-tuple-element.171), channel_id=1, source_target_pairs={{0,2},{1,3},{2,0},{3,1},{4,6},{5,7},{6,4},{7,5},{8,10},{9,11},{10,... | collective-permute-start | bytes 393224 | tf_op jit(solution)/shard_map/ppermute | solution.py:36
  135.3 8.0 %collective-permute-start.36 = (bf16[64,1024]{1,0:T(8,128)(2,1)S(1)}, bf16[64,1024]{1,0:T(8,128)(2,1)S(1)}, u32[]{:S(2)}, u32[]{:S(2)}) collective-permute-start(bf16[64,1024]{1,0:T(8,128)(2,1)S(1)} %get-tuple-element.172), channel_id=1, source_target_pairs={{0,1},{1,2},{2,3},{3,0},{4,5},{5,6},{6,7},{7,4},{8,9},{9,10},{10,1... | collective-permute-start | bytes 393224 | tf_op jit(solution)/shard_map/ppermute | solution.py:36
  137.4 6.3 %collective-permute-start.37 = (bf16[64,1024]{1,0:T(8,128)(2,1)S(1)}, bf16[64,1024]{1,0:T(8,128)(2,1)S(1)}, u32[]{:S(2)}, u32[]{:S(2)}) collective-permute-start(bf16[64,1024]{1,0:T(8,128)(2,1)S(1)} %get-tuple-element.173), channel_id=1, source_target_pairs={{0,3},{1,0},{2,1},{3,2},{4,7},{5,4},{6,5},{7,6},{8,11},{9,8},{10,9... | collective-permute-start | bytes 393224 | tf_op jit(solution)/shard_map/ppermute | solution.py:36
  143.8 6.7 %collective-permute-start.38 = (bf16[64,1024]{1,0:T(8,128)(2,1)S(1)}, bf16[64,1024]{1,0:T(8,128)(2,1)S(1)}, u32[]{:S(2)}, u32[]{:S(2)}) collective-permute-start(bf16[64,1024]{1,0:T(8,128)(2,1)S(1)} %owned.3), channel_id=1, source_target_pairs={{0,64},{32,96},{64,0},{96,32},{1,65},{33,97},{65,1},{97,33},{2,66}... | collective-permute-start | bytes 393224 | tf_op jit(solution)/shard_map/ppermute | solution.py:32
